TPU v7x, 128 devices: a whole 4x4x4 slice. The times are simulated.
128 devices in a mesh: grp: 16 (over y_lo, z, core), tp: 8 (over x, y_hi).
Axes of the slice: x: 4, y: 4 (y_hi: 2, y_lo: 2; y = y_hi * 2 + y_lo), z: 4, core: 2. Of those that a mesh axis runs over, the one named last changes fastest.
Arguments:
- tokens: bfloat16 [2, 5120, 4096], P(None, 'grp', 'tp'), may hold values from -6 to 6
- norm_gain: float32 [4096], replicated, may hold values from 0.5 to 1.5
- up_master: float32 [4096, 16384], P(('grp', 'tp')), may hold values from -6 to 6
- up_gradient: bfloat16 [4096, 16384], P(('grp', 'tp')), may hold values from -0.59765625 to 0.59765625
- up_first: float32 [4096, 16384], P(('grp', 'tp')), may hold values from -0.18 to 0.18
- up_second: float32 [4096, 16384], P(('grp', 'tp')), may hold values from 0.0001 to 0.01
- down_master: float32 [16384, 4096], P(('grp', 'tp')), may hold values from -6 to 6
- down_gradient: bfloat16 [16384, 4096], P(('grp', 'tp')), may hold values from -0.59765625 to 0.59765625
- down_first: float32 [16384, 4096], P(('grp', 'tp')), may hold values from -0.18 to 0.18
- down_second: float32 [16384, 4096], P(('grp', 'tp')), may hold values from 0.0001 to 0.01
Outputs:
- up_updated: float32 [4096, 16384], P(('grp', 'tp'))
- down_updated: float32 [16384, 4096], P(('grp', 'tp'))
- decoded: bfloat16 [2, 5120, 4096], P(None, 'grp', 'tp')
All inputs are finite; a program needn't handle non-finite values.
Results may differ from a plain program's by a relative error of at most 0.015.
Values may be sent and summed in bfloat16 or wider, within the bound.
No kernel may reach another device: no remote copies, remote signals or barrier semaphores. Data moves between devices by JAX's collectives and lax.ppermute only.
A program may use at most 192 MiB of HBM per device.

v0:
```python
import functools

import jax
import jax.numpy as jnp
import numpy as np
from jax import lax
from jax.experimental import pallas as pl
from jax.experimental.pallas import tpu as pltpu
from jax.sharding import Mesh, PartitionSpec as P

learn_rate = 0.05
beta_one = 0.9
beta_two = 0.95
adam_eps = 1e-08
decay_rate = 0.1
step_index = 100
norm_eps = 1e-06

AXES = ("ylo", "z", "core", "x", "yhi")
SIZES = (2, 4, 2, 4, 2)
D, FF = 4096, 16384
CHUNKS = 4
ORDER = ((0, 0), (1, 0), (0, 3), (1, 3), (0, 1), (1, 1), (0, 2), (1, 2))
PLACE = {o: k for k, o in enumerate(ORDER)}
MIB = 1 << 20


def shifted(**steps):
    pairs = []
    for i, c in enumerate(np.ndindex(*SIZES)):
        d = dict(zip(AXES, c))
        for a, s in steps.items():
            d[a] = (d[a] + s) % SIZES[AXES.index(a)]
        pairs.append((i, int(np.ravel_multi_index(tuple(d[a] for a in AXES), SIZES))))
    return pairs


def send(v, **steps):
    return lax.ppermute(v, AXES, shifted(**steps))


ANY = pl.BlockSpec(memory_space=pl.ANY)


def after(v, *deps):
    return pl.pallas_call(
        lambda *refs: None,
        out_shape=jax.ShapeDtypeStruct(v.shape, v.dtype),
        in_specs=[ANY] * (1 + len(deps)),
        out_specs=ANY,
        input_output_aliases={0: 0},
        cost_estimate=pl.CostEstimate(flops=0, bytes_accessed=0, transcendentals=0),
        name="after",
    )(v, *deps)


def adamw(master, gradient, first_moment, second_moment):
    grad_float = gradient.astype(jnp.float32)
    first_new = beta_one * first_moment + (1.0 - beta_one) * grad_float
    second_new = beta_two * second_moment + (1.0 - beta_two) * grad_float * grad_float
    corr_one = 1.0 - beta_one**step_index
    corr_two = 1.0 - beta_two**step_index
    update = first_new * (1.0 / corr_one) / (jnp.sqrt(second_new * (1.0 / corr_two)) + adam_eps)
    return master - learn_rate * (update + decay_rate * master)


def params(limit=24, sem=None):
    return pltpu.CompilerParams(vmem_limit_bytes=limit * MIB)


def cost(flops, nbytes):
    return pl.CostEstimate(flops=int(flops) // 1000, bytes_accessed=int(nbytes) // 1000, transcendentals=0)


def up_kernel(s_ref, w_ref, g_ref, m_ref, v_ref, o_ref, mine_ref, other_ref):
    new = adamw(w_ref[...], g_ref[...], m_ref[...], v_ref[...])
    o_ref[...] = new
    cast = new.astype(jnp.bfloat16)

    def put(lo_ref, hi_ref):
        for t in range(8):
            lo_ref[t] = cast[:, t * 128 : (t + 1) * 128]
            hi_ref[t] = cast[:, 1024 + t * 128 : 1024 + (t + 1) * 128]

    @pl.when(s_ref[0] == 0)
    def _():
        put(mine_ref, other_ref)

    @pl.when(s_ref[0] == 1)
    def _():
        put(other_ref, mine_ref)


def up_step(core, w, g, m, v):
    spec = pl.BlockSpec((32, 2048), lambda i, s: (0, i))
    piece = pl.BlockSpec((8, 32, 128), lambda i, s: (0, 0, i))
    half = jax.ShapeDtypeStruct((8, 32, 1024), jnp.bfloat16)
    return pl.pallas_call(
        up_kernel,
        out_shape=(jax.ShapeDtypeStruct((32, FF), jnp.float32), half, half),
        grid_spec=pltpu.PrefetchScalarGridSpec(
            num_scalar_prefetch=1, grid=(8,), in_specs=[spec] * 4, out_specs=(spec, piece, piece)
        ),
        compiler_params=params(),
        cost_estimate=cost(30 * 32 * FF, 20 * 32 * FF),
        name="adam_up",
    )(core, w, g, m, v)


def down_kernel(w_ref, g_ref, m_ref, v_ref, o_ref, first_ref, rest_ref):
    new = adamw(w_ref[...], g_ref[...], m_ref[...], v_ref[...])
    o_ref[...] = new
    cast = new.astype(jnp.bfloat16)
    for t in range(8):
        for j in range(CHUNKS):
            piece = cast[:, t * 512 + j * 128 : t * 512 + (j + 1) * 128]
            if j == 0:
                first_ref[:, t * 128 : (t + 1) * 128] = piece
            else:
                rest_ref[j - 1, :, t * 128 : (t + 1) * 128] = piece


def down_step(w, g, m, v):
    spec = pl.BlockSpec((32, D), lambda i: (i, 0))
    chunk = pl.BlockSpec((32, 1024), lambda i: (i, 0))
    return pl.pallas_call(
        down_kernel,
        out_shape=(
            jax.ShapeDtypeStruct((128, D), jnp.float32),
            jax.ShapeDtypeStruct((128, 1024), jnp.bfloat16),
            jax.ShapeDtypeStruct((CHUNKS - 1, 128, 1024), jnp.bfloat16),
        ),
        grid=(4,),
        in_specs=[spec] * 4,
        out_specs=(spec, chunk, pl.BlockSpec((CHUNKS - 1, 32, 1024), lambda i: (0, i, 0))),
        compiler_params=params(),
        cost_estimate=cost(30 * 128 * D, 20 * 128 * D),
        name="adam_down",
    )(w, g, m, v)


RELS = tuple((dx, dy) for dx in range(4) for dy in range(2))


def route_kernel(s_ref, mine_ref, recv_ref, dep_ref, *out_refs):
    core, x, yhi = s_ref[0], s_ref[1], s_ref[2]
    for (dx, dy), out in zip(RELS, out_refs):
        t = lax.rem(x + dx, 4) * 2 + lax.rem(yhi + dy, 2)
        out[core] = mine_ref[t]
        out[1 - core] = recv_ref[t]


def route(scalars, mine, recv, dep):
    vm = pl.BlockSpec(memory_space=pltpu.VMEM)
    return pl.pallas_call(
        route_kernel,
        out_shape=(jax.ShapeDtypeStruct((2, 32, 1024), jnp.bfloat16),) * 8,
        in_specs=[pl.BlockSpec(memory_space=pltpu.SMEM), vm, vm, ANY],
        out_specs=(vm,) * 8,
        compiler_params=params(),
        cost_estimate=cost(0, 4 * MIB),
        name="route_up",
    )(scalars, mine, recv, dep)


def place_kernel(s_ref, *refs):
    x, yhi = s_ref[1], s_ref[2]
    out = refs[-1]
    for (dx, dy), piece in zip(RELS, refs):
        t = lax.rem(x - dx + 4, 4) * 2 + lax.rem(yhi + dy, 2)
        out[0, t] = piece[0]
        out[1, t] = piece[1]


def place(scalars, pieces, deps):
    vm = pl.BlockSpec(memory_space=pltpu.VMEM)
    out = pl.pallas_call(
        place_kernel,
        out_shape=jax.ShapeDtypeStruct((2, 8, 32, 1024), jnp.bfloat16),
        in_specs=[pl.BlockSpec(memory_space=pltpu.SMEM)] + [vm] * 8 + [ANY] * len(deps),
        out_specs=vm,
        compiler_params=params(),
        cost_estimate=cost(0, 4 * MIB),
        name="place_up",
    )(scalars, *pieces, *deps)
    return out.reshape(512, 1024)


def both_ways(up, down):
    return send(up, z=1), send(down, z=-1)


def norm_kernel(a_ref, b_ref, g_ref, *refs):
    out = refs[-1]
    total = 0.0
    for ref in (a_ref, b_ref):
        for i in range(4):
            f = ref[i].astype(jnp.float32)
            total += jnp.sum(f * f, axis=-1, keepdims=True)
    scale = lax.rsqrt(total * (1.0 / D) + norm_eps)
    for n, ref in enumerate((a_ref, b_ref)):
        for i in range(4):
            gain = g_ref[n * 4 + i : n * 4 + i + 1]
            out[n * 4 + i] = (ref[i].astype(jnp.float32) * scale * gain).astype(jnp.bfloat16)


def norm_of(feats_a, feats_b, gains, deps):
    rows = 160
    block = pl.BlockSpec((4, rows, 512), lambda i: (0, i, 0))
    return pl.pallas_call(
        norm_kernel,
        out_shape=jax.ShapeDtypeStruct((8, 640, 512), jnp.bfloat16),
        grid=(640 // rows,),
        in_specs=[block, block, pl.BlockSpec((8, 512), lambda i: (0, 0))] + [ANY] * len(deps),
        out_specs=pl.BlockSpec((8, rows, 512), lambda i: (0, i, 0)),
        compiler_params=params(32),
        cost_estimate=cost(8 * 640 * D, 10 * MIB),
        name="norm",
    )(feats_a, feats_b, gains, *deps)


def silu(u):
    return u / (1.0 + jnp.exp(-u))


def first_kernel(s_ref, *refs):
    lhs, ws, acc = refs[:6], refs[6:12], refs[12]
    for k, (a, w) in enumerate(zip(lhs, ws)):
        term = jnp.dot(a[0], w[...], preferred_element_type=jnp.float32)
        if k == 0:
            acc[...] = term
        else:
            acc[...] += term


def last_kernel(s_ref, acc_ref, *refs):
    lhs, ws, out, acc = refs[:2], refs[2:6], refs[6], refs[7]
    acc[...] = acc_ref[...]
    for n, w in enumerate(ws):
        a = lhs[n // 2][0, :, (n % 2) * 256 : (n % 2 + 1) * 256]
        acc[...] += jnp.dot(a, w[...], preferred_element_type=jnp.float32)
    for q in range(8):
        u = acc[:, q * 128 : (q + 1) * 128] * D ** (-0.5)
        at = pl.multiple_of(s_ref[8 + q] * 128, 128)
        out[:, pl.ds(at, 128)] = silu(u).astype(jnp.bfloat16)


def hidden_specs(places, ws):
    rows = 320
    lhs = [pl.BlockSpec((1, rows, 512), functools.partial(lambda k, i, s: (s[k], i, 0), k)) for k in places]
    return lhs, [pl.BlockSpec(w.shape, lambda i, s: (0, 0), pipeline_mode=pl.Buffered(1)) for w in ws]


def hidden_first(scalars, normed, ws):
    lhs, rhs = hidden_specs(range(6), ws)
    return pl.pallas_call(
        first_kernel,
        out_shape=jax.ShapeDtypeStruct((640, 1024), jnp.float32),
        grid_spec=pltpu.PrefetchScalarGridSpec(
            num_scalar_prefetch=1,
            grid=(2,),
            in_specs=lhs + rhs,
            out_specs=pl.BlockSpec((320, 1024), lambda i, s: (i, 0)),
        ),
        compiler_params=params(32),
        cost_estimate=cost(2 * 640 * 1024 * 3072, 14 * MIB),
        name="hidden_first",
    )(scalars, *([normed] * 6), *ws)


def hidden_last(scalars, acc, normed, ws):
    lhs, rhs = hidden_specs((6, 7), ws)
    block = pl.BlockSpec((320, 1024), lambda i, s: (i, 0))
    return pl.pallas_call(
        last_kernel,
        out_shape=jax.ShapeDtypeStruct((640, 1024), jnp.bfloat16),
        grid_spec=pltpu.PrefetchScalarGridSpec(
            num_scalar_prefetch=1,
            grid=(2,),
            in_specs=[block] + lhs + rhs,
            out_specs=block,
            scratch_shapes=[pltpu.VMEM((320, 1024), jnp.float32)],
        ),
        compiler_params=params(32),
        cost_estimate=cost(2 * 640 * 1024 * 1024, 8 * MIB),
        name="hidden_last",
    )(scalars, acc, normed, normed, *ws)


def partial_kernel(s_ref, own_ref, sib_ref, *refs):
    ws, (own_out, sib_out, w_ref) = refs[:5], refs[-3:]

    @pl.when(pl.program_id(0) == 0)
    def _():
        at = 0
        for w in ws:
            w_ref[at : at + w.shape[0]] = w[...]
            at += w.shape[0]

    for src, dst in ((sib_ref, sib_out), (own_ref, own_out)):
        term = jnp.dot(src[...], w_ref[...], preferred_element_type=jnp.float32)
        term = (term * FF ** (-0.5)).astype(jnp.bfloat16)
        for xi in range(4):
            dst[s_ref[xi]] = term[:, xi * 256 : (xi + 1) * 256]


def partial_of(scalars, own, sib, ws, deps):
    rows = 320
    block = pl.BlockSpec((rows, 1024), lambda i, s: (i, 0))
    out = pl.BlockSpec((4, rows, 256), lambda i, s: (0, i, 0))
    shape = jax.ShapeDtypeStruct((4, 640, 256), jnp.bfloat16)
    return pl.pallas_call(
        partial_kernel,
        out_shape=(shape, shape),
        grid_spec=pltpu.PrefetchScalarGridSpec(
            num_scalar_prefetch=1,
            grid=(640 // rows,),
            in_specs=[block, block]
            + [pl.BlockSpec(w.shape, lambda i, s: (0, 0), pipeline_mode=pl.Buffered(1)) for w in ws]
            + [ANY] * len(deps),
            out_specs=(out, out),
            scratch_shapes=[pltpu.VMEM((1024, 1024), jnp.bfloat16)],
        ),
        compiler_params=params(24),
        cost_estimate=cost(4 * 640 * 1024 * 1024, 8 * MIB),
        name="partial",
    )(scalars, own, sib, *ws, *deps)


def body(
    tokens,
    norm_gain,
    up_master,
    up_gradient,
    up_first,
    up_second,
    down_master,
    down_gradient,
    down_first,
    down_second,
):
    ylo, z, core, x, yhi = (lax.axis_index(a) for a in AXES)
    scalars = jnp.stack([core, x, yhi]).astype(jnp.int32)

    tokens_b = send(tokens, yhi=1)
    feats_a = lax.all_gather(tokens, "x", axis=0)

    up_updated, mine, other = up_step(scalars[:1], up_master, up_gradient, up_first, up_second)
    recv = send(other, core=1)
    down_updated, down_a, down_b = down_step(down_master, down_gradient, down_first, down_second)
    ylo_a, ylo_b = send(down_a, ylo=1), send(down_b, ylo=1)

    routed = route(scalars, mine, recv, down_updated)
    moved = [routed[0]] + [send(r, x=dx, yhi=dy) for (dx, dy), r in zip(RELS[1:], routed[1:])]
    st = jnp.concatenate([down_a, ylo_a], axis=0)
    low, high = both_ways(st, st)
    ws_down = [[st, low, high, *both_ways(low[:128], high[128:])]]

    u0 = place(scalars, moved, (low, high))
    feats_b = lax.all_gather(after(tokens_b, u0), "x", axis=0)

    u1 = send(u0, ylo=1)
    low0, high0 = both_ways(u0, u0)
    opp0 = both_ways(after(low0[:256], u1, ylo_b, *ws_down[0][3:]), high0[256:])
    low1, high1 = both_ways(u1, u1)
    opp1 = both_ways(low1[:256], high1[256:])

    gains = norm_gain.reshape(4, 2, 512)
    gains = jnp.concatenate(
        [lax.dynamic_index_in_dim(gains, k, 1, keepdims=False) for k in (yhi, 1 - yhi)], axis=0
    )
    normed = norm_of(feats_a.reshape(4, 640, 512), feats_b.reshape(4, 640, 512), gains, (low1, high1, *opp0))
    normed_sib = send(normed, core=1)

    q = jnp.stack([(ylo ^ dy) * 4 + lax.rem(z + dz, 4) for dy, dz in ORDER])
    slots = ((q % 2) ^ yhi) * 4 + q // 2
    table = jnp.array([[PLACE[(a, b)] for b in range(4)] for a in range(2)], jnp.int32)
    goes = jnp.stack([table[a ^ ylo, lax.rem(b - z + 4, 4)] for a in range(2) for b in range(4)])
    where = jnp.concatenate([slots, goes]).astype(jnp.int32)
    ws_up = (u0, u1, low0, low1, high0, high1)
    firsts = [hidden_first(where, n, ws_up) for n in (normed, normed_sib)]
    hidden_own, hidden_sib = (
        hidden_last(where, f, n, opp0 + opp1) for f, n in zip(firsts, (normed, normed_sib))
    )

    pieces, sums, reduced = [], [], []
    places = jnp.arange(4, dtype=jnp.int32)

    def fetch(j, first, second):
        st = after(jnp.concatenate([down_b[j - 1], ylo_b[j - 1]], axis=0), *first)
        low, high = both_ways(st, st)
        up, down = low[:128], high[128:]
        if second:
            up = after(up, *second)
        ws_down.append([st, low, high, *both_ways(up, down)])

    def multiply(j):
        direct = j % 2 == 1
        deps = sums[-1:]
        if j + 1 < CHUNKS:
            deps += ws_down[j + 1][1:3]
        if j >= 2:
            deps += reduced[j - 2 : j - 1]
        part, part_sib = partial_of(
            (places - x) % 4 if direct else places, hidden_own, hidden_sib, ws_down[j], deps
        )
        part_sib = send(part_sib, core=1)
        add = lambda a, b: (a.astype(jnp.float32) + b.astype(jnp.float32)).astype(jnp.bfloat16)
        if direct:
            terms = [add(part[d], part_sib[d]) for d in range(4)]
            sums.append(terms[1])
            terms = terms[:1] + [send(terms[d], x=d) for d in (1, 2, 3)]
            rows = sum(v.astype(jnp.float32) for v in terms).astype(jnp.bfloat16)
        else:
            both = add(part, part_sib)
            sums.append(both)
            rows = lax.psum_scatter(both, "x", scatter_dimension=0, tiled=True)[0]
        reduced.append(rows)
        keep = lax.dynamic_slice_in_dim(rows, yhi * 128, 128, 1)
        give = lax.dynamic_slice_in_dim(rows, (1 - yhi) * 128, 128, 1)
        pieces.append(add(keep, send(give, yhi=1)))

    fetch(1, (low1,), ())
    fetch(2, opp1, ())
    multiply(0)
    fetch(3, ws_down[1][3:], sums[:1])
    multiply(1)
    multiply(2)
    multiply(3)
    decoded = jnp.concatenate(pieces, axis=1).reshape(2, 320, 512)
    return (up_updated, down_updated, decoded)


def solution(mesh):
    fine = Mesh(mesh.devices.reshape(SIZES), AXES)
    grp, tp = AXES[:3], AXES[3:]
    flat = P(AXES, None)
    in_specs = (P(None, grp, tp), P()) + (flat,) * 8
    out_specs = (flat, flat, P(None, grp, tp))
    return jax.shard_map(body, mesh=fine, in_specs=in_specs, out_specs=out_specs, check_vma=False)
```

profile of v0, /device:TPU:0, one launch (start us, length us, event | category | flops | bytes accessed | tf_op | source)
XLA Modules:
  0.0 352.6 jit_solution(11163502238614487330)
XLA Ops:
  14.0 4.4 %adam_up.1 = (f32[32,16384]{1,0:T(8,128)}, bf16[8,32,1024]{2,1,0:T(8,128)(2,1)S(1)}, bf16[8,32,1024]{2,1,0:T(8,128)(2,1)S(1)}) custom-call(s32[1]{0:T(128)} %bitcast.s_ref, f32[32,16384]{1,0:T(8,128)S(1)} %copy-done.35, bf16[32,16384]{1,0:T(8,128)(2,1)S(1)} %copy-done.50, f32[32,16384]{1,0:T(8,128)S(1)} %copy-done.36, f32[32,16384]{1,0:T(8,128)S(1)} %copy-done.37), custom_call_target="tpu_custom_call" | custom-call | flops 15728 | bytes 10485 | tf_op jit(solution)/shard_map/adam_up/pallas_call | solution.py:98
  18.4 3.1 adam_down.1
  23.2 2.9 collective-permute-start
  32.8 2.2 collective-permute-start.11
  36.5 13.2 %collective-permute-done.2.refs_1_ = bf16[2,32,1024]{2,1,0:T(8,128)(2,1)S(1)} collective-permute-done((bf16[2,32,1024]{2,1,0:T(8,128)(2,1)S(1)}, bf16[2,32,1024]{2,1,0:T(8,128)(2,1)S(1)}, u32[]{:S(2)}, u32[]{:S(2)}) %collective-permute-start.2) | collective-permute-done | bytes 131104 | tf_op jit(solution)/shard_map/ppermute | solution.py:39
  51.2 2.7 collective-permute-start.5
  53.9 4.7 %collective-permute-done.4.refs_3_ = bf16[2,32,1024]{2,1,0:T(8,128)(2,1)S(1)} collective-permute-done((bf16[2,32,1024]{2,1,0:T(8,128)(2,1)S(1)}, bf16[2,32,1024]{2,1,0:T(8,128)(2,1)S(1)}, u32[]{:S(2)}, u32[]{:S(2)}) %collective-permute-start.4) | collective-permute-done | bytes 131104 | tf_op jit(solution)/shard_map/ppermute | solution.py:39
  61.7 5.8 %collective-permute-done.6.refs_5_ = bf16[2,32,1024]{2,1,0:T(8,128)(2,1)S(1)} collective-permute-done((bf16[2,32,1024]{2,1,0:T(8,128)(2,1)S(1)}, bf16[2,32,1024]{2,1,0:T(8,128)(2,1)S(1)}, u32[]{:S(2)}, u32[]{:S(2)}) %collective-permute-start.6) | collective-permute-done | bytes 131104 | tf_op jit(solution)/shard_map/ppermute | solution.py:39
  67.6 2.7 collective-permute-start.8
  70.3 4.7 %collective-permute-done.8.refs_7_ = bf16[2,32,1024]{2,1,0:T(8,128)(2,1)S(1)} collective-permute-done((bf16[2,32,1024]{2,1,0:T(8,128)(2,1)S(1)}, bf16[2,32,1024]{2,1,0:T(8,128)(2,1)S(1)}, u32[]{:S(2)}, u32[]{:S(2)}) %collective-permute-start.8) | collective-permute-done | bytes 131104 | tf_op jit(solution)/shard_map/ppermute | solution.py:39
  85.1 20.1 %collective-permute-done.12.refs_1_.refs_7_ = bf16[512,1024]{1,0:T(8,128)(2,1)} collective-permute-done((bf16[512,1024]{1,0:T(8,128)(2,1)S(1)}, bf16[512,1024]{1,0:T(8,128)(2,1)}, u32[]{:S(2)}, u32[]{:S(2)}) %collective-permute-start.12) | collective-permute-done | bytes 1048608 | tf_op jit(solution)/shard_map/ppermute | solution.py:39
  107.1 2.1 collective-permute-start.14
  111.2 5.9 %collective-permute-done.16.refs_2_ = bf16[3,128,1024]{2,1,0:T(8,128)(2,1)S(1)} collective-permute-done((bf16[3,128,1024]{2,1,0:T(8,128)(2,1)}, bf16[3,128,1024]{2,1,0:T(8,128)(2,1)S(1)}, u32[]{:S(2)}, u32[]{:S(2)}) %collective-permute-start.16) | collective-permute-done | bytes 786464 | tf_op jit(solution)/shard_map/ppermute | solution.py:39
  119.0 3.0 collective-permute-start.18
  123.9 8.6 %collective-permute-done.17.refs_3_ = bf16[128,1024]{1,0:T(8,128)(2,1)S(1)} collective-permute-done((bf16[128,1024]{1,0:T(8,128)(2,1)S(1)}, bf16[128,1024]{1,0:T(8,128)(2,1)S(1)}, u32[]{:S(2)}, u32[]{:S(2)}) %collective-permute-start.17) | collective-permute-done | bytes 262176 | tf_op jit(solution)/shard_map/ppermute | solution.py:39
  138.4 5.5 %collective-permute-done.19.refs_2_ = bf16[256,1024]{1,0:T(8,128)(2,1)} collective-permute-done((bf16[256,1024]{1,0:T(8,128)(2,1)}, bf16[256,1024]{1,0:T(8,128)(2,1)}, u32[]{:S(2)}, u32[]{:S(2)}) %collective-permute-start.19) | collective-permute-done | bytes 524320 | tf_op jit(solution)/shard_map/ppermute | solution.py:39
  143.9 2.3 collective-permute-done.21.refs_3_
  146.3 2.4 copy-done.29
  150.5 4.4 %norm.1.refs_0_.refs_1_.refs_2_.refs_3_.refs_4_.refs_5_ = bf16[8,640,512]{2,1,0:T(8,128)(2,1)} custom-call(bf16[4,640,512]{2,1,0:T(8,128)(2,1)S(1)} %bitcast.78, bf16[4,640,512]{2,1,0:T(8,128)(2,1)S(1)} %bitcast.79, f32[8,512]{1,0:T(8,128)S(1)} %pad_maximum_fusion.4.g_ref, bf16[512,1024]{1,0:T(8,128)(2,1)S(1)} %collective-permute-done.13.refs_0_.refs_9_.refs_1_, ...), custom_call_target="tpu_custom_call" | custom-call | flops 20971 | bytes 10485 | tf_op jit(solution)/shard_map/norm/pallas_call | solution.py:210
  163.8 2.9 collective-permute-start.26
  167.6 5.0 %concatenate.21.s_ref = s32[16]{0:T(128)S(1)} concatenate(s32[8]{0:T(128)S(1)} %fusion.18, s32[1]{0:T(128)} %bitcast.9, s32[1]{0:T(128)} %bitcast.10, s32[1]{0:T(128)} %bitcast.11, s32[1]{0:T(128)} %bitcast.12, s32[1]{0:T(128)} %bitcast.13, s32[1]{0:T(128)} %bitcast.14, s32[1]{0:T(128)} %bitcast.15, s32[1]{0:T(128)} %bitcast.16), dimensions={0} | concatenate | bytes 128 | tf_op jit(solution)/shard_map/concatenate | solution.py:379
  173.8 7.4 %hidden_first.2.acc_ref = f32[640,1024]{1,0:T(8,128)S(1)} custom-call(s32[16]{0:T(128)S(1)} %concatenate.21.s_ref, bf16[8,640,512]{2,1,0:T(8,128)(2,1)} %norm.1.refs_0_.refs_1_.refs_2_.refs_3_.refs_4_.refs_5_, bf16[8,640,512]{2,1,0:T(8,128)(2,1)} %norm.1.refs_0_.refs_1_.refs_2_.refs_3_.refs_4_.refs_5_, ...), custom_call_target="tpu_custom_call" | custom-call | flops 4026531 | bytes 14680 | tf_op jit(solution)/shard_map/hidden_first/pallas_call | solution.py:256
  181.3 4.8 %hidden_last.2.own_ref = bf16[640,1024]{1,0:T(8,128)(2,1)S(1)} custom-call(s32[16]{0:T(128)S(1)} %concatenate.21.s_ref, f32[640,1024]{1,0:T(8,128)S(1)} %hidden_first.2.acc_ref, bf16[8,640,512]{2,1,0:T(8,128)(2,1)} %norm.1.refs_0_.refs_1_.refs_2_.refs_3_.refs_4_.refs_5_, bf16[8,640,512]{2,1,0:T(8,128)(2,1)} %norm.1.refs_0_.refs_1_.refs_2_.refs_3_.refs_4_.refs_5_, ...), custom_call_target="tpu_custom_call" | custom-call | flops 1342177 | bytes 8388 | tf_op jit(solution)/shard_map/hidden_last/pallas_call | solution.py:274
  186.1 7.5 %hidden_first.3.acc_ref = f32[640,1024]{1,0:T(8,128)S(1)} custom-call(s32[16]{0:T(128)S(1)} %concatenate.21.s_ref, bf16[8,640,512]{2,1,0:T(8,128)(2,1)} %collective-permute-done.24.refs_0_.refs_1_.refs_2_.refs_3_.refs_4_.refs_5_, bf16[8,640,512]{2,1,0:T(8,128)(2,1)} %collective-permute-done.24.refs_0_.refs_1_.refs_2_.refs_3_.refs_4_.refs_5_, ...), custom_call_target="tpu_custom_call" | custom-call | flops 4026531 | bytes 14680 | tf_op jit(solution)/shard_map/hidden_first/pallas_call | solution.py:256
  193.7 4.8 %hidden_last.3.sib_ref = bf16[640,1024]{1,0:T(8,128)(2,1)S(1)} custom-call(s32[16]{0:T(128)S(1)} %concatenate.21.s_ref, f32[640,1024]{1,0:T(8,128)S(1)} %hidden_first.3.acc_ref, bf16[8,640,512]{2,1,0:T(8,128)(2,1)} %collective-permute-done.24.refs_0_.refs_1_.refs_2_.refs_3_.refs_4_.refs_5_, ...), custom_call_target="tpu_custom_call" | custom-call | flops 1342177 | bytes 8388 | tf_op jit(solution)/shard_map/hidden_last/pallas_call | solution.py:274
  198.5 4.9 %partial.4 = (bf16[4,640,256]{2,1,0:T(8,128)(2,1)S(1)}, bf16[4,640,256]{2,1,0:T(8,128)(2,1)S(1)}) custom-call(s32[4]{0:T(128)S(1)} %iota.7.s_ref, bf16[640,1024]{1,0:T(8,128)(2,1)S(1)} %hidden_last.2.own_ref, bf16[640,1024]{1,0:T(8,128)(2,1)S(1)} %hidden_last.3.sib_ref, bf16[256,1024]{1,0:T(8,128)(2,1)S(1)} %copy-done.44, bf16[256,1024]{1,0:T(8,128)(2,1)S(1)} %copy-done.26, ...), custom_call_target="tpu_custom_call" | custom-call | flops 2684354 | bytes 8388 | tf_op jit(solution)/shard_map/partial/pallas_call | solution.py:312
  203.6 3.0 collective-permute-done.27
  209.9 3.2 collective-permute-start.32
  215.3 3.3 collective-permute-start.30
  218.6 12.3 %collective-permute-done.29.refs_3_.refs_1_ = bf16[128,1024]{1,0:T(8,128)(2,1)S(1)} collective-permute-done((bf16[128,1024]{1,0:T(8,128)(2,1)S(1)}, bf16[128,1024]{1,0:T(8,128)(2,1)S(1)}, u32[]{:S(2)}, u32[]{:S(2)}) %collective-permute-start.29) | collective-permute-done | bytes 262176 | tf_op jit(solution)/shard_map/ppermute | solution.py:39
  232.6 5.9 %partial.5 = (bf16[4,640,256]{2,1,0:T(8,128)(2,1)S(1)}, bf16[4,640,256]{2,1,0:T(8,128)(2,1)}) custom-call(s32[4]{0:T(128)S(1)} %and_select_fusion.s_ref, bf16[640,1024]{1,0:T(8,128)(2,1)S(1)} %hidden_last.2.own_ref, bf16[640,1024]{1,0:T(8,128)(2,1)S(1)} %hidden_last.3.sib_ref, bf16[256,1024]{1,0:T(8,128)(2,1)S(1)} %copy-done.11, ...), custom_call_target="tpu_custom_call" | custom-call | flops 2684354 | bytes 8388 | tf_op jit(solution)/shard_map/partial/pallas_call | solution.py:312
  240.5 3.2 collective-permute-start.41
  244.9 3.5 collective-permute-start.39
  248.4 2.6 fusion.8
  251.0 5.7 %collective-permute-done.40.refs_6_.refs_1_ = bf16[256,1024]{1,0:T(8,128)(2,1)S(1)} collective-permute-done((bf16[256,1024]{1,0:T(8,128)(2,1)}, bf16[256,1024]{1,0:T(8,128)(2,1)S(1)}, u32[]{:S(2)}, u32[]{:S(2)}) %collective-permute-start.40) | collective-permute-done | bytes 524320 | tf_op jit(solution)/shard_map/ppermute | solution.py:39
  258.3 3.6 %collective-permute-done.38.refs_3_ = bf16[128,1024]{1,0:T(8,128)(2,1)S(1)} collective-permute-done((bf16[128,1024]{1,0:T(8,128)(2,1)S(1)}, bf16[128,1024]{1,0:T(8,128)(2,1)S(1)}, u32[]{:S(2)}, u32[]{:S(2)}) %collective-permute-start.38) | collective-permute-done | bytes 262176 | tf_op jit(solution)/shard_map/ppermute | solution.py:39
  270.4 4.7 %partial.6 = (bf16[4,640,256]{2,1,0:T(8,128)(2,1)S(1)}, bf16[4,640,256]{2,1,0:T(8,128)(2,1)}) custom-call(s32[4]{0:T(128)S(1)} %iota.9.s_ref, bf16[640,1024]{1,0:T(8,128)(2,1)S(1)} %hidden_last.2.own_ref, bf16[640,1024]{1,0:T(8,128)(2,1)S(1)} %hidden_last.3.sib_ref, bf16[256,1024]{1,0:T(8,128)(2,1)S(1)} %copy-done.13, bf16[256,1024]{1,0:T(8,128)(2,1)S(1)} %copy-done.16, ...), custom_call_target="tpu_custom_call" | custom-call | flops 2684354 | bytes 8388 | tf_op jit(solution)/shard_map/partial/pallas_call | solution.py:312
  276.3 3.9 %collective-permute-start.36 = (bf16[640,256]{1,0:T(8,128)(2,1)}, bf16[640,256]{1,0:T(8,128)(2,1)}, u32[]{:S(2)}, u32[]{:S(2)}) collective-permute-start(bf16[640,256]{1,0:T(8,128)(2,1)} %get-tuple-element.51), channel_id=1, source_target_pairs={{0,6},{1,7},{2,0},{3,1},{4,2},{5,3},{6,4},{7,5},{8,14},{9,15},{10,... | collective-permute-start | bytes 983048 | tf_op jit(solution)/shard_map/ppermute | solution.py:39
  281.7 2.2 collective-permute-start.45
  284.7 3.1 add_convert_fusion.refs_5_
  287.8 7.3 %collective-permute-done.36 = bf16[640,256]{1,0:T(8,128)(2,1)} collective-permute-done((bf16[640,256]{1,0:T(8,128)(2,1)}, bf16[640,256]{1,0:T(8,128)(2,1)}, u32[]{:S(2)}, u32[]{:S(2)}) %collective-permute-start.36) | collective-permute-done | bytes 327712 | tf_op jit(solution)/shard_map/ppermute | solution.py:39
  295.1 3.2 collective-permute-done.34
  301.0 5.8 %partial.7 = (bf16[4,640,256]{2,1,0:T(8,128)(2,1)S(1)}, bf16[4,640,256]{2,1,0:T(8,128)(2,1)}) custom-call(s32[4]{0:T(128)S(1)} %and_select_fusion.s_ref, bf16[640,1024]{1,0:T(8,128)(2,1)S(1)} %hidden_last.2.own_ref, bf16[640,1024]{1,0:T(8,128)(2,1)S(1)} %hidden_last.3.sib_ref, bf16[256,1024]{1,0:T(8,128)(2,1)S(1)} %copy-done.12, ...), custom_call_target="tpu_custom_call" | custom-call | flops 2684354 | bytes 8388 | tf_op jit(solution)/shard_map/partial/pallas_call | solution.py:312
  317.8 5.4 %collective-permute-done.49 = bf16[640,256]{1,0:T(8,128)(2,1)S(1)} collective-permute-done((bf16[640,256]{1,0:T(8,128)(2,1)S(1)}, bf16[640,256]{1,0:T(8,128)(2,1)S(1)}, u32[]{:S(2)}, u32[]{:S(2)}) %collective-permute-start.49) | collective-permute-done | bytes 327712 | tf_op jit(solution)/shard_map/ppermute | solution.py:39
  323.2 2.7 collective-permute-done.48
  325.9 5.8 %collective-permute-done.47 = bf16[640,256]{1,0:T(8,128)(2,1)S(1)} collective-permute-done((bf16[640,256]{1,0:T(8,128)(2,1)S(1)}, bf16[640,256]{1,0:T(8,128)(2,1)S(1)}, u32[]{:S(2)}, u32[]{:S(2)}) %collective-permute-start.47) | collective-permute-done | bytes 327712 | tf_op jit(solution)/shard_map/ppermute | solution.py:39
  337.7 3.9 %collective-permute-done.50 = bf16[640,128]{1,0:T(8,128)(2,1)S(1)} collective-permute-done((bf16[640,128]{1,0:T(8,128)(2,1)S(1)}, bf16[640,128]{1,0:T(8,128)(2,1)S(1)}, u32[]{:S(2)}, u32[]{:S(2)}) %collective-permute-start.50) | collective-permute-done | bytes 163872 | tf_op jit(solution)/shard_map/ppermute | solution.py:39
  341.7 2.5 collective-permute-done.43
  (261 shorter events, 102.7 us)
Async XLA Ops:
  7.2 139.1 %all-gather.5.cloned.1.call-start = ((), (), s32[]{:S(2)}) async-start(), calls=%async_computation.4 | async-start | bytes 3276800 | tf_op jit(solution)/shard_map/all_gather | solution.py:346
  7.9 138.4 %all-gather.7.cloned.1.call-start = ((), (), s32[]{:S(2)}) async-start(), calls=%async_computation.5 | async-start | bytes 3276800 | tf_op jit(solution)/shard_map/all_gather | solution.py:360
  21.6 9.1 %collective-permute-start.9 = (bf16[128,1024]{1,0:T(8,128)(2,1)S(1)}, bf16[128,1024]{1,0:T(8,128)(2,1)S(1)}, u32[]{:S(2)}, u32[]{:S(2)}) collective-permute-start(bf16[128,1024]{1,0:T(8,128)(2,1)S(1)} %get-tuple-element.37), channel_id=1, source_target_pairs={{0,64},{1,65},{2,66},{3,67},{4,68},{5,69},{6,70},{7,71},{8,72},{9,... | collective-permute-start | bytes 786440 | tf_op jit(solution)/shard_map/ppermute | solution.py:39
  23.2 53.7 %collective-permute-start = (bf16[2,320,512]{2,1,0:T(8,128)(2,1)S(1)}, bf16[2,320,512]{2,1,0:T(8,128)(2,1)S(1)}, u32[]{:S(2)}, u32[]{:S(2)}) collective-permute-start(bf16[2,320,512]{2,1,0:T(8,128)(2,1)S(1)} %copy-done.62), channel_id=1, source_target_pairs={{0,1},{1,0},{2,3},{3,2},{4,5},{5,4},{6,7},{7,6},{8,9},{9,8},{10,11... | collective-permute-start | bytes 1966088 | tf_op jit(solution)/shard_map/ppermute | solution.py:39
  28.5 21.2 %collective-permute-start.2 = (bf16[2,32,1024]{2,1,0:T(8,128)(2,1)S(1)}, bf16[2,32,1024]{2,1,0:T(8,128)(2,1)S(1)}, u32[]{:S(2)}, u32[]{:S(2)}) collective-permute-start(bf16[2,32,1024]{2,1,0:T(8,128)(2,1)S(1)} %get-tuple-element.30), channel_id=1, source_target_pairs={{0,1},{1,0},{2,3},{3,2},{4,5},{5,4},{6,7},{7,6},{8,9},{9,8},{10,11... | collective-permute-start | bytes 393224 | tf_op jit(solution)/shard_map/ppermute | solution.py:39
  30.7 44.2 %collective-permute-start.10 = (bf16[256,1024]{1,0:T(8,128)(2,1)S(1)}, bf16[256,1024]{1,0:T(8,128)(2,1)S(1)}, u32[]{:S(2)}, u32[]{:S(2)}) collective-permute-start(bf16[256,1024]{1,0:T(8,128)(2,1)S(1)} %constant_dynamic-update-slice_fusion.refs_0_), channel_id=1, source_target_pairs={{0,16},{1,17},{2,18},{3,19},{4,20},{5,21},{6,22},{7,23},{8,24},{9,... | collective-permute-start | bytes 1572872 | tf_op jit(solution)/shard_map/ppermute | solution.py:39
  32.8 42.2 %collective-permute-start.11 = (bf16[256,1024]{1,0:T(8,128)(2,1)S(1)}, bf16[256,1024]{1,0:T(8,128)(2,1)S(1)}, u32[]{:S(2)}, u32[]{:S(2)}) collective-permute-start(bf16[256,1024]{1,0:T(8,128)(2,1)S(1)} %constant_dynamic-update-slice_fusion.refs_0_), channel_id=1, source_target_pairs={{0,48},{1,49},{2,50},{3,51},{4,52},{5,53},{6,54},{7,55},{8,56},{9,... | collective-permute-start | bytes 1572872 | tf_op jit(solution)/shard_map/ppermute | solution.py:39
  35.0 16.2 %collective-permute-start.3 = (bf16[2,32,1024]{2,1,0:T(8,128)(2,1)S(1)}, bf16[2,32,1024]{2,1,0:T(8,128)(2,1)S(1)}, u32[]{:S(2)}, u32[]{:S(2)}) collective-permute-start(bf16[2,32,1024]{2,1,0:T(8,128)(2,1)S(1)} %get-tuple-element.31), channel_id=1, source_target_pairs={{0,2},{1,3},{2,4},{3,5},{4,6},{5,7},{6,0},{7,1},{8,10},{9,11},{10,... | collective-permute-start | bytes 393224 | tf_op jit(solution)/shard_map/ppermute | solution.py:39
  49.7 9.0 %collective-permute-start.4 = (bf16[2,32,1024]{2,1,0:T(8,128)(2,1)S(1)}, bf16[2,32,1024]{2,1,0:T(8,128)(2,1)S(1)}, u32[]{:S(2)}, u32[]{:S(2)}) collective-permute-start(bf16[2,32,1024]{2,1,0:T(8,128)(2,1)S(1)} %get-tuple-element.32), channel_id=1, source_target_pairs={{0,3},{1,2},{2,5},{3,4},{4,7},{5,6},{6,1},{7,0},{8,11},{9,10},{10,... | collective-permute-start | bytes 393224 | tf_op jit(solution)/shard_map/ppermute | solution.py:39
  51.2 9.4 %collective-permute-start.5 = (bf16[2,32,1024]{2,1,0:T(8,128)(2,1)S(1)}, bf16[2,32,1024]{2,1,0:T(8,128)(2,1)S(1)}, u32[]{:S(2)}, u32[]{:S(2)}) collective-permute-start(bf16[2,32,1024]{2,1,0:T(8,128)(2,1)S(1)} %get-tuple-element.33), channel_id=1, source_target_pairs={{0,4},{1,5},{2,6},{3,7},{4,0},{5,1},{6,2},{7,3},{8,12},{9,13},{10,... | collective-permute-start | bytes 393224 | tf_op jit(solution)/shard_map/ppermute | solution.py:39
  58.7 8.9 %collective-permute-start.6 = (bf16[2,32,1024]{2,1,0:T(8,128)(2,1)S(1)}, bf16[2,32,1024]{2,1,0:T(8,128)(2,1)S(1)}, u32[]{:S(2)}, u32[]{:S(2)}) collective-permute-start(bf16[2,32,1024]{2,1,0:T(8,128)(2,1)S(1)} %get-tuple-element.34), channel_id=1, source_target_pairs={{0,5},{1,4},{2,7},{3,6},{4,1},{5,0},{6,3},{7,2},{8,13},{9,12},{10,... | collective-permute-start | bytes 393224 | tf_op jit(solution)/shard_map/ppermute | solution.py:39
  60.6 9.7 %collective-permute-start.7 = (bf16[2,32,1024]{2,1,0:T(8,128)(2,1)S(1)}, bf16[2,32,1024]{2,1,0:T(8,128)(2,1)S(1)}, u32[]{:S(2)}, u32[]{:S(2)}) collective-permute-start(bf16[2,32,1024]{2,1,0:T(8,128)(2,1)S(1)} %get-tuple-element.35), channel_id=1, source_target_pairs={{0,6},{1,7},{2,0},{3,1},{4,2},{5,3},{6,4},{7,5},{8,14},{9,15},{10,... | collective-permute-start | bytes 393224 | tf_op jit(solution)/shard_map/ppermute | solution.py:39
  77.8 185.6 %reduce-scatter.3.cloned.1.call-start = ((), (), s32[]{:S(2)}) async-start(), calls=%async_computation.2 | async-start | bytes 1638400 | tf_op jit(solution)/shard_map/reduce_scatter | solution.py:417
  79.0 26.2 %collective-permute-start.12 = (bf16[512,1024]{1,0:T(8,128)(2,1)S(1)}, bf16[512,1024]{1,0:T(8,128)(2,1)}, u32[]{:S(2)}, u32[]{:S(2)}) collective-permute-start(bf16[512,1024]{1,0:T(8,128)(2,1)S(1)} %bitcast.73), channel_id=1, source_target_pairs={{0,64},{1,65},{2,66},{3,67},{4,68},{5,69},{6,70},{7,71},{8,72},{9,... | collective-permute-start | bytes 3145736 | tf_op jit(solution)/shard_map/ppermute | solution.py:39
  79.3 39.7 %collective-permute-start.15 = (bf16[512,1024]{1,0:T(8,128)(2,1)S(1)}, bf16[512,1024]{1,0:T(8,128)(2,1)S(1)}, u32[]{:S(2)}, u32[]{:S(2)}) collective-permute-start(bf16[512,1024]{1,0:T(8,128)(2,1)S(1)} %bitcast.74), channel_id=1, source_target_pairs={{0,16},{1,17},{2,18},{3,19},{4,20},{5,21},{6,22},{7,23},{8,24},{9,... | collective-permute-start | bytes 3145736 | tf_op jit(solution)/shard_map/ppermute | solution.py:39
  81.3 35.9 %collective-permute-start.16 = (bf16[3,128,1024]{2,1,0:T(8,128)(2,1)}, bf16[3,128,1024]{2,1,0:T(8,128)(2,1)S(1)}, u32[]{:S(2)}, u32[]{:S(2)}) collective-permute-start(bf16[3,128,1024]{2,1,0:T(8,128)(2,1)} %get-tuple-element.38), channel_id=1, source_target_pairs={{0,64},{1,65},{2,66},{3,67},{4,68},{5,69},{6,70},{7,71},{8,72},{9,... | collective-permute-start | bytes 2359304 | tf_op jit(solution)/shard_map/ppermute | solution.py:39
  82.9 51.9 %collective-permute-start.20 = (bf16[512,1024]{1,0:T(8,128)(2,1)S(1)}, bf16[512,1024]{1,0:T(8,128)(2,1)}, u32[]{:S(2)}, u32[]{:S(2)}) collective-permute-start(bf16[512,1024]{1,0:T(8,128)(2,1)S(1)} %bitcast.75), channel_id=1, source_target_pairs={{0,48},{1,49},{2,50},{3,51},{4,52},{5,53},{6,54},{7,55},{8,56},{9,... | collective-permute-start | bytes 3145736 | tf_op jit(solution)/shard_map/ppermute | solution.py:39
  105.2 41.0 %collective-permute-start.13 = (bf16[512,1024]{1,0:T(8,128)(2,1)}, bf16[512,1024]{1,0:T(8,128)(2,1)S(1)}, u32[]{:S(2)}, u32[]{:S(2)}) collective-permute-start(bf16[512,1024]{1,0:T(8,128)(2,1)} %collective-permute-done.12.refs_1_.refs_7_), channel_id=1, source_target_pairs={{0,16},{1,17},{2,18},{3,19},{4,20},{5,21},{6,22},{7,23},{8,24},{9,... | collective-permute-start | bytes 3145736 | tf_op jit(solution)/shard_map/ppermute | solution.py:39
  107.1 39.1 %collective-permute-start.14 = (bf16[512,1024]{1,0:T(8,128)(2,1)}, bf16[512,1024]{1,0:T(8,128)(2,1)S(1)}, u32[]{:S(2)}, u32[]{:S(2)}) collective-permute-start(bf16[512,1024]{1,0:T(8,128)(2,1)} %collective-permute-done.12.refs_1_.refs_7_), channel_id=1, source_target_pairs={{0,48},{1,49},{2,50},{3,51},{4,52},{5,53},{6,54},{7,55},{8,56},{9,... | collective-permute-start | bytes 3145736 | tf_op jit(solution)/shard_map/ppermute | solution.py:39
  117.1 15.3 %collective-permute-start.17 = (bf16[128,1024]{1,0:T(8,128)(2,1)S(1)}, bf16[128,1024]{1,0:T(8,128)(2,1)S(1)}, u32[]{:S(2)}, u32[]{:S(2)}) collective-permute-start(bf16[128,1024]{1,0:T(8,128)(2,1)S(1)} %slice.137), channel_id=1, source_target_pairs={{0,16},{1,17},{2,18},{3,19},{4,20},{5,21},{6,22},{7,23},{8,24},{9,... | collective-permute-start | bytes 786440 | tf_op jit(solution)/shard_map/ppermute | solution.py:39
  119.0 13.9 %collective-permute-start.18 = (bf16[128,1024]{1,0:T(8,128)(2,1)S(1)}, bf16[128,1024]{1,0:T(8,128)(2,1)}, u32[]{:S(2)}, u32[]{:S(2)}) collective-permute-start(bf16[128,1024]{1,0:T(8,128)(2,1)S(1)} %slice.138), channel_id=1, source_target_pairs={{0,48},{1,49},{2,50},{3,51},{4,52},{5,53},{6,54},{7,55},{8,56},{9,... | collective-permute-start | bytes 786440 | tf_op jit(solution)/shard_map/ppermute | solution.py:39
  133.1 10.7 %collective-permute-start.19 = (bf16[256,1024]{1,0:T(8,128)(2,1)}, bf16[256,1024]{1,0:T(8,128)(2,1)}, u32[]{:S(2)}, u32[]{:S(2)}) collective-permute-start(bf16[256,1024]{1,0:T(8,128)(2,1)} %after.7), channel_id=1, source_target_pairs={{0,16},{1,17},{2,18},{3,19},{4,20},{5,21},{6,22},{7,23},{8,24},{9,... | collective-permute-start | bytes 1572872 | tf_op jit(solution)/shard_map/ppermute | solution.py:39
  136.7 9.5 %collective-permute-start.21 = (bf16[256,1024]{1,0:T(8,128)(2,1)}, bf16[256,1024]{1,0:T(8,128)(2,1)}, u32[]{:S(2)}, u32[]{:S(2)}) collective-permute-start(bf16[256,1024]{1,0:T(8,128)(2,1)} %slice.139), channel_id=1, source_target_pairs={{0,48},{1,49},{2,50},{3,51},{4,52},{5,53},{6,54},{7,55},{8,56},{9,... | collective-permute-start | bytes 1572872 | tf_op jit(solution)/shard_map/ppermute | solution.py:39
  154.9 31.2 %collective-permute-start.24 = (bf16[8,640,512]{2,1,0:T(8,128)(2,1)}, bf16[8,640,512]{2,1,0:T(8,128)(2,1)}, u32[]{:S(2)}, u32[]{:S(2)}) collective-permute-start(bf16[8,640,512]{2,1,0:T(8,128)(2,1)} %norm.1.refs_0_.refs_1_.refs_2_.refs_3_.refs_4_.refs_5_), channel_id=1, source_target_pairs={{0,8},{1,9},{2,10},{3,11},{4,12},{5,13},{6,14},{7,15},{8,0},{9,1},... | collective-permute-start | bytes 15728648 | tf_op jit(solution)/shard_map/ppermute | solution.py:39
  158.6 22.6 %collective-permute-start.22 = (bf16[256,1024]{1,0:T(8,128)(2,1)}, bf16[256,1024]{1,0:T(8,128)(2,1)}, u32[]{:S(2)}, u32[]{:S(2)}) collective-permute-start(bf16[256,1024]{1,0:T(8,128)(2,1)} %slice.140), channel_id=1, source_target_pairs={{0,16},{1,17},{2,18},{3,19},{4,20},{5,21},{6,22},{7,23},{8,24},{9,... | collective-permute-start | bytes 1572872 | tf_op jit(solution)/shard_map/ppermute | solution.py:39
  161.0 20.3 %collective-permute-start.23 = (bf16[256,1024]{1,0:T(8,128)(2,1)}, bf16[256,1024]{1,0:T(8,128)(2,1)}, u32[]{:S(2)}, u32[]{:S(2)}) collective-permute-start(bf16[256,1024]{1,0:T(8,128)(2,1)} %slice.141), channel_id=1, source_target_pairs={{0,48},{1,49},{2,50},{3,51},{4,52},{5,53},{6,54},{7,55},{8,56},{9,... | collective-permute-start | bytes 1572872 | tf_op jit(solution)/shard_map/ppermute | solution.py:39
  163.5 34.9 %collective-permute-start.25 = (bf16[256,1024]{1,0:T(8,128)(2,1)}, bf16[256,1024]{1,0:T(8,128)(2,1)}, u32[]{:S(2)}, u32[]{:S(2)}) collective-permute-start(bf16[256,1024]{1,0:T(8,128)(2,1)} %after.8.refs_0_), channel_id=1, source_target_pairs={{0,16},{1,17},{2,18},{3,19},{4,20},{5,21},{6,22},{7,23},{8,24},{9,... | collective-permute-start | bytes 1572872 | tf_op jit(solution)/shard_map/ppermute | solution.py:39
  163.8 34.6 %collective-permute-start.26 = (bf16[256,1024]{1,0:T(8,128)(2,1)}, bf16[256,1024]{1,0:T(8,128)(2,1)}, u32[]{:S(2)}, u32[]{:S(2)}) collective-permute-start(bf16[256,1024]{1,0:T(8,128)(2,1)} %after.8.refs_0_), channel_id=1, source_target_pairs={{0,48},{1,49},{2,50},{3,51},{4,52},{5,53},{6,54},{7,55},{8,56},{9,... | collective-permute-start | bytes 1572872 | tf_op jit(solution)/shard_map/ppermute | solution.py:39
  208.1 126.7 %reduce-scatter.5.cloned.1.call-start = ((), (), s32[]{:S(2)}) async-start(), calls=%async_computation.3 | async-start | bytes 1638400 | tf_op jit(solution)/shard_map/reduce_scatter | solution.py:417
  209.9 21.0 %collective-permute-start.31 = (bf16[256,1024]{1,0:T(8,128)(2,1)}, bf16[256,1024]{1,0:T(8,128)(2,1)S(1)}, u32[]{:S(2)}, u32[]{:S(2)}) collective-permute-start(bf16[256,1024]{1,0:T(8,128)(2,1)} %after.9.refs_0_), channel_id=1, source_target_pairs={{0,16},{1,17},{2,18},{3,19},{4,20},{5,21},{6,22},{7,23},{8,24},{9,... | collective-permute-start | bytes 1572872 | tf_op jit(solution)/shard_map/ppermute | solution.py:39
  209.9 21.0 %collective-permute-start.32 = (bf16[256,1024]{1,0:T(8,128)(2,1)}, bf16[256,1024]{1,0:T(8,128)(2,1)S(1)}, u32[]{:S(2)}, u32[]{:S(2)}) collective-permute-start(bf16[256,1024]{1,0:T(8,128)(2,1)} %after.9.refs_0_), channel_id=1, source_target_pairs={{0,48},{1,49},{2,50},{3,51},{4,52},{5,53},{6,54},{7,55},{8,56},{9,... | collective-permute-start | bytes 1572872 | tf_op jit(solution)/shard_map/ppermute | solution.py:39
  214.1 16.8 %collective-permute-start.29 = (bf16[128,1024]{1,0:T(8,128)(2,1)S(1)}, bf16[128,1024]{1,0:T(8,128)(2,1)S(1)}, u32[]{:S(2)}, u32[]{:S(2)}) collective-permute-start(bf16[128,1024]{1,0:T(8,128)(2,1)S(1)} %slice.143), channel_id=1, source_target_pairs={{0,16},{1,17},{2,18},{3,19},{4,20},{5,21},{6,22},{7,23},{8,24},{9,... | collective-permute-start | bytes 786440 | tf_op jit(solution)/shard_map/ppermute | solution.py:39
  215.3 15.7 %collective-permute-start.30 = (bf16[128,1024]{1,0:T(8,128)(2,1)S(1)}, bf16[128,1024]{1,0:T(8,128)(2,1)S(1)}, u32[]{:S(2)}, u32[]{:S(2)}) collective-permute-start(bf16[128,1024]{1,0:T(8,128)(2,1)S(1)} %slice.144), channel_id=1, source_target_pairs={{0,48},{1,49},{2,50},{3,51},{4,52},{5,53},{6,54},{7,55},{8,56},{9,... | collective-permute-start | bytes 786440 | tf_op jit(solution)/shard_map/ppermute | solution.py:39
  239.7 8.7 %collective-permute-start.33 = (bf16[4,640,256]{2,1,0:T(8,128)(2,1)}, bf16[4,640,256]{2,1,0:T(8,128)(2,1)}, u32[]{:S(2)}, u32[]{:S(2)}) collective-permute-start(bf16[4,640,256]{2,1,0:T(8,128)(2,1)} %get-tuple-element.42), channel_id=1, source_target_pairs={{0,8},{1,9},{2,10},{3,11},{4,12},{5,13},{6,14},{7,15},{8,0},{9,1},... | collective-permute-start | bytes 3932168 | tf_op jit(solution)/shard_map/ppermute | solution.py:39
  240.5 16.1 %collective-permute-start.40 = (bf16[256,1024]{1,0:T(8,128)(2,1)}, bf16[256,1024]{1,0:T(8,128)(2,1)S(1)}, u32[]{:S(2)}, u32[]{:S(2)}) collective-permute-start(bf16[256,1024]{1,0:T(8,128)(2,1)} %after.10.refs_0_), channel_id=1, source_target_pairs={{0,16},{1,17},{2,18},{3,19},{4,20},{5,21},{6,22},{7,23},{8,24},{9,... | collective-permute-start | bytes 1572872 | tf_op jit(solution)/shard_map/ppermute | solution.py:39
  240.5 16.9 %collective-permute-start.41 = (bf16[256,1024]{1,0:T(8,128)(2,1)}, bf16[256,1024]{1,0:T(8,128)(2,1)S(1)}, u32[]{:S(2)}, u32[]{:S(2)}) collective-permute-start(bf16[256,1024]{1,0:T(8,128)(2,1)} %after.10.refs_0_), channel_id=1, source_target_pairs={{0,48},{1,49},{2,50},{3,51},{4,52},{5,53},{6,54},{7,55},{8,56},{9,... | collective-permute-start | bytes 1572872 | tf_op jit(solution)/shard_map/ppermute | solution.py:39
  243.8 18.1 %collective-permute-start.38 = (bf16[128,1024]{1,0:T(8,128)(2,1)S(1)}, bf16[128,1024]{1,0:T(8,128)(2,1)S(1)}, u32[]{:S(2)}, u32[]{:S(2)}) collective-permute-start(bf16[128,1024]{1,0:T(8,128)(2,1)S(1)} %slice.150), channel_id=1, source_target_pairs={{0,16},{1,17},{2,18},{3,19},{4,20},{5,21},{6,22},{7,23},{8,24},{9,... | collective-permute-start | bytes 786440 | tf_op jit(solution)/shard_map/ppermute | solution.py:39
  244.9 17.8 %collective-permute-start.39 = (bf16[128,1024]{1,0:T(8,128)(2,1)S(1)}, bf16[128,1024]{1,0:T(8,128)(2,1)S(1)}, u32[]{:S(2)}, u32[]{:S(2)}) collective-permute-start(bf16[128,1024]{1,0:T(8,128)(2,1)S(1)} %slice.151), channel_id=1, source_target_pairs={{0,48},{1,49},{2,50},{3,51},{4,52},{5,53},{6,54},{7,55},{8,56},{9,... | collective-permute-start | bytes 786440 | tf_op jit(solution)/shard_map/ppermute | solution.py:39
  276.3 18.8 %collective-permute-start.36 = (bf16[640,256]{1,0:T(8,128)(2,1)}, bf16[640,256]{1,0:T(8,128)(2,1)}, u32[]{:S(2)}, u32[]{:S(2)}) collective-permute-start(bf16[640,256]{1,0:T(8,128)(2,1)} %get-tuple-element.51), channel_id=1, source_target_pairs={{0,6},{1,7},{2,0},{3,1},{4,2},{5,3},{6,4},{7,5},{8,14},{9,15},{10,... | collective-permute-start | bytes 983048 | tf_op jit(solution)/shard_map/ppermute | solution.py:39
  280.1 15.0 %collective-permute-start.35 = (bf16[640,256]{1,0:T(8,128)(2,1)}, bf16[640,256]{1,0:T(8,128)(2,1)}, u32[]{:S(2)}, u32[]{:S(2)}) collective-permute-start(bf16[640,256]{1,0:T(8,128)(2,1)} %get-tuple-element.50), channel_id=1, source_target_pairs={{0,4},{1,5},{2,6},{3,7},{4,0},{5,1},{6,2},{7,3},{8,12},{9,13},{10,... | collective-permute-start | bytes 983048 | tf_op jit(solution)/shard_map/ppermute | solution.py:39
  280.1 18.2 %collective-permute-start.34 = (bf16[640,256]{1,0:T(8,128)(2,1)S(1)}, bf16[640,256]{1,0:T(8,128)(2,1)}, u32[]{:S(2)}, u32[]{:S(2)}) collective-permute-start(bf16[640,256]{1,0:T(8,128)(2,1)S(1)} %get-tuple-element.52.refs_5_), channel_id=1, source_target_pairs={{0,2},{1,3},{2,4},{3,5},{4,6},{5,7},{6,0},{7,1},{8,10},{9,11},{10,... | collective-permute-start | bytes 983048 | tf_op jit(solution)/shard_map/ppermute | solution.py:39
  281.7 18.2 %collective-permute-start.45 = (bf16[128,1024]{1,0:T(8,128)(2,1)}, bf16[128,1024]{1,0:T(8,128)(2,1)}, u32[]{:S(2)}, u32[]{:S(2)}) collective-permute-start(bf16[128,1024]{1,0:T(8,128)(2,1)} %slice.154), channel_id=1, source_target_pairs={{0,48},{1,49},{2,50},{3,51},{4,52},{5,53},{6,54},{7,55},{8,56},{9,... | collective-permute-start | bytes 786440 | tf_op jit(solution)/shard_map/ppermute | solution.py:39
  284.7 15.2 %collective-permute-start.44 = (bf16[128,1024]{1,0:T(8,128)(2,1)}, bf16[128,1024]{1,0:T(8,128)(2,1)}, u32[]{:S(2)}, u32[]{:S(2)}) collective-permute-start(bf16[128,1024]{1,0:T(8,128)(2,1)} %after.11), channel_id=1, source_target_pairs={{0,16},{1,17},{2,18},{3,19},{4,20},{5,21},{6,22},{7,23},{8,24},{9,... | collective-permute-start | bytes 786440 | tf_op jit(solution)/shard_map/ppermute | solution.py:39
  312.6 10.6 %collective-permute-start.49 = (bf16[640,256]{1,0:T(8,128)(2,1)S(1)}, bf16[640,256]{1,0:T(8,128)(2,1)S(1)}, u32[]{:S(2)}, u32[]{:S(2)}) collective-permute-start(bf16[640,256]{1,0:T(8,128)(2,1)S(1)} %get-tuple-element.48), channel_id=1, source_target_pairs={{0,6},{1,7},{2,0},{3,1},{4,2},{5,3},{6,4},{7,5},{8,14},{9,15},{10,... | collective-permute-start | bytes 983048 | tf_op jit(solution)/shard_map/ppermute | solution.py:39
  313.8 12.1 %collective-permute-start.48 = (bf16[640,256]{1,0:T(8,128)(2,1)S(1)}, bf16[640,256]{1,0:T(8,128)(2,1)S(1)}, u32[]{:S(2)}, u32[]{:S(2)}) collective-permute-start(bf16[640,256]{1,0:T(8,128)(2,1)S(1)} %get-tuple-element.49), channel_id=1, source_target_pairs={{0,4},{1,5},{2,6},{3,7},{4,0},{5,1},{6,2},{7,3},{8,12},{9,13},{10,... | collective-permute-start | bytes 983048 | tf_op jit(solution)/shard_map/ppermute | solution.py:39
  314.1 17.7 %collective-permute-start.47 = (bf16[640,256]{1,0:T(8,128)(2,1)S(1)}, bf16[640,256]{1,0:T(8,128)(2,1)S(1)}, u32[]{:S(2)}, u32[]{:S(2)}) collective-permute-start(bf16[640,256]{1,0:T(8,128)(2,1)S(1)} %get-tuple-element.47), channel_id=1, source_target_pairs={{0,2},{1,3},{2,4},{3,5},{4,6},{5,7},{6,0},{7,1},{8,10},{9,11},{10,... | collective-permute-start | bytes 983048 | tf_op jit(solution)/shard_map/ppermute | solution.py:39
  316.2 18.5 %collective-permute-start.28 = (bf16[640,128]{1,0:T(8,128)(2,1)S(1)}, bf16[640,128]{1,0:T(8,128)(2,1)S(1)}, u32[]{:S(2)}, u32[]{:S(2)}) collective-permute-start(bf16[640,128]{1,0:T(8,128)(2,1)S(1)} %dynamic-slice_bitcast_fusion.1), channel_id=1, source_target_pairs={{0,1},{1,0},{2,3},{3,2},{4,5},{5,4},{6,7},{7,6},{8,9},{9,8},{10,11... | collective-permute-start | bytes 491528 | tf_op jit(solution)/shard_map/ppermute | solution.py:39
  333.0 8.6 %collective-permute-start.50 = (bf16[640,128]{1,0:T(8,128)(2,1)S(1)}, bf16[640,128]{1,0:T(8,128)(2,1)S(1)}, u32[]{:S(2)}, u32[]{:S(2)}) collective-permute-start(bf16[640,128]{1,0:T(8,128)(2,1)S(1)} %constant_dynamic-slice_fusion), channel_id=1, source_target_pairs={{0,1},{1,0},{2,3},{3,2},{4,5},{5,4},{6,7},{7,6},{8,9},{9,8},{10,11... | collective-permute-start | bytes 491528 | tf_op jit(solution)/shard_map/ppermute | solution.py:39
  (72 other events, 412.2 us)
Sparse Core Ops, SparseCore 0:
  9.7 40.4 all-gather.4
  77.9 35.7 all-gather.6
  208.2 22.8 reduce-scatter.2
  287.9 24.0 reduce-scatter.4
where the time goes:
time: 354 us; the launch traced here: 353 us
  waiting for transfers between devices  132 us (37%)
  starting transfers between devices  75.7 us (21%)
  Pallas kernels  59.2 us (17%)
  local copies, waits for them, and re-layouts  55.1 us (16%)
  other arithmetic  16 us (5%)
  between operations  14.5 us (4%)
    ppermute x51, waiting for transfers between devices, send(): return lax.ppermute(v, AXES, shifted(**steps))  131 us
    ppermute x51, starting transfers between devices, send(): return lax.ppermute(v, AXES, shifted(**steps))  75.5 us
    unnamed x132, local copies, waits for them, and re-layouts  34.7 us
    pallas_call x4, Pallas kernels, partial_of(): pl.pallas_call(partial_kernel, out_shape=(shape, shape), grid_spec=pltpu....  21.4 us
    pallas_call x2, Pallas kernels, hidden_first(): pl.pallas_call(first_kernel, out_shape=jax.ShapeDtypeStruct((640, 1024),...  15 us
    convert_element_type x8, other arithmetic, multiply(): (a.astype(jnp.float32) + b.astype(jnp.float32)).astype(jnp.bfloat16)  9.65 us
    pallas_call x2, Pallas kernels, hidden_last(): pl.pallas_call(last_kernel, out_shape=jax.ShapeDtypeStruct((640, 1024), j...  9.55 us
  transfers between devices with their start and end apart: 55, of which 24 were waited for; matrix products, arithmetic and copies ran while one was open for 9% of the time, Pallas kernels for 13%

commit v1 on v0

v1 whole, which is shorter than its diff:
```python
import functools

import jax
import jax.numpy as jnp
import numpy as np
from jax import lax
from jax.experimental import pallas as pl
from jax.experimental.pallas import tpu as pltpu
from jax.sharding import Mesh, PartitionSpec as P

learn_rate = 0.05
beta_one = 0.9
beta_two = 0.95
adam_eps = 1e-08
decay_rate = 0.1
step_index = 100
norm_eps = 1e-06

AXES = ("ylo", "z", "core", "x", "yhi")
SIZES = (2, 4, 2, 4, 2)
D, FF = 4096, 16384
CHUNKS = 4
ORDER = ((0, 0), (1, 0), (0, 3), (1, 3), (0, 1), (1, 1), (0, 2), (1, 2))
MIB = 1 << 20
VMEM = 56


def shifted(**steps):
    pairs = []
    for i, c in enumerate(np.ndindex(*SIZES)):
        d = dict(zip(AXES, c))
        for a, s in steps.items():
            d[a] = (d[a] + s) % SIZES[AXES.index(a)]
        pairs.append((i, int(np.ravel_multi_index(tuple(d[a] for a in AXES), SIZES))))
    return pairs


def send(v, **steps):
    return lax.ppermute(v, AXES, shifted(**steps))


ANY = pl.BlockSpec(memory_space=pl.ANY)


def after(v, *deps):
    return pl.pallas_call(
        lambda *refs: None,
        out_shape=jax.ShapeDtypeStruct(v.shape, v.dtype),
        in_specs=[ANY] * (1 + len(deps)),
        out_specs=ANY,
        input_output_aliases={0: 0},
        cost_estimate=pl.CostEstimate(flops=0, bytes_accessed=0, transcendentals=0),
        name="after",
    )(v, *deps)


def adamw(master, gradient, first_moment, second_moment):
    grad_float = gradient.astype(jnp.float32)
    first_new = beta_one * first_moment + (1.0 - beta_one) * grad_float
    second_new = beta_two * second_moment + (1.0 - beta_two) * grad_float * grad_float
    corr_one = 1.0 - beta_one**step_index
    corr_two = 1.0 - beta_two**step_index
    update = first_new * (1.0 / corr_one) / (jnp.sqrt(second_new * (1.0 / corr_two)) + adam_eps)
    return master - learn_rate * (update + decay_rate * master)


def params():
    return pltpu.CompilerParams(vmem_limit_bytes=VMEM * MIB)


def cost(flops, nbytes):
    return pl.CostEstimate(flops=int(flops) // 1000, bytes_accessed=int(nbytes) // 1000, transcendentals=0)


def up_kernel(w_ref, g_ref, m_ref, v_ref, o_ref, out_ref):
    new = adamw(w_ref[...], g_ref[...], m_ref[...], v_ref[...])
    o_ref[...] = new
    cast = new.astype(jnp.bfloat16)
    for n in range(16):
        out_ref[n] = cast[:, n * 128 : (n + 1) * 128]


def up_step(w, g, m, v):
    spec = pl.BlockSpec((32, 2048), lambda i: (0, i))
    return pl.pallas_call(
        up_kernel,
        out_shape=(
            jax.ShapeDtypeStruct((32, FF), jnp.float32),
            jax.ShapeDtypeStruct((16, 32, 1024), jnp.bfloat16),
        ),
        grid=(8,),
        in_specs=[spec] * 4,
        out_specs=(spec, pl.BlockSpec((16, 32, 128), lambda i: (0, 0, i))),
        compiler_params=params(),
        cost_estimate=cost(30 * 32 * FF, 20 * 32 * FF),
        name="adam_up",
    )(w, g, m, v)


SPLIT = ((0, 0), (0, 1), (1, 0), (1, 1))


def down_kernel(w_ref, g_ref, m_ref, v_ref, o_ref, *d_refs):
    new = adamw(w_ref[...], g_ref[...], m_ref[...], v_ref[...])
    o_ref[...] = new
    cast = new.astype(jnp.bfloat16)
    for t in range(8):
        for j in range(CHUNKS):
            piece = cast[:, t * 512 + j * 128 : t * 512 + (j + 1) * 128]
            d_refs[SPLIT[j][0]][SPLIT[j][1], :, t * 128 : (t + 1) * 128] = piece


def down_step(w, g, m, v):
    spec = pl.BlockSpec((32, D), lambda i: (i, 0))
    sizes = (2, 2)
    return pl.pallas_call(
        down_kernel,
        out_shape=(jax.ShapeDtypeStruct((128, D), jnp.float32),)
        + tuple(jax.ShapeDtypeStruct((n, 128, 1024), jnp.bfloat16) for n in sizes),
        grid=(4,),
        in_specs=[spec] * 4,
        out_specs=(spec,) + tuple(pl.BlockSpec((n, 32, 1024), lambda i: (0, i, 0)) for n in sizes),
        compiler_params=params(),
        cost_estimate=cost(30 * 128 * D, 20 * 128 * D),
        name="adam_down",
    )(w, g, m, v)


def both_ways(up, down):
    return send(up, z=1), send(down, z=-1)


def norm_kernel(a_ref, a1_ref, a2_ref, a3_ref, b_ref, g_ref, *refs):
    out = refs[-1]
    blocks = [a_ref[...], a1_ref[...], a2_ref[...], a3_ref[...]] + [b_ref[i] for i in range(4)]
    total = 0.0
    for block in blocks:
        f = block.astype(jnp.float32)
        total += jnp.sum(f * f, axis=-1, keepdims=True)
    scale = lax.rsqrt(total * (1.0 / D) + norm_eps)
    for n, block in enumerate(blocks):
        out[n] = (block.astype(jnp.float32) * scale * g_ref[n : n + 1]).astype(jnp.bfloat16)


def norm_of(feats_a, feats_b, gains, deps=()):
    rows = 160
    block = pl.BlockSpec((4, rows, 512), lambda i: (0, i, 0))
    return pl.pallas_call(
        norm_kernel,
        out_shape=jax.ShapeDtypeStruct((8, 640, 512), jnp.bfloat16),
        grid=(640 // rows,),
        in_specs=[pl.BlockSpec((rows, 512), lambda i: (i, 0))] * 4
        + [block, pl.BlockSpec((8, 512), lambda i: (0, 0))] + [ANY] * len(deps),
        out_specs=pl.BlockSpec((8, rows, 512), lambda i: (0, i, 0)),
        compiler_params=params(),
        cost_estimate=cost(8 * 640 * D, 10 * MIB),
        name="norm",
    )(*feats_a, feats_b, gains, *deps)


def silu(u):
    return u / (1.0 + jnp.exp(-u))


def first_kernel(s_ref, *refs):
    lhs, ws, acc = refs[:6], refs[6:12], refs[12]
    for k, (a, w) in enumerate(zip(lhs, ws)):
        term = jnp.dot(a[0], w[...], preferred_element_type=jnp.float32)
        if k == 0:
            acc[...] = term
        else:
            acc[...] += term


def last_kernel(s_ref, acc_ref, *refs):
    lhs, ws, out = refs[:2], refs[2:4], refs[4]
    for n in range(4):
        at = slice(n * 256, (n + 1) * 256)
        u = acc_ref[:, at]
        for a, w in zip(lhs, ws):
            u += jnp.dot(a[0], w[:, at], preferred_element_type=jnp.float32)
        out[:, at] = silu(u * D ** (-0.5)).astype(jnp.bfloat16)


def hidden_specs(places, ws):
    rows = 320
    lhs = [pl.BlockSpec((1, rows, 512), functools.partial(lambda k, i, s: (s[k], i, 0), k)) for k in places]
    return lhs, [pl.BlockSpec(w.shape, lambda i, s: (0, 0), pipeline_mode=pl.Buffered(1)) for w in ws]


def hidden_first(scalars, normed, ws):
    lhs, rhs = hidden_specs(range(6), ws)
    return pl.pallas_call(
        first_kernel,
        out_shape=jax.ShapeDtypeStruct((640, 1024), jnp.float32),
        grid_spec=pltpu.PrefetchScalarGridSpec(
            num_scalar_prefetch=1,
            grid=(2,),
            in_specs=lhs + rhs,
            out_specs=pl.BlockSpec((320, 1024), lambda i, s: (i, 0)),
        ),
        compiler_params=params(),
        cost_estimate=cost(2 * 640 * 1024 * 3072, 14 * MIB),
        name="hidden_first",
    )(scalars, *([normed] * 6), *ws)


def hidden_last(scalars, acc, normed, ws):
    lhs, rhs = hidden_specs((6, 7), ws)
    block = pl.BlockSpec((320, 1024), lambda i, s: (i, 0))
    return pl.pallas_call(
        last_kernel,
        out_shape=jax.ShapeDtypeStruct((640, 1024), jnp.bfloat16),
        grid_spec=pltpu.PrefetchScalarGridSpec(
            num_scalar_prefetch=1,
            grid=(2,),
            in_specs=[block] + lhs + rhs,
            out_specs=block,
        ),
        compiler_params=params(),
        cost_estimate=cost(2 * 640 * 1024 * 1024, 8 * MIB),
        name="hidden_last",
    )(scalars, acc, normed, normed, *ws)


def partial_kernel(s_ref, own_ref, sib_ref, w_ref, *refs):
    own_out, sib_out = refs[-2:]
    w = w_ref[:, 0].reshape(1024, 1024)
    for src, dst in ((sib_ref, sib_out), (own_ref, own_out)):
        term = jnp.dot(src[...], w, preferred_element_type=jnp.float32)
        term = (term * FF ** (-0.5)).astype(jnp.bfloat16)
        for xi in range(4):
            dst[s_ref[xi]] = term[:, xi * 256 : (xi + 1) * 256]


def partial_of(scalars, own, sib, w, j, deps):
    rows = 320
    block = pl.BlockSpec((rows, 1024), lambda i, s: (i, 0))
    out = pl.BlockSpec((4, rows, 256), lambda i, s: (0, i, 0))
    shape = jax.ShapeDtypeStruct((4, 640, 256), jnp.bfloat16)
    weights = pl.BlockSpec((8, 1, 128, 1024), lambda i, s: (0, j, 0, 0), pipeline_mode=pl.Buffered(1))
    return pl.pallas_call(
        partial_kernel,
        out_shape=(shape, shape),
        grid_spec=pltpu.PrefetchScalarGridSpec(
            num_scalar_prefetch=1,
            grid=(640 // rows,),
            in_specs=[block, block, weights] + [ANY] * len(deps),
            out_specs=(out, out),
        ),
        compiler_params=params(),
        cost_estimate=cost(4 * 640 * 1024 * 1024, 8 * MIB),
        name="partial",
    )(scalars, own, sib, w, *deps)


def slot_table():
    rows = []
    for ylo, z, yhi, x in np.ndindex(2, 4, 2, 4):
        qs = [(ylo ^ dy) * 4 + (z + dz) % 4 for dy, dz in ORDER]
        rows.append([(q // 2 - x) % 4 if q % 2 == yhi else 4 + q // 2 for q in qs])
    return np.array(rows, np.int32)


SLOTS = slot_table()


def body(
    tokens,
    norm_gain,
    up_master,
    up_gradient,
    up_first,
    up_second,
    down_master,
    down_gradient,
    down_first,
    down_second,
):
    ylo, z, core, x, yhi = (lax.axis_index(a) for a in AXES)

    tokens_b = send(tokens, yhi=1)
    near = [tokens, send(tokens, x=3), send(tokens, x=2), send(tokens, x=1)]

    up_updated, columns = up_step(up_master, up_gradient, up_first, up_second)
    down_updated, down_a, down_b = down_step(down_master, down_gradient, down_first, down_second)
    plane = ("ylo", "z")
    ws_a = lax.all_gather(down_a, plane, axis=0)

    u0 = lax.all_to_all(after(columns, down_a), ("core", "x", "yhi"), 0, 0, tiled=True).reshape(512, 1024)
    u1 = send(u0, ylo=1)
    low0, high0 = both_ways(u0, u0)
    feats_b = lax.all_gather(after(tokens_b, low0, high0, ws_a, *near[1:]), "x", axis=0)
    low1, high1 = both_ways(u1, u1)
    opp = (send(low0, z=1), send(high1, z=-1))
    ws_b = lax.all_gather(after(down_b, low1), plane, axis=0)

    gains = norm_gain.reshape(4, 2, 512)
    gain_a = lax.dynamic_index_in_dim(gains, yhi, 1, keepdims=False)
    gain_a = lax.dynamic_slice_in_dim(jnp.concatenate([gain_a, gain_a]), x, 4, 0)
    gain_b = lax.dynamic_index_in_dim(gains, 1 - yhi, 1, keepdims=False)
    gains = jnp.concatenate([gain_a, gain_b])
    near = [v.reshape(640, 512) for v in near]
    normed = norm_of(near, feats_b.reshape(4, 640, 512), gains, (low1, high1))
    normed_sib = send(normed, core=1)

    where = lax.dynamic_index_in_dim(jnp.asarray(SLOTS), ((ylo * 4 + z) * 2 + yhi) * 4 + x, 0, keepdims=False)
    ws_up = (u0, u1, low0, low1, high0, high1)
    firsts = [hidden_first(where, n, ws_up) for n in (normed, normed_sib)]
    hidden_own, hidden_sib = (hidden_last(where, f, n, opp) for f, n in zip(firsts, (normed, normed_sib)))

    pieces, parts, sums, reduced = [], [], [], []
    places = jnp.arange(4, dtype=jnp.int32)
    add = lambda a, b: (a.astype(jnp.float32) + b.astype(jnp.float32)).astype(jnp.bfloat16)
    for j in range(CHUNKS):
        direct = j != 2
        part, part_sib = partial_of(
            (places - x) % 4 if direct else places,
            hidden_own,
            hidden_sib,
            (ws_a, ws_b)[SPLIT[j][0]],
            SPLIT[j][1],
            parts[-1:] + sums[-2:-1] + (reduced if j == 2 else []),
        )
        parts.append(part_sib)
        part_sib = send(part_sib, core=1)
        if direct:
            terms = [add(part[d], part_sib[d]) for d in range(4)]
            sums.append(terms[1])
            terms = terms[:1] + [send(terms[d], x=d) for d in (1, 2, 3)]
            rows = sum(v.astype(jnp.float32) for v in terms).astype(jnp.bfloat16)
        else:
            both = add(part, part_sib)
            sums.append(both)
            rows = lax.psum_scatter(both, "x", scatter_dimension=0, tiled=True)[0]
        reduced.append(rows)
        keep = lax.dynamic_slice_in_dim(rows, yhi * 128, 128, 1)
        give = lax.dynamic_slice_in_dim(rows, (1 - yhi) * 128, 128, 1)
        pieces.append(add(keep, send(give, yhi=1)))
    decoded = jnp.concatenate(pieces, axis=1).reshape(2, 320, 512)
    return (up_updated, down_updated, decoded)


def solution(mesh):
    fine = Mesh(mesh.devices.reshape(SIZES), AXES)
    grp, tp = AXES[:3], AXES[3:]
    flat = P(AXES, None)
    in_specs = (P(None, grp, tp), P()) + (flat,) * 8
    out_specs = (flat, flat, P(None, grp, tp))
    return jax.shard_map(body, mesh=fine, in_specs=in_specs, out_specs=out_specs, check_vma=False)
```

time: 354 us -> 372 us (1.051)
  waiting for transfers between devices: 132 us -> 210 us
  local copies, waits for them, and re-layouts: 55.1 us -> 7.91 us
  starting transfers between devices: 75.7 us -> 48.3 us
  Pallas kernels: 59.2 us -> 79.7 us
  other arithmetic: 16 us -> 11 us
    ppermute x51 -> x29, waiting for transfers between devices: 131 us -> 194 us  [send(): return lax.ppermute(v, AXES, shifted(**steps))]
    ppermute x51 -> x29, starting transfers between devices: 75.5 us -> 41 us  [send(): return lax.ppermute(v, AXES, shifted(**steps))]
    unnamed x132 -> x40, local copies, waits for them, and re-layouts: 34.7 us -> 5.2 us
    all_to_all x0 -> x1, waiting for transfers between devices: none -> 16.2 us  [body(): lax.all_to_all(after(columns, down_a), ('core', 'x', 'yhi'), 0, 0, tiled=...]
    slice x12 -> x0, local copies, waits for them, and re-layouts: 10.7 us -> none  [the longest x6 4.45 us: fetch(): up, down = (low[:128], high[128:])]
    all_to_all x0 -> x1, starting transfers between devices: none -> 7.12 us  [body(): lax.all_to_all(after(columns, down_a), ('core', 'x', 'yhi'), 0, 0, tiled=...]
    pallas_call x4, Pallas kernels: 21.4 us -> 27.8 us  [partial_of(): pl.pallas_call(partial_kernel, out_shape=(shape, shape), grid_spec=pltpu....]
    concatenate x2 -> x0, local copies, waits for them, and re-layouts: 4.99 us -> none  [the longest x1 4.97 us: body(): where = jnp.concatenate([slots, goes]).astype(jnp.int32)]
  transfers between devices with their start and end apart: 55 -> 34, of which waited for: 24 -> 19; matrix products, arithmetic and copies ran while one was open for 9% -> 2% of each run, Pallas kernels for 13% -> 16%
where the time goes in v1:
time: 372 us; the launch traced here: 371 us
  waiting for transfers between devices  210 us (56%)
  Pallas kernels  79.7 us (21%)
  starting transfers between devices  48.3 us (13%)
  between operations  14 us (4%)
  other arithmetic  11 us (3%)
  local copies, waits for them, and re-layouts  7.91 us (2%)
    ppermute x29, waiting for transfers between devices, send(): return lax.ppermute(v, AXES, shifted(**steps))  194 us
    ppermute x29, starting transfers between devices, send(): return lax.ppermute(v, AXES, shifted(**steps))  41 us
    pallas_call x4, Pallas kernels, partial_of(): pl.pallas_call(partial_kernel, out_shape=(shape, shape), grid_spec=pltpu....  27.8 us
    pallas_call x2, Pallas kernels, hidden_first(): pl.pallas_call(first_kernel, out_shape=jax.ShapeDtypeStruct((640, 1024),...  20 us
    all_to_all x1, waiting for transfers between devices, body(): lax.all_to_all(after(columns, down_a), ('core', 'x', 'yhi'), 0, 0, tiled=...  16.2 us
    pallas_call x2, Pallas kernels, hidden_last(): pl.pallas_call(last_kernel, out_shape=jax.ShapeDtypeStruct((640, 1024), j...  11.9 us
    pallas_call x1, Pallas kernels, up_step(): pl.pallas_call(up_kernel, out_shape=(jax.ShapeDtypeStruct((32, FF), jnp.f...  7.64 us
  transfers between devices with their start and end apart: 34, of which 19 were waited for; matrix products, arithmetic and copies ran while one was open for 2% of the time, Pallas kernels for 16%

profile of v1, /device:TPU:0, one launch (start us, length us, event | category | flops | bytes accessed | tf_op | source)
XLA Modules:
  0.0 371.1 jit_solution(4470434741938027101)
XLA Ops:
  7.2 5.9 %adam_down.1 = (f32[128,4096]{1,0:T(8,128)}, bf16[2,128,1024]{2,1,0:T(8,128)(2,1)}, bf16[2,128,1024]{2,1,0:T(8,128)(2,1)}) custom-call(f32[128,4096]{1,0:T(8,128)} %w_ref.3, bf16[128,4096]{1,0:T(8,128)(2,1)} %g_ref.3, f32[128,4096]{1,0:T(8,128)} %m_ref.3, f32[128,4096]{1,0:T(8,128)} %v_ref.3), custom_call_target="tpu_custom_call" | custom-call | flops 15728 | bytes 10485 | tf_op jit(solution)/shard_map/adam_down/pallas_call | solution.py:116
  13.1 7.6 %adam_up.1 = (f32[32,16384]{1,0:T(8,128)}, bf16[16,32,1024]{2,1,0:T(8,128)(2,1)}) custom-call(f32[32,16384]{1,0:T(8,128)} %w_ref.2, bf16[32,16384]{1,0:T(8,128)(2,1)} %g_ref.2, f32[32,16384]{1,0:T(8,128)} %m_ref.2, f32[32,16384]{1,0:T(8,128)} %v_ref.2), custom_call_target="tpu_custom_call" | custom-call | flops 15728 | bytes 10485 | tf_op jit(solution)/shard_map/adam_up/pallas_call | solution.py:85
  20.8 7.1 %all-to-all-start = ((bf16[16,32,1024]{2,1,0:T(8,128)(2,1)}), bf16[16,32,1024]{2,1,0:T(8,128)(2,1)S(1)}, u32[]{:S(2)}, u32[]{:S(2)}) async-start(bf16[16,32,1024]{2,1,0:T(8,128)(2,1)} %after.3), calls=%async_computation | async-start | bytes 2097152 | tf_op jit(solution)/shard_map/all_to_all | solution.py:290
  27.9 3.2 collective-permute-start
  31.1 16.2 %all-to-all-done = bf16[16,32,1024]{2,1,0:T(8,128)(2,1)S(1)} async-done(((bf16[16,32,1024]{2,1,0:T(8,128)(2,1)}), bf16[16,32,1024]{2,1,0:T(8,128)(2,1)S(1)}, u32[]{:S(2)}, u32[]{:S(2)}) %all-to-all-start) | async-done | bytes 1048608 | tf_op jit(solution)/shard_map/all_to_all | solution.py:290
  47.4 1.8 collective-permute-start.4
  49.2 2.2 collective-permute-start.5
  51.4 2.5 collective-permute-start.1
  54.5 3.3 collective-permute-done.refs_4_
  57.7 3.0 collective-permute-start.3
  60.7 10.2 %collective-permute-done.1.refs_5_ = bf16[2,320,512]{2,1,0:T(8,128)(2,1)S(1)} collective-permute-done((bf16[2,320,512]{2,1,0:T(8,128)(2,1)}, bf16[2,320,512]{2,1,0:T(8,128)(2,1)S(1)}, u32[]{:S(2)}, u32[]{:S(2)}) %collective-permute-start.1) | collective-permute-done | bytes 655392 | tf_op jit(solution)/shard_map/ppermute | solution.py:39
  70.8 11.6 %collective-permute-done.2.refs_6_ = bf16[2,320,512]{2,1,0:T(8,128)(2,1)S(1)} collective-permute-done((bf16[2,320,512]{2,1,0:T(8,128)(2,1)}, bf16[2,320,512]{2,1,0:T(8,128)(2,1)S(1)}, u32[]{:S(2)}, u32[]{:S(2)}) %collective-permute-start.2) | collective-permute-done | bytes 655392 | tf_op jit(solution)/shard_map/ppermute | solution.py:39
  82.5 7.9 %collective-permute-done.3.refs_0_ = bf16[2,320,512]{2,1,0:T(8,128)(2,1)S(1)} collective-permute-done((bf16[2,320,512]{2,1,0:T(8,128)(2,1)}, bf16[2,320,512]{2,1,0:T(8,128)(2,1)S(1)}, u32[]{:S(2)}, u32[]{:S(2)}) %collective-permute-start.3) | collective-permute-done | bytes 655392 | tf_op jit(solution)/shard_map/ppermute | solution.py:39
  90.3 11.3 %collective-permute-done.4.refs_1_.refs_8_ = bf16[512,1024]{1,0:T(8,128)(2,1)S(1)} collective-permute-done((bf16[512,1024]{1,0:T(8,128)(2,1)S(1)}, bf16[512,1024]{1,0:T(8,128)(2,1)S(1)}, u32[]{:S(2)}, u32[]{:S(2)}) %collective-permute-start.4) | collective-permute-done | bytes 1048608 | tf_op jit(solution)/shard_map/ppermute | solution.py:39
  103.7 24.5 %collective-permute-done.6.refs_7_ = bf16[512,1024]{1,0:T(8,128)(2,1)S(1)} collective-permute-done((bf16[512,1024]{1,0:T(8,128)(2,1)S(1)}, bf16[512,1024]{1,0:T(8,128)(2,1)S(1)}, u32[]{:S(2)}, u32[]{:S(2)}) %collective-permute-start.6) | collective-permute-done | bytes 1048608 | tf_op jit(solution)/shard_map/ppermute | solution.py:39
  128.3 3.2 collective-permute-start.8
  132.2 21.6 %collective-permute-done.7.refs_0_.refs_9_.refs_1_ = bf16[512,1024]{1,0:T(8,128)(2,1)S(1)} collective-permute-done((bf16[512,1024]{1,0:T(8,128)(2,1)S(1)}, bf16[512,1024]{1,0:T(8,128)(2,1)S(1)}, u32[]{:S(2)}, u32[]{:S(2)}) %collective-permute-start.7) | collective-permute-done | bytes 1048608 | tf_op jit(solution)/shard_map/ppermute | solution.py:39
  155.2 6.4 %norm.1.refs_0_.refs_1_.refs_2_.refs_3_.refs_4_.refs_5_ = bf16[8,640,512]{2,1,0:T(8,128)(2,1)} custom-call(bf16[640,512]{1,0:T(8,128)(2,1)} %bitcast.1.a_ref, bf16[640,512]{1,0:T(8,128)(2,1)} %bitcast.2.a1_ref, bf16[640,512]{1,0:T(8,128)(2,1)} %bitcast.65, bf16[640,512]{1,0:T(8,128)(2,1)} %bitcast.66, bf16[4,640,512]{2,1,0:T(8,128)(2,1)} %bitcast.67, ...), custom_call_target="tpu_custom_call" | custom-call | flops 20971 | bytes 10485 | tf_op jit(solution)/shard_map/norm/pallas_call | solution.py:148
  161.8 1.1 copy-done.2
  163.2 2.9 collective-permute-start.10
  166.7 1.2 fusion.24.s_ref
  167.9 10.0 %hidden_first.2.acc_ref = f32[640,1024]{1,0:T(8,128)} custom-call(s32[8]{0:T(128)} %fusion.24.s_ref, bf16[8,640,512]{2,1,0:T(8,128)(2,1)} %norm.1.refs_0_.refs_1_.refs_2_.refs_3_.refs_4_.refs_5_, bf16[8,640,512]{2,1,0:T(8,128)(2,1)} %norm.1.refs_0_.refs_1_.refs_2_.refs_3_.refs_4_.refs_5_, ...), custom_call_target="tpu_custom_call" | custom-call | flops 4026531 | bytes 14680 | tf_op jit(solution)/shard_map/hidden_first/pallas_call | solution.py:193
  178.0 51.0 %collective-permute-done.9.refs_2_ = bf16[512,1024]{1,0:T(8,128)(2,1)S(1)} collective-permute-done((bf16[512,1024]{1,0:T(8,128)(2,1)S(1)}, bf16[512,1024]{1,0:T(8,128)(2,1)S(1)}, u32[]{:S(2)}, u32[]{:S(2)}) %collective-permute-start.9) | collective-permute-done | bytes 1048608 | tf_op jit(solution)/shard_map/ppermute | solution.py:39
  230.0 6.0 %hidden_last.2.own_ref = bf16[640,1024]{1,0:T(8,128)(2,1)} custom-call(s32[8]{0:T(128)} %fusion.24.s_ref, f32[640,1024]{1,0:T(8,128)} %hidden_first.2.acc_ref, bf16[8,640,512]{2,1,0:T(8,128)(2,1)} %norm.1.refs_0_.refs_1_.refs_2_.refs_3_.refs_4_.refs_5_, bf16[8,640,512]{2,1,0:T(8,128)(2,1)} %norm.1.refs_0_.refs_1_.refs_2_.refs_3_.refs_4_.refs_5_, ...), custom_call_target="tpu_custom_call" | custom-call | flops 1342177 | bytes 8388 | tf_op jit(solution)/shard_map/hidden_last/pallas_call | solution.py:211
  236.0 9.9 %hidden_first.3.acc_ref = f32[640,1024]{1,0:T(8,128)} custom-call(s32[8]{0:T(128)} %fusion.24.s_ref, bf16[8,640,512]{2,1,0:T(8,128)(2,1)} %collective-permute-done.11.refs_0_.refs_1_.refs_2_.refs_3_.refs_4_.refs_5_, bf16[8,640,512]{2,1,0:T(8,128)(2,1)} %collective-permute-done.11.refs_0_.refs_1_.refs_2_.refs_3_.refs_4_.refs_5_, ...), custom_call_target="tpu_custom_call" | custom-call | flops 4026531 | bytes 14680 | tf_op jit(solution)/shard_map/hidden_first/pallas_call | solution.py:193
  245.9 6.0 %hidden_last.3.sib_ref = bf16[640,1024]{1,0:T(8,128)(2,1)} custom-call(s32[8]{0:T(128)} %fusion.24.s_ref, f32[640,1024]{1,0:T(8,128)} %hidden_first.3.acc_ref, bf16[8,640,512]{2,1,0:T(8,128)(2,1)} %collective-permute-done.11.refs_0_.refs_1_.refs_2_.refs_3_.refs_4_.refs_5_, ...), custom_call_target="tpu_custom_call" | custom-call | flops 1342177 | bytes 8388 | tf_op jit(solution)/shard_map/hidden_last/pallas_call | solution.py:211
  251.8 6.9 %partial.4 = (bf16[4,640,256]{2,1,0:T(8,128)(2,1)}, bf16[4,640,256]{2,1,0:T(8,128)(2,1)}) custom-call(s32[4]{0:T(128)} %and_select_fusion.s_ref, bf16[640,1024]{1,0:T(8,128)(2,1)} %hidden_last.2.own_ref, bf16[640,1024]{1,0:T(8,128)(2,1)} %hidden_last.3.sib_ref, bf16[8,2,128,1024]{3,2,1,0:T(8,128)(2,1)} %bitcast.56), custom_call_target="tpu_custom_call" | custom-call | flops 2684354 | bytes 8388 | tf_op jit(solution)/shard_map/partial/pallas_call | solution.py:242
  258.7 7.0 %partial.5 = (bf16[4,640,256]{2,1,0:T(8,128)(2,1)}, bf16[4,640,256]{2,1,0:T(8,128)(2,1)}) custom-call(s32[4]{0:T(128)} %and_select_fusion.s_ref, bf16[640,1024]{1,0:T(8,128)(2,1)} %hidden_last.2.own_ref, bf16[640,1024]{1,0:T(8,128)(2,1)} %hidden_last.3.sib_ref, bf16[8,2,128,1024]{3,2,1,0:T(8,128)(2,1)} %bitcast.57, ...), custom_call_target="tpu_custom_call" | custom-call | flops 2684354 | bytes 8388 | tf_op jit(solution)/shard_map/partial/pallas_call | solution.py:242
  266.4 2.8 collective-permute-start.15
  271.1 2.4 collective-permute-start.20
  273.6 1.5 collective-permute-start.19
  275.1 9.0 %collective-permute-done.15 = bf16[640,256]{1,0:T(8,128)(2,1)S(1)} collective-permute-done((bf16[640,256]{1,0:T(8,128)(2,1)S(1)}, bf16[640,256]{1,0:T(8,128)(2,1)S(1)}, u32[]{:S(2)}, u32[]{:S(2)}) %collective-permute-start.15) | collective-permute-done | bytes 327712 | tf_op jit(solution)/shard_map/ppermute | solution.py:39
  284.1 4.3 %collective-permute-done.13 = bf16[640,256]{1,0:T(8,128)(2,1)S(1)} collective-permute-done((bf16[640,256]{1,0:T(8,128)(2,1)S(1)}, bf16[640,256]{1,0:T(8,128)(2,1)S(1)}, u32[]{:S(2)}, u32[]{:S(2)}) %collective-permute-start.13) | collective-permute-done | bytes 327712 | tf_op jit(solution)/shard_map/ppermute | solution.py:39
  289.3 8.2 %collective-permute-done.20 = bf16[640,256]{1,0:T(8,128)(2,1)S(1)} collective-permute-done((bf16[640,256]{1,0:T(8,128)(2,1)S(1)}, bf16[640,256]{1,0:T(8,128)(2,1)S(1)}, u32[]{:S(2)}, u32[]{:S(2)}) %collective-permute-start.20) | collective-permute-done | bytes 327712 | tf_op jit(solution)/shard_map/ppermute | solution.py:39
  297.5 3.7 collective-permute-done.18
  302.7 6.9 %partial.6 = (bf16[4,640,256]{2,1,0:T(8,128)(2,1)}, bf16[4,640,256]{2,1,0:T(8,128)(2,1)}) custom-call(s32[4]{0:T(128)} %iota.6.s_ref, bf16[640,1024]{1,0:T(8,128)(2,1)} %hidden_last.2.own_ref, bf16[640,1024]{1,0:T(8,128)(2,1)} %hidden_last.3.sib_ref, bf16[8,2,128,1024]{3,2,1,0:T(8,128)(2,1)} %bitcast.58, bf16[4,640,256]{2,1,0:T(8,128)(2,1)} %get-tuple-element.23.refs_0_, ...), custom_call_target="tpu_custom_call" | custom-call | flops 2684354 | bytes 8388 | tf_op jit(solution)/shard_map/partial/pallas_call | solution.py:242
  309.6 3.2 collective-permute-done.22
  312.8 2.7 add_convert_fusion
  315.6 7.0 %partial.7 = (bf16[4,640,256]{2,1,0:T(8,128)(2,1)}, bf16[4,640,256]{2,1,0:T(8,128)(2,1)}) custom-call(s32[4]{0:T(128)} %and_select_fusion.s_ref, bf16[640,1024]{1,0:T(8,128)(2,1)} %hidden_last.2.own_ref, bf16[640,1024]{1,0:T(8,128)(2,1)} %hidden_last.3.sib_ref, bf16[8,2,128,1024]{3,2,1,0:T(8,128)(2,1)} %bitcast.59, ...), custom_call_target="tpu_custom_call" | custom-call | flops 2684354 | bytes 8388 | tf_op jit(solution)/shard_map/partial/pallas_call | solution.py:242
  322.8 3.0 collective-permute-start.21
  325.9 1.4 fusion.18
  329.6 3.0 collective-permute-start.16
  332.7 15.7 %collective-permute-done.27 = bf16[640,256]{1,0:T(8,128)(2,1)S(1)} collective-permute-done((bf16[640,256]{1,0:T(8,128)(2,1)S(1)}, bf16[640,256]{1,0:T(8,128)(2,1)S(1)}, u32[]{:S(2)}, u32[]{:S(2)}) %collective-permute-start.27) | collective-permute-done | bytes 327712 | tf_op jit(solution)/shard_map/ppermute | solution.py:39
  348.4 1.6 collective-permute-done.25
  350.0 1.2 fusion.2
  351.2 3.1 collective-permute-start.28
  355.9 3.0 collective-permute-done.28
  358.9 3.7 %collective-permute-done.23 = bf16[640,128]{1,0:T(8,128)(2,1)S(1)} collective-permute-done((bf16[640,128]{1,0:T(8,128)(2,1)S(1)}, bf16[640,128]{1,0:T(8,128)(2,1)S(1)}, u32[]{:S(2)}, u32[]{:S(2)}) %collective-permute-start.23) | collective-permute-done | bytes 163872 | tf_op jit(solution)/shard_map/ppermute | solution.py:39
  (101 shorter events, 17.9 us)
Async XLA Ops:
  7.2 94.5 %all-gather.7.cloned.1.call-start = ((), (), s32[]{:S(2)}) async-start(), calls=%async_computation.3 | async-start | bytes 4718592 | tf_op jit(solution)/shard_map/all_gather | solution.py:288
  20.8 26.6 %all-to-all-start = ((bf16[16,32,1024]{2,1,0:T(8,128)(2,1)}), bf16[16,32,1024]{2,1,0:T(8,128)(2,1)S(1)}, u32[]{:S(2)}, u32[]{:S(2)}) async-start(bf16[16,32,1024]{2,1,0:T(8,128)(2,1)} %after.3), calls=%async_computation | async-start | bytes 2097152 | tf_op jit(solution)/shard_map/all_to_all | solution.py:290
  27.9 126.0 %all-gather.9.cloned.1.call-start = ((), (), s32[]{:S(2)}) async-start(), calls=%async_computation.4 | async-start | bytes 3276800 | tf_op jit(solution)/shard_map/all_gather | solution.py:293
  27.9 29.8 %collective-permute-start = (bf16[2,320,512]{2,1,0:T(8,128)(2,1)}, bf16[2,320,512]{2,1,0:T(8,128)(2,1)}, u32[]{:S(2)}, u32[]{:S(2)}) collective-permute-start(bf16[2,320,512]{2,1,0:T(8,128)(2,1)} %param.11), channel_id=1, source_target_pairs={{0,6},{1,7},{2,0},{3,1},{4,2},{5,3},{6,4},{7,5},{8,14},{9,15},{10,... | collective-permute-start | bytes 1966088 | tf_op jit(solution)/shard_map/ppermute | solution.py:39
  47.4 55.7 %copy-start.6 = (bf16[16,32,1024]{2,1,0:T(8,128)(2,1)}, bf16[16,32,1024]{2,1,0:T(8,128)(2,1)S(1)}, u32[]{:S(2)}) copy-start(bf16[16,32,1024]{2,1,0:T(8,128)(2,1)S(1)} %all-to-all-done) | copy-start | bytes 3145732
  47.4 54.2 %collective-permute-start.4 = (bf16[512,1024]{1,0:T(8,128)(2,1)S(1)}, bf16[512,1024]{1,0:T(8,128)(2,1)S(1)}, u32[]{:S(2)}, u32[]{:S(2)}) collective-permute-start(bf16[512,1024]{1,0:T(8,128)(2,1)S(1)} %bitcast.60), channel_id=1, source_target_pairs={{0,16},{1,17},{2,18},{3,19},{4,20},{5,21},{6,22},{7,23},{8,24},{9,... | collective-permute-start | bytes 3145736 | tf_op jit(solution)/shard_map/ppermute | solution.py:39
  49.2 52.5 %collective-permute-start.5 = (bf16[512,1024]{1,0:T(8,128)(2,1)S(1)}, bf16[512,1024]{1,0:T(8,128)(2,1)S(1)}, u32[]{:S(2)}, u32[]{:S(2)}) collective-permute-start(bf16[512,1024]{1,0:T(8,128)(2,1)S(1)} %bitcast.61), channel_id=1, source_target_pairs={{0,48},{1,49},{2,50},{3,51},{4,52},{5,53},{6,54},{7,55},{8,56},{9,... | collective-permute-start | bytes 3145736 | tf_op jit(solution)/shard_map/ppermute | solution.py:39
  51.4 19.4 %collective-permute-start.1 = (bf16[2,320,512]{2,1,0:T(8,128)(2,1)}, bf16[2,320,512]{2,1,0:T(8,128)(2,1)S(1)}, u32[]{:S(2)}, u32[]{:S(2)}) collective-permute-start(bf16[2,320,512]{2,1,0:T(8,128)(2,1)} %param.11), channel_id=1, source_target_pairs={{0,4},{1,5},{2,6},{3,7},{4,0},{5,1},{6,2},{7,3},{8,12},{9,13},{10,... | collective-permute-start | bytes 1966088 | tf_op jit(solution)/shard_map/ppermute | solution.py:39
  53.9 28.6 %collective-permute-start.2 = (bf16[2,320,512]{2,1,0:T(8,128)(2,1)}, bf16[2,320,512]{2,1,0:T(8,128)(2,1)S(1)}, u32[]{:S(2)}, u32[]{:S(2)}) collective-permute-start(bf16[2,320,512]{2,1,0:T(8,128)(2,1)} %param.11), channel_id=1, source_target_pairs={{0,2},{1,3},{2,4},{3,5},{4,6},{5,7},{6,0},{7,1},{8,10},{9,11},{10,... | collective-permute-start | bytes 1966088 | tf_op jit(solution)/shard_map/ppermute | solution.py:39
  57.7 32.6 %collective-permute-start.3 = (bf16[2,320,512]{2,1,0:T(8,128)(2,1)}, bf16[2,320,512]{2,1,0:T(8,128)(2,1)S(1)}, u32[]{:S(2)}, u32[]{:S(2)}) collective-permute-start(bf16[2,320,512]{2,1,0:T(8,128)(2,1)} %param.11), channel_id=1, source_target_pairs={{0,1},{1,0},{2,3},{3,2},{4,5},{5,4},{6,7},{7,6},{8,9},{9,8},{10,11... | collective-permute-start | bytes 1966088 | tf_op jit(solution)/shard_map/ppermute | solution.py:39
  70.8 30.8 %copy-start.11 = (bf16[2,320,512]{2,1,0:T(8,128)(2,1)}, bf16[2,320,512]{2,1,0:T(8,128)(2,1)S(1)}, u32[]{:S(2)}) copy-start(bf16[2,320,512]{2,1,0:T(8,128)(2,1)S(1)} %collective-permute-done.1.refs_5_) | copy-start | bytes 1966084
  82.5 19.2 %copy-start.12 = (bf16[2,320,512]{2,1,0:T(8,128)(2,1)}, bf16[2,320,512]{2,1,0:T(8,128)(2,1)S(1)}, u32[]{:S(2)}) copy-start(bf16[2,320,512]{2,1,0:T(8,128)(2,1)S(1)} %collective-permute-done.2.refs_6_) | copy-start | bytes 1966084
  90.3 11.3 %copy-start.13 = (bf16[2,320,512]{2,1,0:T(8,128)(2,1)}, bf16[2,320,512]{2,1,0:T(8,128)(2,1)S(1)}, u32[]{:S(2)}) copy-start(bf16[2,320,512]{2,1,0:T(8,128)(2,1)S(1)} %collective-permute-done.3.refs_0_) | copy-start | bytes 1966084
  103.0 28.5 %copy-start.18 = (f32[4096]{0:T(1024)S(1)}, f32[4096]{0:T(1024)}, u32[]{:S(2)}) copy-start(f32[4096]{0:T(1024)} %param.12) | copy-start | bytes 49156
  103.0 199.1 %all-gather.11.cloned.1.call-start = ((), (), s32[]{:S(2)}) async-start(), calls=%async_computation.5 | async-start | bytes 4718592 | tf_op jit(solution)/shard_map/all_gather | solution.py:296
  103.1 25.2 %collective-permute-start.6 = (bf16[512,1024]{1,0:T(8,128)(2,1)S(1)}, bf16[512,1024]{1,0:T(8,128)(2,1)S(1)}, u32[]{:S(2)}, u32[]{:S(2)}) collective-permute-start(bf16[512,1024]{1,0:T(8,128)(2,1)S(1)} %bitcast.62), channel_id=1, source_target_pairs={{0,64},{1,65},{2,66},{3,67},{4,68},{5,69},{6,70},{7,71},{8,72},{9,... | collective-permute-start | bytes 3145736 | tf_op jit(solution)/shard_map/ppermute | solution.py:39
  128.3 33.4 %copy-start.7 = (bf16[512,1024]{1,0:T(8,128)(2,1)}, bf16[512,1024]{1,0:T(8,128)(2,1)S(1)}, u32[]{:S(2)}) copy-start(bf16[512,1024]{1,0:T(8,128)(2,1)S(1)} %collective-permute-done.6.refs_7_) | copy-start | bytes 3145732
  128.3 25.6 %collective-permute-start.7 = (bf16[512,1024]{1,0:T(8,128)(2,1)S(1)}, bf16[512,1024]{1,0:T(8,128)(2,1)S(1)}, u32[]{:S(2)}, u32[]{:S(2)}) collective-permute-start(bf16[512,1024]{1,0:T(8,128)(2,1)S(1)} %collective-permute-done.6.refs_7_), channel_id=1, source_target_pairs={{0,16},{1,17},{2,18},{3,19},{4,20},{5,21},{6,22},{7,23},{8,24},{9,... | collective-permute-start | bytes 3145736 | tf_op jit(solution)/shard_map/ppermute | solution.py:39
  128.3 25.6 %collective-permute-start.8 = (bf16[512,1024]{1,0:T(8,128)(2,1)S(1)}, bf16[512,1024]{1,0:T(8,128)(2,1)S(1)}, u32[]{:S(2)}, u32[]{:S(2)}) collective-permute-start(bf16[512,1024]{1,0:T(8,128)(2,1)S(1)} %collective-permute-done.6.refs_7_), channel_id=1, source_target_pairs={{0,48},{1,49},{2,50},{3,51},{4,52},{5,53},{6,54},{7,55},{8,56},{9,... | collective-permute-start | bytes 3145736 | tf_op jit(solution)/shard_map/ppermute | solution.py:39
  153.8 1.4 copy-start.4
  161.7 74.3 %collective-permute-start.11 = (bf16[8,640,512]{2,1,0:T(8,128)(2,1)}, bf16[8,640,512]{2,1,0:T(8,128)(2,1)}, u32[]{:S(2)}, u32[]{:S(2)}) collective-permute-start(bf16[8,640,512]{2,1,0:T(8,128)(2,1)} %norm.1.refs_0_.refs_1_.refs_2_.refs_3_.refs_4_.refs_5_), channel_id=1, source_target_pairs={{0,8},{1,9},{2,10},{3,11},{4,12},{5,13},{6,14},{7,15},{8,0},{9,1},... | collective-permute-start | bytes 15728648 | tf_op jit(solution)/shard_map/ppermute | solution.py:39
  161.7 1.5 copy-start.5
  161.7 192.6 %reduce-scatter.2.cloned.1.call-start = ((), (), s32[]{:S(2)}) async-start(), calls=%async_computation.2 | async-start | bytes 1638400 | tf_op jit(solution)/shard_map/reduce_scatter | solution.py:335
  162.9 66.1 %collective-permute-start.9 = (bf16[512,1024]{1,0:T(8,128)(2,1)S(1)}, bf16[512,1024]{1,0:T(8,128)(2,1)S(1)}, u32[]{:S(2)}, u32[]{:S(2)}) collective-permute-start(bf16[512,1024]{1,0:T(8,128)(2,1)S(1)} %copy-done.2), channel_id=1, source_target_pairs={{0,16},{1,17},{2,18},{3,19},{4,20},{5,21},{6,22},{7,23},{8,24},{9,... | collective-permute-start | bytes 3145736 | tf_op jit(solution)/shard_map/ppermute | solution.py:39
  163.2 65.8 %collective-permute-start.10 = (bf16[512,1024]{1,0:T(8,128)(2,1)S(1)}, bf16[512,1024]{1,0:T(8,128)(2,1)}, u32[]{:S(2)}, u32[]{:S(2)}) collective-permute-start(bf16[512,1024]{1,0:T(8,128)(2,1)S(1)} %copy-done.5), channel_id=1, source_target_pairs={{0,48},{1,49},{2,50},{3,51},{4,52},{5,53},{6,54},{7,55},{8,56},{9,... | collective-permute-start | bytes 3145736 | tf_op jit(solution)/shard_map/ppermute | solution.py:39
  258.7 7.4 %copy-start.17 = (bf16[4,640,256]{2,1,0:T(8,128)(2,1)S(1)}, bf16[4,640,256]{2,1,0:T(8,128)(2,1)}, u32[]{:S(2)}) copy-start(bf16[4,640,256]{2,1,0:T(8,128)(2,1)} %get-tuple-element.20) | copy-start | bytes 3932164
  258.7 7.4 %collective-permute-start.12 = (bf16[4,640,256]{2,1,0:T(8,128)(2,1)}, bf16[4,640,256]{2,1,0:T(8,128)(2,1)S(1)}, u32[]{:S(2)}, u32[]{:S(2)}) collective-permute-start(bf16[4,640,256]{2,1,0:T(8,128)(2,1)} %get-tuple-element.21.refs_0_), channel_id=1, source_target_pairs={{0,8},{1,9},{2,10},{3,11},{4,12},{5,13},{6,14},{7,15},{8,0},{9,1},... | collective-permute-start | bytes 3932168 | tf_op jit(solution)/shard_map/ppermute | solution.py:39
  265.8 5.1 %collective-permute-start.17 = (bf16[4,640,256]{2,1,0:T(8,128)(2,1)}, bf16[4,640,256]{2,1,0:T(8,128)(2,1)S(1)}, u32[]{:S(2)}, u32[]{:S(2)}) collective-permute-start(bf16[4,640,256]{2,1,0:T(8,128)(2,1)} %get-tuple-element.23.refs_0_), channel_id=1, source_target_pairs={{0,8},{1,9},{2,10},{3,11},{4,12},{5,13},{6,14},{7,15},{8,0},{9,1},... | collective-permute-start | bytes 3932168 | tf_op jit(solution)/shard_map/ppermute | solution.py:39
  266.1 4.7 %copy-start.16 = (bf16[4,640,256]{2,1,0:T(8,128)(2,1)S(1)}, bf16[4,640,256]{2,1,0:T(8,128)(2,1)}, u32[]{:S(2)}) copy-start(bf16[4,640,256]{2,1,0:T(8,128)(2,1)} %get-tuple-element.22) | copy-start | bytes 3932164
  266.4 4.7 %copy-start.15 = (bf16[640,256]{1,0:T(8,128)(2,1)}, bf16[640,256]{1,0:T(8,128)(2,1)S(1)}, u32[]{:S(2)}) copy-start(bf16[640,256]{1,0:T(8,128)(2,1)S(1)} %get-tuple-element.37.refs_1_) | copy-start | bytes 983044
  266.4 17.7 %collective-permute-start.15 = (bf16[640,256]{1,0:T(8,128)(2,1)S(1)}, bf16[640,256]{1,0:T(8,128)(2,1)S(1)}, u32[]{:S(2)}, u32[]{:S(2)}) collective-permute-start(bf16[640,256]{1,0:T(8,128)(2,1)S(1)} %get-tuple-element.36), channel_id=1, source_target_pairs={{0,6},{1,7},{2,0},{3,1},{4,2},{5,3},{6,4},{7,5},{8,14},{9,15},{10,... | collective-permute-start | bytes 983048 | tf_op jit(solution)/shard_map/ppermute | solution.py:39
  269.1 15.0 %collective-permute-start.14 = (bf16[640,256]{1,0:T(8,128)(2,1)S(1)}, bf16[640,256]{1,0:T(8,128)(2,1)S(1)}, u32[]{:S(2)}, u32[]{:S(2)}) collective-permute-start(bf16[640,256]{1,0:T(8,128)(2,1)S(1)} %get-tuple-element.35), channel_id=1, source_target_pairs={{0,4},{1,5},{2,6},{3,7},{4,0},{5,1},{6,2},{7,3},{8,12},{9,13},{10,... | collective-permute-start | bytes 983048 | tf_op jit(solution)/shard_map/ppermute | solution.py:39
  270.0 18.4 %collective-permute-start.13 = (bf16[640,256]{1,0:T(8,128)(2,1)S(1)}, bf16[640,256]{1,0:T(8,128)(2,1)S(1)}, u32[]{:S(2)}, u32[]{:S(2)}) collective-permute-start(bf16[640,256]{1,0:T(8,128)(2,1)S(1)} %get-tuple-element.37.refs_1_), channel_id=1, source_target_pairs={{0,2},{1,3},{2,4},{3,5},{4,6},{5,7},{6,0},{7,1},{8,10},{9,11},{10,... | collective-permute-start | bytes 983048 | tf_op jit(solution)/shard_map/ppermute | solution.py:39
  271.1 31.0 %copy-start.14 = (bf16[640,256]{1,0:T(8,128)(2,1)}, bf16[640,256]{1,0:T(8,128)(2,1)S(1)}, u32[]{:S(2)}) copy-start(bf16[640,256]{1,0:T(8,128)(2,1)S(1)} %get-tuple-element.32.refs_1_) | copy-start | bytes 983044
  271.1 26.4 %collective-permute-start.20 = (bf16[640,256]{1,0:T(8,128)(2,1)S(1)}, bf16[640,256]{1,0:T(8,128)(2,1)S(1)}, u32[]{:S(2)}, u32[]{:S(2)}) collective-permute-start(bf16[640,256]{1,0:T(8,128)(2,1)S(1)} %get-tuple-element.33), channel_id=1, source_target_pairs={{0,6},{1,7},{2,0},{3,1},{4,2},{5,3},{6,4},{7,5},{8,14},{9,15},{10,... | collective-permute-start | bytes 983048 | tf_op jit(solution)/shard_map/ppermute | solution.py:39
  273.6 23.9 %collective-permute-start.19 = (bf16[640,256]{1,0:T(8,128)(2,1)S(1)}, bf16[640,256]{1,0:T(8,128)(2,1)S(1)}, u32[]{:S(2)}, u32[]{:S(2)}) collective-permute-start(bf16[640,256]{1,0:T(8,128)(2,1)S(1)} %get-tuple-element.34), channel_id=1, source_target_pairs={{0,4},{1,5},{2,6},{3,7},{4,0},{5,1},{6,2},{7,3},{8,12},{9,13},{10,... | collective-permute-start | bytes 983048 | tf_op jit(solution)/shard_map/ppermute | solution.py:39
  284.1 17.1 %collective-permute-start.18 = (bf16[640,256]{1,0:T(8,128)(2,1)S(1)}, bf16[640,256]{1,0:T(8,128)(2,1)S(1)}, u32[]{:S(2)}, u32[]{:S(2)}) collective-permute-start(bf16[640,256]{1,0:T(8,128)(2,1)S(1)} %get-tuple-element.32.refs_1_), channel_id=1, source_target_pairs={{0,2},{1,3},{2,4},{3,5},{4,6},{5,7},{6,0},{7,1},{8,10},{9,11},{10,... | collective-permute-start | bytes 983048 | tf_op jit(solution)/shard_map/ppermute | solution.py:39
  309.6 3.2 collective-permute-start.22
  315.6 7.2 %copy-start.10 = (bf16[640,256]{1,0:T(8,128)(2,1)S(1)}, bf16[640,256]{1,0:T(8,128)(2,1)}, u32[]{:S(2)}) copy-start(bf16[640,256]{1,0:T(8,128)(2,1)} %fusion.5.refs_3_) | copy-start | bytes 983044
  322.6 3.2 collective-permute-start.24
  322.8 9.9 %collective-permute-start.21 = (bf16[640,128]{1,0:T(8,128)(2,1)S(1)}, bf16[640,128]{1,0:T(8,128)(2,1)S(1)}, u32[]{:S(2)}, u32[]{:S(2)}) collective-permute-start(bf16[640,128]{1,0:T(8,128)(2,1)S(1)} %constant_dynamic-slice_fusion.1), channel_id=1, source_target_pairs={{0,1},{1,0},{2,3},{3,2},{4,5},{5,4},{6,7},{7,6},{8,9},{9,8},{10,11... | collective-permute-start | bytes 491528 | tf_op jit(solution)/shard_map/ppermute | solution.py:39
  325.8 3.8 %copy-start.9 = (bf16[640,256]{1,0:T(8,128)(2,1)S(1)}, bf16[640,256]{1,0:T(8,128)(2,1)}, u32[]{:S(2)}) copy-start(bf16[640,256]{1,0:T(8,128)(2,1)} %fusion.8.refs_2_) | copy-start | bytes 983044
  327.3 21.1 %collective-permute-start.27 = (bf16[640,256]{1,0:T(8,128)(2,1)S(1)}, bf16[640,256]{1,0:T(8,128)(2,1)S(1)}, u32[]{:S(2)}, u32[]{:S(2)}) collective-permute-start(bf16[640,256]{1,0:T(8,128)(2,1)S(1)} %get-tuple-element.30), channel_id=1, source_target_pairs={{0,6},{1,7},{2,0},{3,1},{4,2},{5,3},{6,4},{7,5},{8,14},{9,15},{10,... | collective-permute-start | bytes 983048 | tf_op jit(solution)/shard_map/ppermute | solution.py:39
  328.0 20.4 %collective-permute-start.26 = (bf16[640,256]{1,0:T(8,128)(2,1)S(1)}, bf16[640,256]{1,0:T(8,128)(2,1)S(1)}, u32[]{:S(2)}, u32[]{:S(2)}) collective-permute-start(bf16[640,256]{1,0:T(8,128)(2,1)S(1)} %get-tuple-element.31), channel_id=1, source_target_pairs={{0,4},{1,5},{2,6},{3,7},{4,0},{5,1},{6,2},{7,3},{8,12},{9,13},{10,... | collective-permute-start | bytes 983048 | tf_op jit(solution)/shard_map/ppermute | solution.py:39
  328.9 21.1 %collective-permute-start.25 = (bf16[640,256]{1,0:T(8,128)(2,1)S(1)}, bf16[640,256]{1,0:T(8,128)(2,1)S(1)}, u32[]{:S(2)}, u32[]{:S(2)}) collective-permute-start(bf16[640,256]{1,0:T(8,128)(2,1)S(1)} %get-tuple-element.29), channel_id=1, source_target_pairs={{0,2},{1,3},{2,4},{3,5},{4,6},{5,7},{6,0},{7,1},{8,10},{9,11},{10,... | collective-permute-start | bytes 983048 | tf_op jit(solution)/shard_map/ppermute | solution.py:39
  329.6 24.7 %collective-permute-start.16 = (bf16[640,128]{1,0:T(8,128)(2,1)S(1)}, bf16[640,128]{1,0:T(8,128)(2,1)S(1)}, u32[]{:S(2)}, u32[]{:S(2)}) collective-permute-start(bf16[640,128]{1,0:T(8,128)(2,1)S(1)} %constant_dynamic-slice_fusion.2), channel_id=1, source_target_pairs={{0,1},{1,0},{2,3},{3,2},{4,5},{5,4},{6,7},{7,6},{8,9},{9,8},{10,11... | collective-permute-start | bytes 491528 | tf_op jit(solution)/shard_map/ppermute | solution.py:39
  351.2 7.7 %collective-permute-start.28 = (bf16[640,128]{1,0:T(8,128)(2,1)S(1)}, bf16[640,128]{1,0:T(8,128)(2,1)S(1)}, u32[]{:S(2)}, u32[]{:S(2)}) collective-permute-start(bf16[640,128]{1,0:T(8,128)(2,1)S(1)} %constant_dynamic-slice_fusion), channel_id=1, source_target_pairs={{0,1},{1,0},{2,3},{3,2},{4,5},{5,4},{6,7},{7,6},{8,9},{9,8},{10,11... | collective-permute-start | bytes 491528 | tf_op jit(solution)/shard_map/ppermute | solution.py:39
  355.3 7.4 %collective-permute-start.23 = (bf16[640,128]{1,0:T(8,128)(2,1)S(1)}, bf16[640,128]{1,0:T(8,128)(2,1)S(1)}, u32[]{:S(2)}, u32[]{:S(2)}) collective-permute-start(bf16[640,128]{1,0:T(8,128)(2,1)S(1)} %dynamic-slice_bitcast_fusion), channel_id=1, source_target_pairs={{0,1},{1,0},{2,3},{3,2},{4,5},{5,4},{6,7},{7,6},{8,9},{9,8},{10,11... | collective-permute-start | bytes 491528 | tf_op jit(solution)/shard_map/ppermute | solution.py:39
  (5 other events, 5.6 us)
Sparse Core Ops, SparseCore 0:
  13.2 82.5 all-gather.6
  103.2 33.5 all-gather.8
  161.9 66.8 all-gather.10
  315.7 32.0 reduce-scatter.1

commit v2 on v1

--- a/solution.py
+++ b/solution.py
@@ -22,7 +22,6 @@
 CHUNKS = 4
 ORDER = ((0, 0), (1, 0), (0, 3), (1, 3), (0, 1), (1, 1), (0, 2), (1, 2))
 MIB = 1 << 20
-VMEM = 56
 
 
 def shifted(**steps):
@@ -64,8 +63,8 @@
     return master - learn_rate * (update + decay_rate * master)
 
 
-def params():
-    return pltpu.CompilerParams(vmem_limit_bytes=VMEM * MIB)
+def params(limit=32):
+    return pltpu.CompilerParams(vmem_limit_bytes=limit * MIB)
 
 
 def cost(flops, nbytes):
@@ -91,7 +90,7 @@
         grid=(8,),
         in_specs=[spec] * 4,
         out_specs=(spec, pl.BlockSpec((16, 32, 128), lambda i: (0, 0, i))),
-        compiler_params=params(),
+        compiler_params=params(56),
         cost_estimate=cost(30 * 32 * FF, 20 * 32 * FF),
         name="adam_up",
     )(w, g, m, v)
@@ -120,7 +119,7 @@
         grid=(4,),
         in_specs=[spec] * 4,
         out_specs=(spec,) + tuple(pl.BlockSpec((n, 32, 1024), lambda i: (0, i, 0)) for n in sizes),
-        compiler_params=params(),
+        compiler_params=params(56),
         cost_estimate=cost(30 * 128 * D, 20 * 128 * D),
         name="adam_down",
     )(w, g, m, v)
@@ -130,9 +129,9 @@
     return send(up, z=1), send(down, z=-1)
 
 
-def norm_kernel(a_ref, a1_ref, a2_ref, a3_ref, b_ref, g_ref, *refs):
+def norm_kernel(a_ref, b_ref, g_ref, *refs):
     out = refs[-1]
-    blocks = [a_ref[...], a1_ref[...], a2_ref[...], a3_ref[...]] + [b_ref[i] for i in range(4)]
+    blocks = [ref[i] for ref in (a_ref, b_ref) for i in range(4)]
     total = 0.0
     for block in blocks:
         f = block.astype(jnp.float32)
@@ -149,13 +148,12 @@
         norm_kernel,
         out_shape=jax.ShapeDtypeStruct((8, 640, 512), jnp.bfloat16),
         grid=(640 // rows,),
-        in_specs=[pl.BlockSpec((rows, 512), lambda i: (i, 0))] * 4
-        + [block, pl.BlockSpec((8, 512), lambda i: (0, 0))] + [ANY] * len(deps),
+        in_specs=[block, block, pl.BlockSpec((8, 512), lambda i: (0, 0))] + [ANY] * len(deps),
         out_specs=pl.BlockSpec((8, rows, 512), lambda i: (0, i, 0)),
         compiler_params=params(),
         cost_estimate=cost(8 * 640 * D, 10 * MIB),
         name="norm",
-    )(*feats_a, feats_b, gains, *deps)
+    )(feats_a, feats_b, gains, *deps)
 
 
 def silu(u):
@@ -173,13 +171,17 @@
 
 
 def last_kernel(s_ref, acc_ref, *refs):
-    lhs, ws, out = refs[:2], refs[2:4], refs[4]
+    lhs, ws, out = refs[:2], refs[2:6], refs[6]
     for n in range(4):
         at = slice(n * 256, (n + 1) * 256)
         u = acc_ref[:, at]
-        for a, w in zip(lhs, ws):
-            u += jnp.dot(a[0], w[:, at], preferred_element_type=jnp.float32)
-        out[:, at] = silu(u * D ** (-0.5)).astype(jnp.bfloat16)
+        for k, w in enumerate(ws):
+            a = lhs[k // 2][0, :, (k % 2) * 256 : (k % 2 + 1) * 256]
+            u += jnp.dot(a, w[:, at], preferred_element_type=jnp.float32)
+        h = silu(u * D ** (-0.5)).astype(jnp.bfloat16)
+        for q in (2 * n, 2 * n + 1):
+            to = pl.multiple_of(s_ref[8 + q] * 128, 128)
+            out[:, pl.ds(to, 128)] = h[:, (q - 2 * n) * 128 : (q - 2 * n + 1) * 128]
 
 
 def hidden_specs(places, ws):
@@ -223,42 +225,52 @@
     )(scalars, acc, normed, normed, *ws)
 
 
-def partial_kernel(s_ref, own_ref, sib_ref, w_ref, *refs):
-    own_out, sib_out = refs[-2:]
-    w = w_ref[:, 0].reshape(1024, 1024)
+def partial_kernel(s_ref, own_ref, sib_ref, *refs):
+    ws, (own_out, sib_out, w_ref) = refs[:5], refs[-3:]
+
+    @pl.when(pl.program_id(0) == 0)
+    def _():
+        at = 0
+        for w in ws:
+            for part in [w[0, 0], w[1, 0]] if len(w.shape) == 4 else [w[0]]:
+                w_ref[at : at + 128] = part
+                at += 128
+
     for src, dst in ((sib_ref, sib_out), (own_ref, own_out)):
-        term = jnp.dot(src[...], w, preferred_element_type=jnp.float32)
+        term = jnp.dot(src[...], w_ref[...], preferred_element_type=jnp.float32)
         term = (term * FF ** (-0.5)).astype(jnp.bfloat16)
         for xi in range(4):
             dst[s_ref[xi]] = term[:, xi * 256 : (xi + 1) * 256]
 
 
-def partial_of(scalars, own, sib, w, j, deps):
+def partial_of(scalars, own, sib, ws, j, deps):
     rows = 320
     block = pl.BlockSpec((rows, 1024), lambda i, s: (i, 0))
     out = pl.BlockSpec((4, rows, 256), lambda i, s: (0, i, 0))
     shape = jax.ShapeDtypeStruct((4, 640, 256), jnp.bfloat16)
-    weights = pl.BlockSpec((8, 1, 128, 1024), lambda i, s: (0, j, 0, 0), pipeline_mode=pl.Buffered(1))
+    two = pl.BlockSpec((2, 1, 128, 1024), lambda i, s: (0, j, 0, 0), pipeline_mode=pl.Buffered(1))
+    one = pl.BlockSpec((1, 128, 1024), lambda i, s: (j, 0, 0), pipeline_mode=pl.Buffered(1))
     return pl.pallas_call(
         partial_kernel,
         out_shape=(shape, shape),
         grid_spec=pltpu.PrefetchScalarGridSpec(
             num_scalar_prefetch=1,
             grid=(640 // rows,),
-            in_specs=[block, block, weights] + [ANY] * len(deps),
+            in_specs=[block, block, two, two, two, one, one] + [ANY] * len(deps),
             out_specs=(out, out),
+            scratch_shapes=[pltpu.VMEM((1024, 1024), jnp.bfloat16)],
         ),
         compiler_params=params(),
         cost_estimate=cost(4 * 640 * 1024 * 1024, 8 * MIB),
         name="partial",
-    )(scalars, own, sib, w, *deps)
+    )(scalars, own, sib, *ws, *deps)
 
 
 def slot_table():
     rows = []
-    for ylo, z, yhi, x in np.ndindex(2, 4, 2, 4):
+    for ylo, z, yhi in np.ndindex(2, 4, 2):
         qs = [(ylo ^ dy) * 4 + (z + dz) % 4 for dy, dz in ORDER]
-        rows.append([(q // 2 - x) % 4 if q % 2 == yhi else 4 + q // 2 for q in qs])
+        rows.append([((q % 2) ^ yhi) * 4 + q // 2 for q in qs] + [qs.index(q) for q in range(8)])
     return np.array(rows, np.int32)
 
 
@@ -280,47 +292,54 @@
     ylo, z, core, x, yhi = (lax.axis_index(a) for a in AXES)
 
     tokens_b = send(tokens, yhi=1)
-    near = [tokens, send(tokens, x=3), send(tokens, x=2), send(tokens, x=1)]
+    feats_a = lax.all_gather(tokens, "x", axis=0)
 
     up_updated, columns = up_step(up_master, up_gradient, up_first, up_second)
     down_updated, down_a, down_b = down_step(down_master, down_gradient, down_first, down_second)
-    plane = ("ylo", "z")
-    ws_a = lax.all_gather(down_a, plane, axis=0)
-
+
+    st_a = jnp.stack([down_a, send(down_a, ylo=1)])
+    low_a, high_a = both_ways(st_a, st_a)
     u0 = lax.all_to_all(after(columns, down_a), ("core", "x", "yhi"), 0, 0, tiled=True).reshape(512, 1024)
+    feats_b = lax.all_gather(after(tokens_b, u0), "x", axis=0)
+    opp_a = both_ways(low_a[0], high_a[1])
+    ws_a = (st_a, low_a, high_a, *opp_a)
+
     u1 = send(u0, ylo=1)
     low0, high0 = both_ways(u0, u0)
-    feats_b = lax.all_gather(after(tokens_b, low0, high0, ws_a, *near[1:]), "x", axis=0)
+    down_b = after(down_b, u1)
+    ylo_b = send(down_b, ylo=1)
     low1, high1 = both_ways(u1, u1)
-    opp = (send(low0, z=1), send(high1, z=-1))
-    ws_b = lax.all_gather(after(down_b, low1), plane, axis=0)
+    opp0 = both_ways(after(low0[:256], u1, *opp_a), high0[256:])
+    opp1 = both_ways(low1[:256], high1[256:])
+    st_b = after(jnp.stack([down_b, ylo_b]), low1)
+    low_b, high_b = both_ways(st_b, st_b)
+    ws_b = (st_b, low_b, high_b, *both_ways(low_b[0], high_b[1]))
 
     gains = norm_gain.reshape(4, 2, 512)
-    gain_a = lax.dynamic_index_in_dim(gains, yhi, 1, keepdims=False)
-    gain_a = lax.dynamic_slice_in_dim(jnp.concatenate([gain_a, gain_a]), x, 4, 0)
-    gain_b = lax.dynamic_index_in_dim(gains, 1 - yhi, 1, keepdims=False)
-    gains = jnp.concatenate([gain_a, gain_b])
-    near = [v.reshape(640, 512) for v in near]
-    normed = norm_of(near, feats_b.reshape(4, 640, 512), gains, (low1, high1))
+    gains = jnp.concatenate([lax.dynamic_index_in_dim(gains, k, 1, keepdims=False) for k in (yhi, 1 - yhi)])
+    feats_a, feats_b = feats_a.reshape(4, 640, 512), feats_b.reshape(4, 640, 512)
+    normed = norm_of(feats_a, feats_b, gains, (low1, high1, *opp0, ylo_b))
     normed_sib = send(normed, core=1)
 
-    where = lax.dynamic_index_in_dim(jnp.asarray(SLOTS), ((ylo * 4 + z) * 2 + yhi) * 4 + x, 0, keepdims=False)
+    where = lax.dynamic_index_in_dim(jnp.asarray(SLOTS), (ylo * 4 + z) * 2 + yhi, 0, keepdims=False)
     ws_up = (u0, u1, low0, low1, high0, high1)
     firsts = [hidden_first(where, n, ws_up) for n in (normed, normed_sib)]
-    hidden_own, hidden_sib = (hidden_last(where, f, n, opp) for f, n in zip(firsts, (normed, normed_sib)))
+    hidden_own, hidden_sib = (
+        hidden_last(where, f, n, opp0 + opp1) for f, n in zip(firsts, (normed, normed_sib))
+    )
 
     pieces, parts, sums, reduced = [], [], [], []
     places = jnp.arange(4, dtype=jnp.int32)
     add = lambda a, b: (a.astype(jnp.float32) + b.astype(jnp.float32)).astype(jnp.bfloat16)
     for j in range(CHUNKS):
-        direct = j != 2
+        direct = j % 2 == 1
         part, part_sib = partial_of(
             (places - x) % 4 if direct else places,
             hidden_own,
             hidden_sib,
             (ws_a, ws_b)[SPLIT[j][0]],
             SPLIT[j][1],
-            parts[-1:] + sums[-2:-1] + (reduced if j == 2 else []),
+            ([], parts + [low_b, high_b], sums + reduced[1:], parts[2:] + reduced[:2])[j],
         )
         parts.append(part_sib)
         part_sib = send(part_sib, core=1)

time: 372 us -> 359 us (0.965)
  waiting for transfers between devices: 210 us -> 177 us
  local copies, waits for them, and re-layouts: 7.91 us -> 33.9 us
  Pallas kernels: 79.7 us -> 64.4 us
  starting transfers between devices: 48.3 us -> 53.3 us
  other arithmetic: 11 us -> 15 us
    ppermute x29 -> x35, waiting for transfers between devices: 194 us -> 176 us  [send(): return lax.ppermute(v, AXES, shifted(**steps))]
    unnamed x40 -> x93, local copies, waits for them, and re-layouts: 5.2 us -> 23.2 us
    all_to_all x1, waiting for transfers between devices: 16.2 us -> 0.01 us  [body(): lax.all_to_all(after(columns, down_a), ('core', 'x', 'yhi'), 0, 0, tiled=...]
    pallas_call x2, Pallas kernels: 20 us -> 14.5 us  [hidden_first(): pl.pallas_call(first_kernel, out_shape=jax.ShapeDtypeStruct((640, 1024),...]
    ppermute x29 -> x35, starting transfers between devices: 41 us -> 45.9 us  [send(): return lax.ppermute(v, AXES, shifted(**steps))]
    pallas_call x4, Pallas kernels: 27.8 us -> 23.1 us  [partial_of(): pl.pallas_call(partial_kernel, out_shape=(shape, shape), grid_spec=pltpu....]
    slice x0 -> x4, local copies, waits for them, and re-layouts: none -> 4.34 us  [the longest x2 2.68 us: body(): opp1 = both_ways(low1[:256], high1[256:])]
    squeeze x1 -> x5, local copies, waits for them, and re-layouts: 1.2 us -> 5.34 us  [the longest x2 2.94 us: body(): ws_b = (st_b, low_b, high_b, *both_ways(low_b[0], high_b[1]))]
  transfers between devices with their start and end apart: 34 -> 40, of which waited for: 19 -> 18; matrix products, arithmetic and copies ran while one was open for 2% -> 7% of each run, Pallas kernels for 16% -> 17%
where the time goes in v2:
time: 359 us; the launch traced here: 357 us
  waiting for transfers between devices  177 us (49%)
  Pallas kernels  64.4 us (18%)
  starting transfers between devices  53.3 us (15%)
  local copies, waits for them, and re-layouts  33.9 us (9%)
  other arithmetic  15 us (4%)
  between operations  14.3 us (4%)
    ppermute x35, waiting for transfers between devices, send(): return lax.ppermute(v, AXES, shifted(**steps))  176 us
    ppermute x35, starting transfers between devices, send(): return lax.ppermute(v, AXES, shifted(**steps))  45.9 us
    unnamed x93, local copies, waits for them, and re-layouts  23.2 us
    pallas_call x4, Pallas kernels, partial_of(): pl.pallas_call(partial_kernel, out_shape=(shape, shape), grid_spec=pltpu....  23.1 us
    pallas_call x2, Pallas kernels, hidden_first(): pl.pallas_call(first_kernel, out_shape=jax.ShapeDtypeStruct((640, 1024),...  14.5 us
    pallas_call x2, Pallas kernels, hidden_last(): pl.pallas_call(last_kernel, out_shape=jax.ShapeDtypeStruct((640, 1024), j...  9.29 us
    convert_element_type x8, other arithmetic, body(): (a.astype(jnp.float32) + b.astype(jnp.float32)).astype(jnp.bfloat16)  8.36 us
    pallas_call x1, Pallas kernels, up_step(): pl.pallas_call(up_kernel, out_shape=(jax.ShapeDtypeStruct((32, FF), jnp.f...  7.64 us
  transfers between devices with their start and end apart: 40, of which 18 were waited for; matrix products, arithmetic and copies ran while one was open for 7% of the time, Pallas kernels for 17%

profile of v2, /device:TPU:0, one launch (start us, length us, event | category | flops | bytes accessed | tf_op | source)
XLA Modules:
  0.0 357.5 jit_solution(5534252456755717791)
XLA Ops:
  7.9 7.6 %adam_up.1 = (f32[32,16384]{1,0:T(8,128)}, bf16[16,32,1024]{2,1,0:T(8,128)(2,1)}) custom-call(f32[32,16384]{1,0:T(8,128)} %w_ref.2, bf16[32,16384]{1,0:T(8,128)(2,1)} %g_ref.2, f32[32,16384]{1,0:T(8,128)} %m_ref.2, f32[32,16384]{1,0:T(8,128)} %v_ref.2), custom_call_target="tpu_custom_call" | custom-call | flops 15728 | bytes 10485 | tf_op jit(solution)/shard_map/adam_up/pallas_call | solution.py:84
  15.5 5.8 %adam_down.1 = (f32[128,4096]{1,0:T(8,128)}, bf16[2,128,1024]{2,1,0:T(8,128)(2,1)}, bf16[2,128,1024]{2,1,0:T(8,128)(2,1)}) custom-call(f32[128,4096]{1,0:T(8,128)} %w_ref.3, bf16[128,4096]{1,0:T(8,128)(2,1)} %g_ref.3, f32[128,4096]{1,0:T(8,128)} %m_ref.3, f32[128,4096]{1,0:T(8,128)} %v_ref.3), custom_call_target="tpu_custom_call" | custom-call | flops 15728 | bytes 10485 | tf_op jit(solution)/shard_map/adam_down/pallas_call | solution.py:115
  21.4 7.3 %all-to-all-start = ((bf16[16,32,1024]{2,1,0:T(8,128)(2,1)}), bf16[16,32,1024]{2,1,0:T(8,128)(2,1)S(1)}, u32[]{:S(2)}, u32[]{:S(2)}) async-start(bf16[16,32,1024]{2,1,0:T(8,128)(2,1)} %after.5), calls=%async_computation | async-start | bytes 2097152 | tf_op jit(solution)/shard_map/all_to_all | solution.py:302
  28.7 3.5 collective-permute-start
  32.2 26.3 %collective-permute-done.refs_0_ = bf16[2,320,512]{2,1,0:T(8,128)(2,1)S(1)} collective-permute-done((bf16[2,320,512]{2,1,0:T(8,128)(2,1)S(1)}, bf16[2,320,512]{2,1,0:T(8,128)(2,1)S(1)}, u32[]{:S(2)}, u32[]{:S(2)}) %collective-permute-start) | collective-permute-done | bytes 655392 | tf_op jit(solution)/shard_map/ppermute | solution.py:38
  60.6 13.0 %collective-permute-done.5 = bf16[2,128,1024]{2,1,0:T(8,128)(2,1)S(1)} collective-permute-done((bf16[2,128,1024]{2,1,0:T(8,128)(2,1)}, bf16[2,128,1024]{2,1,0:T(8,128)(2,1)S(1)}, u32[]{:S(2)}, u32[]{:S(2)}) %collective-permute-start.5) | collective-permute-done | bytes 524320 | tf_op jit(solution)/shard_map/ppermute | solution.py:38
  74.8 2.0 collective-permute-start.6
  76.7 2.4 collective-permute-start.8
  79.8 1.9 collective-permute-start.11
  81.8 21.3 %collective-permute-done.6.refs_1_ = bf16[2,2,128,1024]{3,2,1,0:T(8,128)(2,1)S(1)} collective-permute-done((bf16[2,2,128,1024]{3,2,1,0:T(8,128)(2,1)S(1)}, bf16[2,2,128,1024]{3,2,1,0:T(8,128)(2,1)S(1)}, u32[]{:S(2)}, u32[]{:S(2)}) %collective-permute-start.6) | collective-permute-done | bytes 1048608 | tf_op jit(solution)/shard_map/ppermute | solution.py:38
  105.8 3.2 collective-permute-start.9
  109.1 16.2 %collective-permute-done.11.refs_10_ = bf16[512,1024]{1,0:T(8,128)(2,1)S(1)} collective-permute-done((bf16[512,1024]{1,0:T(8,128)(2,1)S(1)}, bf16[512,1024]{1,0:T(8,128)(2,1)S(1)}, u32[]{:S(2)}, u32[]{:S(2)}) %collective-permute-start.11) | collective-permute-done | bytes 1048608 | tf_op jit(solution)/shard_map/ppermute | solution.py:38
  125.3 3.6 collective-permute-start.3
  133.3 3.6 %collective-permute-done.7.refs_2_.refs_3_ = bf16[2,128,1024]{2,1,0:T(8,128)(2,1)} collective-permute-done((bf16[2,128,1024]{2,1,0:T(8,128)(2,1)}, bf16[2,128,1024]{2,1,0:T(8,128)(2,1)}, u32[]{:S(2)}, u32[]{:S(2)}) %collective-permute-start.7) | collective-permute-done | bytes 524320 | tf_op jit(solution)/shard_map/ppermute | solution.py:38
  138.7 29.2 %collective-permute-done.12.refs_3_ = bf16[256,1024]{1,0:T(8,128)(2,1)S(1)} collective-permute-done((bf16[256,1024]{1,0:T(8,128)(2,1)}, bf16[256,1024]{1,0:T(8,128)(2,1)S(1)}, u32[]{:S(2)}, u32[]{:S(2)}) %collective-permute-start.12) | collective-permute-done | bytes 524320 | tf_op jit(solution)/shard_map/ppermute | solution.py:38
  168.6 2.2 copy-done.30
  170.8 1.7 copy-done.31
  172.6 4.1 %norm.1.refs_0_.refs_1_.refs_2_.refs_3_.refs_4_.refs_5_ = bf16[8,640,512]{2,1,0:T(8,128)(2,1)} custom-call(bf16[4,640,512]{2,1,0:T(8,128)(2,1)S(1)} %bitcast.61, bf16[4,640,512]{2,1,0:T(8,128)(2,1)S(1)} %bitcast.62, f32[8,512]{1,0:T(8,128)S(1)} %pad_maximum_fusion.3.g_ref, bf16[512,1024]{1,0:T(8,128)(2,1)S(1)} %collective-permute-done.2.refs_0_.refs_9_.refs_1_, ...), custom_call_target="tpu_custom_call" | custom-call | flops 20971 | bytes 10485 | tf_op jit(solution)/shard_map/norm/pallas_call | solution.py:147
  176.7 2.1 pad_maximum_fusion.1.refs_0_
  180.3 1.9 collective-permute-start.20
  183.1 1.9 slice.101
  185.0 3.2 collective-permute-start.15
  191.3 7.2 %hidden_first.2.acc_ref = f32[640,1024]{1,0:T(8,128)S(1)} custom-call(s32[16]{0:T(128)S(1)} %fusion.17.s_ref, bf16[8,640,512]{2,1,0:T(8,128)(2,1)} %norm.1.refs_0_.refs_1_.refs_2_.refs_3_.refs_4_.refs_5_, bf16[8,640,512]{2,1,0:T(8,128)(2,1)} %norm.1.refs_0_.refs_1_.refs_2_.refs_3_.refs_4_.refs_5_, ...), custom_call_target="tpu_custom_call" | custom-call | flops 4026531 | bytes 14680 | tf_op jit(solution)/shard_map/hidden_first/pallas_call | solution.py:195
  198.5 18.9 %collective-permute-done.14.refs_4_ = bf16[256,1024]{1,0:T(8,128)(2,1)} collective-permute-done((bf16[256,1024]{1,0:T(8,128)(2,1)}, bf16[256,1024]{1,0:T(8,128)(2,1)}, u32[]{:S(2)}, u32[]{:S(2)}) %collective-permute-start.14) | collective-permute-done | bytes 524320 | tf_op jit(solution)/shard_map/ppermute | solution.py:38
  217.5 4.5 %hidden_last.2.own_ref = bf16[640,1024]{1,0:T(8,128)(2,1)S(1)} custom-call(s32[16]{0:T(128)S(1)} %fusion.17.s_ref, f32[640,1024]{1,0:T(8,128)S(1)} %hidden_first.2.acc_ref, bf16[8,640,512]{2,1,0:T(8,128)(2,1)} %norm.1.refs_0_.refs_1_.refs_2_.refs_3_.refs_4_.refs_5_, bf16[8,640,512]{2,1,0:T(8,128)(2,1)} %norm.1.refs_0_.refs_1_.refs_2_.refs_3_.refs_4_.refs_5_, ...), custom_call_target="tpu_custom_call" | custom-call | flops 1342177 | bytes 8388 | tf_op jit(solution)/shard_map/hidden_last/pallas_call | solution.py:213
  222.0 7.2 %hidden_first.3.acc_ref = f32[640,1024]{1,0:T(8,128)S(1)} custom-call(s32[16]{0:T(128)S(1)} %fusion.17.s_ref, bf16[8,640,512]{2,1,0:T(8,128)(2,1)} %collective-permute-done.16.refs_0_.refs_1_.refs_2_.refs_3_.refs_4_.refs_5_, bf16[8,640,512]{2,1,0:T(8,128)(2,1)} %collective-permute-done.16.refs_0_.refs_1_.refs_2_.refs_3_.refs_4_.refs_5_, ...), custom_call_target="tpu_custom_call" | custom-call | flops 4026531 | bytes 14680 | tf_op jit(solution)/shard_map/hidden_first/pallas_call | solution.py:195
  229.3 4.8 %hidden_last.3.sib_ref = bf16[640,1024]{1,0:T(8,128)(2,1)S(1)} custom-call(s32[16]{0:T(128)S(1)} %fusion.17.s_ref, f32[640,1024]{1,0:T(8,128)S(1)} %hidden_first.3.acc_ref, bf16[8,640,512]{2,1,0:T(8,128)(2,1)} %collective-permute-done.16.refs_0_.refs_1_.refs_2_.refs_3_.refs_4_.refs_5_, ...), custom_call_target="tpu_custom_call" | custom-call | flops 1342177 | bytes 8388 | tf_op jit(solution)/shard_map/hidden_last/pallas_call | solution.py:213
  234.2 5.9 %partial.4 = (bf16[4,640,256]{2,1,0:T(8,128)(2,1)S(1)}, bf16[4,640,256]{2,1,0:T(8,128)(2,1)}) custom-call(s32[4]{0:T(128)S(1)} %iota.7.s_ref, bf16[640,1024]{1,0:T(8,128)(2,1)S(1)} %hidden_last.2.own_ref, bf16[640,1024]{1,0:T(8,128)(2,1)S(1)} %hidden_last.3.sib_ref, bf16[2,2,128,1024]{3,2,1,0:T(8,128)(2,1)S(1)} %copy-done.12, ...), custom_call_target="tpu_custom_call" | custom-call | flops 2684354 | bytes 8388 | tf_op jit(solution)/shard_map/partial/pallas_call | solution.py:253
  244.8 5.9 %partial.5 = (bf16[4,640,256]{2,1,0:T(8,128)(2,1)S(1)}, bf16[4,640,256]{2,1,0:T(8,128)(2,1)}) custom-call(s32[4]{0:T(128)S(1)} %and_select_fusion.s_ref, bf16[640,1024]{1,0:T(8,128)(2,1)S(1)} %hidden_last.2.own_ref, bf16[640,1024]{1,0:T(8,128)(2,1)S(1)} %hidden_last.3.sib_ref, bf16[2,2,128,1024]{3,2,1,0:T(8,128)(2,1)S(1)} %copy-done.13, ...), custom_call_target="tpu_custom_call" | custom-call | flops 2684354 | bytes 8388 | tf_op jit(solution)/shard_map/partial/pallas_call | solution.py:253
  252.4 1.9 slice_bitcast_fusion.1
  255.6 2.7 add_convert_fusion.1.refs_5_
  258.3 1.7 fusion.8
  260.0 2.9 collective-permute-start.24
  265.7 2.2 collective-permute-start.27
  267.9 11.2 %collective-permute-done.24 = bf16[640,256]{1,0:T(8,128)(2,1)S(1)} collective-permute-done((bf16[640,256]{1,0:T(8,128)(2,1)S(1)}, bf16[640,256]{1,0:T(8,128)(2,1)S(1)}, u32[]{:S(2)}, u32[]{:S(2)}) %collective-permute-start.24) | collective-permute-done | bytes 327712 | tf_op jit(solution)/shard_map/ppermute | solution.py:38
  280.4 7.1 %collective-permute-done.22 = bf16[640,256]{1,0:T(8,128)(2,1)S(1)} collective-permute-done((bf16[640,256]{1,0:T(8,128)(2,1)S(1)}, bf16[640,256]{1,0:T(8,128)(2,1)S(1)}, u32[]{:S(2)}, u32[]{:S(2)}) %collective-permute-start.22) | collective-permute-done | bytes 327712 | tf_op jit(solution)/shard_map/ppermute | solution.py:38
  288.8 5.3 %partial.6 = (bf16[4,640,256]{2,1,0:T(8,128)(2,1)S(1)}, bf16[4,640,256]{2,1,0:T(8,128)(2,1)S(1)}) custom-call(s32[4]{0:T(128)S(1)} %iota.9.s_ref, bf16[640,1024]{1,0:T(8,128)(2,1)S(1)} %hidden_last.2.own_ref, bf16[640,1024]{1,0:T(8,128)(2,1)S(1)} %hidden_last.3.sib_ref, bf16[2,2,128,1024]{3,2,1,0:T(8,128)(2,1)S(1)} %copy-done.4, ...), custom_call_target="tpu_custom_call" | custom-call | flops 2684354 | bytes 8388 | tf_op jit(solution)/shard_map/partial/pallas_call | solution.py:253
  295.3 2.0 collective-permute-done.28
  303.3 6.0 %partial.7 = (bf16[4,640,256]{2,1,0:T(8,128)(2,1)S(1)}, bf16[4,640,256]{2,1,0:T(8,128)(2,1)}) custom-call(s32[4]{0:T(128)S(1)} %and_select_fusion.s_ref, bf16[640,1024]{1,0:T(8,128)(2,1)S(1)} %hidden_last.2.own_ref, bf16[640,1024]{1,0:T(8,128)(2,1)S(1)} %hidden_last.3.sib_ref, bf16[2,2,128,1024]{3,2,1,0:T(8,128)(2,1)S(1)} %copy-done.5, ...), custom_call_target="tpu_custom_call" | custom-call | flops 2684354 | bytes 8388 | tf_op jit(solution)/shard_map/partial/pallas_call | solution.py:253
  310.8 2.8 collective-permute-done.30
  315.0 4.2 %collective-permute-start.33 = (bf16[640,256]{1,0:T(8,128)(2,1)S(1)}, bf16[640,256]{1,0:T(8,128)(2,1)S(1)}, u32[]{:S(2)}, u32[]{:S(2)}) collective-permute-start(bf16[640,256]{1,0:T(8,128)(2,1)S(1)} %get-tuple-element.30), channel_id=1, source_target_pairs={{0,6},{1,7},{2,0},{3,1},{4,2},{5,3},{6,4},{7,5},{8,14},{9,15},{10,... | collective-permute-start | bytes 983048 | tf_op jit(solution)/shard_map/ppermute | solution.py:38
  320.9 6.8 %collective-permute-done.33 = bf16[640,256]{1,0:T(8,128)(2,1)S(1)} collective-permute-done((bf16[640,256]{1,0:T(8,128)(2,1)S(1)}, bf16[640,256]{1,0:T(8,128)(2,1)S(1)}, u32[]{:S(2)}, u32[]{:S(2)}) %collective-permute-start.33) | collective-permute-done | bytes 327712 | tf_op jit(solution)/shard_map/ppermute | solution.py:38
  327.7 3.6 %collective-permute-done.32 = bf16[640,256]{1,0:T(8,128)(2,1)S(1)} collective-permute-done((bf16[640,256]{1,0:T(8,128)(2,1)S(1)}, bf16[640,256]{1,0:T(8,128)(2,1)S(1)}, u32[]{:S(2)}, u32[]{:S(2)}) %collective-permute-start.32) | collective-permute-done | bytes 327712 | tf_op jit(solution)/shard_map/ppermute | solution.py:38
  331.3 5.6 %collective-permute-done.31 = bf16[640,256]{1,0:T(8,128)(2,1)S(1)} collective-permute-done((bf16[640,256]{1,0:T(8,128)(2,1)S(1)}, bf16[640,256]{1,0:T(8,128)(2,1)S(1)}, u32[]{:S(2)}, u32[]{:S(2)}) %collective-permute-start.31) | collective-permute-done | bytes 327712 | tf_op jit(solution)/shard_map/ppermute | solution.py:38
  338.1 1.9 collective-permute-start.34
  341.1 1.8 collective-permute-start.29
  342.9 3.4 collective-permute-done.34
  346.3 2.8 collective-permute-done.29
  (177 shorter events, 48.8 us)
Async XLA Ops:
  7.2 161.4 %all-gather.5.cloned.1.call-start = ((), (), s32[]{:S(2)}) async-start(), calls=%async_computation.5 | async-start | bytes 3276800 | tf_op jit(solution)/shard_map/all_gather | solution.py:295
  21.4 37.2 %all-to-all-start = ((bf16[16,32,1024]{2,1,0:T(8,128)(2,1)}), bf16[16,32,1024]{2,1,0:T(8,128)(2,1)S(1)}, u32[]{:S(2)}, u32[]{:S(2)}) async-start(bf16[16,32,1024]{2,1,0:T(8,128)(2,1)} %after.5), calls=%async_computation | async-start | bytes 2097152 | tf_op jit(solution)/shard_map/all_to_all | solution.py:302
  28.7 139.9 %all-gather.7.cloned.1.call-start = ((), (), s32[]{:S(2)}) async-start(), calls=%async_computation.6 | async-start | bytes 3276800 | tf_op jit(solution)/shard_map/all_gather | solution.py:303
  28.7 29.9 %collective-permute-start = (bf16[2,320,512]{2,1,0:T(8,128)(2,1)S(1)}, bf16[2,320,512]{2,1,0:T(8,128)(2,1)S(1)}, u32[]{:S(2)}, u32[]{:S(2)}) collective-permute-start(bf16[2,320,512]{2,1,0:T(8,128)(2,1)S(1)} %copy-done.44), channel_id=1, source_target_pairs={{0,1},{1,0},{2,3},{3,2},{4,5},{5,4},{6,7},{7,6},{8,9},{9,8},{10,11... | collective-permute-start | bytes 1966088 | tf_op jit(solution)/shard_map/ppermute | solution.py:38
  59.8 238.9 %reduce-scatter.3.cloned.1.call-start = ((), (), s32[]{:S(2)}) async-start(), calls=%async_computation.3 | async-start | bytes 1638400 | tf_op jit(solution)/shard_map/reduce_scatter | solution.py:354
  59.8 13.8 %collective-permute-start.5 = (bf16[2,128,1024]{2,1,0:T(8,128)(2,1)}, bf16[2,128,1024]{2,1,0:T(8,128)(2,1)S(1)}, u32[]{:S(2)}, u32[]{:S(2)}) collective-permute-start(bf16[2,128,1024]{2,1,0:T(8,128)(2,1)} %get-tuple-element.19.refs_1_), channel_id=1, source_target_pairs={{0,64},{1,65},{2,66},{3,67},{4,68},{5,69},{6,70},{7,71},{8,72},{9,... | collective-permute-start | bytes 1572872 | tf_op jit(solution)/shard_map/ppermute | solution.py:38
  74.7 34.3 %copy-start.11 = (bf16[2,2,128,1024]{3,2,1,0:T(8,128)(2,1)}, bf16[2,2,128,1024]{3,2,1,0:T(8,128)(2,1)S(1)}, u32[]{:S(2)}) copy-start(bf16[2,2,128,1024]{3,2,1,0:T(8,128)(2,1)S(1)} %pad_maximum_fusion.refs_0_) | copy-start | bytes 3145732
  74.8 28.3 %collective-permute-start.6 = (bf16[2,2,128,1024]{3,2,1,0:T(8,128)(2,1)S(1)}, bf16[2,2,128,1024]{3,2,1,0:T(8,128)(2,1)S(1)}, u32[]{:S(2)}, u32[]{:S(2)}) collective-permute-start(bf16[2,2,128,1024]{3,2,1,0:T(8,128)(2,1)S(1)} %pad_maximum_fusion.refs_0_), channel_id=1, source_target_pairs={{0,16},{1,17},{2,18},{3,19},{4,20},{5,21},{6,22},{7,23},{8,24},{9,... | collective-permute-start | bytes 3145736 | tf_op jit(solution)/shard_map/ppermute | solution.py:38
  76.7 27.3 %collective-permute-start.8 = (bf16[2,2,128,1024]{3,2,1,0:T(8,128)(2,1)S(1)}, bf16[2,2,128,1024]{3,2,1,0:T(8,128)(2,1)S(1)}, u32[]{:S(2)}, u32[]{:S(2)}) collective-permute-start(bf16[2,2,128,1024]{3,2,1,0:T(8,128)(2,1)S(1)} %pad_maximum_fusion.refs_0_), channel_id=1, source_target_pairs={{0,48},{1,49},{2,50},{3,51},{4,52},{5,53},{6,54},{7,55},{8,56},{9,... | collective-permute-start | bytes 3145736 | tf_op jit(solution)/shard_map/ppermute | solution.py:38
  79.1 29.9 %collective-permute-start.1 = (bf16[512,1024]{1,0:T(8,128)(2,1)S(1)}, bf16[512,1024]{1,0:T(8,128)(2,1)S(1)}, u32[]{:S(2)}, u32[]{:S(2)}) collective-permute-start(bf16[512,1024]{1,0:T(8,128)(2,1)S(1)} %bitcast.56), channel_id=1, source_target_pairs={{0,64},{1,65},{2,66},{3,67},{4,68},{5,69},{6,70},{7,71},{8,72},{9,... | collective-permute-start | bytes 3145736 | tf_op jit(solution)/shard_map/ppermute | solution.py:38
  79.8 45.5 %collective-permute-start.11 = (bf16[512,1024]{1,0:T(8,128)(2,1)S(1)}, bf16[512,1024]{1,0:T(8,128)(2,1)S(1)}, u32[]{:S(2)}, u32[]{:S(2)}) collective-permute-start(bf16[512,1024]{1,0:T(8,128)(2,1)S(1)} %bitcast.57), channel_id=1, source_target_pairs={{0,48},{1,49},{2,50},{3,51},{4,52},{5,53},{6,54},{7,55},{8,56},{9,... | collective-permute-start | bytes 3145736 | tf_op jit(solution)/shard_map/ppermute | solution.py:38
  81.7 49.0 %collective-permute-start.4 = (bf16[512,1024]{1,0:T(8,128)(2,1)S(1)}, bf16[512,1024]{1,0:T(8,128)(2,1)S(1)}, u32[]{:S(2)}, u32[]{:S(2)}) collective-permute-start(bf16[512,1024]{1,0:T(8,128)(2,1)S(1)} %bitcast.58), channel_id=1, source_target_pairs={{0,16},{1,17},{2,18},{3,19},{4,20},{5,21},{6,22},{7,23},{8,24},{9,... | collective-permute-start | bytes 3145736 | tf_op jit(solution)/shard_map/ppermute | solution.py:38
  103.1 26.6 %copy-start.20 = (bf16[2,2,128,1024]{3,2,1,0:T(8,128)(2,1)}, bf16[2,2,128,1024]{3,2,1,0:T(8,128)(2,1)S(1)}, u32[]{:S(2)}) copy-start(bf16[2,2,128,1024]{3,2,1,0:T(8,128)(2,1)S(1)} %collective-permute-done.6.refs_1_) | copy-start | bytes 3145732
  104.0 32.9 %collective-permute-start.7 = (bf16[2,128,1024]{2,1,0:T(8,128)(2,1)}, bf16[2,128,1024]{2,1,0:T(8,128)(2,1)}, u32[]{:S(2)}, u32[]{:S(2)}) collective-permute-start(bf16[2,128,1024]{2,1,0:T(8,128)(2,1)} %slice_bitcast_fusion.3), channel_id=1, source_target_pairs={{0,16},{1,17},{2,18},{3,19},{4,20},{5,21},{6,22},{7,23},{8,24},{9,... | collective-permute-start | bytes 1572872 | tf_op jit(solution)/shard_map/ppermute | solution.py:38
  105.8 31.8 %collective-permute-start.9 = (bf16[2,128,1024]{2,1,0:T(8,128)(2,1)}, bf16[2,128,1024]{2,1,0:T(8,128)(2,1)}, u32[]{:S(2)}, u32[]{:S(2)}) collective-permute-start(bf16[2,128,1024]{2,1,0:T(8,128)(2,1)} %slice_bitcast_fusion.2), channel_id=1, source_target_pairs={{0,48},{1,49},{2,50},{3,51},{4,52},{5,53},{6,54},{7,55},{8,56},{9,... | collective-permute-start | bytes 1572872 | tf_op jit(solution)/shard_map/ppermute | solution.py:38
  109.0 24.2 %copy-start.2 = (bf16[512,1024]{1,0:T(8,128)(2,1)}, bf16[512,1024]{1,0:T(8,128)(2,1)S(1)}, u32[]{:S(2)}) copy-start(bf16[512,1024]{1,0:T(8,128)(2,1)S(1)} %collective-permute-done.1.refs_1_.refs_7_) | copy-start | bytes 3145732
  109.0 59.5 %collective-permute-start.2 = (bf16[512,1024]{1,0:T(8,128)(2,1)S(1)}, bf16[512,1024]{1,0:T(8,128)(2,1)S(1)}, u32[]{:S(2)}, u32[]{:S(2)}) collective-permute-start(bf16[512,1024]{1,0:T(8,128)(2,1)S(1)} %collective-permute-done.1.refs_1_.refs_7_), channel_id=1, source_target_pairs={{0,16},{1,17},{2,18},{3,19},{4,20},{5,21},{6,22},{7,23},{8,24},{9,... | collective-permute-start | bytes 3145736 | tf_op jit(solution)/shard_map/ppermute | solution.py:38
  125.3 43.2 %collective-permute-start.3 = (bf16[512,1024]{1,0:T(8,128)(2,1)S(1)}, bf16[512,1024]{1,0:T(8,128)(2,1)}, u32[]{:S(2)}, u32[]{:S(2)}) collective-permute-start(bf16[512,1024]{1,0:T(8,128)(2,1)S(1)} %collective-permute-done.1.refs_1_.refs_7_), channel_id=1, source_target_pairs={{0,48},{1,49},{2,50},{3,51},{4,52},{5,53},{6,54},{7,55},{8,56},{9,... | collective-permute-start | bytes 3145736 | tf_op jit(solution)/shard_map/ppermute | solution.py:38
  130.7 37.2 %collective-permute-start.12 = (bf16[256,1024]{1,0:T(8,128)(2,1)}, bf16[256,1024]{1,0:T(8,128)(2,1)S(1)}, u32[]{:S(2)}, u32[]{:S(2)}) collective-permute-start(bf16[256,1024]{1,0:T(8,128)(2,1)} %slice.99), channel_id=1, source_target_pairs={{0,48},{1,49},{2,50},{3,51},{4,52},{5,53},{6,54},{7,55},{8,56},{9,... | collective-permute-start | bytes 1572872 | tf_op jit(solution)/shard_map/ppermute | solution.py:38
  136.9 31.0 %collective-permute-start.13 = (bf16[2,128,1024]{2,1,0:T(8,128)(2,1)}, bf16[2,128,1024]{2,1,0:T(8,128)(2,1)}, u32[]{:S(2)}, u32[]{:S(2)}) collective-permute-start(bf16[2,128,1024]{2,1,0:T(8,128)(2,1)} %after.8), channel_id=1, source_target_pairs={{0,64},{1,65},{2,66},{3,67},{4,68},{5,69},{6,70},{7,71},{8,72},{9,... | collective-permute-start | bytes 1572872 | tf_op jit(solution)/shard_map/ppermute | solution.py:38
  137.6 30.9 %collective-permute-start.10 = (bf16[256,1024]{1,0:T(8,128)(2,1)}, bf16[256,1024]{1,0:T(8,128)(2,1)S(1)}, u32[]{:S(2)}, u32[]{:S(2)}) collective-permute-start(bf16[256,1024]{1,0:T(8,128)(2,1)} %after.7), channel_id=1, source_target_pairs={{0,16},{1,17},{2,18},{3,19},{4,20},{5,21},{6,22},{7,23},{8,24},{9,... | collective-permute-start | bytes 1572872 | tf_op jit(solution)/shard_map/ppermute | solution.py:38
  176.6 45.4 %collective-permute-start.16 = (bf16[8,640,512]{2,1,0:T(8,128)(2,1)}, bf16[8,640,512]{2,1,0:T(8,128)(2,1)}, u32[]{:S(2)}, u32[]{:S(2)}) collective-permute-start(bf16[8,640,512]{2,1,0:T(8,128)(2,1)} %norm.1.refs_0_.refs_1_.refs_2_.refs_3_.refs_4_.refs_5_), channel_id=1, source_target_pairs={{0,8},{1,9},{2,10},{3,11},{4,12},{5,13},{6,14},{7,15},{8,0},{9,1},... | collective-permute-start | bytes 15728648 | tf_op jit(solution)/shard_map/ppermute | solution.py:38
  178.8 62.3 %collective-permute-start.19 = (bf16[2,2,128,1024]{3,2,1,0:T(8,128)(2,1)}, bf16[2,2,128,1024]{3,2,1,0:T(8,128)(2,1)}, u32[]{:S(2)}, u32[]{:S(2)}) collective-permute-start(bf16[2,2,128,1024]{3,2,1,0:T(8,128)(2,1)} %after.9.refs_0_), channel_id=1, source_target_pairs={{0,16},{1,17},{2,18},{3,19},{4,20},{5,21},{6,22},{7,23},{8,24},{9,... | collective-permute-start | bytes 3145736 | tf_op jit(solution)/shard_map/ppermute | solution.py:38
  180.3 60.9 %collective-permute-start.20 = (bf16[2,2,128,1024]{3,2,1,0:T(8,128)(2,1)}, bf16[2,2,128,1024]{3,2,1,0:T(8,128)(2,1)}, u32[]{:S(2)}, u32[]{:S(2)}) collective-permute-start(bf16[2,2,128,1024]{3,2,1,0:T(8,128)(2,1)} %after.9.refs_0_), channel_id=1, source_target_pairs={{0,48},{1,49},{2,50},{3,51},{4,52},{5,53},{6,54},{7,55},{8,56},{9,... | collective-permute-start | bytes 3145736 | tf_op jit(solution)/shard_map/ppermute | solution.py:38
  183.0 34.4 %collective-permute-start.14 = (bf16[256,1024]{1,0:T(8,128)(2,1)}, bf16[256,1024]{1,0:T(8,128)(2,1)}, u32[]{:S(2)}, u32[]{:S(2)}) collective-permute-start(bf16[256,1024]{1,0:T(8,128)(2,1)} %slice.100), channel_id=1, source_target_pairs={{0,16},{1,17},{2,18},{3,19},{4,20},{5,21},{6,22},{7,23},{8,24},{9,... | collective-permute-start | bytes 1572872 | tf_op jit(solution)/shard_map/ppermute | solution.py:38
  185.0 32.5 %collective-permute-start.15 = (bf16[256,1024]{1,0:T(8,128)(2,1)}, bf16[256,1024]{1,0:T(8,128)(2,1)}, u32[]{:S(2)}, u32[]{:S(2)}) collective-permute-start(bf16[256,1024]{1,0:T(8,128)(2,1)} %slice.101), channel_id=1, source_target_pairs={{0,48},{1,49},{2,50},{3,51},{4,52},{5,53},{6,54},{7,55},{8,56},{9,... | collective-permute-start | bytes 1572872 | tf_op jit(solution)/shard_map/ppermute | solution.py:38
  191.3 26.2 %copy-start.27 = (bf16[256,1024]{1,0:T(8,128)(2,1)S(1)}, bf16[256,1024]{1,0:T(8,128)(2,1)}, u32[]{:S(2)}) copy-start(bf16[256,1024]{1,0:T(8,128)(2,1)} %copy-done.26) | copy-start | bytes 1572868
  191.3 26.2 %copy-start.29 = (bf16[256,1024]{1,0:T(8,128)(2,1)S(1)}, bf16[256,1024]{1,0:T(8,128)(2,1)}, u32[]{:S(2)}) copy-start(bf16[256,1024]{1,0:T(8,128)(2,1)} %copy-done.28) | copy-start | bytes 1572868
  198.5 23.5 %copy-start.9 = (bf16[16,32,1024]{2,1,0:T(8,128)(2,1)S(1)}, bf16[16,32,1024]{2,1,0:T(8,128)(2,1)}, u32[]{:S(2)}) copy-start(bf16[16,32,1024]{2,1,0:T(8,128)(2,1)} %copy-done.6) | copy-start | bytes 3145732
  241.1 14.5 %collective-permute-start.17 = (bf16[4,640,256]{2,1,0:T(8,128)(2,1)}, bf16[4,640,256]{2,1,0:T(8,128)(2,1)}, u32[]{:S(2)}, u32[]{:S(2)}) collective-permute-start(bf16[4,640,256]{2,1,0:T(8,128)(2,1)} %get-tuple-element.22.refs_5_), channel_id=1, source_target_pairs={{0,8},{1,9},{2,10},{3,11},{4,12},{5,13},{6,14},{7,15},{8,0},{9,1},... | collective-permute-start | bytes 3932168 | tf_op jit(solution)/shard_map/ppermute | solution.py:38
  251.9 6.4 %collective-permute-start.21 = (bf16[4,640,256]{2,1,0:T(8,128)(2,1)}, bf16[4,640,256]{2,1,0:T(8,128)(2,1)}, u32[]{:S(2)}, u32[]{:S(2)}) collective-permute-start(bf16[4,640,256]{2,1,0:T(8,128)(2,1)} %get-tuple-element.24), channel_id=1, source_target_pairs={{0,8},{1,9},{2,10},{3,11},{4,12},{5,13},{6,14},{7,15},{8,0},{9,1},... | collective-permute-start | bytes 3932168 | tf_op jit(solution)/shard_map/ppermute | solution.py:38
  254.3 34.5 %collective-permute-start.26 = (bf16[2,128,1024]{2,1,0:T(8,128)(2,1)}, bf16[2,128,1024]{2,1,0:T(8,128)(2,1)S(1)}, u32[]{:S(2)}, u32[]{:S(2)}) collective-permute-start(bf16[2,128,1024]{2,1,0:T(8,128)(2,1)} %slice_bitcast_fusion.1), channel_id=1, source_target_pairs={{0,16},{1,17},{2,18},{3,19},{4,20},{5,21},{6,22},{7,23},{8,24},{9,... | collective-permute-start | bytes 1572872 | tf_op jit(solution)/shard_map/ppermute | solution.py:38
  258.3 81.9 %reduce-scatter.5.cloned.1.call-start = ((), (), s32[]{:S(2)}) async-start(), calls=%async_computation.4 | async-start | bytes 1638400 | tf_op jit(solution)/shard_map/reduce_scatter | solution.py:354
  260.0 19.1 %collective-permute-start.24 = (bf16[640,256]{1,0:T(8,128)(2,1)S(1)}, bf16[640,256]{1,0:T(8,128)(2,1)S(1)}, u32[]{:S(2)}, u32[]{:S(2)}) collective-permute-start(bf16[640,256]{1,0:T(8,128)(2,1)S(1)} %get-tuple-element.33), channel_id=1, source_target_pairs={{0,6},{1,7},{2,0},{3,1},{4,2},{5,3},{6,4},{7,5},{8,14},{9,15},{10,... | collective-permute-start | bytes 983048 | tf_op jit(solution)/shard_map/ppermute | solution.py:38
  262.9 17.5 %collective-permute-start.23 = (bf16[640,256]{1,0:T(8,128)(2,1)S(1)}, bf16[640,256]{1,0:T(8,128)(2,1)S(1)}, u32[]{:S(2)}, u32[]{:S(2)}) collective-permute-start(bf16[640,256]{1,0:T(8,128)(2,1)S(1)} %get-tuple-element.32), channel_id=1, source_target_pairs={{0,4},{1,5},{2,6},{3,7},{4,0},{5,1},{6,2},{7,3},{8,12},{9,13},{10,... | collective-permute-start | bytes 983048 | tf_op jit(solution)/shard_map/ppermute | solution.py:38
  263.8 25.1 %copy-start.4 = (bf16[2,2,128,1024]{3,2,1,0:T(8,128)(2,1)S(1)}, bf16[2,2,128,1024]{3,2,1,0:T(8,128)(2,1)}, u32[]{:S(2)}) copy-start(bf16[2,2,128,1024]{3,2,1,0:T(8,128)(2,1)} %after.9.refs_0_) | copy-start | bytes 3145732
  263.8 25.1 %copy-start.10 = (bf16[4,640,256]{2,1,0:T(8,128)(2,1)S(1)}, bf16[4,640,256]{2,1,0:T(8,128)(2,1)}, u32[]{:S(2)}) copy-start(bf16[4,640,256]{2,1,0:T(8,128)(2,1)} %add_convert_fusion.1.refs_5_) | copy-start | bytes 3932164
  263.8 23.7 %collective-permute-start.22 = (bf16[640,256]{1,0:T(8,128)(2,1)S(1)}, bf16[640,256]{1,0:T(8,128)(2,1)S(1)}, u32[]{:S(2)}, u32[]{:S(2)}) collective-permute-start(bf16[640,256]{1,0:T(8,128)(2,1)S(1)} %get-tuple-element.34.refs_6_), channel_id=1, source_target_pairs={{0,2},{1,3},{2,4},{3,5},{4,6},{5,7},{6,0},{7,1},{8,10},{9,11},{10,... | collective-permute-start | bytes 983048 | tf_op jit(solution)/shard_map/ppermute | solution.py:38
  265.7 23.1 %collective-permute-start.27 = (bf16[2,128,1024]{2,1,0:T(8,128)(2,1)S(1)}, bf16[2,128,1024]{2,1,0:T(8,128)(2,1)S(1)}, u32[]{:S(2)}, u32[]{:S(2)}) collective-permute-start(bf16[2,128,1024]{2,1,0:T(8,128)(2,1)S(1)} %slice_bitcast_fusion), channel_id=1, source_target_pairs={{0,48},{1,49},{2,50},{3,51},{4,52},{5,53},{6,54},{7,55},{8,56},{9,... | collective-permute-start | bytes 1572872 | tf_op jit(solution)/shard_map/ppermute | solution.py:38
  294.1 3.1 collective-permute-start.28
  310.3 3.2 collective-permute-start.30
  310.5 9.7 %collective-permute-start.25 = (bf16[640,128]{1,0:T(8,128)(2,1)S(1)}, bf16[640,128]{1,0:T(8,128)(2,1)S(1)}, u32[]{:S(2)}, u32[]{:S(2)}) collective-permute-start(bf16[640,128]{1,0:T(8,128)(2,1)S(1)} %constant_dynamic-slice_fusion.1), channel_id=1, source_target_pairs={{0,1},{1,0},{2,3},{3,2},{4,5},{5,4},{6,7},{7,6},{8,9},{9,8},{10,11... | collective-permute-start | bytes 491528 | tf_op jit(solution)/shard_map/ppermute | solution.py:38
  315.0 12.7 %collective-permute-start.33 = (bf16[640,256]{1,0:T(8,128)(2,1)S(1)}, bf16[640,256]{1,0:T(8,128)(2,1)S(1)}, u32[]{:S(2)}, u32[]{:S(2)}) collective-permute-start(bf16[640,256]{1,0:T(8,128)(2,1)S(1)} %get-tuple-element.30), channel_id=1, source_target_pairs={{0,6},{1,7},{2,0},{3,1},{4,2},{5,3},{6,4},{7,5},{8,14},{9,15},{10,... | collective-permute-start | bytes 983048 | tf_op jit(solution)/shard_map/ppermute | solution.py:38
  319.2 12.1 %collective-permute-start.32 = (bf16[640,256]{1,0:T(8,128)(2,1)S(1)}, bf16[640,256]{1,0:T(8,128)(2,1)S(1)}, u32[]{:S(2)}, u32[]{:S(2)}) collective-permute-start(bf16[640,256]{1,0:T(8,128)(2,1)S(1)} %get-tuple-element.31), channel_id=1, source_target_pairs={{0,4},{1,5},{2,6},{3,7},{4,0},{5,1},{6,2},{7,3},{8,12},{9,13},{10,... | collective-permute-start | bytes 983048 | tf_op jit(solution)/shard_map/ppermute | solution.py:38
  319.2 17.7 %collective-permute-start.31 = (bf16[640,256]{1,0:T(8,128)(2,1)S(1)}, bf16[640,256]{1,0:T(8,128)(2,1)S(1)}, u32[]{:S(2)}, u32[]{:S(2)}) collective-permute-start(bf16[640,256]{1,0:T(8,128)(2,1)S(1)} %get-tuple-element.29), channel_id=1, source_target_pairs={{0,2},{1,3},{2,4},{3,5},{4,6},{5,7},{6,0},{7,1},{8,10},{9,11},{10,... | collective-permute-start | bytes 983048 | tf_op jit(solution)/shard_map/ppermute | solution.py:38
  320.3 19.8 %collective-permute-start.18 = (bf16[640,128]{1,0:T(8,128)(2,1)S(1)}, bf16[640,128]{1,0:T(8,128)(2,1)S(1)}, u32[]{:S(2)}, u32[]{:S(2)}) collective-permute-start(bf16[640,128]{1,0:T(8,128)(2,1)S(1)} %dynamic-slice_bitcast_fusion.1), channel_id=1, source_target_pairs={{0,1},{1,0},{2,3},{3,2},{4,5},{5,4},{6,7},{7,6},{8,9},{9,8},{10,11... | collective-permute-start | bytes 491528 | tf_op jit(solution)/shard_map/ppermute | solution.py:38
  338.1 8.1 %collective-permute-start.34 = (bf16[640,128]{1,0:T(8,128)(2,1)S(1)}, bf16[640,128]{1,0:T(8,128)(2,1)S(1)}, u32[]{:S(2)}, u32[]{:S(2)}) collective-permute-start(bf16[640,128]{1,0:T(8,128)(2,1)S(1)} %constant_dynamic-slice_fusion), channel_id=1, source_target_pairs={{0,1},{1,0},{2,3},{3,2},{4,5},{5,4},{6,7},{7,6},{8,9},{9,8},{10,11... | collective-permute-start | bytes 491528 | tf_op jit(solution)/shard_map/ppermute | solution.py:38
  341.1 8.0 %collective-permute-start.29 = (bf16[640,128]{1,0:T(8,128)(2,1)S(1)}, bf16[640,128]{1,0:T(8,128)(2,1)S(1)}, u32[]{:S(2)}, u32[]{:S(2)}) collective-permute-start(bf16[640,128]{1,0:T(8,128)(2,1)S(1)} %dynamic-slice_bitcast_fusion), channel_id=1, source_target_pairs={{0,1},{1,0},{2,3},{3,2},{4,5},{5,4},{6,7},{7,6},{8,9},{9,8},{10,11... | collective-permute-start | bytes 491528 | tf_op jit(solution)/shard_map/ppermute | solution.py:38
  (38 other events, 192.7 us)
Sparse Core Ops, SparseCore 0:
  9.7 48.8 all-gather.4
  60.8 35.2 all-gather.6
  258.4 33.5 reduce-scatter.2
  298.8 25.9 reduce-scatter.4

commit v3 on v2

--- a/solution.py
+++ b/solution.py
@@ -71,7 +71,7 @@
     return pl.CostEstimate(flops=int(flops) // 1000, bytes_accessed=int(nbytes) // 1000, transcendentals=0)
 
 
-def up_kernel(w_ref, g_ref, m_ref, v_ref, o_ref, out_ref):
+def up_kernel(w_ref, g_ref, m_ref, v_ref, dep_ref, o_ref, out_ref):
     new = adamw(w_ref[...], g_ref[...], m_ref[...], v_ref[...])
     o_ref[...] = new
     cast = new.astype(jnp.bfloat16)
@@ -79,7 +79,7 @@
         out_ref[n] = cast[:, n * 128 : (n + 1) * 128]
 
 
-def up_step(w, g, m, v):
+def up_step(w, g, m, v, dep):
     spec = pl.BlockSpec((32, 2048), lambda i: (0, i))
     return pl.pallas_call(
         up_kernel,
@@ -88,41 +88,39 @@
             jax.ShapeDtypeStruct((16, 32, 1024), jnp.bfloat16),
         ),
         grid=(8,),
-        in_specs=[spec] * 4,
+        in_specs=[spec] * 4 + [ANY],
         out_specs=(spec, pl.BlockSpec((16, 32, 128), lambda i: (0, 0, i))),
         compiler_params=params(56),
         cost_estimate=cost(30 * 32 * FF, 20 * 32 * FF),
         name="adam_up",
-    )(w, g, m, v)
-
-
-SPLIT = ((0, 0), (0, 1), (1, 0), (1, 1))
-
-
-def down_kernel(w_ref, g_ref, m_ref, v_ref, o_ref, *d_refs):
+    )(w, g, m, v, dep)
+
+
+def down_kernel(w_ref, g_ref, m_ref, v_ref, *refs):
+    o_ref, d_ref = refs[-2:]
     new = adamw(w_ref[...], g_ref[...], m_ref[...], v_ref[...])
     o_ref[...] = new
     cast = new.astype(jnp.bfloat16)
-    for t in range(8):
-        for j in range(CHUNKS):
-            piece = cast[:, t * 512 + j * 128 : t * 512 + (j + 1) * 128]
-            d_refs[SPLIT[j][0]][SPLIT[j][1], :, t * 128 : (t + 1) * 128] = piece
-
-
-def down_step(w, g, m, v):
-    spec = pl.BlockSpec((32, D), lambda i: (i, 0))
-    sizes = (2, 2)
+    d_ref[0] = cast[:, :128]
+    d_ref[1] = cast[:, 128:]
+
+
+def down_step(half, args, done=(), deps=()):
+    spec = pl.BlockSpec((128, 256), lambda i: (0, 2 * i + half))
     return pl.pallas_call(
         down_kernel,
-        out_shape=(jax.ShapeDtypeStruct((128, D), jnp.float32),)
-        + tuple(jax.ShapeDtypeStruct((n, 128, 1024), jnp.bfloat16) for n in sizes),
-        grid=(4,),
-        in_specs=[spec] * 4,
-        out_specs=(spec,) + tuple(pl.BlockSpec((n, 32, 1024), lambda i: (0, i, 0)) for n in sizes),
+        out_shape=(
+            jax.ShapeDtypeStruct((128, D), jnp.float32),
+            jax.ShapeDtypeStruct((2, 128, 1024), jnp.bfloat16),
+        ),
+        grid=(8,),
+        in_specs=[spec] * 4 + [ANY] * (len(done) + len(deps)),
+        out_specs=(spec, pl.BlockSpec((2, 128, 128), lambda i: (0, 0, i))),
+        input_output_aliases={4: 0} if done else {},
         compiler_params=params(56),
-        cost_estimate=cost(30 * 128 * D, 20 * 128 * D),
+        cost_estimate=cost(15 * 128 * D, 10 * 128 * D),
         name="adam_down",
-    )(w, g, m, v)
+    )(*args, *done, *deps)
 
 
 def both_ways(up, down):
@@ -171,7 +169,7 @@
 
 
 def last_kernel(s_ref, acc_ref, *refs):
-    lhs, ws, out = refs[:2], refs[2:6], refs[6]
+    lhs, ws, out = refs[:2], refs[2:6], refs[-1]
     for n in range(4):
         at = slice(n * 256, (n + 1) * 256)
         u = acc_ref[:, at]
@@ -207,7 +205,7 @@
     )(scalars, *([normed] * 6), *ws)
 
 
-def hidden_last(scalars, acc, normed, ws):
+def hidden_last(scalars, acc, normed, ws, deps):
     lhs, rhs = hidden_specs((6, 7), ws)
     block = pl.BlockSpec((320, 1024), lambda i, s: (i, 0))
     return pl.pallas_call(
@@ -216,13 +214,13 @@
         grid_spec=pltpu.PrefetchScalarGridSpec(
             num_scalar_prefetch=1,
             grid=(2,),
-            in_specs=[block] + lhs + rhs,
+            in_specs=[block] + lhs + rhs + [ANY] * len(deps),
             out_specs=block,
         ),
         compiler_params=params(),
         cost_estimate=cost(2 * 640 * 1024 * 1024, 8 * MIB),
         name="hidden_last",
-    )(scalars, acc, normed, normed, *ws)
+    )(scalars, acc, normed, normed, *ws, *deps)
 
 
 def partial_kernel(s_ref, own_ref, sib_ref, *refs):
@@ -260,7 +258,7 @@
             out_specs=(out, out),
             scratch_shapes=[pltpu.VMEM((1024, 1024), jnp.bfloat16)],
         ),
-        compiler_params=params(),
+        compiler_params=params(56),
         cost_estimate=cost(4 * 640 * 1024 * 1024, 8 * MIB),
         name="partial",
     )(scalars, own, sib, *ws, *deps)
@@ -294,12 +292,16 @@
     tokens_b = send(tokens, yhi=1)
     feats_a = lax.all_gather(tokens, "x", axis=0)
 
-    up_updated, columns = up_step(up_master, up_gradient, up_first, up_second)
-    down_updated, down_a, down_b = down_step(down_master, down_gradient, down_first, down_second)
-
-    st_a = jnp.stack([down_a, send(down_a, ylo=1)])
+    down_args = (down_master, down_gradient, down_first, down_second)
+    down_half, down_a = down_step(0, down_args)
+    ylo_a = send(down_a, ylo=1)
+    up_updated, columns = up_step(up_master, up_gradient, up_first, up_second, down_a)
+    down_updated, down_b = down_step(1, down_args, (down_half,), (ylo_a,))
+
+    st_a = jnp.stack([down_a, ylo_a])
     low_a, high_a = both_ways(st_a, st_a)
-    u0 = lax.all_to_all(after(columns, down_a), ("core", "x", "yhi"), 0, 0, tiled=True).reshape(512, 1024)
+    u0 = lax.all_to_all(columns, ("core", "x", "yhi"), 0, 0, tiled=True).reshape(512, 1024)
+    u0 = after(u0, down_b, low_a, high_a)
     feats_b = lax.all_gather(after(tokens_b, u0), "x", axis=0)
     opp_a = both_ways(low_a[0], high_a[1])
     ws_a = (st_a, low_a, high_a, *opp_a)
@@ -313,7 +315,6 @@
     opp1 = both_ways(low1[:256], high1[256:])
     st_b = after(jnp.stack([down_b, ylo_b]), low1)
     low_b, high_b = both_ways(st_b, st_b)
-    ws_b = (st_b, low_b, high_b, *both_ways(low_b[0], high_b[1]))
 
     gains = norm_gain.reshape(4, 2, 512)
     gains = jnp.concatenate([lax.dynamic_index_in_dim(gains, k, 1, keepdims=False) for k in (yhi, 1 - yhi)])
@@ -325,34 +326,36 @@
     ws_up = (u0, u1, low0, low1, high0, high1)
     firsts = [hidden_first(where, n, ws_up) for n in (normed, normed_sib)]
     hidden_own, hidden_sib = (
-        hidden_last(where, f, n, opp0 + opp1) for f, n in zip(firsts, (normed, normed_sib))
+        hidden_last(where, f, n, opp0 + opp1, firsts) for f, n in zip(firsts, (normed, normed_sib))
     )
 
-    pieces, parts, sums, reduced = [], [], [], []
+    pieces, sums, reduced = [], [], []
     places = jnp.arange(4, dtype=jnp.int32)
     add = lambda a, b: (a.astype(jnp.float32) + b.astype(jnp.float32)).astype(jnp.bfloat16)
     for j in range(CHUNKS):
-        direct = j % 2 == 1
+        direct = j in (0, 3)
+        if j == 2:
+            up, down = after(low_b[0], *reduced), after(high_b[1], *reduced)
+            ws_b = (st_b, low_b, high_b, *both_ways(up, down))
         part, part_sib = partial_of(
             (places - x) % 4 if direct else places,
             hidden_own,
             hidden_sib,
-            (ws_a, ws_b)[SPLIT[j][0]],
-            SPLIT[j][1],
-            ([], parts + [low_b, high_b], sums + reduced[1:], parts[2:] + reduced[:2])[j],
+            ws_a if j < 2 else ws_b,
+            j % 2,
+            sums[-1:],
         )
-        parts.append(part_sib)
         part_sib = send(part_sib, core=1)
         if direct:
             terms = [add(part[d], part_sib[d]) for d in range(4)]
             sums.append(terms[1])
             terms = terms[:1] + [send(terms[d], x=d) for d in (1, 2, 3)]
             rows = sum(v.astype(jnp.float32) for v in terms).astype(jnp.bfloat16)
+            reduced.append(rows)
         else:
             both = add(part, part_sib)
             sums.append(both)
             rows = lax.psum_scatter(both, "x", scatter_dimension=0, tiled=True)[0]
-        reduced.append(rows)
         keep = lax.dynamic_slice_in_dim(rows, yhi * 128, 128, 1)
         give = lax.dynamic_slice_in_dim(rows, (1 - yhi) * 128, 128, 1)
         pieces.append(add(keep, send(give, yhi=1)))

time: 359 us -> 353 us (0.983)
  waiting for transfers between devices: 177 us -> 164 us
  Pallas kernels: 64.4 us -> 77.2 us
  local copies, waits for them, and re-layouts: 33.9 us -> 22.2 us
  other arithmetic: 15 us -> 21.1 us
    ppermute x35, waiting for transfers between devices: 176 us -> 154 us  [send(): return lax.ppermute(v, AXES, shifted(**steps))]
    unnamed x93 -> x53, local copies, waits for them, and re-layouts: 23.2 us -> 10.1 us
    all_to_all x1, waiting for transfers between devices: 0.01 us -> 9.62 us  [body(): lax.all_to_all(columns, ('core', 'x', 'yhi'), 0, 0, tiled=True)]
    pallas_call x1 -> x2, Pallas kernels: 5.85 us -> 12.7 us  [down_step(): pl.pallas_call(down_kernel, out_shape=(jax.ShapeDtypeStruct((128, D), jnp...]
    pallas_call x4, Pallas kernels: 23.1 us -> 28.2 us  [partial_of(): pl.pallas_call(partial_kernel, out_shape=(shape, shape), grid_spec=pltpu....]
  transfers between devices with their start and end apart: 40 -> 40, of which waited for: 18 -> 19; matrix products, arithmetic and copies ran while one was open for 7% -> 8% of each run, Pallas kernels for 17% -> 14%
where the time goes in v3:
time: 353 us; the launch traced here: 352 us
  waiting for transfers between devices  164 us (46%)
  Pallas kernels  77.2 us (22%)
  starting transfers between devices  53.2 us (15%)
  local copies, waits for them, and re-layouts  22.2 us (6%)
  other arithmetic  21.1 us (6%)
  between operations  14.1 us (4%)
    ppermute x35, waiting for transfers between devices, send(): return lax.ppermute(v, AXES, shifted(**steps))  154 us
    ppermute x35, starting transfers between devices, send(): return lax.ppermute(v, AXES, shifted(**steps))  46 us
    pallas_call x4, Pallas kernels, partial_of(): pl.pallas_call(partial_kernel, out_shape=(shape, shape), grid_spec=pltpu....  28.2 us
    pallas_call x2, Pallas kernels, hidden_first(): pl.pallas_call(first_kernel, out_shape=jax.ShapeDtypeStruct((640, 1024),...  15 us
    pallas_call x2, Pallas kernels, down_step(): pl.pallas_call(down_kernel, out_shape=(jax.ShapeDtypeStruct((128, D), jnp...  12.7 us
    convert_element_type x8, other arithmetic, body(): (a.astype(jnp.float32) + b.astype(jnp.float32)).astype(jnp.bfloat16)  11.7 us
    unnamed x53, local copies, waits for them, and re-layouts  10.1 us
    pallas_call x2, Pallas kernels, hidden_last(): pl.pallas_call(last_kernel, out_shape=jax.ShapeDtypeStruct((640, 1024), j...  9.62 us
  transfers between devices with their start and end apart: 40, of which 19 were waited for; matrix products, arithmetic and copies ran while one was open for 8% of the time, Pallas kernels for 14%

profile of v3, /device:TPU:0, one launch (start us, length us, event | category | flops | bytes accessed | tf_op | source)
XLA Modules:
  0.0 352.0 jit_solution(3920320998093901737)
XLA Ops:
  7.9 6.3 %adam_down.2 = (f32[128,4096]{1,0:T(8,128)}, bf16[2,128,1024]{2,1,0:T(8,128)(2,1)}) custom-call(f32[128,4096]{1,0:T(8,128)} %w_ref.5, bf16[128,4096]{1,0:T(8,128)(2,1)} %g_ref.5, f32[128,4096]{1,0:T(8,128)} %m_ref.5, f32[128,4096]{1,0:T(8,128)} %v_ref.5), custom_call_target="tpu_custom_call" | custom-call | flops 7864 | bytes 5242 | tf_op jit(solution)/shard_map/adam_down/pallas_call | solution.py:110
  15.9 12.1 %collective-permute-done.refs_1_ = bf16[2,128,1024]{2,1,0:T(8,128)(2,1)S(1)} collective-permute-done((bf16[2,128,1024]{2,1,0:T(8,128)(2,1)}, bf16[2,128,1024]{2,1,0:T(8,128)(2,1)S(1)}, u32[]{:S(2)}, u32[]{:S(2)}) %collective-permute-start) | collective-permute-done | bytes 524320 | tf_op jit(solution)/shard_map/ppermute | solution.py:38
  28.0 2.3 pad_maximum_fusion.refs_0_
  32.5 2.1 collective-permute-start.3
  34.6 7.6 %adam_up.1 = (f32[32,16384]{1,0:T(8,128)}, bf16[16,32,1024]{2,1,0:T(8,128)(2,1)}) custom-call(f32[32,16384]{1,0:T(8,128)} %w_ref.4, bf16[32,16384]{1,0:T(8,128)(2,1)} %g_ref.4, f32[32,16384]{1,0:T(8,128)} %m_ref.4, f32[32,16384]{1,0:T(8,128)} %v_ref.4, bf16[2,128,1024]{2,1,0:T(8,128)(2,1)} %get-tuple-element.17.dep_ref), custom_call_target="tpu_custom_call" | custom-call | flops 15728 | bytes 10485 | tf_op jit(solution)/shard_map/adam_up/pallas_call | solution.py:84
  42.2 7.1 %all-to-all-start = ((bf16[16,32,1024]{2,1,0:T(8,128)(2,1)}), bf16[16,32,1024]{2,1,0:T(8,128)(2,1)S(1)}, u32[]{:S(2)}, u32[]{:S(2)}) async-start(bf16[16,32,1024]{2,1,0:T(8,128)(2,1)} %get-tuple-element.21), calls=%async_computation | async-start | bytes 2097152 | tf_op jit(solution)/shard_map/all_to_all | solution.py:303
  49.3 3.5 collective-permute-start.1
  52.9 6.3 %adam_down.3 = (f32[128,4096]{1,0:T(8,128)}, bf16[2,128,1024]{2,1,0:T(8,128)(2,1)}) custom-call(f32[128,4096]{1,0:T(8,128)} %w_ref.5, bf16[128,4096]{1,0:T(8,128)(2,1)} %g_ref.5, f32[128,4096]{1,0:T(8,128)} %m_ref.5, f32[128,4096]{1,0:T(8,128)} %v_ref.5, f32[128,4096]{1,0:T(8,128)} %get-tuple-element.19.refs_0_, ...), custom_call_target="tpu_custom_call", output_to_operand_aliasing={{0}: (4, {})} | custom-call | flops 7864 | bytes 5242 | tf_op jit(solution)/shard_map/adam_down/pallas_call | solution.py:110
  59.2 9.6 %all-to-all-done = bf16[16,32,1024]{2,1,0:T(8,128)(2,1)S(1)} async-done(((bf16[16,32,1024]{2,1,0:T(8,128)(2,1)}), bf16[16,32,1024]{2,1,0:T(8,128)(2,1)S(1)}, u32[]{:S(2)}, u32[]{:S(2)}) %all-to-all-start) | async-done | bytes 1048608 | tf_op jit(solution)/shard_map/all_to_all | solution.py:303
  70.5 8.9 %collective-permute-done.1.refs_0_ = bf16[2,320,512]{2,1,0:T(8,128)(2,1)} collective-permute-done((bf16[2,320,512]{2,1,0:T(8,128)(2,1)}, bf16[2,320,512]{2,1,0:T(8,128)(2,1)}, u32[]{:S(2)}, u32[]{:S(2)}) %collective-permute-start.1) | collective-permute-done | bytes 655392 | tf_op jit(solution)/shard_map/ppermute | solution.py:38
  80.2 3.2 collective-permute-start.11
  84.6 3.3 collective-permute-start.9
  87.9 16.3 %collective-permute-done.4.refs_1_.refs_7_ = bf16[512,1024]{1,0:T(8,128)(2,1)S(1)} collective-permute-done((bf16[512,1024]{1,0:T(8,128)(2,1)S(1)}, bf16[512,1024]{1,0:T(8,128)(2,1)S(1)}, u32[]{:S(2)}, u32[]{:S(2)}) %collective-permute-start.4) | collective-permute-done | bytes 1048608 | tf_op jit(solution)/shard_map/ppermute | solution.py:38
  104.2 3.3 collective-permute-done.7.refs_8_
  110.1 8.7 %collective-permute-done.8.refs_2_.refs_3_ = bf16[2,128,1024]{2,1,0:T(8,128)(2,1)} collective-permute-done((bf16[2,128,1024]{2,1,0:T(8,128)(2,1)S(1)}, bf16[2,128,1024]{2,1,0:T(8,128)(2,1)}, u32[]{:S(2)}, u32[]{:S(2)}) %collective-permute-start.8) | collective-permute-done | bytes 524320 | tf_op jit(solution)/shard_map/ppermute | solution.py:38
  122.6 2.7 collective-permute-start.12
  125.4 25.4 %collective-permute-done.10.refs_2_ = bf16[256,1024]{1,0:T(8,128)(2,1)} collective-permute-done((bf16[256,1024]{1,0:T(8,128)(2,1)}, bf16[256,1024]{1,0:T(8,128)(2,1)}, u32[]{:S(2)}, u32[]{:S(2)}) %collective-permute-start.10) | collective-permute-done | bytes 524320 | tf_op jit(solution)/shard_map/ppermute | solution.py:38
  154.7 4.1 %norm.1.refs_0_.refs_1_.refs_2_.refs_3_.refs_4_.refs_5_ = bf16[8,640,512]{2,1,0:T(8,128)(2,1)} custom-call(bf16[4,640,512]{2,1,0:T(8,128)(2,1)S(1)} %bitcast.55, bf16[4,640,512]{2,1,0:T(8,128)(2,1)S(1)} %bitcast.56, f32[8,512]{1,0:T(8,128)S(1)} %pad_maximum_fusion.3.g_ref, bf16[512,1024]{1,0:T(8,128)(2,1)S(1)} %collective-permute-done.5.refs_0_.refs_9_.refs_1_, ...), custom_call_target="tpu_custom_call" | custom-call | flops 20971 | bytes 10485 | tf_op jit(solution)/shard_map/norm/pallas_call | solution.py:145
  161.9 2.9 collective-permute-start.15
  167.3 7.5 %hidden_first.2.acc_ref.refs_6_ = f32[640,1024]{1,0:T(8,128)S(1)} custom-call(s32[16]{0:T(128)S(1)} %fusion.17.s_ref, bf16[8,640,512]{2,1,0:T(8,128)(2,1)} %norm.1.refs_0_.refs_1_.refs_2_.refs_3_.refs_4_.refs_5_, bf16[8,640,512]{2,1,0:T(8,128)(2,1)} %norm.1.refs_0_.refs_1_.refs_2_.refs_3_.refs_4_.refs_5_, ...), custom_call_target="tpu_custom_call" | custom-call | flops 4026531 | bytes 14680 | tf_op jit(solution)/shard_map/hidden_first/pallas_call | solution.py:193
  174.8 7.5 %hidden_first.3.refs_7_.acc_ref = f32[640,1024]{1,0:T(8,128)S(1)} custom-call(s32[16]{0:T(128)S(1)} %fusion.17.s_ref, bf16[8,640,512]{2,1,0:T(8,128)(2,1)} %collective-permute-done.16.refs_0_.refs_1_.refs_2_.refs_3_.refs_4_.refs_5_, bf16[8,640,512]{2,1,0:T(8,128)(2,1)} %collective-permute-done.16.refs_0_.refs_1_.refs_2_.refs_3_.refs_4_.refs_5_, ...), custom_call_target="tpu_custom_call" | custom-call | flops 4026531 | bytes 14680 | tf_op jit(solution)/shard_map/hidden_first/pallas_call | solution.py:193
  182.3 4.8 %hidden_last.3.sib_ref = bf16[640,1024]{1,0:T(8,128)(2,1)S(1)} custom-call(s32[16]{0:T(128)S(1)} %fusion.17.s_ref, f32[640,1024]{1,0:T(8,128)S(1)} %hidden_first.3.refs_7_.acc_ref, bf16[8,640,512]{2,1,0:T(8,128)(2,1)} %collective-permute-done.16.refs_0_.refs_1_.refs_2_.refs_3_.refs_4_.refs_5_, ...), custom_call_target="tpu_custom_call" | custom-call | flops 1342177 | bytes 8388 | tf_op jit(solution)/shard_map/hidden_last/pallas_call | solution.py:211
  188.2 4.8 %hidden_last.2.own_ref = bf16[640,1024]{1,0:T(8,128)(2,1)S(1)} custom-call(s32[16]{0:T(128)S(1)} %fusion.17.s_ref, f32[640,1024]{1,0:T(8,128)S(1)} %hidden_first.2.acc_ref.refs_6_, bf16[8,640,512]{2,1,0:T(8,128)(2,1)} %norm.1.refs_0_.refs_1_.refs_2_.refs_3_.refs_4_.refs_5_, bf16[8,640,512]{2,1,0:T(8,128)(2,1)} %norm.1.refs_0_.refs_1_.refs_2_.refs_3_.refs_4_.refs_5_, ...), custom_call_target="tpu_custom_call" | custom-call | flops 1342177 | bytes 8388 | tf_op jit(solution)/shard_map/hidden_last/pallas_call | solution.py:211
  194.1 6.9 %partial.4 = (bf16[4,640,256]{2,1,0:T(8,128)(2,1)}, bf16[4,640,256]{2,1,0:T(8,128)(2,1)}) custom-call(s32[4]{0:T(128)} %and_select_fusion.s_ref, bf16[640,1024]{1,0:T(8,128)(2,1)} %copy-done.1, bf16[640,1024]{1,0:T(8,128)(2,1)} %copy-done, bf16[2,2,128,1024]{3,2,1,0:T(8,128)(2,1)} %pad_maximum_fusion.refs_0_, bf16[2,2,128,1024]{3,2,1,0:T(8,128)(2,1)} %copy-done.12, ...), custom_call_target="tpu_custom_call" | custom-call | flops 2684354 | bytes 8388 | tf_op jit(solution)/shard_map/partial/pallas_call | solution.py:251
  201.1 3.2 collective-permute-done.17
  204.3 2.6 fusion.7
  207.5 7.1 %partial.5 = (bf16[4,640,256]{2,1,0:T(8,128)(2,1)}, bf16[4,640,256]{2,1,0:T(8,128)(2,1)}) custom-call(s32[4]{0:T(128)} %iota.8.s_ref, bf16[640,1024]{1,0:T(8,128)(2,1)} %copy-done.1, bf16[640,1024]{1,0:T(8,128)(2,1)} %copy-done, bf16[2,2,128,1024]{3,2,1,0:T(8,128)(2,1)} %pad_maximum_fusion.refs_0_, bf16[2,2,128,1024]{3,2,1,0:T(8,128)(2,1)} %copy-done.12, ...), custom_call_target="tpu_custom_call" | custom-call | flops 2684354 | bytes 8388 | tf_op jit(solution)/shard_map/partial/pallas_call | solution.py:251
  214.8 2.1 pad_maximum_fusion.1.refs_0_
  218.9 23.6 %collective-permute-done.25.refs_2_ = bf16[2,2,128,1024]{3,2,1,0:T(8,128)(2,1)S(1)} collective-permute-done((bf16[2,2,128,1024]{3,2,1,0:T(8,128)(2,1)}, bf16[2,2,128,1024]{3,2,1,0:T(8,128)(2,1)S(1)}, u32[]{:S(2)}, u32[]{:S(2)}) %collective-permute-start.25) | collective-permute-done | bytes 1048608 | tf_op jit(solution)/shard_map/ppermute | solution.py:38
  244.9 2.7 collective-permute-start.19
  249.1 3.1 add_convert_fusion.1.refs_5_
  254.4 8.3 %collective-permute-done.19 = bf16[640,256]{1,0:T(8,128)(2,1)} collective-permute-done((bf16[640,256]{1,0:T(8,128)(2,1)S(1)}, bf16[640,256]{1,0:T(8,128)(2,1)}, u32[]{:S(2)}, u32[]{:S(2)}) %collective-permute-start.19) | collective-permute-done | bytes 327712 | tf_op jit(solution)/shard_map/ppermute | solution.py:38
  262.7 2.2 collective-permute-done.20
  264.9 2.2 fusion.5.refs_1_
  267.1 3.0 collective-permute-start.27
  270.1 9.6 %collective-permute-done.27.refs_4_ = bf16[2,128,1024]{2,1,0:T(8,128)(2,1)S(1)} collective-permute-done((bf16[2,128,1024]{2,1,0:T(8,128)(2,1)}, bf16[2,128,1024]{2,1,0:T(8,128)(2,1)S(1)}, u32[]{:S(2)}, u32[]{:S(2)}) %collective-permute-start.27) | collective-permute-done | bytes 524320 | tf_op jit(solution)/shard_map/ppermute | solution.py:38
  279.7 3.3 collective-permute-done.26.refs_3_
  283.8 7.0 %partial.6 = (bf16[4,640,256]{2,1,0:T(8,128)(2,1)}, bf16[4,640,256]{2,1,0:T(8,128)(2,1)}) custom-call(s32[4]{0:T(128)} %iota.9.s_ref, bf16[640,1024]{1,0:T(8,128)(2,1)} %copy-done.1, bf16[640,1024]{1,0:T(8,128)(2,1)} %copy-done, bf16[2,2,128,1024]{3,2,1,0:T(8,128)(2,1)} %after.11.refs_0_, bf16[2,2,128,1024]{3,2,1,0:T(8,128)(2,1)} %copy-done.16, ...), custom_call_target="tpu_custom_call" | custom-call | flops 2684354 | bytes 8388 | tf_op jit(solution)/shard_map/partial/pallas_call | solution.py:251
  290.7 3.2 collective-permute-done.28
  294.0 2.8 add_convert_fusion.refs_5_
  296.8 7.1 %partial.7 = (bf16[4,640,256]{2,1,0:T(8,128)(2,1)}, bf16[4,640,256]{2,1,0:T(8,128)(2,1)}) custom-call(s32[4]{0:T(128)} %and_select_fusion.s_ref, bf16[640,1024]{1,0:T(8,128)(2,1)} %copy-done.1, bf16[640,1024]{1,0:T(8,128)(2,1)} %copy-done, bf16[2,2,128,1024]{3,2,1,0:T(8,128)(2,1)} %after.11.refs_0_, bf16[2,2,128,1024]{3,2,1,0:T(8,128)(2,1)} %copy-done.16, ...), custom_call_target="tpu_custom_call" | custom-call | flops 2684354 | bytes 8388 | tf_op jit(solution)/shard_map/partial/pallas_call | solution.py:251
  304.1 3.0 collective-permute-done.30
  307.1 2.1 fusion.11
  310.2 4.3 %collective-permute-start.32 = (bf16[640,256]{1,0:T(8,128)(2,1)S(1)}, bf16[640,256]{1,0:T(8,128)(2,1)S(1)}, u32[]{:S(2)}, u32[]{:S(2)}) collective-permute-start(bf16[640,256]{1,0:T(8,128)(2,1)S(1)} %get-tuple-element.33), channel_id=1, source_target_pairs={{0,4},{1,5},{2,6},{3,7},{4,0},{5,1},{6,2},{7,3},{8,12},{9,13},{10,... | collective-permute-start | bytes 983048 | tf_op jit(solution)/shard_map/ppermute | solution.py:38
  316.2 15.1 %collective-permute-done.31 = bf16[640,256]{1,0:T(8,128)(2,1)S(1)} collective-permute-done((bf16[640,256]{1,0:T(8,128)(2,1)}, bf16[640,256]{1,0:T(8,128)(2,1)S(1)}, u32[]{:S(2)}, u32[]{:S(2)}) %collective-permute-start.31) | collective-permute-done | bytes 327712 | tf_op jit(solution)/shard_map/ppermute | solution.py:38
  332.5 2.9 collective-permute-start.34
  337.3 2.8 collective-permute-done.34
  340.1 3.5 %collective-permute-done.29 = bf16[640,128]{1,0:T(8,128)(2,1)S(1)} collective-permute-done((bf16[640,128]{1,0:T(8,128)(2,1)S(1)}, bf16[640,128]{1,0:T(8,128)(2,1)S(1)}, u32[]{:S(2)}, u32[]{:S(2)}) %collective-permute-start.29) | collective-permute-done | bytes 163872 | tf_op jit(solution)/shard_map/ppermute | solution.py:38
  (140 shorter events, 43.6 us)
Async XLA Ops:
  7.2 143.7 %all-gather.5.cloned.1.call-start = ((), (), s32[]{:S(2)}) async-start(), calls=%async_computation.5 | async-start | bytes 3276800 | tf_op jit(solution)/shard_map/all_gather | solution.py:293
  14.2 13.8 %collective-permute-start = (bf16[2,128,1024]{2,1,0:T(8,128)(2,1)}, bf16[2,128,1024]{2,1,0:T(8,128)(2,1)S(1)}, u32[]{:S(2)}, u32[]{:S(2)}) collective-permute-start(bf16[2,128,1024]{2,1,0:T(8,128)(2,1)} %get-tuple-element.17.dep_ref), channel_id=1, source_target_pairs={{0,64},{1,65},{2,66},{3,67},{4,68},{5,69},{6,70},{7,71},{8,72},{9,... | collective-permute-start | bytes 1572872 | tf_op jit(solution)/shard_map/ppermute | solution.py:38
  30.4 38.4 %collective-permute-start.2 = (bf16[2,2,128,1024]{3,2,1,0:T(8,128)(2,1)}, bf16[2,2,128,1024]{3,2,1,0:T(8,128)(2,1)S(1)}, u32[]{:S(2)}, u32[]{:S(2)}) collective-permute-start(bf16[2,2,128,1024]{3,2,1,0:T(8,128)(2,1)} %pad_maximum_fusion.refs_0_), channel_id=1, source_target_pairs={{0,16},{1,17},{2,18},{3,19},{4,20},{5,21},{6,22},{7,23},{8,24},{9,... | collective-permute-start | bytes 3145736 | tf_op jit(solution)/shard_map/ppermute | solution.py:38
  32.5 36.3 %collective-permute-start.3 = (bf16[2,2,128,1024]{3,2,1,0:T(8,128)(2,1)}, bf16[2,2,128,1024]{3,2,1,0:T(8,128)(2,1)S(1)}, u32[]{:S(2)}, u32[]{:S(2)}) collective-permute-start(bf16[2,2,128,1024]{3,2,1,0:T(8,128)(2,1)} %pad_maximum_fusion.refs_0_), channel_id=1, source_target_pairs={{0,48},{1,49},{2,50},{3,51},{4,52},{5,53},{6,54},{7,55},{8,56},{9,... | collective-permute-start | bytes 3145736 | tf_op jit(solution)/shard_map/ppermute | solution.py:38
  42.2 26.6 %all-to-all-start = ((bf16[16,32,1024]{2,1,0:T(8,128)(2,1)}), bf16[16,32,1024]{2,1,0:T(8,128)(2,1)S(1)}, u32[]{:S(2)}, u32[]{:S(2)}) async-start(bf16[16,32,1024]{2,1,0:T(8,128)(2,1)} %get-tuple-element.21), calls=%async_computation | async-start | bytes 2097152 | tf_op jit(solution)/shard_map/all_to_all | solution.py:303
  49.3 101.6 %all-gather.7.cloned.1.call-start = ((), (), s32[]{:S(2)}) async-start(), calls=%async_computation.6 | async-start | bytes 3276800 | tf_op jit(solution)/shard_map/all_gather | solution.py:305
  49.3 30.0 %collective-permute-start.1 = (bf16[2,320,512]{2,1,0:T(8,128)(2,1)}, bf16[2,320,512]{2,1,0:T(8,128)(2,1)}, u32[]{:S(2)}, u32[]{:S(2)}) collective-permute-start(bf16[2,320,512]{2,1,0:T(8,128)(2,1)} %param.11), channel_id=1, source_target_pairs={{0,1},{1,0},{2,3},{3,2},{4,5},{5,4},{6,7},{7,6},{8,9},{9,8},{10,11... | collective-permute-start | bytes 1966088 | tf_op jit(solution)/shard_map/ppermute | solution.py:38
  70.5 8.9 %copy-start.3 = (bf16[512,1024]{1,0:T(8,128)(2,1)S(1)}, bf16[512,1024]{1,0:T(8,128)(2,1)}, u32[]{:S(2)}) copy-start(bf16[512,1024]{1,0:T(8,128)(2,1)} %after.7.refs_1_.refs_6_) | copy-start | bytes 3145732
  70.5 12.9 %copy-start.13 = (bf16[2,2,128,1024]{3,2,1,0:T(8,128)(2,1)S(1)}, bf16[2,2,128,1024]{3,2,1,0:T(8,128)(2,1)}, u32[]{:S(2)}) copy-start(bf16[2,2,128,1024]{3,2,1,0:T(8,128)(2,1)} %copy-done.12) | copy-start | bytes 3145732
  79.3 235.3 %reduce-scatter.3.cloned.1.call-start = ((), (), s32[]{:S(2)}) async-start(), calls=%async_computation.3 | async-start | bytes 1638400 | tf_op jit(solution)/shard_map/reduce_scatter | solution.py:358
  79.4 24.8 %collective-permute-start.4 = (bf16[512,1024]{1,0:T(8,128)(2,1)S(1)}, bf16[512,1024]{1,0:T(8,128)(2,1)S(1)}, u32[]{:S(2)}, u32[]{:S(2)}) collective-permute-start(bf16[512,1024]{1,0:T(8,128)(2,1)S(1)} %copy-done.3), channel_id=1, source_target_pairs={{0,64},{1,65},{2,66},{3,67},{4,68},{5,69},{6,70},{7,71},{8,72},{9,... | collective-permute-start | bytes 3145736 | tf_op jit(solution)/shard_map/ppermute | solution.py:38
  80.2 27.3 %collective-permute-start.7 = (bf16[512,1024]{1,0:T(8,128)(2,1)S(1)}, bf16[512,1024]{1,0:T(8,128)(2,1)S(1)}, u32[]{:S(2)}, u32[]{:S(2)}) collective-permute-start(bf16[512,1024]{1,0:T(8,128)(2,1)S(1)} %copy-done.3), channel_id=1, source_target_pairs={{0,16},{1,17},{2,18},{3,19},{4,20},{5,21},{6,22},{7,23},{8,24},{9,... | collective-permute-start | bytes 3145736 | tf_op jit(solution)/shard_map/ppermute | solution.py:38
  80.2 40.6 %collective-permute-start.11 = (bf16[512,1024]{1,0:T(8,128)(2,1)S(1)}, bf16[512,1024]{1,0:T(8,128)(2,1)}, u32[]{:S(2)}, u32[]{:S(2)}) collective-permute-start(bf16[512,1024]{1,0:T(8,128)(2,1)S(1)} %copy-done.3), channel_id=1, source_target_pairs={{0,48},{1,49},{2,50},{3,51},{4,52},{5,53},{6,54},{7,55},{8,56},{9,... | collective-permute-start | bytes 3145736 | tf_op jit(solution)/shard_map/ppermute | solution.py:38
  83.4 35.4 %collective-permute-start.8 = (bf16[2,128,1024]{2,1,0:T(8,128)(2,1)S(1)}, bf16[2,128,1024]{2,1,0:T(8,128)(2,1)}, u32[]{:S(2)}, u32[]{:S(2)}) collective-permute-start(bf16[2,128,1024]{2,1,0:T(8,128)(2,1)S(1)} %slice_bitcast_fusion.3), channel_id=1, source_target_pairs={{0,16},{1,17},{2,18},{3,19},{4,20},{5,21},{6,22},{7,23},{8,24},{9,... | collective-permute-start | bytes 1572872 | tf_op jit(solution)/shard_map/ppermute | solution.py:38
  84.6 34.2 %collective-permute-start.9 = (bf16[2,128,1024]{2,1,0:T(8,128)(2,1)S(1)}, bf16[2,128,1024]{2,1,0:T(8,128)(2,1)}, u32[]{:S(2)}, u32[]{:S(2)}) collective-permute-start(bf16[2,128,1024]{2,1,0:T(8,128)(2,1)S(1)} %slice_bitcast_fusion.2), channel_id=1, source_target_pairs={{0,48},{1,49},{2,50},{3,51},{4,52},{5,53},{6,54},{7,55},{8,56},{9,... | collective-permute-start | bytes 1572872 | tf_op jit(solution)/shard_map/ppermute | solution.py:38
  104.2 14.6 %copy-start.5 = (bf16[512,1024]{1,0:T(8,128)(2,1)}, bf16[512,1024]{1,0:T(8,128)(2,1)S(1)}, u32[]{:S(2)}) copy-start(bf16[512,1024]{1,0:T(8,128)(2,1)S(1)} %collective-permute-done.4.refs_1_.refs_7_) | copy-start | bytes 3145732
  104.2 46.7 %collective-permute-start.5 = (bf16[512,1024]{1,0:T(8,128)(2,1)S(1)}, bf16[512,1024]{1,0:T(8,128)(2,1)S(1)}, u32[]{:S(2)}, u32[]{:S(2)}) collective-permute-start(bf16[512,1024]{1,0:T(8,128)(2,1)S(1)} %collective-permute-done.4.refs_1_.refs_7_), channel_id=1, source_target_pairs={{0,16},{1,17},{2,18},{3,19},{4,20},{5,21},{6,22},{7,23},{8,24},{9,... | collective-permute-start | bytes 3145736 | tf_op jit(solution)/shard_map/ppermute | solution.py:38
  107.5 43.4 %collective-permute-start.6 = (bf16[512,1024]{1,0:T(8,128)(2,1)S(1)}, bf16[512,1024]{1,0:T(8,128)(2,1)}, u32[]{:S(2)}, u32[]{:S(2)}) collective-permute-start(bf16[512,1024]{1,0:T(8,128)(2,1)S(1)} %collective-permute-done.4.refs_1_.refs_7_), channel_id=1, source_target_pairs={{0,48},{1,49},{2,50},{3,51},{4,52},{5,53},{6,54},{7,55},{8,56},{9,... | collective-permute-start | bytes 3145736 | tf_op jit(solution)/shard_map/ppermute | solution.py:38
  118.8 32.0 %collective-permute-start.10 = (bf16[256,1024]{1,0:T(8,128)(2,1)}, bf16[256,1024]{1,0:T(8,128)(2,1)}, u32[]{:S(2)}, u32[]{:S(2)}) collective-permute-start(bf16[256,1024]{1,0:T(8,128)(2,1)} %after.9), channel_id=1, source_target_pairs={{0,16},{1,17},{2,18},{3,19},{4,20},{5,21},{6,22},{7,23},{8,24},{9,... | collective-permute-start | bytes 1572872 | tf_op jit(solution)/shard_map/ppermute | solution.py:38
  119.4 31.4 %collective-permute-start.13 = (bf16[2,128,1024]{2,1,0:T(8,128)(2,1)}, bf16[2,128,1024]{2,1,0:T(8,128)(2,1)}, u32[]{:S(2)}, u32[]{:S(2)}) collective-permute-start(bf16[2,128,1024]{2,1,0:T(8,128)(2,1)} %after.10), channel_id=1, source_target_pairs={{0,64},{1,65},{2,66},{3,67},{4,68},{5,69},{6,70},{7,71},{8,72},{9,... | collective-permute-start | bytes 1572872 | tf_op jit(solution)/shard_map/ppermute | solution.py:38
  122.6 28.2 %collective-permute-start.12 = (bf16[256,1024]{1,0:T(8,128)(2,1)}, bf16[256,1024]{1,0:T(8,128)(2,1)}, u32[]{:S(2)}, u32[]{:S(2)}) collective-permute-start(bf16[256,1024]{1,0:T(8,128)(2,1)} %slice.99), channel_id=1, source_target_pairs={{0,48},{1,49},{2,50},{3,51},{4,52},{5,53},{6,54},{7,55},{8,56},{9,... | collective-permute-start | bytes 1572872 | tf_op jit(solution)/shard_map/ppermute | solution.py:38
  150.8 23.9 %copy-start.4 = (bf16[512,1024]{1,0:T(8,128)(2,1)}, bf16[512,1024]{1,0:T(8,128)(2,1)S(1)}, u32[]{:S(2)}) copy-start(bf16[512,1024]{1,0:T(8,128)(2,1)S(1)} %collective-permute-done.5.refs_0_.refs_9_.refs_1_) | copy-start | bytes 3145732
  158.8 16.0 %collective-permute-start.16 = (bf16[8,640,512]{2,1,0:T(8,128)(2,1)}, bf16[8,640,512]{2,1,0:T(8,128)(2,1)}, u32[]{:S(2)}, u32[]{:S(2)}) collective-permute-start(bf16[8,640,512]{2,1,0:T(8,128)(2,1)} %norm.1.refs_0_.refs_1_.refs_2_.refs_3_.refs_4_.refs_5_), channel_id=1, source_target_pairs={{0,8},{1,9},{2,10},{3,11},{4,12},{5,13},{6,14},{7,15},{8,0},{9,1},... | collective-permute-start | bytes 15728648 | tf_op jit(solution)/shard_map/ppermute | solution.py:38
  159.7 22.7 %collective-permute-start.14 = (bf16[256,1024]{1,0:T(8,128)(2,1)}, bf16[256,1024]{1,0:T(8,128)(2,1)}, u32[]{:S(2)}, u32[]{:S(2)}) collective-permute-start(bf16[256,1024]{1,0:T(8,128)(2,1)} %slice.100), channel_id=1, source_target_pairs={{0,16},{1,17},{2,18},{3,19},{4,20},{5,21},{6,22},{7,23},{8,24},{9,... | collective-permute-start | bytes 1572872 | tf_op jit(solution)/shard_map/ppermute | solution.py:38
  161.9 20.5 %collective-permute-start.15 = (bf16[256,1024]{1,0:T(8,128)(2,1)}, bf16[256,1024]{1,0:T(8,128)(2,1)}, u32[]{:S(2)}, u32[]{:S(2)}) collective-permute-start(bf16[256,1024]{1,0:T(8,128)(2,1)} %slice.101), channel_id=1, source_target_pairs={{0,48},{1,49},{2,50},{3,51},{4,52},{5,53},{6,54},{7,55},{8,56},{9,... | collective-permute-start | bytes 1572872 | tf_op jit(solution)/shard_map/ppermute | solution.py:38
  201.1 3.2 collective-permute-start.17
  214.6 34.5 %collective-permute-start.22 = (bf16[4,640,256]{2,1,0:T(8,128)(2,1)}, bf16[4,640,256]{2,1,0:T(8,128)(2,1)}, u32[]{:S(2)}, u32[]{:S(2)}) collective-permute-start(bf16[4,640,256]{2,1,0:T(8,128)(2,1)} %get-tuple-element.26), channel_id=1, source_target_pairs={{0,8},{1,9},{2,10},{3,11},{4,12},{5,13},{6,14},{7,15},{8,0},{9,1},... | collective-permute-start | bytes 3932168 | tf_op jit(solution)/shard_map/ppermute | solution.py:38
  216.9 26.6 %copy-start.22 = (bf16[640,256]{1,0:T(8,128)(2,1)S(1)}, bf16[640,256]{1,0:T(8,128)(2,1)}, u32[]{:S(2)}) copy-start(bf16[640,256]{1,0:T(8,128)(2,1)} %get-tuple-element.34.refs_5_) | copy-start | bytes 983044
  216.9 25.6 %collective-permute-start.25 = (bf16[2,2,128,1024]{3,2,1,0:T(8,128)(2,1)}, bf16[2,2,128,1024]{3,2,1,0:T(8,128)(2,1)S(1)}, u32[]{:S(2)}, u32[]{:S(2)}) collective-permute-start(bf16[2,2,128,1024]{3,2,1,0:T(8,128)(2,1)} %after.11.refs_0_), channel_id=1, source_target_pairs={{0,48},{1,49},{2,50},{3,51},{4,52},{5,53},{6,54},{7,55},{8,56},{9,... | collective-permute-start | bytes 3145736 | tf_op jit(solution)/shard_map/ppermute | solution.py:38
  218.6 33.6 %collective-permute-start.24 = (bf16[2,2,128,1024]{3,2,1,0:T(8,128)(2,1)}, bf16[2,2,128,1024]{3,2,1,0:T(8,128)(2,1)S(1)}, u32[]{:S(2)}, u32[]{:S(2)}) collective-permute-start(bf16[2,2,128,1024]{3,2,1,0:T(8,128)(2,1)} %after.11.refs_0_), channel_id=1, source_target_pairs={{0,16},{1,17},{2,18},{3,19},{4,20},{5,21},{6,22},{7,23},{8,24},{9,... | collective-permute-start | bytes 3145736 | tf_op jit(solution)/shard_map/ppermute | solution.py:38
  242.5 9.6 %copy-start.15 = (bf16[2,2,128,1024]{3,2,1,0:T(8,128)(2,1)}, bf16[2,2,128,1024]{3,2,1,0:T(8,128)(2,1)S(1)}, u32[]{:S(2)}) copy-start(bf16[2,2,128,1024]{3,2,1,0:T(8,128)(2,1)S(1)} %collective-permute-done.25.refs_2_) | copy-start | bytes 3145732
  243.5 10.9 %collective-permute-start.18 = (bf16[640,256]{1,0:T(8,128)(2,1)S(1)}, bf16[640,256]{1,0:T(8,128)(2,1)S(1)}, u32[]{:S(2)}, u32[]{:S(2)}) collective-permute-start(bf16[640,256]{1,0:T(8,128)(2,1)S(1)} %copy-done.22), channel_id=1, source_target_pairs={{0,2},{1,3},{2,4},{3,5},{4,6},{5,7},{6,0},{7,1},{8,10},{9,11},{10,... | collective-permute-start | bytes 983048 | tf_op jit(solution)/shard_map/ppermute | solution.py:38
  244.9 17.7 %collective-permute-start.19 = (bf16[640,256]{1,0:T(8,128)(2,1)S(1)}, bf16[640,256]{1,0:T(8,128)(2,1)}, u32[]{:S(2)}, u32[]{:S(2)}) collective-permute-start(bf16[640,256]{1,0:T(8,128)(2,1)S(1)} %get-tuple-element.36), channel_id=1, source_target_pairs={{0,4},{1,5},{2,6},{3,7},{4,0},{5,1},{6,2},{7,3},{8,12},{9,13},{10,... | collective-permute-start | bytes 983048 | tf_op jit(solution)/shard_map/ppermute | solution.py:38
  247.6 17.2 %collective-permute-start.20 = (bf16[640,256]{1,0:T(8,128)(2,1)S(1)}, bf16[640,256]{1,0:T(8,128)(2,1)}, u32[]{:S(2)}, u32[]{:S(2)}) collective-permute-start(bf16[640,256]{1,0:T(8,128)(2,1)S(1)} %get-tuple-element.35), channel_id=1, source_target_pairs={{0,6},{1,7},{2,0},{3,1},{4,2},{5,3},{6,4},{7,5},{8,14},{9,15},{10,... | collective-permute-start | bytes 983048 | tf_op jit(solution)/shard_map/ppermute | solution.py:38
  252.2 83.3 %reduce-scatter.5.cloned.1.call-start = ((), (), s32[]{:S(2)}) async-start(), calls=%async_computation.4 | async-start | bytes 1638400 | tf_op jit(solution)/shard_map/reduce_scatter | solution.py:358
  252.3 14.8 %copy-start.16 = (bf16[2,2,128,1024]{3,2,1,0:T(8,128)(2,1)}, bf16[2,2,128,1024]{3,2,1,0:T(8,128)(2,1)S(1)}, u32[]{:S(2)}) copy-start(bf16[2,2,128,1024]{3,2,1,0:T(8,128)(2,1)S(1)} %collective-permute-done.24.refs_1_) | copy-start | bytes 3145732
  267.1 12.5 %collective-permute-start.27 = (bf16[2,128,1024]{2,1,0:T(8,128)(2,1)}, bf16[2,128,1024]{2,1,0:T(8,128)(2,1)S(1)}, u32[]{:S(2)}, u32[]{:S(2)}) collective-permute-start(bf16[2,128,1024]{2,1,0:T(8,128)(2,1)} %after.13), channel_id=1, source_target_pairs={{0,48},{1,49},{2,50},{3,51},{4,52},{5,53},{6,54},{7,55},{8,56},{9,... | collective-permute-start | bytes 1572872 | tf_op jit(solution)/shard_map/ppermute | solution.py:38
  270.1 12.9 %collective-permute-start.26 = (bf16[2,128,1024]{2,1,0:T(8,128)(2,1)}, bf16[2,128,1024]{2,1,0:T(8,128)(2,1)S(1)}, u32[]{:S(2)}, u32[]{:S(2)}) collective-permute-start(bf16[2,128,1024]{2,1,0:T(8,128)(2,1)} %after.12), channel_id=1, source_target_pairs={{0,16},{1,17},{2,18},{3,19},{4,20},{5,21},{6,22},{7,23},{8,24},{9,... | collective-permute-start | bytes 1572872 | tf_op jit(solution)/shard_map/ppermute | solution.py:38
  290.7 3.2 collective-permute-start.28
  303.9 3.2 collective-permute-start.30
  304.1 10.5 %collective-permute-start.21 = (bf16[640,128]{1,0:T(8,128)(2,1)S(1)}, bf16[640,128]{1,0:T(8,128)(2,1)S(1)}, u32[]{:S(2)}, u32[]{:S(2)}) collective-permute-start(bf16[640,128]{1,0:T(8,128)(2,1)S(1)} %constant_dynamic-slice_fusion.1), channel_id=1, source_target_pairs={{0,1},{1,0},{2,3},{3,2},{4,5},{5,4},{6,7},{7,6},{8,9},{9,8},{10,11... | collective-permute-start | bytes 491528 | tf_op jit(solution)/shard_map/ppermute | solution.py:38
  309.3 22.1 %collective-permute-start.31 = (bf16[640,256]{1,0:T(8,128)(2,1)}, bf16[640,256]{1,0:T(8,128)(2,1)S(1)}, u32[]{:S(2)}, u32[]{:S(2)}) collective-permute-start(bf16[640,256]{1,0:T(8,128)(2,1)} %get-tuple-element.31), channel_id=1, source_target_pairs={{0,2},{1,3},{2,4},{3,5},{4,6},{5,7},{6,0},{7,1},{8,10},{9,11},{10,... | collective-permute-start | bytes 983048 | tf_op jit(solution)/shard_map/ppermute | solution.py:38
  310.2 21.2 %collective-permute-start.32 = (bf16[640,256]{1,0:T(8,128)(2,1)S(1)}, bf16[640,256]{1,0:T(8,128)(2,1)S(1)}, u32[]{:S(2)}, u32[]{:S(2)}) collective-permute-start(bf16[640,256]{1,0:T(8,128)(2,1)S(1)} %get-tuple-element.33), channel_id=1, source_target_pairs={{0,4},{1,5},{2,6},{3,7},{4,0},{5,1},{6,2},{7,3},{8,12},{9,13},{10,... | collective-permute-start | bytes 983048 | tf_op jit(solution)/shard_map/ppermute | solution.py:38
  314.5 16.8 %collective-permute-start.33 = (bf16[640,256]{1,0:T(8,128)(2,1)S(1)}, bf16[640,256]{1,0:T(8,128)(2,1)S(1)}, u32[]{:S(2)}, u32[]{:S(2)}) collective-permute-start(bf16[640,256]{1,0:T(8,128)(2,1)S(1)} %get-tuple-element.32), channel_id=1, source_target_pairs={{0,6},{1,7},{2,0},{3,1},{4,2},{5,3},{6,4},{7,5},{8,14},{9,15},{10,... | collective-permute-start | bytes 983048 | tf_op jit(solution)/shard_map/ppermute | solution.py:38
  314.6 20.8 %copy-start.24 = (bf16[1,640,256]{2,1,0:T(8,128)(2,1)S(1)}, bf16[1,640,256]{2,1,0:T(8,128)(2,1)}, u32[]{:S(2)}) copy-start(bf16[1,640,256]{2,1,0:T(8,128)(2,1)} %reduce-scatter.3.cloned.1.call-done) | copy-start | bytes 983044
  315.6 19.8 %collective-permute-start.23 = (bf16[640,128]{1,0:T(8,128)(2,1)S(1)}, bf16[640,128]{1,0:T(8,128)(2,1)S(1)}, u32[]{:S(2)}, u32[]{:S(2)}) collective-permute-start(bf16[640,128]{1,0:T(8,128)(2,1)S(1)} %dynamic-slice_bitcast_fusion.1), channel_id=1, source_target_pairs={{0,1},{1,0},{2,3},{3,2},{4,5},{5,4},{6,7},{7,6},{8,9},{9,8},{10,11... | collective-permute-start | bytes 491528 | tf_op jit(solution)/shard_map/ppermute | solution.py:38
  332.5 7.5 %collective-permute-start.34 = (bf16[640,128]{1,0:T(8,128)(2,1)S(1)}, bf16[640,128]{1,0:T(8,128)(2,1)S(1)}, u32[]{:S(2)}, u32[]{:S(2)}) collective-permute-start(bf16[640,128]{1,0:T(8,128)(2,1)S(1)} %constant_dynamic-slice_fusion), channel_id=1, source_target_pairs={{0,1},{1,0},{2,3},{3,2},{4,5},{5,4},{6,7},{7,6},{8,9},{9,8},{10,11... | collective-permute-start | bytes 491528 | tf_op jit(solution)/shard_map/ppermute | solution.py:38
  336.5 7.2 %collective-permute-start.29 = (bf16[640,128]{1,0:T(8,128)(2,1)S(1)}, bf16[640,128]{1,0:T(8,128)(2,1)S(1)}, u32[]{:S(2)}, u32[]{:S(2)}) collective-permute-start(bf16[640,128]{1,0:T(8,128)(2,1)S(1)} %dynamic-slice_bitcast_fusion), channel_id=1, source_target_pairs={{0,1},{1,0},{2,3},{3,2},{4,5},{5,4},{6,7},{7,6},{8,9},{9,8},{10,11... | collective-permute-start | bytes 491528 | tf_op jit(solution)/shard_map/ppermute | solution.py:38
  (18 other events, 57.7 us)
Sparse Core Ops, SparseCore 0:
  9.7 37.6 all-gather.4
  79.5 32.9 all-gather.6
  252.3 22.1 reduce-scatter.2
  296.9 27.5 reduce-scatter.4

commit v4 on v3

--- a/solution.py
+++ b/solution.py
@@ -296,18 +296,19 @@
     down_half, down_a = down_step(0, down_args)
     ylo_a = send(down_a, ylo=1)
     up_updated, columns = up_step(up_master, up_gradient, up_first, up_second, down_a)
+    ylo_a = after(ylo_a, columns)
     down_updated, down_b = down_step(1, down_args, (down_half,), (ylo_a,))
 
     st_a = jnp.stack([down_a, ylo_a])
     low_a, high_a = both_ways(st_a, st_a)
     u0 = lax.all_to_all(columns, ("core", "x", "yhi"), 0, 0, tiled=True).reshape(512, 1024)
     u0 = after(u0, down_b, low_a, high_a)
-    feats_b = lax.all_gather(after(tokens_b, u0), "x", axis=0)
     opp_a = both_ways(low_a[0], high_a[1])
     ws_a = (st_a, low_a, high_a, *opp_a)
 
     u1 = send(u0, ylo=1)
     low0, high0 = both_ways(u0, u0)
+    feats_b = lax.all_gather(after(tokens_b, low0, high0, u1, *opp_a), "x", axis=0)
     down_b = after(down_b, u1)
     ylo_b = send(down_b, ylo=1)
     low1, high1 = both_ways(u1, u1)
@@ -325,26 +326,24 @@
     where = lax.dynamic_index_in_dim(jnp.asarray(SLOTS), (ylo * 4 + z) * 2 + yhi, 0, keepdims=False)
     ws_up = (u0, u1, low0, low1, high0, high1)
     firsts = [hidden_first(where, n, ws_up) for n in (normed, normed_sib)]
-    hidden_own, hidden_sib = (
-        hidden_last(where, f, n, opp0 + opp1, firsts) for f, n in zip(firsts, (normed, normed_sib))
-    )
-
-    pieces, sums, reduced = [], [], []
+    hidden_sib = hidden_last(where, firsts[1], normed_sib, opp0 + opp1, firsts[:1])
+    hidden_own = hidden_last(where, firsts[0], normed, opp0 + opp1, (hidden_sib, low_b, high_b))
+    ws_b = (st_b, low_b, high_b, *both_ways(low_b[0], high_b[1]))
+
+    pieces, parts, sums, reduced = [], [], [], []
     places = jnp.arange(4, dtype=jnp.int32)
     add = lambda a, b: (a.astype(jnp.float32) + b.astype(jnp.float32)).astype(jnp.bfloat16)
     for j in range(CHUNKS):
-        direct = j in (0, 3)
-        if j == 2:
-            up, down = after(low_b[0], *reduced), after(high_b[1], *reduced)
-            ws_b = (st_b, low_b, high_b, *both_ways(up, down))
+        direct = j % 2 == 1
         part, part_sib = partial_of(
             (places - x) % 4 if direct else places,
             hidden_own,
             hidden_sib,
             ws_a if j < 2 else ws_b,
             j % 2,
-            sums[-1:],
+            parts[-1:] + (sums + reduced if j == 2 else []),
         )
+        parts.append(part_sib)
         part_sib = send(part_sib, core=1)
         if direct:
             terms = [add(part[d], part_sib[d]) for d in range(4)]

time: 353 us -> 326 us (0.924)
  waiting for transfers between devices: 164 us -> 137 us
  local copies, waits for them, and re-layouts: 22.2 us -> 31.2 us
  other arithmetic: 21.1 us -> 14.3 us
    ppermute x35, waiting for transfers between devices: 154 us -> 127 us  [send(): return lax.ppermute(v, AXES, shifted(**steps))]
    unnamed x53 -> x81, local copies, waits for them, and re-layouts: 10.1 us -> 18.1 us
    convert_element_type x8, other arithmetic: 11.7 us -> 7.34 us  [body(): (a.astype(jnp.float32) + b.astype(jnp.float32)).astype(jnp.bfloat16)]
  transfers between devices with their start and end apart: 40 -> 40, of which waited for: 19 -> 15; matrix products, arithmetic and copies ran while one was open for 8% -> 8% of each run, Pallas kernels for 14% -> 19%
where the time goes in v4:
time: 326 us; the launch traced here: 324 us
  waiting for transfers between devices  137 us (42%)
  Pallas kernels  75.8 us (23%)
  starting transfers between devices  51.2 us (16%)
  local copies, waits for them, and re-layouts  31.2 us (10%)
  other arithmetic  14.3 us (4%)
  between operations  14.2 us (4%)
    ppermute x35, waiting for transfers between devices, send(): return lax.ppermute(v, AXES, shifted(**steps))  127 us
    ppermute x35, starting transfers between devices, send(): return lax.ppermute(v, AXES, shifted(**steps))  44 us
    pallas_call x4, Pallas kernels, partial_of(): pl.pallas_call(partial_kernel, out_shape=(shape, shape), grid_spec=pltpu....  28.1 us
    unnamed x81, local copies, waits for them, and re-layouts  18.1 us
    pallas_call x2, Pallas kernels, hidden_first(): pl.pallas_call(first_kernel, out_shape=jax.ShapeDtypeStruct((640, 1024),...  13.7 us
    pallas_call x2, Pallas kernels, down_step(): pl.pallas_call(down_kernel, out_shape=(jax.ShapeDtypeStruct((128, D), jnp...  12.7 us
    all_to_all x1, waiting for transfers between devices, body(): lax.all_to_all(columns, ('core', 'x', 'yhi'), 0, 0, tiled=True)  9.94 us
    pallas_call x2, Pallas kernels, hidden_last(): pl.pallas_call(last_kernel, out_shape=jax.ShapeDtypeStruct((640, 1024), j...  9.43 us
  transfers between devices with their start and end apart: 40, of which 15 were waited for; matrix products, arithmetic and copies ran while one was open for 8% of the time, Pallas kernels for 19%

profile of v4, /device:TPU:0, one launch (start us, length us, event | category | flops | bytes accessed | tf_op | source)
XLA Modules:
  0.0 324.0 jit_solution(11384371226793187088)
XLA Ops:
  7.9 6.3 %adam_down.2 = (f32[128,4096]{1,0:T(8,128)}, bf16[2,128,1024]{2,1,0:T(8,128)(2,1)}) custom-call(f32[128,4096]{1,0:T(8,128)} %w_ref.5, bf16[128,4096]{1,0:T(8,128)(2,1)} %g_ref.5, f32[128,4096]{1,0:T(8,128)} %m_ref.5, f32[128,4096]{1,0:T(8,128)} %v_ref.5), custom_call_target="tpu_custom_call" | custom-call | flops 7864 | bytes 5242 | tf_op jit(solution)/shard_map/adam_down/pallas_call | solution.py:110
  14.2 1.7 collective-permute-start
  15.9 7.8 %adam_up.1 = (f32[32,16384]{1,0:T(8,128)}, bf16[16,32,1024]{2,1,0:T(8,128)(2,1)}) custom-call(f32[32,16384]{1,0:T(8,128)} %w_ref.4, bf16[32,16384]{1,0:T(8,128)(2,1)} %g_ref.4, f32[32,16384]{1,0:T(8,128)} %m_ref.4, f32[32,16384]{1,0:T(8,128)} %v_ref.4, bf16[2,128,1024]{2,1,0:T(8,128)(2,1)} %get-tuple-element.17.dep_ref), custom_call_target="tpu_custom_call" | custom-call | flops 15728 | bytes 10485 | tf_op jit(solution)/shard_map/adam_up/pallas_call | solution.py:84
  23.7 4.3 %collective-permute-done.refs_0_ = bf16[2,128,1024]{2,1,0:T(8,128)(2,1)S(1)} collective-permute-done((bf16[2,128,1024]{2,1,0:T(8,128)(2,1)}, bf16[2,128,1024]{2,1,0:T(8,128)(2,1)S(1)}, u32[]{:S(2)}, u32[]{:S(2)}) %collective-permute-start) | collective-permute-done | bytes 524320 | tf_op jit(solution)/shard_map/ppermute | solution.py:38
  28.9 2.2 pad_maximum_fusion.refs_0_
  31.1 2.1 collective-permute-start.2
  33.1 2.1 collective-permute-start.3
  35.3 7.0 %all-to-all-start = ((bf16[16,32,1024]{2,1,0:T(8,128)(2,1)}), bf16[16,32,1024]{2,1,0:T(8,128)(2,1)S(1)}, u32[]{:S(2)}, u32[]{:S(2)}) async-start(bf16[16,32,1024]{2,1,0:T(8,128)(2,1)} %get-tuple-element.20.refs_1_), calls=%async_computation | async-start | bytes 2097152 | tf_op jit(solution)/shard_map/all_to_all | solution.py:304
  42.4 3.5 %collective-permute-start.1 = (bf16[2,320,512]{2,1,0:T(8,128)(2,1)}, bf16[2,320,512]{2,1,0:T(8,128)(2,1)}, u32[]{:S(2)}, u32[]{:S(2)}) collective-permute-start(bf16[2,320,512]{2,1,0:T(8,128)(2,1)} %param.11), channel_id=1, source_target_pairs={{0,1},{1,0},{2,3},{3,2},{4,5},{5,4},{6,7},{7,6},{8,9},{9,8},{10,11... | collective-permute-start | bytes 1966088 | tf_op jit(solution)/shard_map/ppermute | solution.py:38
  45.9 6.3 %adam_down.3 = (f32[128,4096]{1,0:T(8,128)}, bf16[2,128,1024]{2,1,0:T(8,128)(2,1)}) custom-call(f32[128,4096]{1,0:T(8,128)} %w_ref.5, bf16[128,4096]{1,0:T(8,128)(2,1)} %g_ref.5, f32[128,4096]{1,0:T(8,128)} %m_ref.5, f32[128,4096]{1,0:T(8,128)} %v_ref.5, f32[128,4096]{1,0:T(8,128)} %get-tuple-element.19.refs_0_, ...), custom_call_target="tpu_custom_call", output_to_operand_aliasing={{0}: (4, {})} | custom-call | flops 7864 | bytes 5242 | tf_op jit(solution)/shard_map/adam_down/pallas_call | solution.py:110
  52.2 9.9 %all-to-all-done = bf16[16,32,1024]{2,1,0:T(8,128)(2,1)S(1)} async-done(((bf16[16,32,1024]{2,1,0:T(8,128)(2,1)}), bf16[16,32,1024]{2,1,0:T(8,128)(2,1)S(1)}, u32[]{:S(2)}, u32[]{:S(2)}) %all-to-all-start) | async-done | bytes 1048608 | tf_op jit(solution)/shard_map/all_to_all | solution.py:304
  63.7 1.5 collective-permute-start.4
  65.3 1.7 collective-permute-start.5
  69.1 3.7 %collective-permute-done.1.refs_0_ = bf16[2,320,512]{2,1,0:T(8,128)(2,1)} collective-permute-done((bf16[2,320,512]{2,1,0:T(8,128)(2,1)}, bf16[2,320,512]{2,1,0:T(8,128)(2,1)}, u32[]{:S(2)}, u32[]{:S(2)}) %collective-permute-start.1) | collective-permute-done | bytes 655392 | tf_op jit(solution)/shard_map/ppermute | solution.py:38
  72.8 2.0 collective-permute-start.8
  74.8 26.3 %collective-permute-done.7.refs_4_.refs_2_.refs_3_ = bf16[2,128,1024]{2,1,0:T(8,128)(2,1)S(1)} collective-permute-done((bf16[2,128,1024]{2,1,0:T(8,128)(2,1)S(1)}, bf16[2,128,1024]{2,1,0:T(8,128)(2,1)S(1)}, u32[]{:S(2)}, u32[]{:S(2)}) %collective-permute-start.7) | collective-permute-done | bytes 524320 | tf_op jit(solution)/shard_map/ppermute | solution.py:38
  105.7 1.8 collective-permute-start.10
  107.5 1.9 slice.98.refs_0_
  111.5 1.9 collective-permute-start.12
  114.2 26.7 %collective-permute-done.11.refs_2_ = bf16[256,1024]{1,0:T(8,128)(2,1)} collective-permute-done((bf16[256,1024]{1,0:T(8,128)(2,1)}, bf16[256,1024]{1,0:T(8,128)(2,1)}, u32[]{:S(2)}, u32[]{:S(2)}) %collective-permute-start.11) | collective-permute-done | bytes 524320 | tf_op jit(solution)/shard_map/ppermute | solution.py:38
  141.0 2.6 copy-done.20
  143.6 1.7 copy-done.21
  145.3 4.1 %norm.1.refs_0_.refs_1_.refs_2_.refs_3_.refs_4_.refs_5_ = bf16[8,640,512]{2,1,0:T(8,128)(2,1)} custom-call(bf16[4,640,512]{2,1,0:T(8,128)(2,1)S(1)} %bitcast.55, bf16[4,640,512]{2,1,0:T(8,128)(2,1)S(1)} %bitcast.56, f32[8,512]{1,0:T(8,128)S(1)} %pad_maximum_fusion.3.g_ref, bf16[512,1024]{1,0:T(8,128)(2,1)S(1)} %collective-permute-done.9.refs_0_.refs_9_.refs_1_, ...), custom_call_target="tpu_custom_call" | custom-call | flops 20971 | bytes 10485 | tf_op jit(solution)/shard_map/norm/pallas_call | solution.py:145
  151.3 2.5 collective-permute-start.18
  154.7 1.9 slice.101
  156.5 3.2 collective-permute-start.15
  164.1 7.0 %hidden_first.2.refs_6_.acc_ref = f32[640,1024]{1,0:T(8,128)S(1)} custom-call(s32[16]{0:T(128)S(1)} %fusion.17.s_ref, bf16[8,640,512]{2,1,0:T(8,128)(2,1)} %norm.1.refs_0_.refs_1_.refs_2_.refs_3_.refs_4_.refs_5_, bf16[8,640,512]{2,1,0:T(8,128)(2,1)} %norm.1.refs_0_.refs_1_.refs_2_.refs_3_.refs_4_.refs_5_, ...), custom_call_target="tpu_custom_call" | custom-call | flops 4026531 | bytes 14680 | tf_op jit(solution)/shard_map/hidden_first/pallas_call | solution.py:193
  171.2 6.7 %hidden_first.3.acc_ref = f32[640,1024]{1,0:T(8,128)S(1)} custom-call(s32[16]{0:T(128)S(1)} %fusion.17.s_ref, bf16[8,640,512]{2,1,0:T(8,128)(2,1)} %collective-permute-done.16.refs_0_.refs_1_.refs_2_.refs_3_.refs_4_.refs_5_, bf16[8,640,512]{2,1,0:T(8,128)(2,1)} %collective-permute-done.16.refs_0_.refs_1_.refs_2_.refs_3_.refs_4_.refs_5_, ...), custom_call_target="tpu_custom_call" | custom-call | flops 4026531 | bytes 14680 | tf_op jit(solution)/shard_map/hidden_first/pallas_call | solution.py:193
  177.9 11.0 %collective-permute-done.14.refs_4_ = bf16[256,1024]{1,0:T(8,128)(2,1)} collective-permute-done((bf16[256,1024]{1,0:T(8,128)(2,1)}, bf16[256,1024]{1,0:T(8,128)(2,1)}, u32[]{:S(2)}, u32[]{:S(2)}) %collective-permute-start.14) | collective-permute-done | bytes 524320 | tf_op jit(solution)/shard_map/ppermute | solution.py:38
  188.9 4.7 %hidden_last.2.refs_6_.sib_ref = bf16[640,1024]{1,0:T(8,128)(2,1)S(1)} custom-call(s32[16]{0:T(128)S(1)} %fusion.17.s_ref, f32[640,1024]{1,0:T(8,128)S(1)} %hidden_first.3.acc_ref, bf16[8,640,512]{2,1,0:T(8,128)(2,1)} %collective-permute-done.16.refs_0_.refs_1_.refs_2_.refs_3_.refs_4_.refs_5_, ...), custom_call_target="tpu_custom_call" | custom-call | flops 1342177 | bytes 8388 | tf_op jit(solution)/shard_map/hidden_last/pallas_call | solution.py:211
  193.6 4.7 %hidden_last.3.own_ref = bf16[640,1024]{1,0:T(8,128)(2,1)S(1)} custom-call(s32[16]{0:T(128)S(1)} %fusion.17.s_ref, f32[640,1024]{1,0:T(8,128)S(1)} %hidden_first.2.refs_6_.acc_ref, bf16[8,640,512]{2,1,0:T(8,128)(2,1)} %norm.1.refs_0_.refs_1_.refs_2_.refs_3_.refs_4_.refs_5_, bf16[8,640,512]{2,1,0:T(8,128)(2,1)} %norm.1.refs_0_.refs_1_.refs_2_.refs_3_.refs_4_.refs_5_, ...), custom_call_target="tpu_custom_call" | custom-call | flops 1342177 | bytes 8388 | tf_op jit(solution)/shard_map/hidden_last/pallas_call | solution.py:211
  199.9 6.9 %partial.4 = (bf16[4,640,256]{2,1,0:T(8,128)(2,1)}, bf16[4,640,256]{2,1,0:T(8,128)(2,1)}) custom-call(s32[4]{0:T(128)} %iota.7.s_ref, bf16[640,1024]{1,0:T(8,128)(2,1)} %copy-done.1, bf16[640,1024]{1,0:T(8,128)(2,1)} %copy-done, bf16[2,2,128,1024]{3,2,1,0:T(8,128)(2,1)} %pad_maximum_fusion.refs_0_, bf16[2,2,128,1024]{3,2,1,0:T(8,128)(2,1)} %copy-done.22, ...), custom_call_target="tpu_custom_call" | custom-call | flops 2684354 | bytes 8388 | tf_op jit(solution)/shard_map/partial/pallas_call | solution.py:251
  207.4 7.1 %partial.5 = (bf16[4,640,256]{2,1,0:T(8,128)(2,1)}, bf16[4,640,256]{2,1,0:T(8,128)(2,1)}) custom-call(s32[4]{0:T(128)} %and_select_fusion.s_ref, bf16[640,1024]{1,0:T(8,128)(2,1)} %copy-done.1, bf16[640,1024]{1,0:T(8,128)(2,1)} %copy-done, bf16[2,2,128,1024]{3,2,1,0:T(8,128)(2,1)} %pad_maximum_fusion.refs_0_, bf16[2,2,128,1024]{3,2,1,0:T(8,128)(2,1)} %copy-done.22, ...), custom_call_target="tpu_custom_call" | custom-call | flops 2684354 | bytes 8388 | tf_op jit(solution)/shard_map/partial/pallas_call | solution.py:251
  215.0 1.9 slice_bitcast_fusion.1
  217.8 2.7 add_convert_fusion.1.refs_6_
  222.1 1.6 collective-permute-start.24
  226.0 2.3 collective-permute-start.27
  228.3 7.5 %collective-permute-done.24 = bf16[640,256]{1,0:T(8,128)(2,1)S(1)} collective-permute-done((bf16[640,256]{1,0:T(8,128)(2,1)S(1)}, bf16[640,256]{1,0:T(8,128)(2,1)S(1)}, u32[]{:S(2)}, u32[]{:S(2)}) %collective-permute-start.24) | collective-permute-done | bytes 327712 | tf_op jit(solution)/shard_map/ppermute | solution.py:38
  235.8 4.8 %collective-permute-done.23 = bf16[640,256]{1,0:T(8,128)(2,1)S(1)} collective-permute-done((bf16[640,256]{1,0:T(8,128)(2,1)S(1)}, bf16[640,256]{1,0:T(8,128)(2,1)S(1)}, u32[]{:S(2)}, u32[]{:S(2)}) %collective-permute-start.23) | collective-permute-done | bytes 327712 | tf_op jit(solution)/shard_map/ppermute | solution.py:38
  240.6 7.7 %collective-permute-done.22 = bf16[640,256]{1,0:T(8,128)(2,1)S(1)} collective-permute-done((bf16[640,256]{1,0:T(8,128)(2,1)S(1)}, bf16[640,256]{1,0:T(8,128)(2,1)S(1)}, u32[]{:S(2)}, u32[]{:S(2)}) %collective-permute-start.22) | collective-permute-done | bytes 327712 | tf_op jit(solution)/shard_map/ppermute | solution.py:38
  250.2 7.0 %partial.6 = (bf16[4,640,256]{2,1,0:T(8,128)(2,1)}, bf16[4,640,256]{2,1,0:T(8,128)(2,1)}) custom-call(s32[4]{0:T(128)} %iota.9.s_ref, bf16[640,1024]{1,0:T(8,128)(2,1)} %copy-done.1, bf16[640,1024]{1,0:T(8,128)(2,1)} %copy-done, bf16[2,2,128,1024]{3,2,1,0:T(8,128)(2,1)} %after.11.refs_0_, bf16[2,2,128,1024]{3,2,1,0:T(8,128)(2,1)} %collective-permute-done.17.refs_7_.refs_1_, ...), custom_call_target="tpu_custom_call" | custom-call | flops 2684354 | bytes 8388 | tf_op jit(solution)/shard_map/partial/pallas_call | solution.py:251
  257.5 7.1 %partial.7 = (bf16[4,640,256]{2,1,0:T(8,128)(2,1)}, bf16[4,640,256]{2,1,0:T(8,128)(2,1)}) custom-call(s32[4]{0:T(128)} %and_select_fusion.s_ref, bf16[640,1024]{1,0:T(8,128)(2,1)} %copy-done.1, bf16[640,1024]{1,0:T(8,128)(2,1)} %copy-done, bf16[2,2,128,1024]{3,2,1,0:T(8,128)(2,1)} %after.11.refs_0_, ...), custom_call_target="tpu_custom_call" | custom-call | flops 2684354 | bytes 8388 | tf_op jit(solution)/shard_map/partial/pallas_call | solution.py:251
  268.9 3.6 %collective-permute-start.33 = (bf16[640,256]{1,0:T(8,128)(2,1)}, bf16[640,256]{1,0:T(8,128)(2,1)S(1)}, u32[]{:S(2)}, u32[]{:S(2)}) collective-permute-start(bf16[640,256]{1,0:T(8,128)(2,1)} %get-tuple-element.32), channel_id=1, source_target_pairs={{0,6},{1,7},{2,0},{3,1},{4,2},{5,3},{6,4},{7,5},{8,14},{9,15},{10,... | collective-permute-start | bytes 983048 | tf_op jit(solution)/shard_map/ppermute | solution.py:38
  273.7 17.1 %collective-permute-done.33 = bf16[640,256]{1,0:T(8,128)(2,1)S(1)} collective-permute-done((bf16[640,256]{1,0:T(8,128)(2,1)}, bf16[640,256]{1,0:T(8,128)(2,1)S(1)}, u32[]{:S(2)}, u32[]{:S(2)}) %collective-permute-start.33) | collective-permute-done | bytes 327712 | tf_op jit(solution)/shard_map/ppermute | solution.py:38
  291.5 6.3 %collective-permute-done.31 = bf16[640,256]{1,0:T(8,128)(2,1)} collective-permute-done((bf16[640,256]{1,0:T(8,128)(2,1)}, bf16[640,256]{1,0:T(8,128)(2,1)}, u32[]{:S(2)}, u32[]{:S(2)}) %collective-permute-start.31) | collective-permute-done | bytes 327712 | tf_op jit(solution)/shard_map/ppermute | solution.py:38
  300.6 3.3 %collective-permute-start.20 = (bf16[640,128]{1,0:T(8,128)(2,1)S(1)}, bf16[640,128]{1,0:T(8,128)(2,1)S(1)}, u32[]{:S(2)}, u32[]{:S(2)}) collective-permute-start(bf16[640,128]{1,0:T(8,128)(2,1)S(1)} %dynamic-slice_bitcast_fusion.1), channel_id=1, source_target_pairs={{0,1},{1,0},{2,3},{3,2},{4,5},{5,4},{6,7},{7,6},{8,9},{9,8},{10,11... | collective-permute-start | bytes 491528 | tf_op jit(solution)/shard_map/ppermute | solution.py:38
  303.9 3.7 %collective-permute-done.34 = bf16[640,128]{1,0:T(8,128)(2,1)S(1)} collective-permute-done((bf16[640,128]{1,0:T(8,128)(2,1)S(1)}, bf16[640,128]{1,0:T(8,128)(2,1)S(1)}, u32[]{:S(2)}, u32[]{:S(2)}) %collective-permute-start.34) | collective-permute-done | bytes 163872 | tf_op jit(solution)/shard_map/ppermute | solution.py:38
  310.6 5.0 %collective-permute-done.29 = bf16[640,128]{1,0:T(8,128)(2,1)S(1)} collective-permute-done((bf16[640,128]{1,0:T(8,128)(2,1)S(1)}, bf16[640,128]{1,0:T(8,128)(2,1)S(1)}, u32[]{:S(2)}, u32[]{:S(2)}) %collective-permute-start.29) | collective-permute-done | bytes 163872 | tf_op jit(solution)/shard_map/ppermute | solution.py:38
  (167 shorter events, 43.1 us)
Async XLA Ops:
  7.2 133.8 %all-gather.5.cloned.1.call-start = ((), (), s32[]{:S(2)}) async-start(), calls=%async_computation.5 | async-start | bytes 3276800 | tf_op jit(solution)/shard_map/all_gather | solution.py:293
  14.2 13.8 %collective-permute-start = (bf16[2,128,1024]{2,1,0:T(8,128)(2,1)}, bf16[2,128,1024]{2,1,0:T(8,128)(2,1)S(1)}, u32[]{:S(2)}, u32[]{:S(2)}) collective-permute-start(bf16[2,128,1024]{2,1,0:T(8,128)(2,1)} %get-tuple-element.17.dep_ref), channel_id=1, source_target_pairs={{0,64},{1,65},{2,66},{3,67},{4,68},{5,69},{6,70},{7,71},{8,72},{9,... | collective-permute-start | bytes 1572872 | tf_op jit(solution)/shard_map/ppermute | solution.py:38
  31.1 31.1 %collective-permute-start.2 = (bf16[2,2,128,1024]{3,2,1,0:T(8,128)(2,1)}, bf16[2,2,128,1024]{3,2,1,0:T(8,128)(2,1)S(1)}, u32[]{:S(2)}, u32[]{:S(2)}) collective-permute-start(bf16[2,2,128,1024]{3,2,1,0:T(8,128)(2,1)} %pad_maximum_fusion.refs_0_), channel_id=1, source_target_pairs={{0,16},{1,17},{2,18},{3,19},{4,20},{5,21},{6,22},{7,23},{8,24},{9,... | collective-permute-start | bytes 3145736 | tf_op jit(solution)/shard_map/ppermute | solution.py:38
  33.1 29.0 %collective-permute-start.3 = (bf16[2,2,128,1024]{3,2,1,0:T(8,128)(2,1)}, bf16[2,2,128,1024]{3,2,1,0:T(8,128)(2,1)S(1)}, u32[]{:S(2)}, u32[]{:S(2)}) collective-permute-start(bf16[2,2,128,1024]{3,2,1,0:T(8,128)(2,1)} %pad_maximum_fusion.refs_0_), channel_id=1, source_target_pairs={{0,48},{1,49},{2,50},{3,51},{4,52},{5,53},{6,54},{7,55},{8,56},{9,... | collective-permute-start | bytes 3145736 | tf_op jit(solution)/shard_map/ppermute | solution.py:38
  35.3 26.8 %all-to-all-start = ((bf16[16,32,1024]{2,1,0:T(8,128)(2,1)}), bf16[16,32,1024]{2,1,0:T(8,128)(2,1)S(1)}, u32[]{:S(2)}, u32[]{:S(2)}) async-start(bf16[16,32,1024]{2,1,0:T(8,128)(2,1)} %get-tuple-element.20.refs_1_), calls=%async_computation | async-start | bytes 2097152 | tf_op jit(solution)/shard_map/all_to_all | solution.py:304
  42.3 98.6 %all-gather.7.cloned.1.call-start = ((), (), s32[]{:S(2)}) async-start(), calls=%async_computation.6 | async-start | bytes 3276800 | tf_op jit(solution)/shard_map/all_gather | solution.py:311
  42.4 30.4 %collective-permute-start.1 = (bf16[2,320,512]{2,1,0:T(8,128)(2,1)}, bf16[2,320,512]{2,1,0:T(8,128)(2,1)}, u32[]{:S(2)}, u32[]{:S(2)}) collective-permute-start(bf16[2,320,512]{2,1,0:T(8,128)(2,1)} %param.11), channel_id=1, source_target_pairs={{0,1},{1,0},{2,3},{3,2},{4,5},{5,4},{6,7},{7,6},{8,9},{9,8},{10,11... | collective-permute-start | bytes 1966088 | tf_op jit(solution)/shard_map/ppermute | solution.py:38
  63.7 37.4 %collective-permute-start.4 = (bf16[512,1024]{1,0:T(8,128)(2,1)}, bf16[512,1024]{1,0:T(8,128)(2,1)S(1)}, u32[]{:S(2)}, u32[]{:S(2)}) collective-permute-start(bf16[512,1024]{1,0:T(8,128)(2,1)} %after.7.refs_6_), channel_id=1, source_target_pairs={{0,16},{1,17},{2,18},{3,19},{4,20},{5,21},{6,22},{7,23},{8,24},{9,... | collective-permute-start | bytes 3145736 | tf_op jit(solution)/shard_map/ppermute | solution.py:38
  65.3 35.9 %collective-permute-start.5 = (bf16[512,1024]{1,0:T(8,128)(2,1)}, bf16[512,1024]{1,0:T(8,128)(2,1)S(1)}, u32[]{:S(2)}, u32[]{:S(2)}) collective-permute-start(bf16[512,1024]{1,0:T(8,128)(2,1)} %after.7.refs_6_), channel_id=1, source_target_pairs={{0,48},{1,49},{2,50},{3,51},{4,52},{5,53},{6,54},{7,55},{8,56},{9,... | collective-permute-start | bytes 3145736 | tf_op jit(solution)/shard_map/ppermute | solution.py:38
  67.0 35.2 %collective-permute-start.6 = (bf16[512,1024]{1,0:T(8,128)(2,1)}, bf16[512,1024]{1,0:T(8,128)(2,1)S(1)}, u32[]{:S(2)}, u32[]{:S(2)}) collective-permute-start(bf16[512,1024]{1,0:T(8,128)(2,1)} %after.7.refs_6_), channel_id=1, source_target_pairs={{0,64},{1,65},{2,66},{3,67},{4,68},{5,69},{6,70},{7,71},{8,72},{9,... | collective-permute-start | bytes 3145736 | tf_op jit(solution)/shard_map/ppermute | solution.py:38
  68.6 32.5 %collective-permute-start.7 = (bf16[2,128,1024]{2,1,0:T(8,128)(2,1)S(1)}, bf16[2,128,1024]{2,1,0:T(8,128)(2,1)S(1)}, u32[]{:S(2)}, u32[]{:S(2)}) collective-permute-start(bf16[2,128,1024]{2,1,0:T(8,128)(2,1)S(1)} %slice_bitcast_fusion.3), channel_id=1, source_target_pairs={{0,16},{1,17},{2,18},{3,19},{4,20},{5,21},{6,22},{7,23},{8,24},{9,... | collective-permute-start | bytes 1572872 | tf_op jit(solution)/shard_map/ppermute | solution.py:38
  72.8 28.3 %collective-permute-start.8 = (bf16[2,128,1024]{2,1,0:T(8,128)(2,1)S(1)}, bf16[2,128,1024]{2,1,0:T(8,128)(2,1)S(1)}, u32[]{:S(2)}, u32[]{:S(2)}) collective-permute-start(bf16[2,128,1024]{2,1,0:T(8,128)(2,1)S(1)} %slice_bitcast_fusion.2), channel_id=1, source_target_pairs={{0,48},{1,49},{2,50},{3,51},{4,52},{5,53},{6,54},{7,55},{8,56},{9,... | collective-permute-start | bytes 1572872 | tf_op jit(solution)/shard_map/ppermute | solution.py:38
  104.2 195.5 %reduce-scatter.3.cloned.1.call-start = ((), (), s32[]{:S(2)}) async-start(), calls=%async_computation.3 | async-start | bytes 1638400 | tf_op jit(solution)/shard_map/reduce_scatter | solution.py:357
  104.2 36.6 %collective-permute-start.9 = (bf16[512,1024]{1,0:T(8,128)(2,1)}, bf16[512,1024]{1,0:T(8,128)(2,1)S(1)}, u32[]{:S(2)}, u32[]{:S(2)}) collective-permute-start(bf16[512,1024]{1,0:T(8,128)(2,1)} %copy-done.2), channel_id=1, source_target_pairs={{0,16},{1,17},{2,18},{3,19},{4,20},{5,21},{6,22},{7,23},{8,24},{9,... | collective-permute-start | bytes 3145736 | tf_op jit(solution)/shard_map/ppermute | solution.py:38
  105.7 35.2 %collective-permute-start.10 = (bf16[512,1024]{1,0:T(8,128)(2,1)}, bf16[512,1024]{1,0:T(8,128)(2,1)S(1)}, u32[]{:S(2)}, u32[]{:S(2)}) collective-permute-start(bf16[512,1024]{1,0:T(8,128)(2,1)} %copy-done.2), channel_id=1, source_target_pairs={{0,48},{1,49},{2,50},{3,51},{4,52},{5,53},{6,54},{7,55},{8,56},{9,... | collective-permute-start | bytes 3145736 | tf_op jit(solution)/shard_map/ppermute | solution.py:38
  109.4 31.4 %collective-permute-start.11 = (bf16[256,1024]{1,0:T(8,128)(2,1)}, bf16[256,1024]{1,0:T(8,128)(2,1)}, u32[]{:S(2)}, u32[]{:S(2)}) collective-permute-start(bf16[256,1024]{1,0:T(8,128)(2,1)} %after.9), channel_id=1, source_target_pairs={{0,16},{1,17},{2,18},{3,19},{4,20},{5,21},{6,22},{7,23},{8,24},{9,... | collective-permute-start | bytes 1572872 | tf_op jit(solution)/shard_map/ppermute | solution.py:38
  111.5 29.3 %collective-permute-start.12 = (bf16[256,1024]{1,0:T(8,128)(2,1)}, bf16[256,1024]{1,0:T(8,128)(2,1)S(1)}, u32[]{:S(2)}, u32[]{:S(2)}) collective-permute-start(bf16[256,1024]{1,0:T(8,128)(2,1)} %slice.99), channel_id=1, source_target_pairs={{0,48},{1,49},{2,50},{3,51},{4,52},{5,53},{6,54},{7,55},{8,56},{9,... | collective-permute-start | bytes 1572872 | tf_op jit(solution)/shard_map/ppermute | solution.py:38
  113.5 27.4 %collective-permute-start.13 = (bf16[2,128,1024]{2,1,0:T(8,128)(2,1)}, bf16[2,128,1024]{2,1,0:T(8,128)(2,1)S(1)}, u32[]{:S(2)}, u32[]{:S(2)}) collective-permute-start(bf16[2,128,1024]{2,1,0:T(8,128)(2,1)} %after.10), channel_id=1, source_target_pairs={{0,64},{1,65},{2,66},{3,67},{4,68},{5,69},{6,70},{7,71},{8,72},{9,... | collective-permute-start | bytes 1572872 | tf_op jit(solution)/shard_map/ppermute | solution.py:38
  140.8 8.6 %copy-start.18 = (bf16[256,1024]{1,0:T(8,128)(2,1)}, bf16[256,1024]{1,0:T(8,128)(2,1)S(1)}, u32[]{:S(2)}) copy-start(bf16[256,1024]{1,0:T(8,128)(2,1)S(1)} %collective-permute-done.12.refs_3_) | copy-start | bytes 1572868
  140.9 8.5 %copy-start.4 = (bf16[512,1024]{1,0:T(8,128)(2,1)}, bf16[512,1024]{1,0:T(8,128)(2,1)S(1)}, u32[]{:S(2)}) copy-start(bf16[512,1024]{1,0:T(8,128)(2,1)S(1)} %collective-permute-done.9.refs_0_.refs_9_.refs_1_) | copy-start | bytes 3145732
  140.9 8.5 %copy-start.15 = (bf16[512,1024]{1,0:T(8,128)(2,1)}, bf16[512,1024]{1,0:T(8,128)(2,1)S(1)}, u32[]{:S(2)}) copy-start(bf16[512,1024]{1,0:T(8,128)(2,1)S(1)} %collective-permute-done.10.refs_1_.refs_11_) | copy-start | bytes 3145732
  149.4 21.8 %collective-permute-start.16 = (bf16[8,640,512]{2,1,0:T(8,128)(2,1)}, bf16[8,640,512]{2,1,0:T(8,128)(2,1)}, u32[]{:S(2)}, u32[]{:S(2)}) collective-permute-start(bf16[8,640,512]{2,1,0:T(8,128)(2,1)} %norm.1.refs_0_.refs_1_.refs_2_.refs_3_.refs_4_.refs_5_), channel_id=1, source_target_pairs={{0,8},{1,9},{2,10},{3,11},{4,12},{5,13},{6,14},{7,15},{8,0},{9,1},... | collective-permute-start | bytes 15728648 | tf_op jit(solution)/shard_map/ppermute | solution.py:38
  150.6 9.9 %copy-start.3 = (bf16[512,1024]{1,0:T(8,128)(2,1)S(1)}, bf16[512,1024]{1,0:T(8,128)(2,1)}, u32[]{:S(2)}) copy-start(bf16[512,1024]{1,0:T(8,128)(2,1)} %copy-done.2) | copy-start | bytes 3145732
  150.6 9.9 %copy-start.7 = (bf16[512,1024]{1,0:T(8,128)(2,1)S(1)}, bf16[512,1024]{1,0:T(8,128)(2,1)}, u32[]{:S(2)}) copy-start(bf16[512,1024]{1,0:T(8,128)(2,1)} %after.7.refs_6_) | copy-start | bytes 3145732
  150.6 43.0 %collective-permute-start.17 = (bf16[2,2,128,1024]{3,2,1,0:T(8,128)(2,1)}, bf16[2,2,128,1024]{3,2,1,0:T(8,128)(2,1)}, u32[]{:S(2)}, u32[]{:S(2)}) collective-permute-start(bf16[2,2,128,1024]{3,2,1,0:T(8,128)(2,1)} %after.11.refs_0_), channel_id=1, source_target_pairs={{0,16},{1,17},{2,18},{3,19},{4,20},{5,21},{6,22},{7,23},{8,24},{9,... | collective-permute-start | bytes 3145736 | tf_op jit(solution)/shard_map/ppermute | solution.py:38
  151.3 42.3 %collective-permute-start.18 = (bf16[2,2,128,1024]{3,2,1,0:T(8,128)(2,1)}, bf16[2,2,128,1024]{3,2,1,0:T(8,128)(2,1)}, u32[]{:S(2)}, u32[]{:S(2)}) collective-permute-start(bf16[2,2,128,1024]{3,2,1,0:T(8,128)(2,1)} %after.11.refs_0_), channel_id=1, source_target_pairs={{0,48},{1,49},{2,50},{3,51},{4,52},{5,53},{6,54},{7,55},{8,56},{9,... | collective-permute-start | bytes 3145736 | tf_op jit(solution)/shard_map/ppermute | solution.py:38
  154.6 34.2 %collective-permute-start.14 = (bf16[256,1024]{1,0:T(8,128)(2,1)}, bf16[256,1024]{1,0:T(8,128)(2,1)}, u32[]{:S(2)}, u32[]{:S(2)}) collective-permute-start(bf16[256,1024]{1,0:T(8,128)(2,1)} %slice.100), channel_id=1, source_target_pairs={{0,16},{1,17},{2,18},{3,19},{4,20},{5,21},{6,22},{7,23},{8,24},{9,... | collective-permute-start | bytes 1572872 | tf_op jit(solution)/shard_map/ppermute | solution.py:38
  156.5 32.4 %collective-permute-start.15 = (bf16[256,1024]{1,0:T(8,128)(2,1)}, bf16[256,1024]{1,0:T(8,128)(2,1)}, u32[]{:S(2)}, u32[]{:S(2)}) collective-permute-start(bf16[256,1024]{1,0:T(8,128)(2,1)} %slice.101), channel_id=1, source_target_pairs={{0,48},{1,49},{2,50},{3,51},{4,52},{5,53},{6,54},{7,55},{8,56},{9,... | collective-permute-start | bytes 1572872 | tf_op jit(solution)/shard_map/ppermute | solution.py:38
  171.2 17.7 %copy-start.19 = (bf16[256,1024]{1,0:T(8,128)(2,1)S(1)}, bf16[256,1024]{1,0:T(8,128)(2,1)}, u32[]{:S(2)}) copy-start(bf16[256,1024]{1,0:T(8,128)(2,1)} %copy-done.18) | copy-start | bytes 1572868
  206.9 10.9 %collective-permute-start.19 = (bf16[4,640,256]{2,1,0:T(8,128)(2,1)}, bf16[4,640,256]{2,1,0:T(8,128)(2,1)}, u32[]{:S(2)}, u32[]{:S(2)}) collective-permute-start(bf16[4,640,256]{2,1,0:T(8,128)(2,1)} %get-tuple-element.24.refs_5_), channel_id=1, source_target_pairs={{0,8},{1,9},{2,10},{3,11},{4,12},{5,13},{6,14},{7,15},{8,0},{9,1},... | collective-permute-start | bytes 3932168 | tf_op jit(solution)/shard_map/ppermute | solution.py:38
  207.4 10.4 %copy-start.36 = (bf16[4,640,256]{2,1,0:T(8,128)(2,1)S(1)}, bf16[4,640,256]{2,1,0:T(8,128)(2,1)}, u32[]{:S(2)}) copy-start(bf16[4,640,256]{2,1,0:T(8,128)(2,1)} %get-tuple-element.23) | copy-start | bytes 3932164
  214.5 6.1 %collective-permute-start.21 = (bf16[4,640,256]{2,1,0:T(8,128)(2,1)}, bf16[4,640,256]{2,1,0:T(8,128)(2,1)S(1)}, u32[]{:S(2)}, u32[]{:S(2)}) collective-permute-start(bf16[4,640,256]{2,1,0:T(8,128)(2,1)} %get-tuple-element.26.refs_5_), channel_id=1, source_target_pairs={{0,8},{1,9},{2,10},{3,11},{4,12},{5,13},{6,14},{7,15},{8,0},{9,1},... | collective-permute-start | bytes 3932168 | tf_op jit(solution)/shard_map/ppermute | solution.py:38
  216.9 32.4 %collective-permute-start.26 = (bf16[2,128,1024]{2,1,0:T(8,128)(2,1)}, bf16[2,128,1024]{2,1,0:T(8,128)(2,1)S(1)}, u32[]{:S(2)}, u32[]{:S(2)}) collective-permute-start(bf16[2,128,1024]{2,1,0:T(8,128)(2,1)} %slice_bitcast_fusion.1), channel_id=1, source_target_pairs={{0,16},{1,17},{2,18},{3,19},{4,20},{5,21},{6,22},{7,23},{8,24},{9,... | collective-permute-start | bytes 1572872 | tf_op jit(solution)/shard_map/ppermute | solution.py:38
  220.5 87.2 %reduce-scatter.5.cloned.1.call-start = ((), (), s32[]{:S(2)}) async-start(), calls=%async_computation.4 | async-start | bytes 1638400 | tf_op jit(solution)/shard_map/reduce_scatter | solution.py:357
  222.1 27.2 %copy-start.33 = (bf16[640,256]{1,0:T(8,128)(2,1)}, bf16[640,256]{1,0:T(8,128)(2,1)S(1)}, u32[]{:S(2)}) copy-start(bf16[640,256]{1,0:T(8,128)(2,1)S(1)} %get-tuple-element.36.refs_7_) | copy-start | bytes 983044
  222.1 13.8 %collective-permute-start.24 = (bf16[640,256]{1,0:T(8,128)(2,1)S(1)}, bf16[640,256]{1,0:T(8,128)(2,1)S(1)}, u32[]{:S(2)}, u32[]{:S(2)}) collective-permute-start(bf16[640,256]{1,0:T(8,128)(2,1)S(1)} %get-tuple-element.35), channel_id=1, source_target_pairs={{0,6},{1,7},{2,0},{3,1},{4,2},{5,3},{6,4},{7,5},{8,14},{9,15},{10,... | collective-permute-start | bytes 983048 | tf_op jit(solution)/shard_map/ppermute | solution.py:38
  223.7 16.9 %collective-permute-start.23 = (bf16[640,256]{1,0:T(8,128)(2,1)S(1)}, bf16[640,256]{1,0:T(8,128)(2,1)S(1)}, u32[]{:S(2)}, u32[]{:S(2)}) collective-permute-start(bf16[640,256]{1,0:T(8,128)(2,1)S(1)} %get-tuple-element.34), channel_id=1, source_target_pairs={{0,4},{1,5},{2,6},{3,7},{4,0},{5,1},{6,2},{7,3},{8,12},{9,13},{10,... | collective-permute-start | bytes 983048 | tf_op jit(solution)/shard_map/ppermute | solution.py:38
  224.9 23.4 %collective-permute-start.22 = (bf16[640,256]{1,0:T(8,128)(2,1)S(1)}, bf16[640,256]{1,0:T(8,128)(2,1)S(1)}, u32[]{:S(2)}, u32[]{:S(2)}) collective-permute-start(bf16[640,256]{1,0:T(8,128)(2,1)S(1)} %get-tuple-element.36.refs_7_), channel_id=1, source_target_pairs={{0,2},{1,3},{2,4},{3,5},{4,6},{5,7},{6,0},{7,1},{8,10},{9,11},{10,... | collective-permute-start | bytes 983048 | tf_op jit(solution)/shard_map/ppermute | solution.py:38
  226.0 23.3 %collective-permute-start.27 = (bf16[2,128,1024]{2,1,0:T(8,128)(2,1)S(1)}, bf16[2,128,1024]{2,1,0:T(8,128)(2,1)S(1)}, u32[]{:S(2)}, u32[]{:S(2)}) collective-permute-start(bf16[2,128,1024]{2,1,0:T(8,128)(2,1)S(1)} %slice_bitcast_fusion), channel_id=1, source_target_pairs={{0,48},{1,49},{2,50},{3,51},{4,52},{5,53},{6,54},{7,55},{8,56},{9,... | collective-permute-start | bytes 1572872 | tf_op jit(solution)/shard_map/ppermute | solution.py:38
  257.2 7.7 %collective-permute-start.28 = (bf16[4,640,256]{2,1,0:T(8,128)(2,1)}, bf16[4,640,256]{2,1,0:T(8,128)(2,1)S(1)}, u32[]{:S(2)}, u32[]{:S(2)}) collective-permute-start(bf16[4,640,256]{2,1,0:T(8,128)(2,1)} %get-tuple-element.28.refs_5_), channel_id=1, source_target_pairs={{0,8},{1,9},{2,10},{3,11},{4,12},{5,13},{6,14},{7,15},{8,0},{9,1},... | collective-permute-start | bytes 3932168 | tf_op jit(solution)/shard_map/ppermute | solution.py:38
  264.6 3.2 %collective-permute-start.30 = (bf16[4,640,256]{2,1,0:T(8,128)(2,1)}, bf16[4,640,256]{2,1,0:T(8,128)(2,1)S(1)}, u32[]{:S(2)}, u32[]{:S(2)}) collective-permute-start(bf16[4,640,256]{2,1,0:T(8,128)(2,1)} %get-tuple-element.30), channel_id=1, source_target_pairs={{0,8},{1,9},{2,10},{3,11},{4,12},{5,13},{6,14},{7,15},{8,0},{9,1},... | collective-permute-start | bytes 3932168 | tf_op jit(solution)/shard_map/ppermute | solution.py:38
  268.9 21.8 %collective-permute-start.33 = (bf16[640,256]{1,0:T(8,128)(2,1)}, bf16[640,256]{1,0:T(8,128)(2,1)S(1)}, u32[]{:S(2)}, u32[]{:S(2)}) collective-permute-start(bf16[640,256]{1,0:T(8,128)(2,1)} %get-tuple-element.32), channel_id=1, source_target_pairs={{0,6},{1,7},{2,0},{3,1},{4,2},{5,3},{6,4},{7,5},{8,14},{9,15},{10,... | collective-permute-start | bytes 983048 | tf_op jit(solution)/shard_map/ppermute | solution.py:38
  272.5 18.2 %collective-permute-start.32 = (bf16[640,256]{1,0:T(8,128)(2,1)}, bf16[640,256]{1,0:T(8,128)(2,1)}, u32[]{:S(2)}, u32[]{:S(2)}) collective-permute-start(bf16[640,256]{1,0:T(8,128)(2,1)} %get-tuple-element.33), channel_id=1, source_target_pairs={{0,4},{1,5},{2,6},{3,7},{4,0},{5,1},{6,2},{7,3},{8,12},{9,13},{10,... | collective-permute-start | bytes 983048 | tf_op jit(solution)/shard_map/ppermute | solution.py:38
  272.5 25.2 %collective-permute-start.31 = (bf16[640,256]{1,0:T(8,128)(2,1)}, bf16[640,256]{1,0:T(8,128)(2,1)}, u32[]{:S(2)}, u32[]{:S(2)}) collective-permute-start(bf16[640,256]{1,0:T(8,128)(2,1)} %get-tuple-element.31), channel_id=1, source_target_pairs={{0,2},{1,3},{2,4},{3,5},{4,6},{5,7},{6,0},{7,1},{8,10},{9,11},{10,... | collective-permute-start | bytes 983048 | tf_op jit(solution)/shard_map/ppermute | solution.py:38
  273.4 26.2 %collective-permute-start.25 = (bf16[640,128]{1,0:T(8,128)(2,1)S(1)}, bf16[640,128]{1,0:T(8,128)(2,1)S(1)}, u32[]{:S(2)}, u32[]{:S(2)}) collective-permute-start(bf16[640,128]{1,0:T(8,128)(2,1)S(1)} %constant_dynamic-slice_fusion.1), channel_id=1, source_target_pairs={{0,1},{1,0},{2,3},{3,2},{4,5},{5,4},{6,7},{7,6},{8,9},{9,8},{10,11... | collective-permute-start | bytes 491528 | tf_op jit(solution)/shard_map/ppermute | solution.py:38
  299.2 8.5 %collective-permute-start.34 = (bf16[640,128]{1,0:T(8,128)(2,1)S(1)}, bf16[640,128]{1,0:T(8,128)(2,1)S(1)}, u32[]{:S(2)}, u32[]{:S(2)}) collective-permute-start(bf16[640,128]{1,0:T(8,128)(2,1)S(1)} %constant_dynamic-slice_fusion), channel_id=1, source_target_pairs={{0,1},{1,0},{2,3},{3,2},{4,5},{5,4},{6,7},{7,6},{8,9},{9,8},{10,11... | collective-permute-start | bytes 491528 | tf_op jit(solution)/shard_map/ppermute | solution.py:38
  300.6 8.9 %collective-permute-start.20 = (bf16[640,128]{1,0:T(8,128)(2,1)S(1)}, bf16[640,128]{1,0:T(8,128)(2,1)S(1)}, u32[]{:S(2)}, u32[]{:S(2)}) collective-permute-start(bf16[640,128]{1,0:T(8,128)(2,1)S(1)} %dynamic-slice_bitcast_fusion.1), channel_id=1, source_target_pairs={{0,1},{1,0},{2,3},{3,2},{4,5},{5,4},{6,7},{7,6},{8,9},{9,8},{10,11... | collective-permute-start | bytes 491528 | tf_op jit(solution)/shard_map/ppermute | solution.py:38
  308.7 6.9 %collective-permute-start.29 = (bf16[640,128]{1,0:T(8,128)(2,1)S(1)}, bf16[640,128]{1,0:T(8,128)(2,1)S(1)}, u32[]{:S(2)}, u32[]{:S(2)}) collective-permute-start(bf16[640,128]{1,0:T(8,128)(2,1)S(1)} %dynamic-slice_bitcast_fusion), channel_id=1, source_target_pairs={{0,1},{1,0},{2,3},{3,2},{4,5},{5,4},{6,7},{7,6},{8,9},{9,8},{10,11... | collective-permute-start | bytes 491528 | tf_op jit(solution)/shard_map/ppermute | solution.py:38
  (32 other events, 85.5 us)
Sparse Core Ops, SparseCore 0:
  9.7 38.4 all-gather.4
  104.3 32.4 all-gather.6
  220.7 32.1 reduce-scatter.2
  266.5 35.6 reduce-scatter.4

commit v5 on v4

--- a/solution.py
+++ b/solution.py
@@ -330,18 +330,18 @@
     hidden_own = hidden_last(where, firsts[0], normed, opp0 + opp1, (hidden_sib, low_b, high_b))
     ws_b = (st_b, low_b, high_b, *both_ways(low_b[0], high_b[1]))
 
-    pieces, parts, sums, reduced = [], [], [], []
+    pieces, parts, sums, near = [], [], [], []
     places = jnp.arange(4, dtype=jnp.int32)
     add = lambda a, b: (a.astype(jnp.float32) + b.astype(jnp.float32)).astype(jnp.bfloat16)
     for j in range(CHUNKS):
-        direct = j % 2 == 1
+        direct = j in (0, 3)
         part, part_sib = partial_of(
             (places - x) % 4 if direct else places,
             hidden_own,
             hidden_sib,
             ws_a if j < 2 else ws_b,
             j % 2,
-            parts[-1:] + (sums + reduced if j == 2 else []),
+            parts[-1:] + ([], [], sums[1:] + near, [])[j],
         )
         parts.append(part_sib)
         part_sib = send(part_sib, core=1)
@@ -349,16 +349,20 @@
             terms = [add(part[d], part_sib[d]) for d in range(4)]
             sums.append(terms[1])
             terms = terms[:1] + [send(terms[d], x=d) for d in (1, 2, 3)]
+            near = terms[3:]
             rows = sum(v.astype(jnp.float32) for v in terms).astype(jnp.bfloat16)
-            reduced.append(rows)
         else:
             both = add(part, part_sib)
             sums.append(both)
             rows = lax.psum_scatter(both, "x", scatter_dimension=0, tiled=True)[0]
-        keep = lax.dynamic_slice_in_dim(rows, yhi * 128, 128, 1)
-        give = lax.dynamic_slice_in_dim(rows, (1 - yhi) * 128, 128, 1)
-        pieces.append(add(keep, send(give, yhi=1)))
-    decoded = jnp.concatenate(pieces, axis=1).reshape(2, 320, 512)
+        pieces.append(rows)
+    halves = []
+    for pair in (pieces[:2], pieces[2:]):
+        keep = [lax.dynamic_slice_in_dim(v, yhi * 128, 128, 1) for v in pair]
+        give = jnp.stack([lax.dynamic_slice_in_dim(v, (1 - yhi) * 128, 128, 1) for v in pair])
+        got = send(give, yhi=1)
+        halves += [add(k, got[n]) for n, k in enumerate(keep)]
+    decoded = jnp.concatenate(halves, axis=1).reshape(2, 320, 512)
     return (up_updated, down_updated, decoded)
 
 

time: 326 us -> 336 us (1.031)
  waiting for transfers between devices: 137 us -> 149 us
    ppermute x35 -> x33, waiting for transfers between devices: 127 us -> 139 us  [send(): return lax.ppermute(v, AXES, shifted(**steps))]
    unnamed x81 -> x79, local copies, waits for them, and re-layouts: 18.1 us -> 15.9 us
    ppermute x35 -> x33, starting transfers between devices: 44 us -> 43.7 us  [send(): return lax.ppermute(v, AXES, shifted(**steps))]
  transfers between devices with their start and end apart: 40 -> 38, of which waited for: 15 -> 18; matrix products, arithmetic and copies ran while one was open for 8% -> 8% of each run, Pallas kernels for 19% -> 16%
where the time goes in v5:
time: 336 us; the launch traced here: 334 us
  waiting for transfers between devices  149 us (44%)
  Pallas kernels  75.6 us (22%)
  starting transfers between devices  50.8 us (15%)
  local copies, waits for them, and re-layouts  28.5 us (8%)
  other arithmetic  15.9 us (5%)
  between operations  14.2 us (4%)
    ppermute x33, waiting for transfers between devices, send(): return lax.ppermute(v, AXES, shifted(**steps))  139 us
    ppermute x33, starting transfers between devices, send(): return lax.ppermute(v, AXES, shifted(**steps))  43.7 us
    pallas_call x4, Pallas kernels, partial_of(): pl.pallas_call(partial_kernel, out_shape=(shape, shape), grid_spec=pltpu....  28 us
    unnamed x79, local copies, waits for them, and re-layouts  15.9 us
    pallas_call x2, Pallas kernels, hidden_first(): pl.pallas_call(first_kernel, out_shape=jax.ShapeDtypeStruct((640, 1024),...  13.7 us
    pallas_call x2, Pallas kernels, down_step(): pl.pallas_call(down_kernel, out_shape=(jax.ShapeDtypeStruct((128, D), jnp...  12.7 us
    all_to_all x1, waiting for transfers between devices, body(): lax.all_to_all(columns, ('core', 'x', 'yhi'), 0, 0, tiled=True)  9.98 us
    pallas_call x2, Pallas kernels, hidden_last(): pl.pallas_call(last_kernel, out_shape=jax.ShapeDtypeStruct((640, 1024), j...  9.38 us
  transfers between devices with their start and end apart: 38, of which 18 were waited for; matrix products, arithmetic and copies ran while one was open for 8% of the time, Pallas kernels for 16%

profile of v5, /device:TPU:0, one launch (start us, length us, event | category | flops | bytes accessed | tf_op | source)
XLA Modules:
  0.0 334.4 jit_solution(15692563380687236891)
XLA Ops:
  7.9 6.3 %adam_down.2 = (f32[128,4096]{1,0:T(8,128)}, bf16[2,128,1024]{2,1,0:T(8,128)(2,1)}) custom-call(f32[128,4096]{1,0:T(8,128)} %w_ref.5, bf16[128,4096]{1,0:T(8,128)(2,1)} %g_ref.5, f32[128,4096]{1,0:T(8,128)} %m_ref.5, f32[128,4096]{1,0:T(8,128)} %v_ref.5), custom_call_target="tpu_custom_call" | custom-call | flops 7864 | bytes 5242 | tf_op jit(solution)/shard_map/adam_down/pallas_call | solution.py:110
  15.9 7.8 %adam_up.1 = (f32[32,16384]{1,0:T(8,128)}, bf16[16,32,1024]{2,1,0:T(8,128)(2,1)}) custom-call(f32[32,16384]{1,0:T(8,128)} %w_ref.4, bf16[32,16384]{1,0:T(8,128)(2,1)} %g_ref.4, f32[32,16384]{1,0:T(8,128)} %m_ref.4, f32[32,16384]{1,0:T(8,128)} %v_ref.4, bf16[2,128,1024]{2,1,0:T(8,128)(2,1)} %get-tuple-element.17.dep_ref), custom_call_target="tpu_custom_call" | custom-call | flops 15728 | bytes 10485 | tf_op jit(solution)/shard_map/adam_up/pallas_call | solution.py:84
  23.7 4.3 %collective-permute-done.refs_0_ = bf16[2,128,1024]{2,1,0:T(8,128)(2,1)S(1)} collective-permute-done((bf16[2,128,1024]{2,1,0:T(8,128)(2,1)}, bf16[2,128,1024]{2,1,0:T(8,128)(2,1)S(1)}, u32[]{:S(2)}, u32[]{:S(2)}) %collective-permute-start) | collective-permute-done | bytes 524320 | tf_op jit(solution)/shard_map/ppermute | solution.py:38
  28.9 2.1 pad_maximum_fusion.refs_0_
  31.0 2.1 collective-permute-start.2
  33.1 2.1 collective-permute-start.3
  35.2 7.0 %all-to-all-start = ((bf16[16,32,1024]{2,1,0:T(8,128)(2,1)}), bf16[16,32,1024]{2,1,0:T(8,128)(2,1)S(1)}, u32[]{:S(2)}, u32[]{:S(2)}) async-start(bf16[16,32,1024]{2,1,0:T(8,128)(2,1)} %get-tuple-element.20.refs_1_), calls=%async_computation | async-start | bytes 2097152 | tf_op jit(solution)/shard_map/all_to_all | solution.py:304
  42.3 3.5 %collective-permute-start.1 = (bf16[2,320,512]{2,1,0:T(8,128)(2,1)}, bf16[2,320,512]{2,1,0:T(8,128)(2,1)}, u32[]{:S(2)}, u32[]{:S(2)}) collective-permute-start(bf16[2,320,512]{2,1,0:T(8,128)(2,1)} %param.11), channel_id=1, source_target_pairs={{0,1},{1,0},{2,3},{3,2},{4,5},{5,4},{6,7},{7,6},{8,9},{9,8},{10,11... | collective-permute-start | bytes 1966088 | tf_op jit(solution)/shard_map/ppermute | solution.py:38
  45.8 6.3 %adam_down.3 = (f32[128,4096]{1,0:T(8,128)}, bf16[2,128,1024]{2,1,0:T(8,128)(2,1)}) custom-call(f32[128,4096]{1,0:T(8,128)} %w_ref.5, bf16[128,4096]{1,0:T(8,128)(2,1)} %g_ref.5, f32[128,4096]{1,0:T(8,128)} %m_ref.5, f32[128,4096]{1,0:T(8,128)} %v_ref.5, f32[128,4096]{1,0:T(8,128)} %get-tuple-element.19.refs_0_, ...), custom_call_target="tpu_custom_call", output_to_operand_aliasing={{0}: (4, {})} | custom-call | flops 7864 | bytes 5242 | tf_op jit(solution)/shard_map/adam_down/pallas_call | solution.py:110
  52.1 10.0 %all-to-all-done = bf16[16,32,1024]{2,1,0:T(8,128)(2,1)S(1)} async-done(((bf16[16,32,1024]{2,1,0:T(8,128)(2,1)}), bf16[16,32,1024]{2,1,0:T(8,128)(2,1)S(1)}, u32[]{:S(2)}, u32[]{:S(2)}) %all-to-all-start) | async-done | bytes 1048608 | tf_op jit(solution)/shard_map/all_to_all | solution.py:304
  65.3 1.7 collective-permute-start.5
  69.1 3.7 %collective-permute-done.1.refs_0_ = bf16[2,320,512]{2,1,0:T(8,128)(2,1)} collective-permute-done((bf16[2,320,512]{2,1,0:T(8,128)(2,1)}, bf16[2,320,512]{2,1,0:T(8,128)(2,1)}, u32[]{:S(2)}, u32[]{:S(2)}) %collective-permute-start.1) | collective-permute-done | bytes 655392 | tf_op jit(solution)/shard_map/ppermute | solution.py:38
  72.8 2.0 collective-permute-start.8
  74.8 26.3 %collective-permute-done.7.refs_4_.refs_2_.refs_3_ = bf16[2,128,1024]{2,1,0:T(8,128)(2,1)S(1)} collective-permute-done((bf16[2,128,1024]{2,1,0:T(8,128)(2,1)S(1)}, bf16[2,128,1024]{2,1,0:T(8,128)(2,1)S(1)}, u32[]{:S(2)}, u32[]{:S(2)}) %collective-permute-start.7) | collective-permute-done | bytes 524320 | tf_op jit(solution)/shard_map/ppermute | solution.py:38
  105.7 1.8 collective-permute-start.10
  107.5 1.9 slice.114.refs_0_
  111.5 1.9 collective-permute-start.12
  114.2 26.7 %collective-permute-done.11.refs_2_ = bf16[256,1024]{1,0:T(8,128)(2,1)} collective-permute-done((bf16[256,1024]{1,0:T(8,128)(2,1)}, bf16[256,1024]{1,0:T(8,128)(2,1)}, u32[]{:S(2)}, u32[]{:S(2)}) %collective-permute-start.11) | collective-permute-done | bytes 524320 | tf_op jit(solution)/shard_map/ppermute | solution.py:38
  141.0 2.6 copy-done.20
  145.3 4.0 %norm.1.refs_0_.refs_1_.refs_2_.refs_3_.refs_4_.refs_5_ = bf16[8,640,512]{2,1,0:T(8,128)(2,1)} custom-call(bf16[4,640,512]{2,1,0:T(8,128)(2,1)S(1)} %bitcast.63, bf16[4,640,512]{2,1,0:T(8,128)(2,1)S(1)} %bitcast.64, f32[8,512]{1,0:T(8,128)S(1)} %pad_maximum_fusion.5.g_ref, bf16[512,1024]{1,0:T(8,128)(2,1)S(1)} %collective-permute-done.9.refs_0_.refs_9_.refs_1_, ...), custom_call_target="tpu_custom_call" | custom-call | flops 20971 | bytes 10485 | tf_op jit(solution)/shard_map/norm/pallas_call | solution.py:145
  151.3 2.5 collective-permute-start.18
  154.6 1.9 slice.117
  156.5 3.2 collective-permute-start.15
  164.6 7.0 %hidden_first.2.refs_6_.acc_ref = f32[640,1024]{1,0:T(8,128)S(1)} custom-call(s32[16]{0:T(128)S(1)} %fusion.19.s_ref, bf16[8,640,512]{2,1,0:T(8,128)(2,1)} %norm.1.refs_0_.refs_1_.refs_2_.refs_3_.refs_4_.refs_5_, bf16[8,640,512]{2,1,0:T(8,128)(2,1)} %norm.1.refs_0_.refs_1_.refs_2_.refs_3_.refs_4_.refs_5_, ...), custom_call_target="tpu_custom_call" | custom-call | flops 4026531 | bytes 14680 | tf_op jit(solution)/shard_map/hidden_first/pallas_call | solution.py:193
  171.7 6.7 %hidden_first.3.acc_ref = f32[640,1024]{1,0:T(8,128)S(1)} custom-call(s32[16]{0:T(128)S(1)} %fusion.19.s_ref, bf16[8,640,512]{2,1,0:T(8,128)(2,1)} %collective-permute-done.16.refs_0_.refs_1_.refs_2_.refs_3_.refs_4_.refs_5_, bf16[8,640,512]{2,1,0:T(8,128)(2,1)} %collective-permute-done.16.refs_0_.refs_1_.refs_2_.refs_3_.refs_4_.refs_5_, ...), custom_call_target="tpu_custom_call" | custom-call | flops 4026531 | bytes 14680 | tf_op jit(solution)/shard_map/hidden_first/pallas_call | solution.py:193
  178.4 10.5 %collective-permute-done.14.refs_4_ = bf16[256,1024]{1,0:T(8,128)(2,1)} collective-permute-done((bf16[256,1024]{1,0:T(8,128)(2,1)}, bf16[256,1024]{1,0:T(8,128)(2,1)}, u32[]{:S(2)}, u32[]{:S(2)}) %collective-permute-start.14) | collective-permute-done | bytes 524320 | tf_op jit(solution)/shard_map/ppermute | solution.py:38
  188.9 4.7 %hidden_last.2.refs_6_.sib_ref = bf16[640,1024]{1,0:T(8,128)(2,1)S(1)} custom-call(s32[16]{0:T(128)S(1)} %fusion.19.s_ref, f32[640,1024]{1,0:T(8,128)S(1)} %hidden_first.3.acc_ref, bf16[8,640,512]{2,1,0:T(8,128)(2,1)} %collective-permute-done.16.refs_0_.refs_1_.refs_2_.refs_3_.refs_4_.refs_5_, ...), custom_call_target="tpu_custom_call" | custom-call | flops 1342177 | bytes 8388 | tf_op jit(solution)/shard_map/hidden_last/pallas_call | solution.py:211
  193.6 4.7 %hidden_last.3.own_ref = bf16[640,1024]{1,0:T(8,128)(2,1)S(1)} custom-call(s32[16]{0:T(128)S(1)} %fusion.19.s_ref, f32[640,1024]{1,0:T(8,128)S(1)} %hidden_first.2.refs_6_.acc_ref, bf16[8,640,512]{2,1,0:T(8,128)(2,1)} %norm.1.refs_0_.refs_1_.refs_2_.refs_3_.refs_4_.refs_5_, bf16[8,640,512]{2,1,0:T(8,128)(2,1)} %norm.1.refs_0_.refs_1_.refs_2_.refs_3_.refs_4_.refs_5_, ...), custom_call_target="tpu_custom_call" | custom-call | flops 1342177 | bytes 8388 | tf_op jit(solution)/shard_map/hidden_last/pallas_call | solution.py:211
  199.3 6.9 %partial.4 = (bf16[4,640,256]{2,1,0:T(8,128)(2,1)}, bf16[4,640,256]{2,1,0:T(8,128)(2,1)}) custom-call(s32[4]{0:T(128)} %and_select_fusion.s_ref, bf16[640,1024]{1,0:T(8,128)(2,1)} %copy-done.1, bf16[640,1024]{1,0:T(8,128)(2,1)} %copy-done, bf16[2,2,128,1024]{3,2,1,0:T(8,128)(2,1)} %pad_maximum_fusion.refs_0_, bf16[2,2,128,1024]{3,2,1,0:T(8,128)(2,1)} %copy-done.22, ...), custom_call_target="tpu_custom_call" | custom-call | flops 2684354 | bytes 8388 | tf_op jit(solution)/shard_map/partial/pallas_call | solution.py:251
  206.8 7.1 %partial.5 = (bf16[4,640,256]{2,1,0:T(8,128)(2,1)}, bf16[4,640,256]{2,1,0:T(8,128)(2,1)}) custom-call(s32[4]{0:T(128)} %iota.8.s_ref, bf16[640,1024]{1,0:T(8,128)(2,1)} %copy-done.1, bf16[640,1024]{1,0:T(8,128)(2,1)} %copy-done, bf16[2,2,128,1024]{3,2,1,0:T(8,128)(2,1)} %pad_maximum_fusion.refs_0_, bf16[2,2,128,1024]{3,2,1,0:T(8,128)(2,1)} %copy-done.22, ...), custom_call_target="tpu_custom_call" | custom-call | flops 2684354 | bytes 8388 | tf_op jit(solution)/shard_map/partial/pallas_call | solution.py:251
  214.4 3.7 %collective-permute-done.23 = bf16[4,640,256]{2,1,0:T(8,128)(2,1)S(1)} collective-permute-done((bf16[4,640,256]{2,1,0:T(8,128)(2,1)}, bf16[4,640,256]{2,1,0:T(8,128)(2,1)S(1)}, u32[]{:S(2)}, u32[]{:S(2)}) %collective-permute-start.23) | collective-permute-done | bytes 1310752 | tf_op jit(solution)/shard_map/ppermute | solution.py:38
  218.1 2.7 add_convert_fusion.1.refs_6_
  224.2 2.3 collective-permute-start.26
  229.6 7.7 %collective-permute-done.25.refs_3_ = bf16[2,128,1024]{2,1,0:T(8,128)(2,1)S(1)} collective-permute-done((bf16[2,128,1024]{2,1,0:T(8,128)(2,1)S(1)}, bf16[2,128,1024]{2,1,0:T(8,128)(2,1)S(1)}, u32[]{:S(2)}, u32[]{:S(2)}) %collective-permute-start.25) | collective-permute-done | bytes 524320 | tf_op jit(solution)/shard_map/ppermute | solution.py:38
  237.9 7.1 %collective-permute-done.22.refs_7_ = bf16[640,256]{1,0:T(8,128)(2,1)S(1)} collective-permute-done((bf16[640,256]{1,0:T(8,128)(2,1)S(1)}, bf16[640,256]{1,0:T(8,128)(2,1)S(1)}, u32[]{:S(2)}, u32[]{:S(2)}) %collective-permute-start.22) | collective-permute-done | bytes 327712 | tf_op jit(solution)/shard_map/ppermute | solution.py:38
  245.8 7.0 %partial.6 = (bf16[4,640,256]{2,1,0:T(8,128)(2,1)}, bf16[4,640,256]{2,1,0:T(8,128)(2,1)}) custom-call(s32[4]{0:T(128)} %iota.9.s_ref, bf16[640,1024]{1,0:T(8,128)(2,1)} %copy-done.1, bf16[640,1024]{1,0:T(8,128)(2,1)} %copy-done, bf16[2,2,128,1024]{3,2,1,0:T(8,128)(2,1)} %after.11.refs_0_, bf16[2,2,128,1024]{3,2,1,0:T(8,128)(2,1)} %collective-permute-done.17.refs_7_.refs_1_, ...), custom_call_target="tpu_custom_call" | custom-call | flops 2684354 | bytes 8388 | tf_op jit(solution)/shard_map/partial/pallas_call | solution.py:251
  252.8 3.2 collective-permute-done.27
  256.0 2.8 add_convert_fusion
  258.9 7.0 %partial.7 = (bf16[4,640,256]{2,1,0:T(8,128)(2,1)}, bf16[4,640,256]{2,1,0:T(8,128)(2,1)}) custom-call(s32[4]{0:T(128)} %and_select_fusion.s_ref, bf16[640,1024]{1,0:T(8,128)(2,1)} %copy-done.1, bf16[640,1024]{1,0:T(8,128)(2,1)} %copy-done, bf16[2,2,128,1024]{3,2,1,0:T(8,128)(2,1)} %after.11.refs_0_, ...), custom_call_target="tpu_custom_call" | custom-call | flops 2684354 | bytes 8388 | tf_op jit(solution)/shard_map/partial/pallas_call | solution.py:251
  266.8 2.2 collective-permute-start.20
  270.5 2.2 collective-permute-start.31
  273.7 9.8 %collective-permute-done.21 = bf16[640,256]{1,0:T(8,128)(2,1)S(1)} collective-permute-done((bf16[640,256]{1,0:T(8,128)(2,1)S(1)}, bf16[640,256]{1,0:T(8,128)(2,1)S(1)}, u32[]{:S(2)}, u32[]{:S(2)}) %collective-permute-start.21) | collective-permute-done | bytes 327712 | tf_op jit(solution)/shard_map/ppermute | solution.py:38
  283.6 8.5 %collective-permute-done.20 = bf16[640,256]{1,0:T(8,128)(2,1)S(1)} collective-permute-done((bf16[640,256]{1,0:T(8,128)(2,1)S(1)}, bf16[640,256]{1,0:T(8,128)(2,1)S(1)}, u32[]{:S(2)}, u32[]{:S(2)}) %collective-permute-start.20) | collective-permute-done | bytes 327712 | tf_op jit(solution)/shard_map/ppermute | solution.py:38
  293.5 6.4 %collective-permute-done.30 = bf16[640,256]{1,0:T(8,128)(2,1)S(1)} collective-permute-done((bf16[640,256]{1,0:T(8,128)(2,1)S(1)}, bf16[640,256]{1,0:T(8,128)(2,1)S(1)}, u32[]{:S(2)}, u32[]{:S(2)}) %collective-permute-start.30) | collective-permute-done | bytes 327712 | tf_op jit(solution)/shard_map/ppermute | solution.py:38
  299.9 6.5 %collective-permute-done.29 = bf16[640,256]{1,0:T(8,128)(2,1)S(1)} collective-permute-done((bf16[640,256]{1,0:T(8,128)(2,1)S(1)}, bf16[640,256]{1,0:T(8,128)(2,1)S(1)}, u32[]{:S(2)}, u32[]{:S(2)}) %collective-permute-start.29) | collective-permute-done | bytes 327712 | tf_op jit(solution)/shard_map/ppermute | solution.py:38
  308.7 2.0 collective-permute-start.24
  313.5 7.4 %collective-permute-done.24 = bf16[2,640,128]{2,1,0:T(8,128)(2,1)S(1)} collective-permute-done((bf16[2,640,128]{2,1,0:T(8,128)(2,1)S(1)}, bf16[2,640,128]{2,1,0:T(8,128)(2,1)S(1)}, u32[]{:S(2)}, u32[]{:S(2)}) %collective-permute-start.24) | collective-permute-done | bytes 327712 | tf_op jit(solution)/shard_map/ppermute | solution.py:38
  321.0 5.9 %collective-permute-done.32 = bf16[2,640,128]{2,1,0:T(8,128)(2,1)S(1)} collective-permute-done((bf16[2,640,128]{2,1,0:T(8,128)(2,1)S(1)}, bf16[2,640,128]{2,1,0:T(8,128)(2,1)S(1)}, u32[]{:S(2)}, u32[]{:S(2)}) %collective-permute-start.32) | collective-permute-done | bytes 327712 | tf_op jit(solution)/shard_map/ppermute | solution.py:38
  (163 shorter events, 45.9 us)
Async XLA Ops:
  7.2 133.8 %all-gather.5.cloned.1.call-start = ((), (), s32[]{:S(2)}) async-start(), calls=%async_computation.5 | async-start | bytes 3276800 | tf_op jit(solution)/shard_map/all_gather | solution.py:293
  14.2 13.8 %collective-permute-start = (bf16[2,128,1024]{2,1,0:T(8,128)(2,1)}, bf16[2,128,1024]{2,1,0:T(8,128)(2,1)S(1)}, u32[]{:S(2)}, u32[]{:S(2)}) collective-permute-start(bf16[2,128,1024]{2,1,0:T(8,128)(2,1)} %get-tuple-element.17.dep_ref), channel_id=1, source_target_pairs={{0,64},{1,65},{2,66},{3,67},{4,68},{5,69},{6,70},{7,71},{8,72},{9,... | collective-permute-start | bytes 1572872 | tf_op jit(solution)/shard_map/ppermute | solution.py:38
  31.0 31.1 %collective-permute-start.2 = (bf16[2,2,128,1024]{3,2,1,0:T(8,128)(2,1)}, bf16[2,2,128,1024]{3,2,1,0:T(8,128)(2,1)S(1)}, u32[]{:S(2)}, u32[]{:S(2)}) collective-permute-start(bf16[2,2,128,1024]{3,2,1,0:T(8,128)(2,1)} %pad_maximum_fusion.refs_0_), channel_id=1, source_target_pairs={{0,16},{1,17},{2,18},{3,19},{4,20},{5,21},{6,22},{7,23},{8,24},{9,... | collective-permute-start | bytes 3145736 | tf_op jit(solution)/shard_map/ppermute | solution.py:38
  33.1 29.0 %collective-permute-start.3 = (bf16[2,2,128,1024]{3,2,1,0:T(8,128)(2,1)}, bf16[2,2,128,1024]{3,2,1,0:T(8,128)(2,1)S(1)}, u32[]{:S(2)}, u32[]{:S(2)}) collective-permute-start(bf16[2,2,128,1024]{3,2,1,0:T(8,128)(2,1)} %pad_maximum_fusion.refs_0_), channel_id=1, source_target_pairs={{0,48},{1,49},{2,50},{3,51},{4,52},{5,53},{6,54},{7,55},{8,56},{9,... | collective-permute-start | bytes 3145736 | tf_op jit(solution)/shard_map/ppermute | solution.py:38
  35.2 26.9 %all-to-all-start = ((bf16[16,32,1024]{2,1,0:T(8,128)(2,1)}), bf16[16,32,1024]{2,1,0:T(8,128)(2,1)S(1)}, u32[]{:S(2)}, u32[]{:S(2)}) async-start(bf16[16,32,1024]{2,1,0:T(8,128)(2,1)} %get-tuple-element.20.refs_1_), calls=%async_computation | async-start | bytes 2097152 | tf_op jit(solution)/shard_map/all_to_all | solution.py:304
  42.3 98.7 %all-gather.7.cloned.1.call-start = ((), (), s32[]{:S(2)}) async-start(), calls=%async_computation.6 | async-start | bytes 3276800 | tf_op jit(solution)/shard_map/all_gather | solution.py:311
  42.3 30.4 %collective-permute-start.1 = (bf16[2,320,512]{2,1,0:T(8,128)(2,1)}, bf16[2,320,512]{2,1,0:T(8,128)(2,1)}, u32[]{:S(2)}, u32[]{:S(2)}) collective-permute-start(bf16[2,320,512]{2,1,0:T(8,128)(2,1)} %param.11), channel_id=1, source_target_pairs={{0,1},{1,0},{2,3},{3,2},{4,5},{5,4},{6,7},{7,6},{8,9},{9,8},{10,11... | collective-permute-start | bytes 1966088 | tf_op jit(solution)/shard_map/ppermute | solution.py:38
  63.8 37.4 %collective-permute-start.4 = (bf16[512,1024]{1,0:T(8,128)(2,1)}, bf16[512,1024]{1,0:T(8,128)(2,1)S(1)}, u32[]{:S(2)}, u32[]{:S(2)}) collective-permute-start(bf16[512,1024]{1,0:T(8,128)(2,1)} %after.7.refs_6_), channel_id=1, source_target_pairs={{0,16},{1,17},{2,18},{3,19},{4,20},{5,21},{6,22},{7,23},{8,24},{9,... | collective-permute-start | bytes 3145736 | tf_op jit(solution)/shard_map/ppermute | solution.py:38
  65.3 35.9 %collective-permute-start.5 = (bf16[512,1024]{1,0:T(8,128)(2,1)}, bf16[512,1024]{1,0:T(8,128)(2,1)S(1)}, u32[]{:S(2)}, u32[]{:S(2)}) collective-permute-start(bf16[512,1024]{1,0:T(8,128)(2,1)} %after.7.refs_6_), channel_id=1, source_target_pairs={{0,48},{1,49},{2,50},{3,51},{4,52},{5,53},{6,54},{7,55},{8,56},{9,... | collective-permute-start | bytes 3145736 | tf_op jit(solution)/shard_map/ppermute | solution.py:38
  67.0 35.2 %collective-permute-start.6 = (bf16[512,1024]{1,0:T(8,128)(2,1)}, bf16[512,1024]{1,0:T(8,128)(2,1)S(1)}, u32[]{:S(2)}, u32[]{:S(2)}) collective-permute-start(bf16[512,1024]{1,0:T(8,128)(2,1)} %after.7.refs_6_), channel_id=1, source_target_pairs={{0,64},{1,65},{2,66},{3,67},{4,68},{5,69},{6,70},{7,71},{8,72},{9,... | collective-permute-start | bytes 3145736 | tf_op jit(solution)/shard_map/ppermute | solution.py:38
  68.7 32.5 %collective-permute-start.7 = (bf16[2,128,1024]{2,1,0:T(8,128)(2,1)S(1)}, bf16[2,128,1024]{2,1,0:T(8,128)(2,1)S(1)}, u32[]{:S(2)}, u32[]{:S(2)}) collective-permute-start(bf16[2,128,1024]{2,1,0:T(8,128)(2,1)S(1)} %slice_bitcast_fusion.3), channel_id=1, source_target_pairs={{0,16},{1,17},{2,18},{3,19},{4,20},{5,21},{6,22},{7,23},{8,24},{9,... | collective-permute-start | bytes 1572872 | tf_op jit(solution)/shard_map/ppermute | solution.py:38
  72.8 28.4 %collective-permute-start.8 = (bf16[2,128,1024]{2,1,0:T(8,128)(2,1)S(1)}, bf16[2,128,1024]{2,1,0:T(8,128)(2,1)S(1)}, u32[]{:S(2)}, u32[]{:S(2)}) collective-permute-start(bf16[2,128,1024]{2,1,0:T(8,128)(2,1)S(1)} %slice_bitcast_fusion.2), channel_id=1, source_target_pairs={{0,48},{1,49},{2,50},{3,51},{4,52},{5,53},{6,54},{7,55},{8,56},{9,... | collective-permute-start | bytes 1572872 | tf_op jit(solution)/shard_map/ppermute | solution.py:38
  104.2 203.4 %reduce-scatter.3.cloned.1.call-start = ((), (), s32[]{:S(2)}) async-start(), calls=%async_computation.3 | async-start | bytes 1638400 | tf_op jit(solution)/shard_map/reduce_scatter | solution.py:357
  104.2 36.6 %collective-permute-start.9 = (bf16[512,1024]{1,0:T(8,128)(2,1)}, bf16[512,1024]{1,0:T(8,128)(2,1)S(1)}, u32[]{:S(2)}, u32[]{:S(2)}) collective-permute-start(bf16[512,1024]{1,0:T(8,128)(2,1)} %copy-done.2), channel_id=1, source_target_pairs={{0,16},{1,17},{2,18},{3,19},{4,20},{5,21},{6,22},{7,23},{8,24},{9,... | collective-permute-start | bytes 3145736 | tf_op jit(solution)/shard_map/ppermute | solution.py:38
  105.7 35.2 %collective-permute-start.10 = (bf16[512,1024]{1,0:T(8,128)(2,1)}, bf16[512,1024]{1,0:T(8,128)(2,1)S(1)}, u32[]{:S(2)}, u32[]{:S(2)}) collective-permute-start(bf16[512,1024]{1,0:T(8,128)(2,1)} %copy-done.2), channel_id=1, source_target_pairs={{0,48},{1,49},{2,50},{3,51},{4,52},{5,53},{6,54},{7,55},{8,56},{9,... | collective-permute-start | bytes 3145736 | tf_op jit(solution)/shard_map/ppermute | solution.py:38
  109.4 31.4 %collective-permute-start.11 = (bf16[256,1024]{1,0:T(8,128)(2,1)}, bf16[256,1024]{1,0:T(8,128)(2,1)}, u32[]{:S(2)}, u32[]{:S(2)}) collective-permute-start(bf16[256,1024]{1,0:T(8,128)(2,1)} %after.9), channel_id=1, source_target_pairs={{0,16},{1,17},{2,18},{3,19},{4,20},{5,21},{6,22},{7,23},{8,24},{9,... | collective-permute-start | bytes 1572872 | tf_op jit(solution)/shard_map/ppermute | solution.py:38
  111.5 29.3 %collective-permute-start.12 = (bf16[256,1024]{1,0:T(8,128)(2,1)}, bf16[256,1024]{1,0:T(8,128)(2,1)S(1)}, u32[]{:S(2)}, u32[]{:S(2)}) collective-permute-start(bf16[256,1024]{1,0:T(8,128)(2,1)} %slice.115), channel_id=1, source_target_pairs={{0,48},{1,49},{2,50},{3,51},{4,52},{5,53},{6,54},{7,55},{8,56},{9,... | collective-permute-start | bytes 1572872 | tf_op jit(solution)/shard_map/ppermute | solution.py:38
  113.5 27.4 %collective-permute-start.13 = (bf16[2,128,1024]{2,1,0:T(8,128)(2,1)}, bf16[2,128,1024]{2,1,0:T(8,128)(2,1)S(1)}, u32[]{:S(2)}, u32[]{:S(2)}) collective-permute-start(bf16[2,128,1024]{2,1,0:T(8,128)(2,1)} %after.10), channel_id=1, source_target_pairs={{0,64},{1,65},{2,66},{3,67},{4,68},{5,69},{6,70},{7,71},{8,72},{9,... | collective-permute-start | bytes 1572872 | tf_op jit(solution)/shard_map/ppermute | solution.py:38
  140.9 8.5 %copy-start.18 = (bf16[256,1024]{1,0:T(8,128)(2,1)}, bf16[256,1024]{1,0:T(8,128)(2,1)S(1)}, u32[]{:S(2)}) copy-start(bf16[256,1024]{1,0:T(8,128)(2,1)S(1)} %collective-permute-done.12.refs_3_) | copy-start | bytes 1572868
  140.9 8.5 %copy-start.4 = (bf16[512,1024]{1,0:T(8,128)(2,1)}, bf16[512,1024]{1,0:T(8,128)(2,1)S(1)}, u32[]{:S(2)}) copy-start(bf16[512,1024]{1,0:T(8,128)(2,1)S(1)} %collective-permute-done.9.refs_0_.refs_9_.refs_1_) | copy-start | bytes 3145732
  140.9 8.4 %copy-start.15 = (bf16[512,1024]{1,0:T(8,128)(2,1)}, bf16[512,1024]{1,0:T(8,128)(2,1)S(1)}, u32[]{:S(2)}) copy-start(bf16[512,1024]{1,0:T(8,128)(2,1)S(1)} %collective-permute-done.10.refs_1_.refs_11_) | copy-start | bytes 3145732
  149.4 22.3 %collective-permute-start.16 = (bf16[8,640,512]{2,1,0:T(8,128)(2,1)}, bf16[8,640,512]{2,1,0:T(8,128)(2,1)}, u32[]{:S(2)}, u32[]{:S(2)}) collective-permute-start(bf16[8,640,512]{2,1,0:T(8,128)(2,1)} %norm.1.refs_0_.refs_1_.refs_2_.refs_3_.refs_4_.refs_5_), channel_id=1, source_target_pairs={{0,8},{1,9},{2,10},{3,11},{4,12},{5,13},{6,14},{7,15},{8,0},{9,1},... | collective-permute-start | bytes 15728648 | tf_op jit(solution)/shard_map/ppermute | solution.py:38
  150.5 10.4 %copy-start.3 = (bf16[512,1024]{1,0:T(8,128)(2,1)S(1)}, bf16[512,1024]{1,0:T(8,128)(2,1)}, u32[]{:S(2)}) copy-start(bf16[512,1024]{1,0:T(8,128)(2,1)} %copy-done.2) | copy-start | bytes 3145732
  150.5 10.4 %copy-start.7 = (bf16[512,1024]{1,0:T(8,128)(2,1)S(1)}, bf16[512,1024]{1,0:T(8,128)(2,1)}, u32[]{:S(2)}) copy-start(bf16[512,1024]{1,0:T(8,128)(2,1)} %after.7.refs_6_) | copy-start | bytes 3145732
  150.5 43.0 %collective-permute-start.17 = (bf16[2,2,128,1024]{3,2,1,0:T(8,128)(2,1)}, bf16[2,2,128,1024]{3,2,1,0:T(8,128)(2,1)}, u32[]{:S(2)}, u32[]{:S(2)}) collective-permute-start(bf16[2,2,128,1024]{3,2,1,0:T(8,128)(2,1)} %after.11.refs_0_), channel_id=1, source_target_pairs={{0,16},{1,17},{2,18},{3,19},{4,20},{5,21},{6,22},{7,23},{8,24},{9,... | collective-permute-start | bytes 3145736 | tf_op jit(solution)/shard_map/ppermute | solution.py:38
  151.3 42.3 %collective-permute-start.18 = (bf16[2,2,128,1024]{3,2,1,0:T(8,128)(2,1)}, bf16[2,2,128,1024]{3,2,1,0:T(8,128)(2,1)}, u32[]{:S(2)}, u32[]{:S(2)}) collective-permute-start(bf16[2,2,128,1024]{3,2,1,0:T(8,128)(2,1)} %after.11.refs_0_), channel_id=1, source_target_pairs={{0,48},{1,49},{2,50},{3,51},{4,52},{5,53},{6,54},{7,55},{8,56},{9,... | collective-permute-start | bytes 3145736 | tf_op jit(solution)/shard_map/ppermute | solution.py:38
  154.6 34.2 %collective-permute-start.14 = (bf16[256,1024]{1,0:T(8,128)(2,1)}, bf16[256,1024]{1,0:T(8,128)(2,1)}, u32[]{:S(2)}, u32[]{:S(2)}) collective-permute-start(bf16[256,1024]{1,0:T(8,128)(2,1)} %slice.116), channel_id=1, source_target_pairs={{0,16},{1,17},{2,18},{3,19},{4,20},{5,21},{6,22},{7,23},{8,24},{9,... | collective-permute-start | bytes 1572872 | tf_op jit(solution)/shard_map/ppermute | solution.py:38
  156.5 32.4 %collective-permute-start.15 = (bf16[256,1024]{1,0:T(8,128)(2,1)}, bf16[256,1024]{1,0:T(8,128)(2,1)}, u32[]{:S(2)}, u32[]{:S(2)}) collective-permute-start(bf16[256,1024]{1,0:T(8,128)(2,1)} %slice.117), channel_id=1, source_target_pairs={{0,48},{1,49},{2,50},{3,51},{4,52},{5,53},{6,54},{7,55},{8,56},{9,... | collective-permute-start | bytes 1572872 | tf_op jit(solution)/shard_map/ppermute | solution.py:38
  171.7 17.2 %copy-start.19 = (bf16[256,1024]{1,0:T(8,128)(2,1)S(1)}, bf16[256,1024]{1,0:T(8,128)(2,1)}, u32[]{:S(2)}) copy-start(bf16[256,1024]{1,0:T(8,128)(2,1)} %copy-done.18) | copy-start | bytes 1572868
  213.9 4.2 %collective-permute-start.23 = (bf16[4,640,256]{2,1,0:T(8,128)(2,1)}, bf16[4,640,256]{2,1,0:T(8,128)(2,1)S(1)}, u32[]{:S(2)}, u32[]{:S(2)}) collective-permute-start(bf16[4,640,256]{2,1,0:T(8,128)(2,1)} %get-tuple-element.26.refs_5_), channel_id=1, source_target_pairs={{0,8},{1,9},{2,10},{3,11},{4,12},{5,13},{6,14},{7,15},{8,0},{9,1},... | collective-permute-start | bytes 3932168 | tf_op jit(solution)/shard_map/ppermute | solution.py:38
  213.9 12.6 %collective-permute-start.19 = (bf16[4,640,256]{2,1,0:T(8,128)(2,1)S(1)}, bf16[4,640,256]{2,1,0:T(8,128)(2,1)}, u32[]{:S(2)}, u32[]{:S(2)}) collective-permute-start(bf16[4,640,256]{2,1,0:T(8,128)(2,1)S(1)} %copy-done.32), channel_id=1, source_target_pairs={{0,8},{1,9},{2,10},{3,11},{4,12},{5,13},{6,14},{7,15},{8,0},{9,1},... | collective-permute-start | bytes 3932168 | tf_op jit(solution)/shard_map/ppermute | solution.py:38
  220.8 89.9 %reduce-scatter.5.cloned.1.call-start = ((), (), s32[]{:S(2)}) async-start(), calls=%async_computation.4 | async-start | bytes 1638400 | tf_op jit(solution)/shard_map/reduce_scatter | solution.py:357
  222.1 15.2 %collective-permute-start.25 = (bf16[2,128,1024]{2,1,0:T(8,128)(2,1)S(1)}, bf16[2,128,1024]{2,1,0:T(8,128)(2,1)S(1)}, u32[]{:S(2)}, u32[]{:S(2)}) collective-permute-start(bf16[2,128,1024]{2,1,0:T(8,128)(2,1)S(1)} %slice_bitcast_fusion.1), channel_id=1, source_target_pairs={{0,16},{1,17},{2,18},{3,19},{4,20},{5,21},{6,22},{7,23},{8,24},{9,... | collective-permute-start | bytes 1572872 | tf_op jit(solution)/shard_map/ppermute | solution.py:38
  224.2 13.8 %collective-permute-start.26 = (bf16[2,128,1024]{2,1,0:T(8,128)(2,1)S(1)}, bf16[2,128,1024]{2,1,0:T(8,128)(2,1)S(1)}, u32[]{:S(2)}, u32[]{:S(2)}) collective-permute-start(bf16[2,128,1024]{2,1,0:T(8,128)(2,1)S(1)} %slice_bitcast_fusion), channel_id=1, source_target_pairs={{0,48},{1,49},{2,50},{3,51},{4,52},{5,53},{6,54},{7,55},{8,56},{9,... | collective-permute-start | bytes 1572872 | tf_op jit(solution)/shard_map/ppermute | solution.py:38
  228.0 17.0 %collective-permute-start.22 = (bf16[640,256]{1,0:T(8,128)(2,1)S(1)}, bf16[640,256]{1,0:T(8,128)(2,1)S(1)}, u32[]{:S(2)}, u32[]{:S(2)}) collective-permute-start(bf16[640,256]{1,0:T(8,128)(2,1)S(1)} %get-tuple-element.32), channel_id=1, source_target_pairs={{0,6},{1,7},{2,0},{3,1},{4,2},{5,3},{6,4},{7,5},{8,14},{9,15},{10,... | collective-permute-start | bytes 983048 | tf_op jit(solution)/shard_map/ppermute | solution.py:38
  237.3 8.4 %copy-start.29 = (bf16[2,128,1024]{2,1,0:T(8,128)(2,1)}, bf16[2,128,1024]{2,1,0:T(8,128)(2,1)S(1)}, u32[]{:S(2)}) copy-start(bf16[2,128,1024]{2,1,0:T(8,128)(2,1)S(1)} %collective-permute-done.25.refs_3_) | copy-start | bytes 1572868
  252.8 3.2 collective-permute-start.27
  265.8 3.2 collective-permute-start.28
  266.0 17.6 %collective-permute-start.21 = (bf16[640,256]{1,0:T(8,128)(2,1)S(1)}, bf16[640,256]{1,0:T(8,128)(2,1)S(1)}, u32[]{:S(2)}, u32[]{:S(2)}) collective-permute-start(bf16[640,256]{1,0:T(8,128)(2,1)S(1)} %get-tuple-element.33), channel_id=1, source_target_pairs={{0,4},{1,5},{2,6},{3,7},{4,0},{5,1},{6,2},{7,3},{8,12},{9,13},{10,... | collective-permute-start | bytes 983048 | tf_op jit(solution)/shard_map/ppermute | solution.py:38
  266.8 25.3 %collective-permute-start.20 = (bf16[640,256]{1,0:T(8,128)(2,1)S(1)}, bf16[640,256]{1,0:T(8,128)(2,1)S(1)}, u32[]{:S(2)}, u32[]{:S(2)}) collective-permute-start(bf16[640,256]{1,0:T(8,128)(2,1)S(1)} %get-tuple-element.31), channel_id=1, source_target_pairs={{0,2},{1,3},{2,4},{3,5},{4,6},{5,7},{6,0},{7,1},{8,10},{9,11},{10,... | collective-permute-start | bytes 983048 | tf_op jit(solution)/shard_map/ppermute | solution.py:38
  269.1 23.0 %copy-start.34 = (bf16[640,256]{1,0:T(8,128)(2,1)S(1)}, bf16[640,256]{1,0:T(8,128)(2,1)}, u32[]{:S(2)}) copy-start(bf16[640,256]{1,0:T(8,128)(2,1)} %copy-done.33) | copy-start | bytes 983044
  270.5 22.9 %collective-permute-start.31 = (bf16[640,256]{1,0:T(8,128)(2,1)S(1)}, bf16[640,256]{1,0:T(8,128)(2,1)S(1)}, u32[]{:S(2)}, u32[]{:S(2)}) collective-permute-start(bf16[640,256]{1,0:T(8,128)(2,1)S(1)} %get-tuple-element.35), channel_id=1, source_target_pairs={{0,6},{1,7},{2,0},{3,1},{4,2},{5,3},{6,4},{7,5},{8,14},{9,15},{10,... | collective-permute-start | bytes 983048 | tf_op jit(solution)/shard_map/ppermute | solution.py:38
  272.8 27.1 %collective-permute-start.30 = (bf16[640,256]{1,0:T(8,128)(2,1)S(1)}, bf16[640,256]{1,0:T(8,128)(2,1)S(1)}, u32[]{:S(2)}, u32[]{:S(2)}) collective-permute-start(bf16[640,256]{1,0:T(8,128)(2,1)S(1)} %get-tuple-element.36), channel_id=1, source_target_pairs={{0,4},{1,5},{2,6},{3,7},{4,0},{5,1},{6,2},{7,3},{8,12},{9,13},{10,... | collective-permute-start | bytes 983048 | tf_op jit(solution)/shard_map/ppermute | solution.py:38
  273.2 33.2 %collective-permute-start.29 = (bf16[640,256]{1,0:T(8,128)(2,1)S(1)}, bf16[640,256]{1,0:T(8,128)(2,1)S(1)}, u32[]{:S(2)}, u32[]{:S(2)}) collective-permute-start(bf16[640,256]{1,0:T(8,128)(2,1)S(1)} %get-tuple-element.34), channel_id=1, source_target_pairs={{0,2},{1,3},{2,4},{3,5},{4,6},{5,7},{6,0},{7,1},{8,10},{9,11},{10,... | collective-permute-start | bytes 983048 | tf_op jit(solution)/shard_map/ppermute | solution.py:38
  307.6 13.2 %copy-start.36 = (bf16[1,640,256]{2,1,0:T(8,128)(2,1)S(1)}, bf16[1,640,256]{2,1,0:T(8,128)(2,1)}, u32[]{:S(2)}) copy-start(bf16[1,640,256]{2,1,0:T(8,128)(2,1)} %reduce-scatter.3.cloned.1.call-done) | copy-start | bytes 983044
  308.7 12.2 %collective-permute-start.24 = (bf16[2,640,128]{2,1,0:T(8,128)(2,1)S(1)}, bf16[2,640,128]{2,1,0:T(8,128)(2,1)S(1)}, u32[]{:S(2)}, u32[]{:S(2)}) collective-permute-start(bf16[2,640,128]{2,1,0:T(8,128)(2,1)S(1)} %pad_maximum_fusion.3), channel_id=1, source_target_pairs={{0,1},{1,0},{2,3},{3,2},{4,5},{5,4},{6,7},{7,6},{8,9},{9,8},{10,11... | collective-permute-start | bytes 983048 | tf_op jit(solution)/shard_map/ppermute | solution.py:38
  310.8 16.1 %copy-start.37 = (bf16[1,640,256]{2,1,0:T(8,128)(2,1)S(1)}, bf16[1,640,256]{2,1,0:T(8,128)(2,1)}, u32[]{:S(2)}) copy-start(bf16[1,640,256]{2,1,0:T(8,128)(2,1)} %reduce-scatter.5.cloned.1.call-done) | copy-start | bytes 983044
  311.8 15.0 %collective-permute-start.32 = (bf16[2,640,128]{2,1,0:T(8,128)(2,1)S(1)}, bf16[2,640,128]{2,1,0:T(8,128)(2,1)S(1)}, u32[]{:S(2)}, u32[]{:S(2)}) collective-permute-start(bf16[2,640,128]{2,1,0:T(8,128)(2,1)S(1)} %pad_maximum_fusion.4), channel_id=1, source_target_pairs={{0,1},{1,0},{2,3},{3,2},{4,5},{5,4},{6,7},{7,6},{8,9},{9,8},{10,11... | collective-permute-start | bytes 983048 | tf_op jit(solution)/shard_map/ppermute | solution.py:38
  (29 other events, 88.0 us)
Sparse Core Ops, SparseCore 0:
  9.7 39.2 all-gather.4
  104.3 32.4 all-gather.6
  220.9 26.8 reduce-scatter.2
  259.0 42.1 reduce-scatter.4

commit v6 on v4

--- a/solution.py
+++ b/solution.py
@@ -313,7 +313,7 @@
     ylo_b = send(down_b, ylo=1)
     low1, high1 = both_ways(u1, u1)
     opp0 = both_ways(after(low0[:256], u1, *opp_a), high0[256:])
-    opp1 = both_ways(low1[:256], high1[256:])
+    opp1 = tuple(send(o, ylo=1) for o in opp0)
     st_b = after(jnp.stack([down_b, ylo_b]), low1)
     low_b, high_b = both_ways(st_b, st_b)
 
@@ -330,7 +330,7 @@
     hidden_own = hidden_last(where, firsts[0], normed, opp0 + opp1, (hidden_sib, low_b, high_b))
     ws_b = (st_b, low_b, high_b, *both_ways(low_b[0], high_b[1]))
 
-    pieces, parts, sums, reduced = [], [], [], []
+    pieces, parts, sums, reduced, gots = [], [], [], [], []
     places = jnp.arange(4, dtype=jnp.int32)
     add = lambda a, b: (a.astype(jnp.float32) + b.astype(jnp.float32)).astype(jnp.bfloat16)
     for j in range(CHUNKS):
@@ -341,7 +341,7 @@
             hidden_sib,
             ws_a if j < 2 else ws_b,
             j % 2,
-            parts[-1:] + (sums + reduced if j == 2 else []),
+            parts[-1:] + ([], [], sums + reduced, gots[:2])[j],
         )
         parts.append(part_sib)
         part_sib = send(part_sib, core=1)
@@ -357,7 +357,8 @@
             rows = lax.psum_scatter(both, "x", scatter_dimension=0, tiled=True)[0]
         keep = lax.dynamic_slice_in_dim(rows, yhi * 128, 128, 1)
         give = lax.dynamic_slice_in_dim(rows, (1 - yhi) * 128, 128, 1)
-        pieces.append(add(keep, send(give, yhi=1)))
+        gots.append(send(give, yhi=1))
+        pieces.append(add(keep, gots[-1]))
     decoded = jnp.concatenate(pieces, axis=1).reshape(2, 320, 512)
     return (up_updated, down_updated, decoded)
 

time: 326 us -> 317 us (0.972)
  waiting for transfers between devices: 137 us -> 129 us
    ppermute x35, waiting for transfers between devices: 127 us -> 118 us  [send(): return lax.ppermute(v, AXES, shifted(**steps))]
    unnamed x81 -> x83, local copies, waits for them, and re-layouts: 18.1 us -> 18.7 us
  transfers between devices with their start and end apart: 40 -> 40, of which waited for: 15 -> 17; matrix products, arithmetic and copies ran while one was open for 8% -> 8% of each run, Pallas kernels for 19% -> 19%
where the time goes in v6:
time: 317 us; the launch traced here: 316 us
  waiting for transfers between devices  129 us (41%)
  Pallas kernels  75.4 us (24%)
  starting transfers between devices  52 us (16%)
  local copies, waits for them, and re-layouts  28.4 us (9%)
  other arithmetic  16.6 us (5%)
  between operations  14.2 us (4%)
    ppermute x35, waiting for transfers between devices, send(): return lax.ppermute(v, AXES, shifted(**steps))  118 us
    ppermute x35, starting transfers between devices, send(): return lax.ppermute(v, AXES, shifted(**steps))  44.8 us
    pallas_call x4, Pallas kernels, partial_of(): pl.pallas_call(partial_kernel, out_shape=(shape, shape), grid_spec=pltpu....  28.2 us
    unnamed x83, local copies, waits for them, and re-layouts  18.7 us
    pallas_call x2, Pallas kernels, hidden_first(): pl.pallas_call(first_kernel, out_shape=jax.ShapeDtypeStruct((640, 1024),...  13.4 us
    pallas_call x2, Pallas kernels, down_step(): pl.pallas_call(down_kernel, out_shape=(jax.ShapeDtypeStruct((128, D), jnp...  12.7 us
    all_to_all x1, waiting for transfers between devices, body(): lax.all_to_all(columns, ('core', 'x', 'yhi'), 0, 0, tiled=True)  9.97 us
    pallas_call x2, Pallas kernels, hidden_last(): pl.pallas_call(last_kernel, out_shape=jax.ShapeDtypeStruct((640, 1024), j...  9.32 us
  transfers between devices with their start and end apart: 40, of which 17 were waited for; matrix products, arithmetic and copies ran while one was open for 8% of the time, Pallas kernels for 19%

profile of v6, /device:TPU:0, one launch (start us, length us, event | category | flops | bytes accessed | tf_op | source)
XLA Modules:
  0.0 315.9 jit_solution(9933477412202677390)
XLA Ops:
  7.9 6.3 %adam_down.2 = (f32[128,4096]{1,0:T(8,128)}, bf16[2,128,1024]{2,1,0:T(8,128)(2,1)}) custom-call(f32[128,4096]{1,0:T(8,128)} %w_ref.5, bf16[128,4096]{1,0:T(8,128)(2,1)} %g_ref.5, f32[128,4096]{1,0:T(8,128)} %m_ref.5, f32[128,4096]{1,0:T(8,128)} %v_ref.5), custom_call_target="tpu_custom_call" | custom-call | flops 7864 | bytes 5242 | tf_op jit(solution)/shard_map/adam_down/pallas_call | solution.py:110
  14.2 1.7 collective-permute-start
  15.9 7.8 %adam_up.1 = (f32[32,16384]{1,0:T(8,128)}, bf16[16,32,1024]{2,1,0:T(8,128)(2,1)}) custom-call(f32[32,16384]{1,0:T(8,128)} %w_ref.4, bf16[32,16384]{1,0:T(8,128)(2,1)} %g_ref.4, f32[32,16384]{1,0:T(8,128)} %m_ref.4, f32[32,16384]{1,0:T(8,128)} %v_ref.4, bf16[2,128,1024]{2,1,0:T(8,128)(2,1)} %get-tuple-element.17.dep_ref), custom_call_target="tpu_custom_call" | custom-call | flops 15728 | bytes 10485 | tf_op jit(solution)/shard_map/adam_up/pallas_call | solution.py:84
  23.7 4.3 %collective-permute-done.refs_0_ = bf16[2,128,1024]{2,1,0:T(8,128)(2,1)S(1)} collective-permute-done((bf16[2,128,1024]{2,1,0:T(8,128)(2,1)}, bf16[2,128,1024]{2,1,0:T(8,128)(2,1)S(1)}, u32[]{:S(2)}, u32[]{:S(2)}) %collective-permute-start) | collective-permute-done | bytes 524320 | tf_op jit(solution)/shard_map/ppermute | solution.py:38
  28.9 2.1 pad_maximum_fusion.refs_0_
  31.0 2.1 collective-permute-start.2
  33.1 2.1 collective-permute-start.3
  35.2 7.0 %all-to-all-start = ((bf16[16,32,1024]{2,1,0:T(8,128)(2,1)}), bf16[16,32,1024]{2,1,0:T(8,128)(2,1)S(1)}, u32[]{:S(2)}, u32[]{:S(2)}) async-start(bf16[16,32,1024]{2,1,0:T(8,128)(2,1)} %get-tuple-element.20.refs_1_), calls=%async_computation | async-start | bytes 2097152 | tf_op jit(solution)/shard_map/all_to_all | solution.py:304
  42.3 3.5 %collective-permute-start.1 = (bf16[2,320,512]{2,1,0:T(8,128)(2,1)}, bf16[2,320,512]{2,1,0:T(8,128)(2,1)}, u32[]{:S(2)}, u32[]{:S(2)}) collective-permute-start(bf16[2,320,512]{2,1,0:T(8,128)(2,1)} %param.11), channel_id=1, source_target_pairs={{0,1},{1,0},{2,3},{3,2},{4,5},{5,4},{6,7},{7,6},{8,9},{9,8},{10,11... | collective-permute-start | bytes 1966088 | tf_op jit(solution)/shard_map/ppermute | solution.py:38
  45.8 6.3 %adam_down.3 = (f32[128,4096]{1,0:T(8,128)}, bf16[2,128,1024]{2,1,0:T(8,128)(2,1)}) custom-call(f32[128,4096]{1,0:T(8,128)} %w_ref.5, bf16[128,4096]{1,0:T(8,128)(2,1)} %g_ref.5, f32[128,4096]{1,0:T(8,128)} %m_ref.5, f32[128,4096]{1,0:T(8,128)} %v_ref.5, f32[128,4096]{1,0:T(8,128)} %get-tuple-element.19.refs_0_, ...), custom_call_target="tpu_custom_call", output_to_operand_aliasing={{0}: (4, {})} | custom-call | flops 7864 | bytes 5242 | tf_op jit(solution)/shard_map/adam_down/pallas_call | solution.py:110
  52.1 10.0 %all-to-all-done = bf16[16,32,1024]{2,1,0:T(8,128)(2,1)S(1)} async-done(((bf16[16,32,1024]{2,1,0:T(8,128)(2,1)}), bf16[16,32,1024]{2,1,0:T(8,128)(2,1)S(1)}, u32[]{:S(2)}, u32[]{:S(2)}) %all-to-all-start) | async-done | bytes 1048608 | tf_op jit(solution)/shard_map/all_to_all | solution.py:304
  65.3 1.7 collective-permute-start.5
  69.1 3.7 %collective-permute-done.1.refs_0_ = bf16[2,320,512]{2,1,0:T(8,128)(2,1)} collective-permute-done((bf16[2,320,512]{2,1,0:T(8,128)(2,1)}, bf16[2,320,512]{2,1,0:T(8,128)(2,1)}, u32[]{:S(2)}, u32[]{:S(2)}) %collective-permute-start.1) | collective-permute-done | bytes 655392 | tf_op jit(solution)/shard_map/ppermute | solution.py:38
  72.8 2.0 collective-permute-start.8
  74.8 26.3 %collective-permute-done.7.refs_4_.refs_2_.refs_3_ = bf16[2,128,1024]{2,1,0:T(8,128)(2,1)S(1)} collective-permute-done((bf16[2,128,1024]{2,1,0:T(8,128)(2,1)S(1)}, bf16[2,128,1024]{2,1,0:T(8,128)(2,1)S(1)}, u32[]{:S(2)}, u32[]{:S(2)}) %collective-permute-start.7) | collective-permute-done | bytes 524320 | tf_op jit(solution)/shard_map/ppermute | solution.py:38
  105.7 1.9 collective-permute-start.10
  107.5 1.9 slice.90.refs_0_
  111.6 1.9 collective-permute-start.12
  114.2 26.7 %collective-permute-done.11.refs_2_ = bf16[256,1024]{1,0:T(8,128)(2,1)} collective-permute-done((bf16[256,1024]{1,0:T(8,128)(2,1)}, bf16[256,1024]{1,0:T(8,128)(2,1)}, u32[]{:S(2)}, u32[]{:S(2)}) %collective-permute-start.11) | collective-permute-done | bytes 524320 | tf_op jit(solution)/shard_map/ppermute | solution.py:38
  141.0 2.6 copy-done.19
  143.6 1.7 copy-done.20
  145.3 4.1 %norm.1.refs_0_.refs_1_.refs_2_.refs_3_.refs_4_.refs_5_ = bf16[8,640,512]{2,1,0:T(8,128)(2,1)} custom-call(bf16[4,640,512]{2,1,0:T(8,128)(2,1)S(1)} %bitcast.55, bf16[4,640,512]{2,1,0:T(8,128)(2,1)S(1)} %bitcast.56, f32[8,512]{1,0:T(8,128)S(1)} %pad_maximum_fusion.3.g_ref, bf16[512,1024]{1,0:T(8,128)(2,1)S(1)} %collective-permute-done.9.refs_0_.refs_9_.refs_1_, ...), custom_call_target="tpu_custom_call" | custom-call | flops 20971 | bytes 10485 | tf_op jit(solution)/shard_map/norm/pallas_call | solution.py:145
  151.3 2.5 collective-permute-start.18
  160.2 6.7 %hidden_first.2.refs_6_.acc_ref = f32[640,1024]{1,0:T(8,128)S(1)} custom-call(s32[16]{0:T(128)S(1)} %fusion.17.s_ref, bf16[8,640,512]{2,1,0:T(8,128)(2,1)} %norm.1.refs_0_.refs_1_.refs_2_.refs_3_.refs_4_.refs_5_, bf16[8,640,512]{2,1,0:T(8,128)(2,1)} %norm.1.refs_0_.refs_1_.refs_2_.refs_3_.refs_4_.refs_5_, ...), custom_call_target="tpu_custom_call" | custom-call | flops 4026531 | bytes 14680 | tf_op jit(solution)/shard_map/hidden_first/pallas_call | solution.py:193
  167.0 6.7 %hidden_first.3.acc_ref = f32[640,1024]{1,0:T(8,128)S(1)} custom-call(s32[16]{0:T(128)S(1)} %fusion.17.s_ref, bf16[8,640,512]{2,1,0:T(8,128)(2,1)} %collective-permute-done.16.refs_0_.refs_1_.refs_2_.refs_3_.refs_4_.refs_5_, bf16[8,640,512]{2,1,0:T(8,128)(2,1)} %collective-permute-done.16.refs_0_.refs_1_.refs_2_.refs_3_.refs_4_.refs_5_, ...), custom_call_target="tpu_custom_call" | custom-call | flops 4026531 | bytes 14680 | tf_op jit(solution)/shard_map/hidden_first/pallas_call | solution.py:193
  173.7 5.4 %collective-permute-done.15.refs_5_ = bf16[256,1024]{1,0:T(8,128)(2,1)} collective-permute-done((bf16[256,1024]{1,0:T(8,128)(2,1)}, bf16[256,1024]{1,0:T(8,128)(2,1)}, u32[]{:S(2)}, u32[]{:S(2)}) %collective-permute-start.15) | collective-permute-done | bytes 524320 | tf_op jit(solution)/shard_map/ppermute | solution.py:38
  179.1 4.7 %hidden_last.2.refs_6_.sib_ref = bf16[640,1024]{1,0:T(8,128)(2,1)S(1)} custom-call(s32[16]{0:T(128)S(1)} %fusion.17.s_ref, f32[640,1024]{1,0:T(8,128)S(1)} %hidden_first.3.acc_ref, bf16[8,640,512]{2,1,0:T(8,128)(2,1)} %collective-permute-done.16.refs_0_.refs_1_.refs_2_.refs_3_.refs_4_.refs_5_, ...), custom_call_target="tpu_custom_call" | custom-call | flops 1342177 | bytes 8388 | tf_op jit(solution)/shard_map/hidden_last/pallas_call | solution.py:211
  183.8 4.7 %hidden_last.3.own_ref = bf16[640,1024]{1,0:T(8,128)(2,1)S(1)} custom-call(s32[16]{0:T(128)S(1)} %fusion.17.s_ref, f32[640,1024]{1,0:T(8,128)S(1)} %hidden_first.2.refs_6_.acc_ref, bf16[8,640,512]{2,1,0:T(8,128)(2,1)} %norm.1.refs_0_.refs_1_.refs_2_.refs_3_.refs_4_.refs_5_, bf16[8,640,512]{2,1,0:T(8,128)(2,1)} %norm.1.refs_0_.refs_1_.refs_2_.refs_3_.refs_4_.refs_5_, ...), custom_call_target="tpu_custom_call" | custom-call | flops 1342177 | bytes 8388 | tf_op jit(solution)/shard_map/hidden_last/pallas_call | solution.py:211
  190.1 7.0 %partial.4 = (bf16[4,640,256]{2,1,0:T(8,128)(2,1)}, bf16[4,640,256]{2,1,0:T(8,128)(2,1)}) custom-call(s32[4]{0:T(128)} %iota.7.s_ref, bf16[640,1024]{1,0:T(8,128)(2,1)} %copy-done.1, bf16[640,1024]{1,0:T(8,128)(2,1)} %copy-done, bf16[2,2,128,1024]{3,2,1,0:T(8,128)(2,1)} %pad_maximum_fusion.refs_0_, bf16[2,2,128,1024]{3,2,1,0:T(8,128)(2,1)} %copy-done.21, ...), custom_call_target="tpu_custom_call" | custom-call | flops 2684354 | bytes 8388 | tf_op jit(solution)/shard_map/partial/pallas_call | solution.py:251
  197.7 7.1 %partial.5 = (bf16[4,640,256]{2,1,0:T(8,128)(2,1)}, bf16[4,640,256]{2,1,0:T(8,128)(2,1)}) custom-call(s32[4]{0:T(128)} %and_select_fusion.s_ref, bf16[640,1024]{1,0:T(8,128)(2,1)} %copy-done.1, bf16[640,1024]{1,0:T(8,128)(2,1)} %copy-done, bf16[2,2,128,1024]{3,2,1,0:T(8,128)(2,1)} %pad_maximum_fusion.refs_0_, bf16[2,2,128,1024]{3,2,1,0:T(8,128)(2,1)} %copy-done.21, ...), custom_call_target="tpu_custom_call" | custom-call | flops 2684354 | bytes 8388 | tf_op jit(solution)/shard_map/partial/pallas_call | solution.py:251
  214.6 3.3 %collective-permute-start.27 = (bf16[2,128,1024]{2,1,0:T(8,128)(2,1)S(1)}, bf16[2,128,1024]{2,1,0:T(8,128)(2,1)S(1)}, u32[]{:S(2)}, u32[]{:S(2)}) collective-permute-start(bf16[2,128,1024]{2,1,0:T(8,128)(2,1)S(1)} %slice_bitcast_fusion), channel_id=1, source_target_pairs={{0,48},{1,49},{2,50},{3,51},{4,52},{5,53},{6,54},{7,55},{8,56},{9,... | collective-permute-start | bytes 1572872 | tf_op jit(solution)/shard_map/ppermute | solution.py:38
  217.8 7.8 %collective-permute-done.24 = bf16[640,256]{1,0:T(8,128)(2,1)S(1)} collective-permute-done((bf16[640,256]{1,0:T(8,128)(2,1)S(1)}, bf16[640,256]{1,0:T(8,128)(2,1)S(1)}, u32[]{:S(2)}, u32[]{:S(2)}) %collective-permute-start.24) | collective-permute-done | bytes 327712 | tf_op jit(solution)/shard_map/ppermute | solution.py:38
  225.7 3.8 %collective-permute-done.23 = bf16[640,256]{1,0:T(8,128)(2,1)S(1)} collective-permute-done((bf16[640,256]{1,0:T(8,128)(2,1)S(1)}, bf16[640,256]{1,0:T(8,128)(2,1)S(1)}, u32[]{:S(2)}, u32[]{:S(2)}) %collective-permute-start.23) | collective-permute-done | bytes 327712 | tf_op jit(solution)/shard_map/ppermute | solution.py:38
  229.5 7.7 %collective-permute-done.22 = bf16[640,256]{1,0:T(8,128)(2,1)S(1)} collective-permute-done((bf16[640,256]{1,0:T(8,128)(2,1)S(1)}, bf16[640,256]{1,0:T(8,128)(2,1)S(1)}, u32[]{:S(2)}, u32[]{:S(2)}) %collective-permute-start.22) | collective-permute-done | bytes 327712 | tf_op jit(solution)/shard_map/ppermute | solution.py:38
  237.2 1.9 fusion.5.refs_8_
  240.0 7.0 %partial.6 = (bf16[4,640,256]{2,1,0:T(8,128)(2,1)}, bf16[4,640,256]{2,1,0:T(8,128)(2,1)}) custom-call(s32[4]{0:T(128)} %iota.9.s_ref, bf16[640,1024]{1,0:T(8,128)(2,1)} %copy-done.1, bf16[640,1024]{1,0:T(8,128)(2,1)} %copy-done, bf16[2,2,128,1024]{3,2,1,0:T(8,128)(2,1)} %after.11.refs_0_, bf16[2,2,128,1024]{3,2,1,0:T(8,128)(2,1)} %collective-permute-done.17.refs_7_.refs_1_, ...), custom_call_target="tpu_custom_call" | custom-call | flops 2684354 | bytes 8388 | tf_op jit(solution)/shard_map/partial/pallas_call | solution.py:251
  247.1 3.2 %collective-permute-done.28 = bf16[4,640,256]{2,1,0:T(8,128)(2,1)S(1)} collective-permute-done((bf16[4,640,256]{2,1,0:T(8,128)(2,1)}, bf16[4,640,256]{2,1,0:T(8,128)(2,1)S(1)}, u32[]{:S(2)}, u32[]{:S(2)}) %collective-permute-start.28) | collective-permute-done | bytes 1310752 | tf_op jit(solution)/shard_map/ppermute | solution.py:38
  250.3 2.7 add_convert_fusion
  256.1 2.6 collective-permute-start.20
  258.7 4.0 %collective-permute-done.25.refs_7_ = bf16[640,128]{1,0:T(8,128)(2,1)S(1)} collective-permute-done((bf16[640,128]{1,0:T(8,128)(2,1)S(1)}, bf16[640,128]{1,0:T(8,128)(2,1)S(1)}, u32[]{:S(2)}, u32[]{:S(2)}) %collective-permute-start.25) | collective-permute-done | bytes 163872 | tf_op jit(solution)/shard_map/ppermute | solution.py:38
  262.7 2.7 collective-permute-done.20.refs_6_
  266.1 7.0 %partial.7 = (bf16[4,640,256]{2,1,0:T(8,128)(2,1)}, bf16[4,640,256]{2,1,0:T(8,128)(2,1)}) custom-call(s32[4]{0:T(128)} %and_select_fusion.s_ref, bf16[640,1024]{1,0:T(8,128)(2,1)} %copy-done.1, bf16[640,1024]{1,0:T(8,128)(2,1)} %copy-done, bf16[2,2,128,1024]{3,2,1,0:T(8,128)(2,1)} %after.11.refs_0_, ...), custom_call_target="tpu_custom_call" | custom-call | flops 2684354 | bytes 8388 | tf_op jit(solution)/shard_map/partial/pallas_call | solution.py:251
  274.1 2.3 collective-permute-done.30
  276.3 2.2 fusion.11
  278.5 3.5 %collective-permute-start.33 = (bf16[640,256]{1,0:T(8,128)(2,1)}, bf16[640,256]{1,0:T(8,128)(2,1)S(1)}, u32[]{:S(2)}, u32[]{:S(2)}) collective-permute-start(bf16[640,256]{1,0:T(8,128)(2,1)} %get-tuple-element.32), channel_id=1, source_target_pairs={{0,6},{1,7},{2,0},{3,1},{4,2},{5,3},{6,4},{7,5},{8,14},{9,15},{10,... | collective-permute-start | bytes 983048 | tf_op jit(solution)/shard_map/ppermute | solution.py:38
  285.6 11.1 %collective-permute-done.33 = bf16[640,256]{1,0:T(8,128)(2,1)S(1)} collective-permute-done((bf16[640,256]{1,0:T(8,128)(2,1)}, bf16[640,256]{1,0:T(8,128)(2,1)S(1)}, u32[]{:S(2)}, u32[]{:S(2)}) %collective-permute-start.33) | collective-permute-done | bytes 327712 | tf_op jit(solution)/shard_map/ppermute | solution.py:38
  296.7 3.1 collective-permute-done.31
  302.6 5.8 %collective-permute-done.34 = bf16[640,128]{1,0:T(8,128)(2,1)S(1)} collective-permute-done((bf16[640,128]{1,0:T(8,128)(2,1)S(1)}, bf16[640,128]{1,0:T(8,128)(2,1)S(1)}, u32[]{:S(2)}, u32[]{:S(2)}) %collective-permute-start.34) | collective-permute-done | bytes 163872 | tf_op jit(solution)/shard_map/ppermute | solution.py:38
  (167 shorter events, 47.1 us)
Async XLA Ops:
  7.2 133.8 %all-gather.5.cloned.1.call-start = ((), (), s32[]{:S(2)}) async-start(), calls=%async_computation.5 | async-start | bytes 3276800 | tf_op jit(solution)/shard_map/all_gather | solution.py:293
  14.2 13.8 %collective-permute-start = (bf16[2,128,1024]{2,1,0:T(8,128)(2,1)}, bf16[2,128,1024]{2,1,0:T(8,128)(2,1)S(1)}, u32[]{:S(2)}, u32[]{:S(2)}) collective-permute-start(bf16[2,128,1024]{2,1,0:T(8,128)(2,1)} %get-tuple-element.17.dep_ref), channel_id=1, source_target_pairs={{0,64},{1,65},{2,66},{3,67},{4,68},{5,69},{6,70},{7,71},{8,72},{9,... | collective-permute-start | bytes 1572872 | tf_op jit(solution)/shard_map/ppermute | solution.py:38
  31.0 31.1 %collective-permute-start.2 = (bf16[2,2,128,1024]{3,2,1,0:T(8,128)(2,1)}, bf16[2,2,128,1024]{3,2,1,0:T(8,128)(2,1)S(1)}, u32[]{:S(2)}, u32[]{:S(2)}) collective-permute-start(bf16[2,2,128,1024]{3,2,1,0:T(8,128)(2,1)} %pad_maximum_fusion.refs_0_), channel_id=1, source_target_pairs={{0,16},{1,17},{2,18},{3,19},{4,20},{5,21},{6,22},{7,23},{8,24},{9,... | collective-permute-start | bytes 3145736 | tf_op jit(solution)/shard_map/ppermute | solution.py:38
  33.1 29.0 %collective-permute-start.3 = (bf16[2,2,128,1024]{3,2,1,0:T(8,128)(2,1)}, bf16[2,2,128,1024]{3,2,1,0:T(8,128)(2,1)S(1)}, u32[]{:S(2)}, u32[]{:S(2)}) collective-permute-start(bf16[2,2,128,1024]{3,2,1,0:T(8,128)(2,1)} %pad_maximum_fusion.refs_0_), channel_id=1, source_target_pairs={{0,48},{1,49},{2,50},{3,51},{4,52},{5,53},{6,54},{7,55},{8,56},{9,... | collective-permute-start | bytes 3145736 | tf_op jit(solution)/shard_map/ppermute | solution.py:38
  35.2 26.9 %all-to-all-start = ((bf16[16,32,1024]{2,1,0:T(8,128)(2,1)}), bf16[16,32,1024]{2,1,0:T(8,128)(2,1)S(1)}, u32[]{:S(2)}, u32[]{:S(2)}) async-start(bf16[16,32,1024]{2,1,0:T(8,128)(2,1)} %get-tuple-element.20.refs_1_), calls=%async_computation | async-start | bytes 2097152 | tf_op jit(solution)/shard_map/all_to_all | solution.py:304
  42.3 98.7 %all-gather.7.cloned.1.call-start = ((), (), s32[]{:S(2)}) async-start(), calls=%async_computation.6 | async-start | bytes 3276800 | tf_op jit(solution)/shard_map/all_gather | solution.py:311
  42.3 30.4 %collective-permute-start.1 = (bf16[2,320,512]{2,1,0:T(8,128)(2,1)}, bf16[2,320,512]{2,1,0:T(8,128)(2,1)}, u32[]{:S(2)}, u32[]{:S(2)}) collective-permute-start(bf16[2,320,512]{2,1,0:T(8,128)(2,1)} %param.11), channel_id=1, source_target_pairs={{0,1},{1,0},{2,3},{3,2},{4,5},{5,4},{6,7},{7,6},{8,9},{9,8},{10,11... | collective-permute-start | bytes 1966088 | tf_op jit(solution)/shard_map/ppermute | solution.py:38
  63.8 37.4 %collective-permute-start.4 = (bf16[512,1024]{1,0:T(8,128)(2,1)}, bf16[512,1024]{1,0:T(8,128)(2,1)S(1)}, u32[]{:S(2)}, u32[]{:S(2)}) collective-permute-start(bf16[512,1024]{1,0:T(8,128)(2,1)} %after.7.refs_6_), channel_id=1, source_target_pairs={{0,16},{1,17},{2,18},{3,19},{4,20},{5,21},{6,22},{7,23},{8,24},{9,... | collective-permute-start | bytes 3145736 | tf_op jit(solution)/shard_map/ppermute | solution.py:38
  65.3 35.9 %collective-permute-start.5 = (bf16[512,1024]{1,0:T(8,128)(2,1)}, bf16[512,1024]{1,0:T(8,128)(2,1)S(1)}, u32[]{:S(2)}, u32[]{:S(2)}) collective-permute-start(bf16[512,1024]{1,0:T(8,128)(2,1)} %after.7.refs_6_), channel_id=1, source_target_pairs={{0,48},{1,49},{2,50},{3,51},{4,52},{5,53},{6,54},{7,55},{8,56},{9,... | collective-permute-start | bytes 3145736 | tf_op jit(solution)/shard_map/ppermute | solution.py:38
  67.0 35.2 %collective-permute-start.6 = (bf16[512,1024]{1,0:T(8,128)(2,1)}, bf16[512,1024]{1,0:T(8,128)(2,1)S(1)}, u32[]{:S(2)}, u32[]{:S(2)}) collective-permute-start(bf16[512,1024]{1,0:T(8,128)(2,1)} %after.7.refs_6_), channel_id=1, source_target_pairs={{0,64},{1,65},{2,66},{3,67},{4,68},{5,69},{6,70},{7,71},{8,72},{9,... | collective-permute-start | bytes 3145736 | tf_op jit(solution)/shard_map/ppermute | solution.py:38
  68.7 32.5 %collective-permute-start.7 = (bf16[2,128,1024]{2,1,0:T(8,128)(2,1)S(1)}, bf16[2,128,1024]{2,1,0:T(8,128)(2,1)S(1)}, u32[]{:S(2)}, u32[]{:S(2)}) collective-permute-start(bf16[2,128,1024]{2,1,0:T(8,128)(2,1)S(1)} %slice_bitcast_fusion.3), channel_id=1, source_target_pairs={{0,16},{1,17},{2,18},{3,19},{4,20},{5,21},{6,22},{7,23},{8,24},{9,... | collective-permute-start | bytes 1572872 | tf_op jit(solution)/shard_map/ppermute | solution.py:38
  72.8 28.4 %collective-permute-start.8 = (bf16[2,128,1024]{2,1,0:T(8,128)(2,1)S(1)}, bf16[2,128,1024]{2,1,0:T(8,128)(2,1)S(1)}, u32[]{:S(2)}, u32[]{:S(2)}) collective-permute-start(bf16[2,128,1024]{2,1,0:T(8,128)(2,1)S(1)} %slice_bitcast_fusion.2), channel_id=1, source_target_pairs={{0,48},{1,49},{2,50},{3,51},{4,52},{5,53},{6,54},{7,55},{8,56},{9,... | collective-permute-start | bytes 1572872 | tf_op jit(solution)/shard_map/ppermute | solution.py:38
  104.2 151.0 %reduce-scatter.3.cloned.1.call-start = ((), (), s32[]{:S(2)}) async-start(), calls=%async_computation.3 | async-start | bytes 1638400 | tf_op jit(solution)/shard_map/reduce_scatter | solution.py:357
  104.2 36.6 %collective-permute-start.9 = (bf16[512,1024]{1,0:T(8,128)(2,1)}, bf16[512,1024]{1,0:T(8,128)(2,1)S(1)}, u32[]{:S(2)}, u32[]{:S(2)}) collective-permute-start(bf16[512,1024]{1,0:T(8,128)(2,1)} %copy-done.2), channel_id=1, source_target_pairs={{0,16},{1,17},{2,18},{3,19},{4,20},{5,21},{6,22},{7,23},{8,24},{9,... | collective-permute-start | bytes 3145736 | tf_op jit(solution)/shard_map/ppermute | solution.py:38
  105.7 35.2 %collective-permute-start.10 = (bf16[512,1024]{1,0:T(8,128)(2,1)}, bf16[512,1024]{1,0:T(8,128)(2,1)S(1)}, u32[]{:S(2)}, u32[]{:S(2)}) collective-permute-start(bf16[512,1024]{1,0:T(8,128)(2,1)} %copy-done.2), channel_id=1, source_target_pairs={{0,48},{1,49},{2,50},{3,51},{4,52},{5,53},{6,54},{7,55},{8,56},{9,... | collective-permute-start | bytes 3145736 | tf_op jit(solution)/shard_map/ppermute | solution.py:38
  109.4 31.4 %collective-permute-start.11 = (bf16[256,1024]{1,0:T(8,128)(2,1)}, bf16[256,1024]{1,0:T(8,128)(2,1)}, u32[]{:S(2)}, u32[]{:S(2)}) collective-permute-start(bf16[256,1024]{1,0:T(8,128)(2,1)} %after.9), channel_id=1, source_target_pairs={{0,16},{1,17},{2,18},{3,19},{4,20},{5,21},{6,22},{7,23},{8,24},{9,... | collective-permute-start | bytes 1572872 | tf_op jit(solution)/shard_map/ppermute | solution.py:38
  111.6 29.3 %collective-permute-start.12 = (bf16[256,1024]{1,0:T(8,128)(2,1)}, bf16[256,1024]{1,0:T(8,128)(2,1)S(1)}, u32[]{:S(2)}, u32[]{:S(2)}) collective-permute-start(bf16[256,1024]{1,0:T(8,128)(2,1)} %slice.91), channel_id=1, source_target_pairs={{0,48},{1,49},{2,50},{3,51},{4,52},{5,53},{6,54},{7,55},{8,56},{9,... | collective-permute-start | bytes 1572872 | tf_op jit(solution)/shard_map/ppermute | solution.py:38
  113.5 27.4 %collective-permute-start.13 = (bf16[2,128,1024]{2,1,0:T(8,128)(2,1)}, bf16[2,128,1024]{2,1,0:T(8,128)(2,1)S(1)}, u32[]{:S(2)}, u32[]{:S(2)}) collective-permute-start(bf16[2,128,1024]{2,1,0:T(8,128)(2,1)} %after.10), channel_id=1, source_target_pairs={{0,64},{1,65},{2,66},{3,67},{4,68},{5,69},{6,70},{7,71},{8,72},{9,... | collective-permute-start | bytes 1572872 | tf_op jit(solution)/shard_map/ppermute | solution.py:38
  140.9 8.5 %copy-start.17 = (bf16[256,1024]{1,0:T(8,128)(2,1)}, bf16[256,1024]{1,0:T(8,128)(2,1)S(1)}, u32[]{:S(2)}) copy-start(bf16[256,1024]{1,0:T(8,128)(2,1)S(1)} %collective-permute-done.12.refs_3_) | copy-start | bytes 1572868
  140.9 8.5 %copy-start.6 = (bf16[512,1024]{1,0:T(8,128)(2,1)}, bf16[512,1024]{1,0:T(8,128)(2,1)S(1)}, u32[]{:S(2)}) copy-start(bf16[512,1024]{1,0:T(8,128)(2,1)S(1)} %collective-permute-done.9.refs_0_.refs_9_.refs_1_) | copy-start | bytes 3145732
  140.9 8.5 %copy-start.15 = (bf16[512,1024]{1,0:T(8,128)(2,1)}, bf16[512,1024]{1,0:T(8,128)(2,1)S(1)}, u32[]{:S(2)}) copy-start(bf16[512,1024]{1,0:T(8,128)(2,1)S(1)} %collective-permute-done.10.refs_1_.refs_11_) | copy-start | bytes 3145732
  149.4 17.6 %collective-permute-start.16 = (bf16[8,640,512]{2,1,0:T(8,128)(2,1)}, bf16[8,640,512]{2,1,0:T(8,128)(2,1)}, u32[]{:S(2)}, u32[]{:S(2)}) collective-permute-start(bf16[8,640,512]{2,1,0:T(8,128)(2,1)} %norm.1.refs_0_.refs_1_.refs_2_.refs_3_.refs_4_.refs_5_), channel_id=1, source_target_pairs={{0,8},{1,9},{2,10},{3,11},{4,12},{5,13},{6,14},{7,15},{8,0},{9,1},... | collective-permute-start | bytes 15728648 | tf_op jit(solution)/shard_map/ppermute | solution.py:38
  150.6 33.2 %collective-permute-start.17 = (bf16[2,2,128,1024]{3,2,1,0:T(8,128)(2,1)}, bf16[2,2,128,1024]{3,2,1,0:T(8,128)(2,1)}, u32[]{:S(2)}, u32[]{:S(2)}) collective-permute-start(bf16[2,2,128,1024]{3,2,1,0:T(8,128)(2,1)} %after.11.refs_0_), channel_id=1, source_target_pairs={{0,16},{1,17},{2,18},{3,19},{4,20},{5,21},{6,22},{7,23},{8,24},{9,... | collective-permute-start | bytes 3145736 | tf_op jit(solution)/shard_map/ppermute | solution.py:38
  151.3 32.5 %collective-permute-start.18 = (bf16[2,2,128,1024]{3,2,1,0:T(8,128)(2,1)}, bf16[2,2,128,1024]{3,2,1,0:T(8,128)(2,1)}, u32[]{:S(2)}, u32[]{:S(2)}) collective-permute-start(bf16[2,2,128,1024]{3,2,1,0:T(8,128)(2,1)} %after.11.refs_0_), channel_id=1, source_target_pairs={{0,48},{1,49},{2,50},{3,51},{4,52},{5,53},{6,54},{7,55},{8,56},{9,... | collective-permute-start | bytes 3145736 | tf_op jit(solution)/shard_map/ppermute | solution.py:38
  153.8 19.9 %collective-permute-start.14 = (bf16[256,1024]{1,0:T(8,128)(2,1)}, bf16[256,1024]{1,0:T(8,128)(2,1)}, u32[]{:S(2)}, u32[]{:S(2)}) collective-permute-start(bf16[256,1024]{1,0:T(8,128)(2,1)} %collective-permute-done.11.refs_2_), channel_id=1, source_target_pairs={{0,64},{1,65},{2,66},{3,67},{4,68},{5,69},{6,70},{7,71},{8,72},{9,... | collective-permute-start | bytes 1572872 | tf_op jit(solution)/shard_map/ppermute | solution.py:38
  154.4 24.7 %collective-permute-start.15 = (bf16[256,1024]{1,0:T(8,128)(2,1)}, bf16[256,1024]{1,0:T(8,128)(2,1)}, u32[]{:S(2)}, u32[]{:S(2)}) collective-permute-start(bf16[256,1024]{1,0:T(8,128)(2,1)} %copy-done.17), channel_id=1, source_target_pairs={{0,64},{1,65},{2,66},{3,67},{4,68},{5,69},{6,70},{7,71},{8,72},{9,... | collective-permute-start | bytes 1572872 | tf_op jit(solution)/shard_map/ppermute | solution.py:38
  160.2 6.8 %copy-start.14 = (bf16[512,1024]{1,0:T(8,128)(2,1)S(1)}, bf16[512,1024]{1,0:T(8,128)(2,1)}, u32[]{:S(2)}) copy-start(bf16[512,1024]{1,0:T(8,128)(2,1)} %copy-done.11) | copy-start | bytes 3145732
  166.9 12.2 %copy-start.18 = (bf16[256,1024]{1,0:T(8,128)(2,1)S(1)}, bf16[256,1024]{1,0:T(8,128)(2,1)}, u32[]{:S(2)}) copy-start(bf16[256,1024]{1,0:T(8,128)(2,1)} %copy-done.17) | copy-start | bytes 1572868
  197.1 9.4 %collective-permute-start.19 = (bf16[4,640,256]{2,1,0:T(8,128)(2,1)}, bf16[4,640,256]{2,1,0:T(8,128)(2,1)S(1)}, u32[]{:S(2)}, u32[]{:S(2)}) collective-permute-start(bf16[4,640,256]{2,1,0:T(8,128)(2,1)} %get-tuple-element.24.refs_5_), channel_id=1, source_target_pairs={{0,8},{1,9},{2,10},{3,11},{4,12},{5,13},{6,14},{7,15},{8,0},{9,1},... | collective-permute-start | bytes 3932168 | tf_op jit(solution)/shard_map/ppermute | solution.py:38
  197.7 8.8 %copy-start.34 = (bf16[4,640,256]{2,1,0:T(8,128)(2,1)S(1)}, bf16[4,640,256]{2,1,0:T(8,128)(2,1)}, u32[]{:S(2)}) copy-start(bf16[4,640,256]{2,1,0:T(8,128)(2,1)} %get-tuple-element.23) | copy-start | bytes 3932164
  204.8 3.5 %collective-permute-start.21 = (bf16[4,640,256]{2,1,0:T(8,128)(2,1)}, bf16[4,640,256]{2,1,0:T(8,128)(2,1)}, u32[]{:S(2)}, u32[]{:S(2)}) collective-permute-start(bf16[4,640,256]{2,1,0:T(8,128)(2,1)} %get-tuple-element.26.refs_5_), channel_id=1, source_target_pairs={{0,8},{1,9},{2,10},{3,11},{4,12},{5,13},{6,14},{7,15},{8,0},{9,1},... | collective-permute-start | bytes 3932168 | tf_op jit(solution)/shard_map/ppermute | solution.py:38
  206.4 32.7 %collective-permute-start.26 = (bf16[2,128,1024]{2,1,0:T(8,128)(2,1)S(1)}, bf16[2,128,1024]{2,1,0:T(8,128)(2,1)S(1)}, u32[]{:S(2)}, u32[]{:S(2)}) collective-permute-start(bf16[2,128,1024]{2,1,0:T(8,128)(2,1)S(1)} %slice_bitcast_fusion.1), channel_id=1, source_target_pairs={{0,16},{1,17},{2,18},{3,19},{4,20},{5,21},{6,22},{7,23},{8,24},{9,... | collective-permute-start | bytes 1572872 | tf_op jit(solution)/shard_map/ppermute | solution.py:38
  207.9 75.1 %reduce-scatter.5.cloned.1.call-start = ((), (), s32[]{:S(2)}) async-start(), calls=%async_computation.4 | async-start | bytes 1638400 | tf_op jit(solution)/shard_map/reduce_scatter | solution.py:357
  210.6 28.4 %copy-start.32 = (bf16[640,256]{1,0:T(8,128)(2,1)}, bf16[640,256]{1,0:T(8,128)(2,1)S(1)}, u32[]{:S(2)}) copy-start(bf16[640,256]{1,0:T(8,128)(2,1)S(1)} %get-tuple-element.36.refs_7_) | copy-start | bytes 983044
  210.6 15.0 %collective-permute-start.24 = (bf16[640,256]{1,0:T(8,128)(2,1)S(1)}, bf16[640,256]{1,0:T(8,128)(2,1)S(1)}, u32[]{:S(2)}, u32[]{:S(2)}) collective-permute-start(bf16[640,256]{1,0:T(8,128)(2,1)S(1)} %get-tuple-element.35), channel_id=1, source_target_pairs={{0,6},{1,7},{2,0},{3,1},{4,2},{5,3},{6,4},{7,5},{8,14},{9,15},{10,... | collective-permute-start | bytes 983048 | tf_op jit(solution)/shard_map/ppermute | solution.py:38
  212.3 17.2 %collective-permute-start.23 = (bf16[640,256]{1,0:T(8,128)(2,1)S(1)}, bf16[640,256]{1,0:T(8,128)(2,1)S(1)}, u32[]{:S(2)}, u32[]{:S(2)}) collective-permute-start(bf16[640,256]{1,0:T(8,128)(2,1)S(1)} %get-tuple-element.34), channel_id=1, source_target_pairs={{0,4},{1,5},{2,6},{3,7},{4,0},{5,1},{6,2},{7,3},{8,12},{9,13},{10,... | collective-permute-start | bytes 983048 | tf_op jit(solution)/shard_map/ppermute | solution.py:38
  213.4 23.7 %collective-permute-start.22 = (bf16[640,256]{1,0:T(8,128)(2,1)S(1)}, bf16[640,256]{1,0:T(8,128)(2,1)S(1)}, u32[]{:S(2)}, u32[]{:S(2)}) collective-permute-start(bf16[640,256]{1,0:T(8,128)(2,1)S(1)} %get-tuple-element.36.refs_7_), channel_id=1, source_target_pairs={{0,2},{1,3},{2,4},{3,5},{4,6},{5,7},{6,0},{7,1},{8,10},{9,11},{10,... | collective-permute-start | bytes 983048 | tf_op jit(solution)/shard_map/ppermute | solution.py:38
  214.6 24.5 %collective-permute-start.27 = (bf16[2,128,1024]{2,1,0:T(8,128)(2,1)S(1)}, bf16[2,128,1024]{2,1,0:T(8,128)(2,1)S(1)}, u32[]{:S(2)}, u32[]{:S(2)}) collective-permute-start(bf16[2,128,1024]{2,1,0:T(8,128)(2,1)S(1)} %slice_bitcast_fusion), channel_id=1, source_target_pairs={{0,48},{1,49},{2,50},{3,51},{4,52},{5,53},{6,54},{7,55},{8,56},{9,... | collective-permute-start | bytes 1572872 | tf_op jit(solution)/shard_map/ppermute | solution.py:38
  247.1 3.2 %collective-permute-start.28 = (bf16[4,640,256]{2,1,0:T(8,128)(2,1)}, bf16[4,640,256]{2,1,0:T(8,128)(2,1)S(1)}, u32[]{:S(2)}, u32[]{:S(2)}) collective-permute-start(bf16[4,640,256]{2,1,0:T(8,128)(2,1)} %get-tuple-element.28.refs_5_), channel_id=1, source_target_pairs={{0,8},{1,9},{2,10},{3,11},{4,12},{5,13},{6,14},{7,15},{8,0},{9,1},... | collective-permute-start | bytes 3932168 | tf_op jit(solution)/shard_map/ppermute | solution.py:38
  254.0 8.6 %collective-permute-start.25 = (bf16[640,128]{1,0:T(8,128)(2,1)S(1)}, bf16[640,128]{1,0:T(8,128)(2,1)S(1)}, u32[]{:S(2)}, u32[]{:S(2)}) collective-permute-start(bf16[640,128]{1,0:T(8,128)(2,1)S(1)} %constant_dynamic-slice_fusion.1), channel_id=1, source_target_pairs={{0,1},{1,0},{2,3},{3,2},{4,5},{5,4},{6,7},{7,6},{8,9},{9,8},{10,11... | collective-permute-start | bytes 491528 | tf_op jit(solution)/shard_map/ppermute | solution.py:38
  256.1 9.3 %collective-permute-start.20 = (bf16[640,128]{1,0:T(8,128)(2,1)S(1)}, bf16[640,128]{1,0:T(8,128)(2,1)S(1)}, u32[]{:S(2)}, u32[]{:S(2)}) collective-permute-start(bf16[640,128]{1,0:T(8,128)(2,1)S(1)} %dynamic-slice_bitcast_fusion.1), channel_id=1, source_target_pairs={{0,1},{1,0},{2,3},{3,2},{4,5},{5,4},{6,7},{7,6},{8,9},{9,8},{10,11... | collective-permute-start | bytes 491528 | tf_op jit(solution)/shard_map/ppermute | solution.py:38
  273.1 3.2 %collective-permute-start.30 = (bf16[4,640,256]{2,1,0:T(8,128)(2,1)}, bf16[4,640,256]{2,1,0:T(8,128)(2,1)S(1)}, u32[]{:S(2)}, u32[]{:S(2)}) collective-permute-start(bf16[4,640,256]{2,1,0:T(8,128)(2,1)} %get-tuple-element.30), channel_id=1, source_target_pairs={{0,8},{1,9},{2,10},{3,11},{4,12},{5,13},{6,14},{7,15},{8,0},{9,1},... | collective-permute-start | bytes 3932168 | tf_op jit(solution)/shard_map/ppermute | solution.py:38
  278.5 18.1 %collective-permute-start.33 = (bf16[640,256]{1,0:T(8,128)(2,1)}, bf16[640,256]{1,0:T(8,128)(2,1)S(1)}, u32[]{:S(2)}, u32[]{:S(2)}) collective-permute-start(bf16[640,256]{1,0:T(8,128)(2,1)} %get-tuple-element.32), channel_id=1, source_target_pairs={{0,6},{1,7},{2,0},{3,1},{4,2},{5,3},{6,4},{7,5},{8,14},{9,15},{10,... | collective-permute-start | bytes 983048 | tf_op jit(solution)/shard_map/ppermute | solution.py:38
  282.1 14.6 %collective-permute-start.32 = (bf16[640,256]{1,0:T(8,128)(2,1)S(1)}, bf16[640,256]{1,0:T(8,128)(2,1)S(1)}, u32[]{:S(2)}, u32[]{:S(2)}) collective-permute-start(bf16[640,256]{1,0:T(8,128)(2,1)S(1)} %get-tuple-element.33), channel_id=1, source_target_pairs={{0,4},{1,5},{2,6},{3,7},{4,0},{5,1},{6,2},{7,3},{8,12},{9,13},{10,... | collective-permute-start | bytes 983048 | tf_op jit(solution)/shard_map/ppermute | solution.py:38
  282.1 17.7 %collective-permute-start.31 = (bf16[640,256]{1,0:T(8,128)(2,1)S(1)}, bf16[640,256]{1,0:T(8,128)(2,1)S(1)}, u32[]{:S(2)}, u32[]{:S(2)}) collective-permute-start(bf16[640,256]{1,0:T(8,128)(2,1)S(1)} %get-tuple-element.31), channel_id=1, source_target_pairs={{0,2},{1,3},{2,4},{3,5},{4,6},{5,7},{6,0},{7,1},{8,10},{9,11},{10,... | collective-permute-start | bytes 983048 | tf_op jit(solution)/shard_map/ppermute | solution.py:38
  283.0 19.5 %copy-start.39 = (bf16[1,640,256]{2,1,0:T(8,128)(2,1)S(1)}, bf16[1,640,256]{2,1,0:T(8,128)(2,1)}, u32[]{:S(2)}) copy-start(bf16[1,640,256]{2,1,0:T(8,128)(2,1)} %reduce-scatter.5.cloned.1.call-done) | copy-start | bytes 983044
  284.0 18.5 %collective-permute-start.29 = (bf16[640,128]{1,0:T(8,128)(2,1)S(1)}, bf16[640,128]{1,0:T(8,128)(2,1)S(1)}, u32[]{:S(2)}, u32[]{:S(2)}) collective-permute-start(bf16[640,128]{1,0:T(8,128)(2,1)S(1)} %dynamic-slice_bitcast_fusion), channel_id=1, source_target_pairs={{0,1},{1,0},{2,3},{3,2},{4,5},{5,4},{6,7},{7,6},{8,9},{9,8},{10,11... | collective-permute-start | bytes 491528 | tf_op jit(solution)/shard_map/ppermute | solution.py:38
  301.0 7.4 %collective-permute-start.34 = (bf16[640,128]{1,0:T(8,128)(2,1)S(1)}, bf16[640,128]{1,0:T(8,128)(2,1)S(1)}, u32[]{:S(2)}, u32[]{:S(2)}) collective-permute-start(bf16[640,128]{1,0:T(8,128)(2,1)S(1)} %constant_dynamic-slice_fusion), channel_id=1, source_target_pairs={{0,1},{1,0},{2,3},{3,2},{4,5},{5,4},{6,7},{7,6},{8,9},{9,8},{10,11... | collective-permute-start | bytes 491528 | tf_op jit(solution)/shard_map/ppermute | solution.py:38
  (33 other events, 87.6 us)
Sparse Core Ops, SparseCore 0:
  9.7 39.2 all-gather.4
  104.3 32.4 all-gather.6
  208.1 33.5 reduce-scatter.2
  253.2 24.7 reduce-scatter.4

commit v7 on v6

--- a/solution.py
+++ b/solution.py
@@ -148,7 +148,7 @@
         grid=(640 // rows,),
         in_specs=[block, block, pl.BlockSpec((8, 512), lambda i: (0, 0))] + [ANY] * len(deps),
         out_specs=pl.BlockSpec((8, rows, 512), lambda i: (0, i, 0)),
-        compiler_params=params(),
+        compiler_params=params(56),
         cost_estimate=cost(8 * 640 * D, 10 * MIB),
         name="norm",
     )(feats_a, feats_b, gains, *deps)
@@ -341,7 +341,7 @@
             hidden_sib,
             ws_a if j < 2 else ws_b,
             j % 2,
-            parts[-1:] + ([], [], sums + reduced, gots[:2])[j],
+            parts[-1:] + ([], [], sums + reduced, [])[j],
         )
         parts.append(part_sib)
         part_sib = send(part_sib, core=1)
@@ -357,7 +357,7 @@
             rows = lax.psum_scatter(both, "x", scatter_dimension=0, tiled=True)[0]
         keep = lax.dynamic_slice_in_dim(rows, yhi * 128, 128, 1)
         give = lax.dynamic_slice_in_dim(rows, (1 - yhi) * 128, 128, 1)
-        gots.append(send(give, yhi=1))
+        gots.append(send(after(give, *gots[:2]) if j == 3 else give, yhi=1))
         pieces.append(add(keep, gots[-1]))
     decoded = jnp.concatenate(pieces, axis=1).reshape(2, 320, 512)
     return (up_updated, down_updated, decoded)

time: 317 us -> 315 us (level)
  waiting for transfers between devices: 129 us -> 125 us
    ppermute x35, waiting for transfers between devices: 118 us -> 114 us  [send(): return lax.ppermute(v, AXES, shifted(**steps))]
  transfers between devices with their start and end apart: 40 -> 40, of which waited for: 17 -> 16; matrix products, arithmetic and copies ran while one was open for 8% -> 9% of each run, Pallas kernels for 19% -> 18%
where the time goes in v7:
time: 315 us; the launch traced here: 313 us
  waiting for transfers between devices  125 us (40%)
  Pallas kernels  75.4 us (24%)
  starting transfers between devices  51.7 us (16%)
  local copies, waits for them, and re-layouts  27.7 us (9%)
  other arithmetic  19.3 us (6%)
  between operations  14.3 us (5%)
    ppermute x35, waiting for transfers between devices, send(): return lax.ppermute(v, AXES, shifted(**steps))  114 us
    ppermute x35, starting transfers between devices, send(): return lax.ppermute(v, AXES, shifted(**steps))  44.5 us
    pallas_call x4, Pallas kernels, partial_of(): pl.pallas_call(partial_kernel, out_shape=(shape, shape), grid_spec=pltpu....  28.2 us
    unnamed x83, local copies, waits for them, and re-layouts  17.3 us
    pallas_call x2, Pallas kernels, down_step(): pl.pallas_call(down_kernel, out_shape=(jax.ShapeDtypeStruct((128, D), jnp...  12.7 us
    pallas_call x2, Pallas kernels, hidden_first(): pl.pallas_call(first_kernel, out_shape=jax.ShapeDtypeStruct((640, 1024),...  11.5 us
    all_to_all x1, waiting for transfers between devices, body(): lax.all_to_all(columns, ('core', 'x', 'yhi'), 0, 0, tiled=True)  9.99 us
    convert_element_type x8, other arithmetic, body(): (a.astype(jnp.float32) + b.astype(jnp.float32)).astype(jnp.bfloat16)  9.74 us
  transfers between devices with their start and end apart: 40, of which 16 were waited for; matrix products, arithmetic and copies ran while one was open for 9% of the time, Pallas kernels for 18%

profile of v7, /device:TPU:0, one launch (start us, length us, event | category | flops | bytes accessed | tf_op | source)
XLA Modules:
  0.0 313.3 jit_solution(16939569189888541986)
XLA Ops:
  7.9 6.3 %adam_down.2 = (f32[128,4096]{1,0:T(8,128)}, bf16[2,128,1024]{2,1,0:T(8,128)(2,1)}) custom-call(f32[128,4096]{1,0:T(8,128)} %w_ref.5, bf16[128,4096]{1,0:T(8,128)(2,1)} %g_ref.5, f32[128,4096]{1,0:T(8,128)} %m_ref.5, f32[128,4096]{1,0:T(8,128)} %v_ref.5), custom_call_target="tpu_custom_call" | custom-call | flops 7864 | bytes 5242 | tf_op jit(solution)/shard_map/adam_down/pallas_call | solution.py:110
  14.2 1.7 collective-permute-start
  15.9 7.8 %adam_up.1 = (f32[32,16384]{1,0:T(8,128)}, bf16[16,32,1024]{2,1,0:T(8,128)(2,1)}) custom-call(f32[32,16384]{1,0:T(8,128)} %w_ref.4, bf16[32,16384]{1,0:T(8,128)(2,1)} %g_ref.4, f32[32,16384]{1,0:T(8,128)} %m_ref.4, f32[32,16384]{1,0:T(8,128)} %v_ref.4, bf16[2,128,1024]{2,1,0:T(8,128)(2,1)} %get-tuple-element.17.dep_ref), custom_call_target="tpu_custom_call" | custom-call | flops 15728 | bytes 10485 | tf_op jit(solution)/shard_map/adam_up/pallas_call | solution.py:84
  23.7 4.3 %collective-permute-done.refs_0_ = bf16[2,128,1024]{2,1,0:T(8,128)(2,1)S(1)} collective-permute-done((bf16[2,128,1024]{2,1,0:T(8,128)(2,1)}, bf16[2,128,1024]{2,1,0:T(8,128)(2,1)S(1)}, u32[]{:S(2)}, u32[]{:S(2)}) %collective-permute-start) | collective-permute-done | bytes 524320 | tf_op jit(solution)/shard_map/ppermute | solution.py:38
  28.8 2.2 pad_maximum_fusion.refs_0_
  31.0 2.1 collective-permute-start.2
  33.1 2.1 collective-permute-start.3
  35.2 7.0 %all-to-all-start = ((bf16[16,32,1024]{2,1,0:T(8,128)(2,1)}), bf16[16,32,1024]{2,1,0:T(8,128)(2,1)S(1)}, u32[]{:S(2)}, u32[]{:S(2)}) async-start(bf16[16,32,1024]{2,1,0:T(8,128)(2,1)} %get-tuple-element.20.refs_1_), calls=%async_computation | async-start | bytes 2097152 | tf_op jit(solution)/shard_map/all_to_all | solution.py:304
  42.3 3.5 %collective-permute-start.1 = (bf16[2,320,512]{2,1,0:T(8,128)(2,1)}, bf16[2,320,512]{2,1,0:T(8,128)(2,1)}, u32[]{:S(2)}, u32[]{:S(2)}) collective-permute-start(bf16[2,320,512]{2,1,0:T(8,128)(2,1)} %param.11), channel_id=1, source_target_pairs={{0,1},{1,0},{2,3},{3,2},{4,5},{5,4},{6,7},{7,6},{8,9},{9,8},{10,11... | collective-permute-start | bytes 1966088 | tf_op jit(solution)/shard_map/ppermute | solution.py:38
  45.8 6.3 %adam_down.3 = (f32[128,4096]{1,0:T(8,128)}, bf16[2,128,1024]{2,1,0:T(8,128)(2,1)}) custom-call(f32[128,4096]{1,0:T(8,128)} %w_ref.5, bf16[128,4096]{1,0:T(8,128)(2,1)} %g_ref.5, f32[128,4096]{1,0:T(8,128)} %m_ref.5, f32[128,4096]{1,0:T(8,128)} %v_ref.5, f32[128,4096]{1,0:T(8,128)} %get-tuple-element.19.refs_0_, ...), custom_call_target="tpu_custom_call", output_to_operand_aliasing={{0}: (4, {})} | custom-call | flops 7864 | bytes 5242 | tf_op jit(solution)/shard_map/adam_down/pallas_call | solution.py:110
  52.1 10.0 %all-to-all-done = bf16[16,32,1024]{2,1,0:T(8,128)(2,1)S(1)} async-done(((bf16[16,32,1024]{2,1,0:T(8,128)(2,1)}), bf16[16,32,1024]{2,1,0:T(8,128)(2,1)S(1)}, u32[]{:S(2)}, u32[]{:S(2)}) %all-to-all-start) | async-done | bytes 1048608 | tf_op jit(solution)/shard_map/all_to_all | solution.py:304
  65.2 1.7 collective-permute-start.5
  69.1 3.7 %collective-permute-done.1.refs_0_ = bf16[2,320,512]{2,1,0:T(8,128)(2,1)} collective-permute-done((bf16[2,320,512]{2,1,0:T(8,128)(2,1)}, bf16[2,320,512]{2,1,0:T(8,128)(2,1)}, u32[]{:S(2)}, u32[]{:S(2)}) %collective-permute-start.1) | collective-permute-done | bytes 655392 | tf_op jit(solution)/shard_map/ppermute | solution.py:38
  72.7 2.0 collective-permute-start.8
  74.8 26.3 %collective-permute-done.7.refs_4_.refs_2_.refs_3_ = bf16[2,128,1024]{2,1,0:T(8,128)(2,1)S(1)} collective-permute-done((bf16[2,128,1024]{2,1,0:T(8,128)(2,1)S(1)}, bf16[2,128,1024]{2,1,0:T(8,128)(2,1)S(1)}, u32[]{:S(2)}, u32[]{:S(2)}) %collective-permute-start.7) | collective-permute-done | bytes 524320 | tf_op jit(solution)/shard_map/ppermute | solution.py:38
  105.7 1.8 collective-permute-start.10
  107.5 1.9 slice.90.refs_0_
  111.5 1.9 collective-permute-start.12
  114.7 26.1 %collective-permute-done.11.refs_2_ = bf16[256,1024]{1,0:T(8,128)(2,1)} collective-permute-done((bf16[256,1024]{1,0:T(8,128)(2,1)}, bf16[256,1024]{1,0:T(8,128)(2,1)}, u32[]{:S(2)}, u32[]{:S(2)}) %collective-permute-start.11) | collective-permute-done | bytes 524320 | tf_op jit(solution)/shard_map/ppermute | solution.py:38
  142.6 6.3 %norm.1.refs_0_.refs_1_.refs_2_.refs_3_.refs_4_.refs_5_ = bf16[8,640,512]{2,1,0:T(8,128)(2,1)} custom-call(bf16[4,640,512]{2,1,0:T(8,128)(2,1)} %bitcast.59, bf16[4,640,512]{2,1,0:T(8,128)(2,1)} %bitcast.60, f32[8,512]{1,0:T(8,128)} %pad_maximum_fusion.3.g_ref, bf16[512,1024]{1,0:T(8,128)(2,1)} %copy-done.7, bf16[512,1024]{1,0:T(8,128)(2,1)} %copy-done.16, ...), custom_call_target="tpu_custom_call" | custom-call | flops 20971 | bytes 10485 | tf_op jit(solution)/shard_map/norm/pallas_call | solution.py:145
  148.9 2.1 pad_maximum_fusion.1.refs_0_
  151.8 2.5 collective-permute-start.18
  157.0 2.5 copy-done
  163.2 4.9 %hidden_first.2.refs_6_.acc_ref = f32[640,1024]{1,0:T(8,128)S(1)} custom-call(s32[16]{0:T(128)S(1)} %fusion.17.s_ref, bf16[8,640,512]{2,1,0:T(8,128)(2,1)S(1)} %copy-done, bf16[8,640,512]{2,1,0:T(8,128)(2,1)S(1)} %copy-done, bf16[8,640,512]{2,1,0:T(8,128)(2,1)S(1)} %copy-done, bf16[8,640,512]{2,1,0:T(8,128)(2,1)S(1)} %copy-done, ...), custom_call_target="tpu_custom_call" | custom-call | flops 4026531 | bytes 14680 | tf_op jit(solution)/shard_map/hidden_first/pallas_call | solution.py:193
  168.2 6.6 %hidden_first.3.acc_ref = f32[640,1024]{1,0:T(8,128)S(1)} custom-call(s32[16]{0:T(128)S(1)} %fusion.17.s_ref, bf16[8,640,512]{2,1,0:T(8,128)(2,1)} %collective-permute-done.16.refs_0_.refs_1_.refs_2_.refs_3_.refs_4_.refs_5_, bf16[8,640,512]{2,1,0:T(8,128)(2,1)} %collective-permute-done.16.refs_0_.refs_1_.refs_2_.refs_3_.refs_4_.refs_5_, ...), custom_call_target="tpu_custom_call" | custom-call | flops 4026531 | bytes 14680 | tf_op jit(solution)/shard_map/hidden_first/pallas_call | solution.py:193
  174.8 4.8 %collective-permute-done.15.refs_5_ = bf16[256,1024]{1,0:T(8,128)(2,1)} collective-permute-done((bf16[256,1024]{1,0:T(8,128)(2,1)}, bf16[256,1024]{1,0:T(8,128)(2,1)}, u32[]{:S(2)}, u32[]{:S(2)}) %collective-permute-start.15) | collective-permute-done | bytes 524320 | tf_op jit(solution)/shard_map/ppermute | solution.py:38
  179.6 4.6 %hidden_last.2.refs_6_.sib_ref = bf16[640,1024]{1,0:T(8,128)(2,1)S(1)} custom-call(s32[16]{0:T(128)S(1)} %fusion.17.s_ref, f32[640,1024]{1,0:T(8,128)S(1)} %hidden_first.3.acc_ref, bf16[8,640,512]{2,1,0:T(8,128)(2,1)} %collective-permute-done.16.refs_0_.refs_1_.refs_2_.refs_3_.refs_4_.refs_5_, ...), custom_call_target="tpu_custom_call" | custom-call | flops 1342177 | bytes 8388 | tf_op jit(solution)/shard_map/hidden_last/pallas_call | solution.py:211
  184.3 4.4 %hidden_last.3.own_ref = bf16[640,1024]{1,0:T(8,128)(2,1)S(1)} custom-call(s32[16]{0:T(128)S(1)} %fusion.17.s_ref, f32[640,1024]{1,0:T(8,128)S(1)} %hidden_first.2.refs_6_.acc_ref, bf16[8,640,512]{2,1,0:T(8,128)(2,1)S(1)} %bitcast.55, bf16[8,640,512]{2,1,0:T(8,128)(2,1)S(1)} %bitcast.55, bf16[256,1024]{1,0:T(8,128)(2,1)} %collective-permute-done.11.refs_2_, ...), custom_call_target="tpu_custom_call" | custom-call | flops 1342177 | bytes 8388 | tf_op jit(solution)/shard_map/hidden_last/pallas_call | solution.py:211
  190.3 7.0 %partial.4 = (bf16[4,640,256]{2,1,0:T(8,128)(2,1)}, bf16[4,640,256]{2,1,0:T(8,128)(2,1)}) custom-call(s32[4]{0:T(128)} %iota.7.s_ref, bf16[640,1024]{1,0:T(8,128)(2,1)} %copy-done.2, bf16[640,1024]{1,0:T(8,128)(2,1)} %copy-done.1, bf16[2,2,128,1024]{3,2,1,0:T(8,128)(2,1)} %pad_maximum_fusion.refs_0_, bf16[2,2,128,1024]{3,2,1,0:T(8,128)(2,1)} %copy-done.20, ...), custom_call_target="tpu_custom_call" | custom-call | flops 2684354 | bytes 8388 | tf_op jit(solution)/shard_map/partial/pallas_call | solution.py:251
  197.9 7.1 %partial.5 = (bf16[4,640,256]{2,1,0:T(8,128)(2,1)}, bf16[4,640,256]{2,1,0:T(8,128)(2,1)}) custom-call(s32[4]{0:T(128)} %and_select_fusion.s_ref, bf16[640,1024]{1,0:T(8,128)(2,1)} %copy-done.2, bf16[640,1024]{1,0:T(8,128)(2,1)} %copy-done.1, bf16[2,2,128,1024]{3,2,1,0:T(8,128)(2,1)} %pad_maximum_fusion.refs_0_, bf16[2,2,128,1024]{3,2,1,0:T(8,128)(2,1)} %copy-done.20, ...), custom_call_target="tpu_custom_call" | custom-call | flops 2684354 | bytes 8388 | tf_op jit(solution)/shard_map/partial/pallas_call | solution.py:251
  210.8 1.6 collective-permute-start.24
  214.7 3.3 %collective-permute-start.27 = (bf16[2,128,1024]{2,1,0:T(8,128)(2,1)S(1)}, bf16[2,128,1024]{2,1,0:T(8,128)(2,1)S(1)}, u32[]{:S(2)}, u32[]{:S(2)}) collective-permute-start(bf16[2,128,1024]{2,1,0:T(8,128)(2,1)S(1)} %slice_bitcast_fusion), channel_id=1, source_target_pairs={{0,48},{1,49},{2,50},{3,51},{4,52},{5,53},{6,54},{7,55},{8,56},{9,... | collective-permute-start | bytes 1572872 | tf_op jit(solution)/shard_map/ppermute | solution.py:38
  218.0 7.8 %collective-permute-done.24 = bf16[640,256]{1,0:T(8,128)(2,1)S(1)} collective-permute-done((bf16[640,256]{1,0:T(8,128)(2,1)S(1)}, bf16[640,256]{1,0:T(8,128)(2,1)S(1)}, u32[]{:S(2)}, u32[]{:S(2)}) %collective-permute-start.24) | collective-permute-done | bytes 327712 | tf_op jit(solution)/shard_map/ppermute | solution.py:38
  225.8 3.8 %collective-permute-done.23 = bf16[640,256]{1,0:T(8,128)(2,1)S(1)} collective-permute-done((bf16[640,256]{1,0:T(8,128)(2,1)S(1)}, bf16[640,256]{1,0:T(8,128)(2,1)S(1)}, u32[]{:S(2)}, u32[]{:S(2)}) %collective-permute-start.23) | collective-permute-done | bytes 327712 | tf_op jit(solution)/shard_map/ppermute | solution.py:38
  229.6 7.7 %collective-permute-done.22 = bf16[640,256]{1,0:T(8,128)(2,1)S(1)} collective-permute-done((bf16[640,256]{1,0:T(8,128)(2,1)S(1)}, bf16[640,256]{1,0:T(8,128)(2,1)S(1)}, u32[]{:S(2)}, u32[]{:S(2)}) %collective-permute-start.22) | collective-permute-done | bytes 327712 | tf_op jit(solution)/shard_map/ppermute | solution.py:38
  237.3 1.9 fusion.5.refs_8_
  240.2 7.0 %partial.6 = (bf16[4,640,256]{2,1,0:T(8,128)(2,1)}, bf16[4,640,256]{2,1,0:T(8,128)(2,1)}) custom-call(s32[4]{0:T(128)} %iota.9.s_ref, bf16[640,1024]{1,0:T(8,128)(2,1)} %copy-done.2, bf16[640,1024]{1,0:T(8,128)(2,1)} %copy-done.1, bf16[2,2,128,1024]{3,2,1,0:T(8,128)(2,1)} %after.12.refs_0_, ...), custom_call_target="tpu_custom_call" | custom-call | flops 2684354 | bytes 8388 | tf_op jit(solution)/shard_map/partial/pallas_call | solution.py:251
  247.2 3.2 %collective-permute-done.28 = bf16[4,640,256]{2,1,0:T(8,128)(2,1)S(1)} collective-permute-done((bf16[4,640,256]{2,1,0:T(8,128)(2,1)}, bf16[4,640,256]{2,1,0:T(8,128)(2,1)S(1)}, u32[]{:S(2)}, u32[]{:S(2)}) %collective-permute-start.28) | collective-permute-done | bytes 1310752 | tf_op jit(solution)/shard_map/ppermute | solution.py:38
  250.4 2.7 add_convert_fusion
  253.2 7.1 %partial.7 = (bf16[4,640,256]{2,1,0:T(8,128)(2,1)}, bf16[4,640,256]{2,1,0:T(8,128)(2,1)}) custom-call(s32[4]{0:T(128)} %and_select_fusion.s_ref, bf16[640,1024]{1,0:T(8,128)(2,1)} %copy-done.2, bf16[640,1024]{1,0:T(8,128)(2,1)} %copy-done.1, bf16[2,2,128,1024]{3,2,1,0:T(8,128)(2,1)} %after.12.refs_0_, ...), custom_call_target="tpu_custom_call" | custom-call | flops 2684354 | bytes 8388 | tf_op jit(solution)/shard_map/partial/pallas_call | solution.py:251
  261.6 2.0 collective-permute-done.30
  263.5 2.2 fusion.11
  265.8 3.6 %collective-permute-start.33 = (bf16[640,256]{1,0:T(8,128)(2,1)}, bf16[640,256]{1,0:T(8,128)(2,1)S(1)}, u32[]{:S(2)}, u32[]{:S(2)}) collective-permute-start(bf16[640,256]{1,0:T(8,128)(2,1)} %get-tuple-element.32), channel_id=1, source_target_pairs={{0,6},{1,7},{2,0},{3,1},{4,2},{5,3},{6,4},{7,5},{8,14},{9,15},{10,... | collective-permute-start | bytes 983048 | tf_op jit(solution)/shard_map/ppermute | solution.py:38
  272.8 15.6 %collective-permute-done.33 = bf16[640,256]{1,0:T(8,128)(2,1)S(1)} collective-permute-done((bf16[640,256]{1,0:T(8,128)(2,1)}, bf16[640,256]{1,0:T(8,128)(2,1)S(1)}, u32[]{:S(2)}, u32[]{:S(2)}) %collective-permute-start.33) | collective-permute-done | bytes 327712 | tf_op jit(solution)/shard_map/ppermute | solution.py:38
  288.4 1.9 collective-permute-done.31
  292.9 2.8 collective-permute-start.34
  298.4 2.2 collective-permute-done.34
  300.7 4.2 %collective-permute-done.29 = bf16[640,128]{1,0:T(8,128)(2,1)S(1)} collective-permute-done((bf16[640,128]{1,0:T(8,128)(2,1)S(1)}, bf16[640,128]{1,0:T(8,128)(2,1)S(1)}, u32[]{:S(2)}, u32[]{:S(2)}) %collective-permute-start.29) | collective-permute-done | bytes 163872 | tf_op jit(solution)/shard_map/ppermute | solution.py:38
  (169 shorter events, 46.7 us)
Async XLA Ops:
  7.2 133.8 %all-gather.5.cloned.1.call-start = ((), (), s32[]{:S(2)}) async-start(), calls=%async_computation.5 | async-start | bytes 3276800 | tf_op jit(solution)/shard_map/all_gather | solution.py:293
  14.2 13.8 %collective-permute-start = (bf16[2,128,1024]{2,1,0:T(8,128)(2,1)}, bf16[2,128,1024]{2,1,0:T(8,128)(2,1)S(1)}, u32[]{:S(2)}, u32[]{:S(2)}) collective-permute-start(bf16[2,128,1024]{2,1,0:T(8,128)(2,1)} %get-tuple-element.17.dep_ref), channel_id=1, source_target_pairs={{0,64},{1,65},{2,66},{3,67},{4,68},{5,69},{6,70},{7,71},{8,72},{9,... | collective-permute-start | bytes 1572872 | tf_op jit(solution)/shard_map/ppermute | solution.py:38
  31.0 31.1 %collective-permute-start.2 = (bf16[2,2,128,1024]{3,2,1,0:T(8,128)(2,1)}, bf16[2,2,128,1024]{3,2,1,0:T(8,128)(2,1)S(1)}, u32[]{:S(2)}, u32[]{:S(2)}) collective-permute-start(bf16[2,2,128,1024]{3,2,1,0:T(8,128)(2,1)} %pad_maximum_fusion.refs_0_), channel_id=1, source_target_pairs={{0,16},{1,17},{2,18},{3,19},{4,20},{5,21},{6,22},{7,23},{8,24},{9,... | collective-permute-start | bytes 3145736 | tf_op jit(solution)/shard_map/ppermute | solution.py:38
  33.1 29.0 %collective-permute-start.3 = (bf16[2,2,128,1024]{3,2,1,0:T(8,128)(2,1)}, bf16[2,2,128,1024]{3,2,1,0:T(8,128)(2,1)S(1)}, u32[]{:S(2)}, u32[]{:S(2)}) collective-permute-start(bf16[2,2,128,1024]{3,2,1,0:T(8,128)(2,1)} %pad_maximum_fusion.refs_0_), channel_id=1, source_target_pairs={{0,48},{1,49},{2,50},{3,51},{4,52},{5,53},{6,54},{7,55},{8,56},{9,... | collective-permute-start | bytes 3145736 | tf_op jit(solution)/shard_map/ppermute | solution.py:38
  35.2 26.9 %all-to-all-start = ((bf16[16,32,1024]{2,1,0:T(8,128)(2,1)}), bf16[16,32,1024]{2,1,0:T(8,128)(2,1)S(1)}, u32[]{:S(2)}, u32[]{:S(2)}) async-start(bf16[16,32,1024]{2,1,0:T(8,128)(2,1)} %get-tuple-element.20.refs_1_), calls=%async_computation | async-start | bytes 2097152 | tf_op jit(solution)/shard_map/all_to_all | solution.py:304
  42.2 98.7 %all-gather.7.cloned.1.call-start = ((), (), s32[]{:S(2)}) async-start(), calls=%async_computation.6 | async-start | bytes 3276800 | tf_op jit(solution)/shard_map/all_gather | solution.py:311
  42.3 30.4 %collective-permute-start.1 = (bf16[2,320,512]{2,1,0:T(8,128)(2,1)}, bf16[2,320,512]{2,1,0:T(8,128)(2,1)}, u32[]{:S(2)}, u32[]{:S(2)}) collective-permute-start(bf16[2,320,512]{2,1,0:T(8,128)(2,1)} %param.11), channel_id=1, source_target_pairs={{0,1},{1,0},{2,3},{3,2},{4,5},{5,4},{6,7},{7,6},{8,9},{9,8},{10,11... | collective-permute-start | bytes 1966088 | tf_op jit(solution)/shard_map/ppermute | solution.py:38
  63.7 37.4 %collective-permute-start.4 = (bf16[512,1024]{1,0:T(8,128)(2,1)}, bf16[512,1024]{1,0:T(8,128)(2,1)S(1)}, u32[]{:S(2)}, u32[]{:S(2)}) collective-permute-start(bf16[512,1024]{1,0:T(8,128)(2,1)} %after.8.refs_6_), channel_id=1, source_target_pairs={{0,16},{1,17},{2,18},{3,19},{4,20},{5,21},{6,22},{7,23},{8,24},{9,... | collective-permute-start | bytes 3145736 | tf_op jit(solution)/shard_map/ppermute | solution.py:38
  65.2 35.9 %collective-permute-start.5 = (bf16[512,1024]{1,0:T(8,128)(2,1)}, bf16[512,1024]{1,0:T(8,128)(2,1)S(1)}, u32[]{:S(2)}, u32[]{:S(2)}) collective-permute-start(bf16[512,1024]{1,0:T(8,128)(2,1)} %after.8.refs_6_), channel_id=1, source_target_pairs={{0,48},{1,49},{2,50},{3,51},{4,52},{5,53},{6,54},{7,55},{8,56},{9,... | collective-permute-start | bytes 3145736 | tf_op jit(solution)/shard_map/ppermute | solution.py:38
  67.0 35.2 %collective-permute-start.6 = (bf16[512,1024]{1,0:T(8,128)(2,1)}, bf16[512,1024]{1,0:T(8,128)(2,1)S(1)}, u32[]{:S(2)}, u32[]{:S(2)}) collective-permute-start(bf16[512,1024]{1,0:T(8,128)(2,1)} %after.8.refs_6_), channel_id=1, source_target_pairs={{0,64},{1,65},{2,66},{3,67},{4,68},{5,69},{6,70},{7,71},{8,72},{9,... | collective-permute-start | bytes 3145736 | tf_op jit(solution)/shard_map/ppermute | solution.py:38
  68.7 32.5 %collective-permute-start.7 = (bf16[2,128,1024]{2,1,0:T(8,128)(2,1)S(1)}, bf16[2,128,1024]{2,1,0:T(8,128)(2,1)S(1)}, u32[]{:S(2)}, u32[]{:S(2)}) collective-permute-start(bf16[2,128,1024]{2,1,0:T(8,128)(2,1)S(1)} %slice_bitcast_fusion.3), channel_id=1, source_target_pairs={{0,16},{1,17},{2,18},{3,19},{4,20},{5,21},{6,22},{7,23},{8,24},{9,... | collective-permute-start | bytes 1572872 | tf_op jit(solution)/shard_map/ppermute | solution.py:38
  72.7 28.4 %collective-permute-start.8 = (bf16[2,128,1024]{2,1,0:T(8,128)(2,1)S(1)}, bf16[2,128,1024]{2,1,0:T(8,128)(2,1)S(1)}, u32[]{:S(2)}, u32[]{:S(2)}) collective-permute-start(bf16[2,128,1024]{2,1,0:T(8,128)(2,1)S(1)} %slice_bitcast_fusion.2), channel_id=1, source_target_pairs={{0,48},{1,49},{2,50},{3,51},{4,52},{5,53},{6,54},{7,55},{8,56},{9,... | collective-permute-start | bytes 1572872 | tf_op jit(solution)/shard_map/ppermute | solution.py:38
  104.2 166.1 %reduce-scatter.3.cloned.1.call-start = ((), (), s32[]{:S(2)}) async-start(), calls=%async_computation.3 | async-start | bytes 1638400 | tf_op jit(solution)/shard_map/reduce_scatter | solution.py:357
  104.2 36.7 %collective-permute-start.9 = (bf16[512,1024]{1,0:T(8,128)(2,1)}, bf16[512,1024]{1,0:T(8,128)(2,1)S(1)}, u32[]{:S(2)}, u32[]{:S(2)}) collective-permute-start(bf16[512,1024]{1,0:T(8,128)(2,1)} %copy-done.3), channel_id=1, source_target_pairs={{0,16},{1,17},{2,18},{3,19},{4,20},{5,21},{6,22},{7,23},{8,24},{9,... | collective-permute-start | bytes 3145736 | tf_op jit(solution)/shard_map/ppermute | solution.py:38
  105.7 35.2 %collective-permute-start.10 = (bf16[512,1024]{1,0:T(8,128)(2,1)}, bf16[512,1024]{1,0:T(8,128)(2,1)S(1)}, u32[]{:S(2)}, u32[]{:S(2)}) collective-permute-start(bf16[512,1024]{1,0:T(8,128)(2,1)} %copy-done.3), channel_id=1, source_target_pairs={{0,48},{1,49},{2,50},{3,51},{4,52},{5,53},{6,54},{7,55},{8,56},{9,... | collective-permute-start | bytes 3145736 | tf_op jit(solution)/shard_map/ppermute | solution.py:38
  109.4 31.5 %collective-permute-start.11 = (bf16[256,1024]{1,0:T(8,128)(2,1)}, bf16[256,1024]{1,0:T(8,128)(2,1)}, u32[]{:S(2)}, u32[]{:S(2)}) collective-permute-start(bf16[256,1024]{1,0:T(8,128)(2,1)} %after.10), channel_id=1, source_target_pairs={{0,16},{1,17},{2,18},{3,19},{4,20},{5,21},{6,22},{7,23},{8,24},{9,... | collective-permute-start | bytes 1572872 | tf_op jit(solution)/shard_map/ppermute | solution.py:38
  111.5 29.3 %collective-permute-start.12 = (bf16[256,1024]{1,0:T(8,128)(2,1)}, bf16[256,1024]{1,0:T(8,128)(2,1)S(1)}, u32[]{:S(2)}, u32[]{:S(2)}) collective-permute-start(bf16[256,1024]{1,0:T(8,128)(2,1)} %slice.91), channel_id=1, source_target_pairs={{0,48},{1,49},{2,50},{3,51},{4,52},{5,53},{6,54},{7,55},{8,56},{9,... | collective-permute-start | bytes 1572872 | tf_op jit(solution)/shard_map/ppermute | solution.py:38
  113.5 27.4 %collective-permute-start.13 = (bf16[2,128,1024]{2,1,0:T(8,128)(2,1)}, bf16[2,128,1024]{2,1,0:T(8,128)(2,1)S(1)}, u32[]{:S(2)}, u32[]{:S(2)}) collective-permute-start(bf16[2,128,1024]{2,1,0:T(8,128)(2,1)} %after.11), channel_id=1, source_target_pairs={{0,64},{1,65},{2,66},{3,67},{4,68},{5,69},{6,70},{7,71},{8,72},{9,... | collective-permute-start | bytes 1572872 | tf_op jit(solution)/shard_map/ppermute | solution.py:38
  148.9 19.3 %collective-permute-start.16 = (bf16[8,640,512]{2,1,0:T(8,128)(2,1)}, bf16[8,640,512]{2,1,0:T(8,128)(2,1)}, u32[]{:S(2)}, u32[]{:S(2)}) collective-permute-start(bf16[8,640,512]{2,1,0:T(8,128)(2,1)} %norm.1.refs_0_.refs_1_.refs_2_.refs_3_.refs_4_.refs_5_), channel_id=1, source_target_pairs={{0,8},{1,9},{2,10},{3,11},{4,12},{5,13},{6,14},{7,15},{8,0},{9,1},... | collective-permute-start | bytes 15728648 | tf_op jit(solution)/shard_map/ppermute | solution.py:38
  151.0 33.3 %collective-permute-start.17 = (bf16[2,2,128,1024]{3,2,1,0:T(8,128)(2,1)}, bf16[2,2,128,1024]{3,2,1,0:T(8,128)(2,1)}, u32[]{:S(2)}, u32[]{:S(2)}) collective-permute-start(bf16[2,2,128,1024]{3,2,1,0:T(8,128)(2,1)} %after.12.refs_0_), channel_id=1, source_target_pairs={{0,16},{1,17},{2,18},{3,19},{4,20},{5,21},{6,22},{7,23},{8,24},{9,... | collective-permute-start | bytes 3145736 | tf_op jit(solution)/shard_map/ppermute | solution.py:38
  151.8 32.5 %collective-permute-start.18 = (bf16[2,2,128,1024]{3,2,1,0:T(8,128)(2,1)}, bf16[2,2,128,1024]{3,2,1,0:T(8,128)(2,1)}, u32[]{:S(2)}, u32[]{:S(2)}) collective-permute-start(bf16[2,2,128,1024]{3,2,1,0:T(8,128)(2,1)} %after.12.refs_0_), channel_id=1, source_target_pairs={{0,48},{1,49},{2,50},{3,51},{4,52},{5,53},{6,54},{7,55},{8,56},{9,... | collective-permute-start | bytes 3145736 | tf_op jit(solution)/shard_map/ppermute | solution.py:38
  154.3 20.5 %collective-permute-start.14 = (bf16[256,1024]{1,0:T(8,128)(2,1)}, bf16[256,1024]{1,0:T(8,128)(2,1)}, u32[]{:S(2)}, u32[]{:S(2)}) collective-permute-start(bf16[256,1024]{1,0:T(8,128)(2,1)} %collective-permute-done.11.refs_2_), channel_id=1, source_target_pairs={{0,64},{1,65},{2,66},{3,67},{4,68},{5,69},{6,70},{7,71},{8,72},{9,... | collective-permute-start | bytes 1572872 | tf_op jit(solution)/shard_map/ppermute | solution.py:38
  154.9 24.7 %collective-permute-start.15 = (bf16[256,1024]{1,0:T(8,128)(2,1)}, bf16[256,1024]{1,0:T(8,128)(2,1)}, u32[]{:S(2)}, u32[]{:S(2)}) collective-permute-start(bf16[256,1024]{1,0:T(8,128)(2,1)} %copy-done.18), channel_id=1, source_target_pairs={{0,64},{1,65},{2,66},{3,67},{4,68},{5,69},{6,70},{7,71},{8,72},{9,... | collective-permute-start | bytes 1572872 | tf_op jit(solution)/shard_map/ppermute | solution.py:38
  163.2 21.1 %slice-start = ((s8[5242880]{0:T(1024)(128)(4,1)}), s8[4194304]{0:T(1024)(128)(4,1)S(1)}, s32[]{:S(2)}) async-start(s8[5242880]{0:T(1024)(128)(4,1)} %bitcast.54), calls=%async_computation.7 | async-start | bytes 8388608
  168.1 11.5 %copy-start.19 = (bf16[256,1024]{1,0:T(8,128)(2,1)S(1)}, bf16[256,1024]{1,0:T(8,128)(2,1)}, u32[]{:S(2)}) copy-start(bf16[256,1024]{1,0:T(8,128)(2,1)} %copy-done.18) | copy-start | bytes 1572868
  168.1 16.1 %slice-start.1 = ((s8[5242880]{0:T(1024)(128)(4,1)}), s8[1048576]{0:T(1024)(128)(4,1)S(1)}, s32[]{:S(2)}) async-start(s8[5242880]{0:T(1024)(128)(4,1)} %bitcast.54), calls=%async_computation.8 | async-start | bytes 2097152
  197.3 9.4 %collective-permute-start.19 = (bf16[4,640,256]{2,1,0:T(8,128)(2,1)}, bf16[4,640,256]{2,1,0:T(8,128)(2,1)S(1)}, u32[]{:S(2)}, u32[]{:S(2)}) collective-permute-start(bf16[4,640,256]{2,1,0:T(8,128)(2,1)} %get-tuple-element.24.refs_5_), channel_id=1, source_target_pairs={{0,8},{1,9},{2,10},{3,11},{4,12},{5,13},{6,14},{7,15},{8,0},{9,1},... | collective-permute-start | bytes 3932168 | tf_op jit(solution)/shard_map/ppermute | solution.py:38
  197.9 8.7 %copy-start.34 = (bf16[4,640,256]{2,1,0:T(8,128)(2,1)S(1)}, bf16[4,640,256]{2,1,0:T(8,128)(2,1)}, u32[]{:S(2)}) copy-start(bf16[4,640,256]{2,1,0:T(8,128)(2,1)} %get-tuple-element.23) | copy-start | bytes 3932164
  205.0 3.5 %collective-permute-start.21 = (bf16[4,640,256]{2,1,0:T(8,128)(2,1)}, bf16[4,640,256]{2,1,0:T(8,128)(2,1)}, u32[]{:S(2)}, u32[]{:S(2)}) collective-permute-start(bf16[4,640,256]{2,1,0:T(8,128)(2,1)} %get-tuple-element.26.refs_5_), channel_id=1, source_target_pairs={{0,8},{1,9},{2,10},{3,11},{4,12},{5,13},{6,14},{7,15},{8,0},{9,1},... | collective-permute-start | bytes 3932168 | tf_op jit(solution)/shard_map/ppermute | solution.py:38
  206.6 32.6 %collective-permute-start.26 = (bf16[2,128,1024]{2,1,0:T(8,128)(2,1)S(1)}, bf16[2,128,1024]{2,1,0:T(8,128)(2,1)S(1)}, u32[]{:S(2)}, u32[]{:S(2)}) collective-permute-start(bf16[2,128,1024]{2,1,0:T(8,128)(2,1)S(1)} %slice_bitcast_fusion.1), channel_id=1, source_target_pairs={{0,16},{1,17},{2,18},{3,19},{4,20},{5,21},{6,22},{7,23},{8,24},{9,... | collective-permute-start | bytes 1572872 | tf_op jit(solution)/shard_map/ppermute | solution.py:38
  208.1 88.6 %reduce-scatter.5.cloned.1.call-start = ((), (), s32[]{:S(2)}) async-start(), calls=%async_computation.4 | async-start | bytes 1638400 | tf_op jit(solution)/shard_map/reduce_scatter | solution.py:357
  210.7 28.4 %copy-start.32 = (bf16[640,256]{1,0:T(8,128)(2,1)}, bf16[640,256]{1,0:T(8,128)(2,1)S(1)}, u32[]{:S(2)}) copy-start(bf16[640,256]{1,0:T(8,128)(2,1)S(1)} %get-tuple-element.36.refs_7_) | copy-start | bytes 983044
  210.8 15.0 %collective-permute-start.24 = (bf16[640,256]{1,0:T(8,128)(2,1)S(1)}, bf16[640,256]{1,0:T(8,128)(2,1)S(1)}, u32[]{:S(2)}, u32[]{:S(2)}) collective-permute-start(bf16[640,256]{1,0:T(8,128)(2,1)S(1)} %get-tuple-element.35), channel_id=1, source_target_pairs={{0,6},{1,7},{2,0},{3,1},{4,2},{5,3},{6,4},{7,5},{8,14},{9,15},{10,... | collective-permute-start | bytes 983048 | tf_op jit(solution)/shard_map/ppermute | solution.py:38
  212.4 17.2 %collective-permute-start.23 = (bf16[640,256]{1,0:T(8,128)(2,1)S(1)}, bf16[640,256]{1,0:T(8,128)(2,1)S(1)}, u32[]{:S(2)}, u32[]{:S(2)}) collective-permute-start(bf16[640,256]{1,0:T(8,128)(2,1)S(1)} %get-tuple-element.34), channel_id=1, source_target_pairs={{0,4},{1,5},{2,6},{3,7},{4,0},{5,1},{6,2},{7,3},{8,12},{9,13},{10,... | collective-permute-start | bytes 983048 | tf_op jit(solution)/shard_map/ppermute | solution.py:38
  213.5 23.7 %collective-permute-start.22 = (bf16[640,256]{1,0:T(8,128)(2,1)S(1)}, bf16[640,256]{1,0:T(8,128)(2,1)S(1)}, u32[]{:S(2)}, u32[]{:S(2)}) collective-permute-start(bf16[640,256]{1,0:T(8,128)(2,1)S(1)} %get-tuple-element.36.refs_7_), channel_id=1, source_target_pairs={{0,2},{1,3},{2,4},{3,5},{4,6},{5,7},{6,0},{7,1},{8,10},{9,11},{10,... | collective-permute-start | bytes 983048 | tf_op jit(solution)/shard_map/ppermute | solution.py:38
  214.7 24.5 %collective-permute-start.27 = (bf16[2,128,1024]{2,1,0:T(8,128)(2,1)S(1)}, bf16[2,128,1024]{2,1,0:T(8,128)(2,1)S(1)}, u32[]{:S(2)}, u32[]{:S(2)}) collective-permute-start(bf16[2,128,1024]{2,1,0:T(8,128)(2,1)S(1)} %slice_bitcast_fusion), channel_id=1, source_target_pairs={{0,48},{1,49},{2,50},{3,51},{4,52},{5,53},{6,54},{7,55},{8,56},{9,... | collective-permute-start | bytes 1572872 | tf_op jit(solution)/shard_map/ppermute | solution.py:38
  247.2 3.2 %collective-permute-start.28 = (bf16[4,640,256]{2,1,0:T(8,128)(2,1)}, bf16[4,640,256]{2,1,0:T(8,128)(2,1)S(1)}, u32[]{:S(2)}, u32[]{:S(2)}) collective-permute-start(bf16[4,640,256]{2,1,0:T(8,128)(2,1)} %get-tuple-element.28.refs_5_), channel_id=1, source_target_pairs={{0,8},{1,9},{2,10},{3,11},{4,12},{5,13},{6,14},{7,15},{8,0},{9,1},... | collective-permute-start | bytes 3932168 | tf_op jit(solution)/shard_map/ppermute | solution.py:38
  253.2 7.2 %copy-start.27 = (bf16[640,256]{1,0:T(8,128)(2,1)S(1)}, bf16[640,256]{1,0:T(8,128)(2,1)}, u32[]{:S(2)}) copy-start(bf16[640,256]{1,0:T(8,128)(2,1)} %fusion.5.refs_8_) | copy-start | bytes 983044
  260.3 3.2 %collective-permute-start.30 = (bf16[4,640,256]{2,1,0:T(8,128)(2,1)}, bf16[4,640,256]{2,1,0:T(8,128)(2,1)S(1)}, u32[]{:S(2)}, u32[]{:S(2)}) collective-permute-start(bf16[4,640,256]{2,1,0:T(8,128)(2,1)} %get-tuple-element.30), channel_id=1, source_target_pairs={{0,8},{1,9},{2,10},{3,11},{4,12},{5,13},{6,14},{7,15},{8,0},{9,1},... | collective-permute-start | bytes 3932168 | tf_op jit(solution)/shard_map/ppermute | solution.py:38
  260.4 9.8 %collective-permute-start.25 = (bf16[640,128]{1,0:T(8,128)(2,1)S(1)}, bf16[640,128]{1,0:T(8,128)(2,1)S(1)}, u32[]{:S(2)}, u32[]{:S(2)}) collective-permute-start(bf16[640,128]{1,0:T(8,128)(2,1)S(1)} %constant_dynamic-slice_fusion.1), channel_id=1, source_target_pairs={{0,1},{1,0},{2,3},{3,2},{4,5},{5,4},{6,7},{7,6},{8,9},{9,8},{10,11... | collective-permute-start | bytes 491528 | tf_op jit(solution)/shard_map/ppermute | solution.py:38
  265.8 22.6 %collective-permute-start.33 = (bf16[640,256]{1,0:T(8,128)(2,1)}, bf16[640,256]{1,0:T(8,128)(2,1)S(1)}, u32[]{:S(2)}, u32[]{:S(2)}) collective-permute-start(bf16[640,256]{1,0:T(8,128)(2,1)} %get-tuple-element.32), channel_id=1, source_target_pairs={{0,6},{1,7},{2,0},{3,1},{4,2},{5,3},{6,4},{7,5},{8,14},{9,15},{10,... | collective-permute-start | bytes 983048 | tf_op jit(solution)/shard_map/ppermute | solution.py:38
  269.4 19.0 %collective-permute-start.32 = (bf16[640,256]{1,0:T(8,128)(2,1)}, bf16[640,256]{1,0:T(8,128)(2,1)S(1)}, u32[]{:S(2)}, u32[]{:S(2)}) collective-permute-start(bf16[640,256]{1,0:T(8,128)(2,1)} %get-tuple-element.33), channel_id=1, source_target_pairs={{0,4},{1,5},{2,6},{3,7},{4,0},{5,1},{6,2},{7,3},{8,12},{9,13},{10,... | collective-permute-start | bytes 983048 | tf_op jit(solution)/shard_map/ppermute | solution.py:38
  269.4 20.9 %collective-permute-start.31 = (bf16[640,256]{1,0:T(8,128)(2,1)S(1)}, bf16[640,256]{1,0:T(8,128)(2,1)}, u32[]{:S(2)}, u32[]{:S(2)}) collective-permute-start(bf16[640,256]{1,0:T(8,128)(2,1)S(1)} %get-tuple-element.31), channel_id=1, source_target_pairs={{0,2},{1,3},{2,4},{3,5},{4,6},{5,7},{6,0},{7,1},{8,10},{9,11},{10,... | collective-permute-start | bytes 983048 | tf_op jit(solution)/shard_map/ppermute | solution.py:38
  270.2 21.3 %copy-start.35 = (bf16[640,128]{1,0:T(8,128)(2,1)}, bf16[640,128]{1,0:T(8,128)(2,1)S(1)}, u32[]{:S(2)}) copy-start(bf16[640,128]{1,0:T(8,128)(2,1)S(1)} %collective-permute-done.25.refs_2_) | copy-start | bytes 491524
  271.3 24.4 %copy-start.37 = (bf16[1,640,256]{2,1,0:T(8,128)(2,1)S(1)}, bf16[1,640,256]{2,1,0:T(8,128)(2,1)}, u32[]{:S(2)}) copy-start(bf16[1,640,256]{2,1,0:T(8,128)(2,1)} %reduce-scatter.3.cloned.1.call-done) | copy-start | bytes 983044
  271.3 21.0 %collective-permute-start.20 = (bf16[640,128]{1,0:T(8,128)(2,1)S(1)}, bf16[640,128]{1,0:T(8,128)(2,1)S(1)}, u32[]{:S(2)}, u32[]{:S(2)}) collective-permute-start(bf16[640,128]{1,0:T(8,128)(2,1)S(1)} %dynamic-slice_bitcast_fusion.1), channel_id=1, source_target_pairs={{0,1},{1,0},{2,3},{3,2},{4,5},{5,4},{6,7},{7,6},{8,9},{9,8},{10,11... | collective-permute-start | bytes 491528 | tf_op jit(solution)/shard_map/ppermute | solution.py:38
  292.9 7.7 %collective-permute-start.34 = (bf16[640,128]{1,0:T(8,128)(2,1)}, bf16[640,128]{1,0:T(8,128)(2,1)S(1)}, u32[]{:S(2)}, u32[]{:S(2)}) collective-permute-start(bf16[640,128]{1,0:T(8,128)(2,1)} %after.13), channel_id=1, source_target_pairs={{0,1},{1,0},{2,3},{3,2},{4,5},{5,4},{6,7},{7,6},{8,9},{9,8},{10,11... | collective-permute-start | bytes 491528 | tf_op jit(solution)/shard_map/ppermute | solution.py:38
  297.6 7.3 %collective-permute-start.29 = (bf16[640,128]{1,0:T(8,128)(2,1)S(1)}, bf16[640,128]{1,0:T(8,128)(2,1)S(1)}, u32[]{:S(2)}, u32[]{:S(2)}) collective-permute-start(bf16[640,128]{1,0:T(8,128)(2,1)S(1)} %dynamic-slice_bitcast_fusion), channel_id=1, source_target_pairs={{0,1},{1,0},{2,3},{3,2},{4,5},{5,4},{6,7},{7,6},{8,9},{9,8},{10,11... | collective-permute-start | bytes 491528 | tf_op jit(solution)/shard_map/ppermute | solution.py:38
  (33 other events, 78.8 us)
Sparse Core Ops, SparseCore 0:
  9.7 39.2 all-gather.4
  104.3 32.4 all-gather.6
  208.2 33.5 reduce-scatter.2
  253.3 34.7 reduce-scatter.4

commit v8 on v7

--- a/solution.py
+++ b/solution.py
@@ -296,7 +296,7 @@
     down_half, down_a = down_step(0, down_args)
     ylo_a = send(down_a, ylo=1)
     up_updated, columns = up_step(up_master, up_gradient, up_first, up_second, down_a)
-    ylo_a = after(ylo_a, columns)
+    ylo_a = after(ylo_a, columns, tokens_b)
     down_updated, down_b = down_step(1, down_args, (down_half,), (ylo_a,))
 
     st_a = jnp.stack([down_a, ylo_a])
@@ -308,7 +308,7 @@
 
     u1 = send(u0, ylo=1)
     low0, high0 = both_ways(u0, u0)
-    feats_b = lax.all_gather(after(tokens_b, low0, high0, u1, *opp_a), "x", axis=0)
+    feats_b = lax.all_gather(after(tokens_b, u0), "x", axis=0)
     down_b = after(down_b, u1)
     ylo_b = send(down_b, ylo=1)
     low1, high1 = both_ways(u1, u1)
@@ -320,7 +320,7 @@
     gains = norm_gain.reshape(4, 2, 512)
     gains = jnp.concatenate([lax.dynamic_index_in_dim(gains, k, 1, keepdims=False) for k in (yhi, 1 - yhi)])
     feats_a, feats_b = feats_a.reshape(4, 640, 512), feats_b.reshape(4, 640, 512)
-    normed = norm_of(feats_a, feats_b, gains, (low1, high1, *opp0, ylo_b))
+    normed = norm_of(feats_a, feats_b, gains, (low0, high0, u1, *opp_a))
     normed_sib = send(normed, core=1)
 
     where = lax.dynamic_index_in_dim(jnp.asarray(SLOTS), (ylo * 4 + z) * 2 + yhi, 0, keepdims=False)

time: 315 us -> 318 us (level)
  waiting for transfers between devices: 125 us -> 131 us
  starting transfers between devices: 51.7 us -> 47.7 us
  Pallas kernels: 75.4 us -> 79.3 us
    unnamed x83 -> x55, local copies, waits for them, and re-layouts: 17.3 us -> 13.1 us
    pallas_call x2, Pallas kernels: 11.5 us -> 15.1 us  [hidden_first(): pl.pallas_call(first_kernel, out_shape=jax.ShapeDtypeStruct((640, 1024),...]
    ppermute x35, waiting for transfers between devices: 114 us -> 118 us  [send(): return lax.ppermute(v, AXES, shifted(**steps))]
  transfers between devices with their start and end apart: 40 -> 40, of which waited for: 16 -> 17; matrix products, arithmetic and copies ran while one was open for 9% -> 9% of each run, Pallas kernels for 18% -> 19%
where the time goes in v8:
time: 318 us; the launch traced here: 317 us
  waiting for transfers between devices  131 us (41%)
  Pallas kernels  79.3 us (25%)
  starting transfers between devices  47.7 us (15%)
  local copies, waits for them, and re-layouts  25.1 us (8%)
  other arithmetic  19.3 us (6%)
  between operations  14.1 us (4%)
    ppermute x35, waiting for transfers between devices, send(): return lax.ppermute(v, AXES, shifted(**steps))  118 us
    ppermute x35, starting transfers between devices, send(): return lax.ppermute(v, AXES, shifted(**steps))  41.8 us
    pallas_call x4, Pallas kernels, partial_of(): pl.pallas_call(partial_kernel, out_shape=(shape, shape), grid_spec=pltpu....  28.2 us
    pallas_call x2, Pallas kernels, hidden_first(): pl.pallas_call(first_kernel, out_shape=jax.ShapeDtypeStruct((640, 1024),...  15.1 us
    unnamed x55, local copies, waits for them, and re-layouts  13.1 us
    all_to_all x1, waiting for transfers between devices, body(): lax.all_to_all(columns, ('core', 'x', 'yhi'), 0, 0, tiled=True)  13 us
    pallas_call x2, Pallas kernels, down_step(): pl.pallas_call(down_kernel, out_shape=(jax.ShapeDtypeStruct((128, D), jnp...  12.7 us
    convert_element_type x8, other arithmetic, body(): (a.astype(jnp.float32) + b.astype(jnp.float32)).astype(jnp.bfloat16)  9.74 us
  transfers between devices with their start and end apart: 40, of which 17 were waited for; matrix products, arithmetic and copies ran while one was open for 9% of the time, Pallas kernels for 19%

profile of v8, /device:TPU:0, one launch (start us, length us, event | category | flops | bytes accessed | tf_op | source)
XLA Modules:
  0.0 316.9 jit_solution(5513813078073613911)
XLA Ops:
  7.9 3.4 %collective-permute-start.1 = (bf16[2,320,512]{2,1,0:T(8,128)(2,1)}, bf16[2,320,512]{2,1,0:T(8,128)(2,1)S(1)}, u32[]{:S(2)}, u32[]{:S(2)}) collective-permute-start(bf16[2,320,512]{2,1,0:T(8,128)(2,1)} %param.11), channel_id=1, source_target_pairs={{0,1},{1,0},{2,3},{3,2},{4,5},{5,4},{6,7},{7,6},{8,9},{9,8},{10,11... | collective-permute-start | bytes 1966088 | tf_op jit(solution)/shard_map/ppermute | solution.py:38
  11.3 6.3 %adam_down.2 = (f32[128,4096]{1,0:T(8,128)}, bf16[2,128,1024]{2,1,0:T(8,128)(2,1)}) custom-call(f32[128,4096]{1,0:T(8,128)} %w_ref.5, bf16[128,4096]{1,0:T(8,128)(2,1)} %g_ref.5, f32[128,4096]{1,0:T(8,128)} %m_ref.5, f32[128,4096]{1,0:T(8,128)} %v_ref.5), custom_call_target="tpu_custom_call" | custom-call | flops 7864 | bytes 5242 | tf_op jit(solution)/shard_map/adam_down/pallas_call | solution.py:110
  18.3 7.7 %adam_up.1 = (f32[32,16384]{1,0:T(8,128)}, bf16[16,32,1024]{2,1,0:T(8,128)(2,1)}) custom-call(f32[32,16384]{1,0:T(8,128)} %w_ref.4, bf16[32,16384]{1,0:T(8,128)(2,1)} %g_ref.4, f32[32,16384]{1,0:T(8,128)} %m_ref.4, f32[32,16384]{1,0:T(8,128)} %v_ref.4, bf16[2,128,1024]{2,1,0:T(8,128)(2,1)} %get-tuple-element.17.dep_ref), custom_call_target="tpu_custom_call" | custom-call | flops 15728 | bytes 10485 | tf_op jit(solution)/shard_map/adam_up/pallas_call | solution.py:84
  26.0 11.9 %collective-permute-done.refs_0_ = bf16[2,128,1024]{2,1,0:T(8,128)(2,1)S(1)} collective-permute-done((bf16[2,128,1024]{2,1,0:T(8,128)(2,1)}, bf16[2,128,1024]{2,1,0:T(8,128)(2,1)S(1)}, u32[]{:S(2)}, u32[]{:S(2)}) %collective-permute-start) | collective-permute-done | bytes 524320 | tf_op jit(solution)/shard_map/ppermute | solution.py:38
  39.9 2.1 pad_maximum_fusion.refs_0_
  42.0 1.9 collective-permute-start.2
  44.0 2.1 collective-permute-start.3
  46.1 5.7 %all-to-all-start = ((bf16[16,32,1024]{2,1,0:T(8,128)(2,1)}), bf16[16,32,1024]{2,1,0:T(8,128)(2,1)S(1)}, u32[]{:S(2)}, u32[]{:S(2)}) async-start(bf16[16,32,1024]{2,1,0:T(8,128)(2,1)} %get-tuple-element.20.refs_1_), calls=%async_computation | async-start | bytes 2097152 | tf_op jit(solution)/shard_map/all_to_all | solution.py:304
  51.8 6.4 %adam_down.3 = (f32[128,4096]{1,0:T(8,128)}, bf16[2,128,1024]{2,1,0:T(8,128)(2,1)}) custom-call(f32[128,4096]{1,0:T(8,128)} %w_ref.5, bf16[128,4096]{1,0:T(8,128)(2,1)} %g_ref.5, f32[128,4096]{1,0:T(8,128)} %m_ref.5, f32[128,4096]{1,0:T(8,128)} %v_ref.5, f32[128,4096]{1,0:T(8,128)} %get-tuple-element.19.refs_0_, ...), custom_call_target="tpu_custom_call", output_to_operand_aliasing={{0}: (4, {})} | custom-call | flops 7864 | bytes 5242 | tf_op jit(solution)/shard_map/adam_down/pallas_call | solution.py:110
  58.2 13.0 %all-to-all-done = bf16[16,32,1024]{2,1,0:T(8,128)(2,1)S(1)} async-done(((bf16[16,32,1024]{2,1,0:T(8,128)(2,1)}), bf16[16,32,1024]{2,1,0:T(8,128)(2,1)S(1)}, u32[]{:S(2)}, u32[]{:S(2)}) %all-to-all-start) | async-done | bytes 1048608 | tf_op jit(solution)/shard_map/all_to_all | solution.py:304
  74.1 3.2 %collective-permute-start.5 = (bf16[512,1024]{1,0:T(8,128)(2,1)S(1)}, bf16[512,1024]{1,0:T(8,128)(2,1)S(1)}, u32[]{:S(2)}, u32[]{:S(2)}) collective-permute-start(bf16[512,1024]{1,0:T(8,128)(2,1)S(1)} %copy-done.4), channel_id=1, source_target_pairs={{0,48},{1,49},{2,50},{3,51},{4,52},{5,53},{6,54},{7,55},{8,56},{9,... | collective-permute-start | bytes 3145736 | tf_op jit(solution)/shard_map/ppermute | solution.py:38
  77.4 1.9 slice_bitcast_fusion.3
  81.2 3.2 %collective-permute-start.8 = (bf16[2,128,1024]{2,1,0:T(8,128)(2,1)}, bf16[2,128,1024]{2,1,0:T(8,128)(2,1)}, u32[]{:S(2)}, u32[]{:S(2)}) collective-permute-start(bf16[2,128,1024]{2,1,0:T(8,128)(2,1)} %slice_bitcast_fusion.2), channel_id=1, source_target_pairs={{0,48},{1,49},{2,50},{3,51},{4,52},{5,53},{6,54},{7,55},{8,56},{9,... | collective-permute-start | bytes 1572872 | tf_op jit(solution)/shard_map/ppermute | solution.py:38
  85.1 25.3 %collective-permute-done.7.refs_3_.refs_2_ = bf16[2,128,1024]{2,1,0:T(8,128)(2,1)} collective-permute-done((bf16[2,128,1024]{2,1,0:T(8,128)(2,1)}, bf16[2,128,1024]{2,1,0:T(8,128)(2,1)}, u32[]{:S(2)}, u32[]{:S(2)}) %collective-permute-start.7) | collective-permute-done | bytes 524320 | tf_op jit(solution)/shard_map/ppermute | solution.py:38
  111.7 6.2 %norm.1.refs_0_.refs_1_.refs_2_.refs_3_.refs_4_.refs_5_ = bf16[8,640,512]{2,1,0:T(8,128)(2,1)} custom-call(bf16[4,640,512]{2,1,0:T(8,128)(2,1)} %bitcast.59, bf16[4,640,512]{2,1,0:T(8,128)(2,1)} %bitcast.60, f32[8,512]{1,0:T(8,128)} %pad_maximum_fusion.3.g_ref, bf16[512,1024]{1,0:T(8,128)(2,1)} %copy-done.5, bf16[512,1024]{1,0:T(8,128)(2,1)} %copy-done.7, ...), custom_call_target="tpu_custom_call" | custom-call | flops 20971 | bytes 10485 | tf_op jit(solution)/shard_map/norm/pallas_call | solution.py:145
  118.4 2.9 collective-permute-start.10
  124.1 8.4 %collective-permute-done.16 = bf16[2,128,1024]{2,1,0:T(8,128)(2,1)} collective-permute-done((bf16[2,128,1024]{2,1,0:T(8,128)(2,1)}, bf16[2,128,1024]{2,1,0:T(8,128)(2,1)}, u32[]{:S(2)}, u32[]{:S(2)}) %collective-permute-start.16) | collective-permute-done | bytes 524320 | tf_op jit(solution)/shard_map/ppermute | solution.py:38
  132.6 2.9 collective-permute-start.12
  135.5 2.1 pad_maximum_fusion.1.refs_0_
  137.6 7.8 %collective-permute-done.9.refs_9_.refs_1_ = bf16[512,1024]{1,0:T(8,128)(2,1)} collective-permute-done((bf16[512,1024]{1,0:T(8,128)(2,1)}, bf16[512,1024]{1,0:T(8,128)(2,1)}, u32[]{:S(2)}, u32[]{:S(2)}) %collective-permute-start.9) | collective-permute-done | bytes 1048608 | tf_op jit(solution)/shard_map/ppermute | solution.py:38
  145.5 11.2 %collective-permute-done.11.refs_2_ = bf16[256,1024]{1,0:T(8,128)(2,1)} collective-permute-done((bf16[256,1024]{1,0:T(8,128)(2,1)}, bf16[256,1024]{1,0:T(8,128)(2,1)}, u32[]{:S(2)}, u32[]{:S(2)}) %collective-permute-start.11) | collective-permute-done | bytes 524320 | tf_op jit(solution)/shard_map/ppermute | solution.py:38
  158.5 2.0 collective-permute-start.14
  161.2 2.5 copy-done
  163.6 7.3 %hidden_first.2.refs_6_.acc_ref = f32[640,1024]{1,0:T(8,128)S(1)} custom-call(s32[16]{0:T(128)S(1)} %fusion.17.s_ref, bf16[8,640,512]{2,1,0:T(8,128)(2,1)S(1)} %copy-done, bf16[8,640,512]{2,1,0:T(8,128)(2,1)S(1)} %copy-done, bf16[8,640,512]{2,1,0:T(8,128)(2,1)S(1)} %copy-done, bf16[8,640,512]{2,1,0:T(8,128)(2,1)S(1)} %copy-done, ...), custom_call_target="tpu_custom_call" | custom-call | flops 4026531 | bytes 14680 | tf_op jit(solution)/shard_map/hidden_first/pallas_call | solution.py:193
  171.0 7.8 %hidden_first.3.acc_ref = f32[640,1024]{1,0:T(8,128)S(1)} custom-call(s32[16]{0:T(128)S(1)} %fusion.17.s_ref, bf16[8,640,512]{2,1,0:T(8,128)(2,1)} %collective-permute-done.15.refs_0_.refs_1_.refs_2_.refs_3_.refs_4_.refs_5_, bf16[8,640,512]{2,1,0:T(8,128)(2,1)} %collective-permute-done.15.refs_0_.refs_1_.refs_2_.refs_3_.refs_4_.refs_5_, ...), custom_call_target="tpu_custom_call" | custom-call | flops 4026531 | bytes 14680 | tf_op jit(solution)/shard_map/hidden_first/pallas_call | solution.py:193
  178.8 3.9 %collective-permute-done.14.refs_5_ = bf16[256,1024]{1,0:T(8,128)(2,1)} collective-permute-done((bf16[256,1024]{1,0:T(8,128)(2,1)}, bf16[256,1024]{1,0:T(8,128)(2,1)}, u32[]{:S(2)}, u32[]{:S(2)}) %collective-permute-start.14) | collective-permute-done | bytes 524320 | tf_op jit(solution)/shard_map/ppermute | solution.py:38
  182.7 4.8 %hidden_last.2.refs_6_.sib_ref = bf16[640,1024]{1,0:T(8,128)(2,1)S(1)} custom-call(s32[16]{0:T(128)S(1)} %fusion.17.s_ref, f32[640,1024]{1,0:T(8,128)S(1)} %hidden_first.3.acc_ref, bf16[8,640,512]{2,1,0:T(8,128)(2,1)} %collective-permute-done.15.refs_0_.refs_1_.refs_2_.refs_3_.refs_4_.refs_5_, ...), custom_call_target="tpu_custom_call" | custom-call | flops 1342177 | bytes 8388 | tf_op jit(solution)/shard_map/hidden_last/pallas_call | solution.py:211
  187.6 4.6 %hidden_last.3.own_ref = bf16[640,1024]{1,0:T(8,128)(2,1)S(1)} custom-call(s32[16]{0:T(128)S(1)} %fusion.17.s_ref, f32[640,1024]{1,0:T(8,128)S(1)} %hidden_first.2.refs_6_.acc_ref, bf16[8,640,512]{2,1,0:T(8,128)(2,1)S(1)} %bitcast.55, bf16[8,640,512]{2,1,0:T(8,128)(2,1)S(1)} %bitcast.55, bf16[256,1024]{1,0:T(8,128)(2,1)} %collective-permute-done.11.refs_2_, ...), custom_call_target="tpu_custom_call" | custom-call | flops 1342177 | bytes 8388 | tf_op jit(solution)/shard_map/hidden_last/pallas_call | solution.py:211
  193.8 7.0 %partial.4 = (bf16[4,640,256]{2,1,0:T(8,128)(2,1)}, bf16[4,640,256]{2,1,0:T(8,128)(2,1)}) custom-call(s32[4]{0:T(128)} %iota.7.s_ref, bf16[640,1024]{1,0:T(8,128)(2,1)} %copy-done.2, bf16[640,1024]{1,0:T(8,128)(2,1)} %copy-done.1, bf16[2,2,128,1024]{3,2,1,0:T(8,128)(2,1)} %pad_maximum_fusion.refs_0_, bf16[2,2,128,1024]{3,2,1,0:T(8,128)(2,1)} %copy-done.9, ...), custom_call_target="tpu_custom_call" | custom-call | flops 2684354 | bytes 8388 | tf_op jit(solution)/shard_map/partial/pallas_call | solution.py:251
  201.3 7.1 %partial.5 = (bf16[4,640,256]{2,1,0:T(8,128)(2,1)}, bf16[4,640,256]{2,1,0:T(8,128)(2,1)}) custom-call(s32[4]{0:T(128)} %and_select_fusion.s_ref, bf16[640,1024]{1,0:T(8,128)(2,1)} %copy-done.2, bf16[640,1024]{1,0:T(8,128)(2,1)} %copy-done.1, bf16[2,2,128,1024]{3,2,1,0:T(8,128)(2,1)} %pad_maximum_fusion.refs_0_, bf16[2,2,128,1024]{3,2,1,0:T(8,128)(2,1)} %copy-done.9, ...), custom_call_target="tpu_custom_call" | custom-call | flops 2684354 | bytes 8388 | tf_op jit(solution)/shard_map/partial/pallas_call | solution.py:251
  214.4 2.0 collective-permute-start.24
  218.6 3.0 collective-permute-start.27
  221.6 8.3 %collective-permute-done.24 = bf16[640,256]{1,0:T(8,128)(2,1)S(1)} collective-permute-done((bf16[640,256]{1,0:T(8,128)(2,1)S(1)}, bf16[640,256]{1,0:T(8,128)(2,1)S(1)}, u32[]{:S(2)}, u32[]{:S(2)}) %collective-permute-start.24) | collective-permute-done | bytes 327712 | tf_op jit(solution)/shard_map/ppermute | solution.py:38
  229.9 4.4 %collective-permute-done.23 = bf16[640,256]{1,0:T(8,128)(2,1)S(1)} collective-permute-done((bf16[640,256]{1,0:T(8,128)(2,1)S(1)}, bf16[640,256]{1,0:T(8,128)(2,1)S(1)}, u32[]{:S(2)}, u32[]{:S(2)}) %collective-permute-start.23) | collective-permute-done | bytes 327712 | tf_op jit(solution)/shard_map/ppermute | solution.py:38
  234.2 6.8 %collective-permute-done.22 = bf16[640,256]{1,0:T(8,128)(2,1)S(1)} collective-permute-done((bf16[640,256]{1,0:T(8,128)(2,1)S(1)}, bf16[640,256]{1,0:T(8,128)(2,1)S(1)}, u32[]{:S(2)}, u32[]{:S(2)}) %collective-permute-start.22) | collective-permute-done | bytes 327712 | tf_op jit(solution)/shard_map/ppermute | solution.py:38
  241.0 1.9 fusion.5.refs_8_
  243.9 7.1 %partial.6 = (bf16[4,640,256]{2,1,0:T(8,128)(2,1)}, bf16[4,640,256]{2,1,0:T(8,128)(2,1)}) custom-call(s32[4]{0:T(128)} %iota.9.s_ref, bf16[640,1024]{1,0:T(8,128)(2,1)} %copy-done.2, bf16[640,1024]{1,0:T(8,128)(2,1)} %copy-done.1, bf16[2,2,128,1024]{3,2,1,0:T(8,128)(2,1)} %after.12.refs_0_, ...), custom_call_target="tpu_custom_call" | custom-call | flops 2684354 | bytes 8388 | tf_op jit(solution)/shard_map/partial/pallas_call | solution.py:251
  251.0 3.2 %collective-permute-done.28 = bf16[4,640,256]{2,1,0:T(8,128)(2,1)S(1)} collective-permute-done((bf16[4,640,256]{2,1,0:T(8,128)(2,1)}, bf16[4,640,256]{2,1,0:T(8,128)(2,1)S(1)}, u32[]{:S(2)}, u32[]{:S(2)}) %collective-permute-start.28) | collective-permute-done | bytes 1310752 | tf_op jit(solution)/shard_map/ppermute | solution.py:38
  254.2 2.7 add_convert_fusion
  257.0 7.1 %partial.7 = (bf16[4,640,256]{2,1,0:T(8,128)(2,1)}, bf16[4,640,256]{2,1,0:T(8,128)(2,1)}) custom-call(s32[4]{0:T(128)} %and_select_fusion.s_ref, bf16[640,1024]{1,0:T(8,128)(2,1)} %copy-done.2, bf16[640,1024]{1,0:T(8,128)(2,1)} %copy-done.1, bf16[2,2,128,1024]{3,2,1,0:T(8,128)(2,1)} %after.12.refs_0_, ...), custom_call_target="tpu_custom_call" | custom-call | flops 2684354 | bytes 8388 | tf_op jit(solution)/shard_map/partial/pallas_call | solution.py:251
  265.0 2.3 collective-permute-done.30
  267.3 2.2 fusion.11
  269.6 4.2 %collective-permute-start.33 = (bf16[640,256]{1,0:T(8,128)(2,1)}, bf16[640,256]{1,0:T(8,128)(2,1)S(1)}, u32[]{:S(2)}, u32[]{:S(2)}) collective-permute-start(bf16[640,256]{1,0:T(8,128)(2,1)} %get-tuple-element.32), channel_id=1, source_target_pairs={{0,6},{1,7},{2,0},{3,1},{4,2},{5,3},{6,4},{7,5},{8,14},{9,15},{10,... | collective-permute-start | bytes 983048 | tf_op jit(solution)/shard_map/ppermute | solution.py:38
  276.4 15.6 %collective-permute-done.33 = bf16[640,256]{1,0:T(8,128)(2,1)S(1)} collective-permute-done((bf16[640,256]{1,0:T(8,128)(2,1)}, bf16[640,256]{1,0:T(8,128)(2,1)S(1)}, u32[]{:S(2)}, u32[]{:S(2)}) %collective-permute-start.33) | collective-permute-done | bytes 327712 | tf_op jit(solution)/shard_map/ppermute | solution.py:38
  292.0 2.2 collective-permute-done.31
  296.9 2.4 collective-permute-start.34
  302.4 2.1 collective-permute-done.34
  304.6 3.9 %collective-permute-done.29 = bf16[640,128]{1,0:T(8,128)(2,1)S(1)} collective-permute-done((bf16[640,128]{1,0:T(8,128)(2,1)S(1)}, bf16[640,128]{1,0:T(8,128)(2,1)S(1)}, u32[]{:S(2)}, u32[]{:S(2)}) %collective-permute-start.29) | collective-permute-done | bytes 163872 | tf_op jit(solution)/shard_map/ppermute | solution.py:38
  (141 shorter events, 38.6 us)
Async XLA Ops:
  7.2 103.2 %all-gather.5.cloned.1.call-start = ((), (), s32[]{:S(2)}) async-start(), calls=%async_computation.5 | async-start | bytes 3276800 | tf_op jit(solution)/shard_map/all_gather | solution.py:293
  7.9 29.9 %collective-permute-start.1 = (bf16[2,320,512]{2,1,0:T(8,128)(2,1)}, bf16[2,320,512]{2,1,0:T(8,128)(2,1)S(1)}, u32[]{:S(2)}, u32[]{:S(2)}) collective-permute-start(bf16[2,320,512]{2,1,0:T(8,128)(2,1)} %param.11), channel_id=1, source_target_pairs={{0,1},{1,0},{2,3},{3,2},{4,5},{5,4},{6,7},{7,6},{8,9},{9,8},{10,11... | collective-permute-start | bytes 1966088 | tf_op jit(solution)/shard_map/ppermute | solution.py:38
  17.6 20.2 %collective-permute-start = (bf16[2,128,1024]{2,1,0:T(8,128)(2,1)}, bf16[2,128,1024]{2,1,0:T(8,128)(2,1)S(1)}, u32[]{:S(2)}, u32[]{:S(2)}) collective-permute-start(bf16[2,128,1024]{2,1,0:T(8,128)(2,1)} %get-tuple-element.17.dep_ref), channel_id=1, source_target_pairs={{0,64},{1,65},{2,66},{3,67},{4,68},{5,69},{6,70},{7,71},{8,72},{9,... | collective-permute-start | bytes 1572872 | tf_op jit(solution)/shard_map/ppermute | solution.py:38
  42.0 29.1 %collective-permute-start.2 = (bf16[2,2,128,1024]{3,2,1,0:T(8,128)(2,1)}, bf16[2,2,128,1024]{3,2,1,0:T(8,128)(2,1)S(1)}, u32[]{:S(2)}, u32[]{:S(2)}) collective-permute-start(bf16[2,2,128,1024]{3,2,1,0:T(8,128)(2,1)} %pad_maximum_fusion.refs_0_), channel_id=1, source_target_pairs={{0,16},{1,17},{2,18},{3,19},{4,20},{5,21},{6,22},{7,23},{8,24},{9,... | collective-permute-start | bytes 3145736 | tf_op jit(solution)/shard_map/ppermute | solution.py:38
  44.0 27.2 %collective-permute-start.3 = (bf16[2,2,128,1024]{3,2,1,0:T(8,128)(2,1)}, bf16[2,2,128,1024]{3,2,1,0:T(8,128)(2,1)S(1)}, u32[]{:S(2)}, u32[]{:S(2)}) collective-permute-start(bf16[2,2,128,1024]{3,2,1,0:T(8,128)(2,1)} %pad_maximum_fusion.refs_0_), channel_id=1, source_target_pairs={{0,48},{1,49},{2,50},{3,51},{4,52},{5,53},{6,54},{7,55},{8,56},{9,... | collective-permute-start | bytes 3145736 | tf_op jit(solution)/shard_map/ppermute | solution.py:38
  46.1 25.1 %all-to-all-start = ((bf16[16,32,1024]{2,1,0:T(8,128)(2,1)}), bf16[16,32,1024]{2,1,0:T(8,128)(2,1)S(1)}, u32[]{:S(2)}, u32[]{:S(2)}) async-start(bf16[16,32,1024]{2,1,0:T(8,128)(2,1)} %get-tuple-element.20.refs_1_), calls=%async_computation | async-start | bytes 2097152 | tf_op jit(solution)/shard_map/all_to_all | solution.py:304
  51.8 58.7 %all-gather.7.cloned.1.call-start = ((), (), s32[]{:S(2)}) async-start(), calls=%async_computation.6 | async-start | bytes 3276800 | tf_op jit(solution)/shard_map/all_gather | solution.py:311
  72.8 11.6 %copy-start.24 = (f32[4096]{0:T(1024)S(1)}, f32[4096]{0:T(1024)}, u32[]{:S(2)}) copy-start(f32[4096]{0:T(1024)} %param.12) | copy-start | bytes 49156
  72.9 201.8 %reduce-scatter.3.cloned.1.call-start = ((), (), s32[]{:S(2)}) async-start(), calls=%async_computation.3 | async-start | bytes 1638400 | tf_op jit(solution)/shard_map/reduce_scatter | solution.py:357
  74.1 36.3 %collective-permute-start.4 = (bf16[512,1024]{1,0:T(8,128)(2,1)S(1)}, bf16[512,1024]{1,0:T(8,128)(2,1)S(1)}, u32[]{:S(2)}, u32[]{:S(2)}) collective-permute-start(bf16[512,1024]{1,0:T(8,128)(2,1)S(1)} %copy-done.4), channel_id=1, source_target_pairs={{0,16},{1,17},{2,18},{3,19},{4,20},{5,21},{6,22},{7,23},{8,24},{9,... | collective-permute-start | bytes 3145736 | tf_op jit(solution)/shard_map/ppermute | solution.py:38
  74.1 36.3 %collective-permute-start.5 = (bf16[512,1024]{1,0:T(8,128)(2,1)S(1)}, bf16[512,1024]{1,0:T(8,128)(2,1)S(1)}, u32[]{:S(2)}, u32[]{:S(2)}) collective-permute-start(bf16[512,1024]{1,0:T(8,128)(2,1)S(1)} %copy-done.4), channel_id=1, source_target_pairs={{0,48},{1,49},{2,50},{3,51},{4,52},{5,53},{6,54},{7,55},{8,56},{9,... | collective-permute-start | bytes 3145736 | tf_op jit(solution)/shard_map/ppermute | solution.py:38
  77.3 33.1 %collective-permute-start.6 = (bf16[512,1024]{1,0:T(8,128)(2,1)S(1)}, bf16[512,1024]{1,0:T(8,128)(2,1)}, u32[]{:S(2)}, u32[]{:S(2)}) collective-permute-start(bf16[512,1024]{1,0:T(8,128)(2,1)S(1)} %copy-done.4), channel_id=1, source_target_pairs={{0,64},{1,65},{2,66},{3,67},{4,68},{5,69},{6,70},{7,71},{8,72},{9,... | collective-permute-start | bytes 3145736 | tf_op jit(solution)/shard_map/ppermute | solution.py:38
  79.3 31.1 %collective-permute-start.7 = (bf16[2,128,1024]{2,1,0:T(8,128)(2,1)}, bf16[2,128,1024]{2,1,0:T(8,128)(2,1)}, u32[]{:S(2)}, u32[]{:S(2)}) collective-permute-start(bf16[2,128,1024]{2,1,0:T(8,128)(2,1)} %slice_bitcast_fusion.3), channel_id=1, source_target_pairs={{0,16},{1,17},{2,18},{3,19},{4,20},{5,21},{6,22},{7,23},{8,24},{9,... | collective-permute-start | bytes 1572872 | tf_op jit(solution)/shard_map/ppermute | solution.py:38
  81.2 29.2 %collective-permute-start.8 = (bf16[2,128,1024]{2,1,0:T(8,128)(2,1)}, bf16[2,128,1024]{2,1,0:T(8,128)(2,1)}, u32[]{:S(2)}, u32[]{:S(2)}) collective-permute-start(bf16[2,128,1024]{2,1,0:T(8,128)(2,1)} %slice_bitcast_fusion.2), channel_id=1, source_target_pairs={{0,48},{1,49},{2,50},{3,51},{4,52},{5,53},{6,54},{7,55},{8,56},{9,... | collective-permute-start | bytes 1572872 | tf_op jit(solution)/shard_map/ppermute | solution.py:38
  117.9 53.1 %collective-permute-start.15 = (bf16[8,640,512]{2,1,0:T(8,128)(2,1)}, bf16[8,640,512]{2,1,0:T(8,128)(2,1)}, u32[]{:S(2)}, u32[]{:S(2)}) collective-permute-start(bf16[8,640,512]{2,1,0:T(8,128)(2,1)} %norm.1.refs_0_.refs_1_.refs_2_.refs_3_.refs_4_.refs_5_), channel_id=1, source_target_pairs={{0,8},{1,9},{2,10},{3,11},{4,12},{5,13},{6,14},{7,15},{8,0},{9,1},... | collective-permute-start | bytes 15728648 | tf_op jit(solution)/shard_map/ppermute | solution.py:38
  117.9 27.6 %collective-permute-start.9 = (bf16[512,1024]{1,0:T(8,128)(2,1)}, bf16[512,1024]{1,0:T(8,128)(2,1)}, u32[]{:S(2)}, u32[]{:S(2)}) collective-permute-start(bf16[512,1024]{1,0:T(8,128)(2,1)} %collective-permute-done.6.refs_2_.refs_7_.refs_1_), channel_id=1, source_target_pairs={{0,16},{1,17},{2,18},{3,19},{4,20},{5,21},{6,22},{7,23},{8,24},{9,... | collective-permute-start | bytes 3145736 | tf_op jit(solution)/shard_map/ppermute | solution.py:38
  118.3 14.3 %collective-permute-start.16 = (bf16[2,128,1024]{2,1,0:T(8,128)(2,1)}, bf16[2,128,1024]{2,1,0:T(8,128)(2,1)}, u32[]{:S(2)}, u32[]{:S(2)}) collective-permute-start(bf16[2,128,1024]{2,1,0:T(8,128)(2,1)} %after.11), channel_id=1, source_target_pairs={{0,64},{1,65},{2,66},{3,67},{4,68},{5,69},{6,70},{7,71},{8,72},{9,... | collective-permute-start | bytes 1572872 | tf_op jit(solution)/shard_map/ppermute | solution.py:38
  118.4 40.1 %collective-permute-start.10 = (bf16[512,1024]{1,0:T(8,128)(2,1)}, bf16[512,1024]{1,0:T(8,128)(2,1)}, u32[]{:S(2)}, u32[]{:S(2)}) collective-permute-start(bf16[512,1024]{1,0:T(8,128)(2,1)} %collective-permute-done.6.refs_2_.refs_7_.refs_1_), channel_id=1, source_target_pairs={{0,48},{1,49},{2,50},{3,51},{4,52},{5,53},{6,54},{7,55},{8,56},{9,... | collective-permute-start | bytes 3145736 | tf_op jit(solution)/shard_map/ppermute | solution.py:38
  122.1 13.4 %copy-start.12 = (bf16[2,128,1024]{2,1,0:T(8,128)(2,1)S(1)}, bf16[2,128,1024]{2,1,0:T(8,128)(2,1)}, u32[]{:S(2)}) copy-start(bf16[2,128,1024]{2,1,0:T(8,128)(2,1)} %after.11) | copy-start | bytes 1572868
  122.1 34.6 %collective-permute-start.11 = (bf16[256,1024]{1,0:T(8,128)(2,1)}, bf16[256,1024]{1,0:T(8,128)(2,1)}, u32[]{:S(2)}, u32[]{:S(2)}) collective-permute-start(bf16[256,1024]{1,0:T(8,128)(2,1)} %after.10), channel_id=1, source_target_pairs={{0,16},{1,17},{2,18},{3,19},{4,20},{5,21},{6,22},{7,23},{8,24},{9,... | collective-permute-start | bytes 1572872 | tf_op jit(solution)/shard_map/ppermute | solution.py:38
  132.6 25.8 %collective-permute-start.12 = (bf16[256,1024]{1,0:T(8,128)(2,1)}, bf16[256,1024]{1,0:T(8,128)(2,1)}, u32[]{:S(2)}, u32[]{:S(2)}) collective-permute-start(bf16[256,1024]{1,0:T(8,128)(2,1)} %slice.91), channel_id=1, source_target_pairs={{0,48},{1,49},{2,50},{3,51},{4,52},{5,53},{6,54},{7,55},{8,56},{9,... | collective-permute-start | bytes 1572872 | tf_op jit(solution)/shard_map/ppermute | solution.py:38
  145.4 42.1 %collective-permute-start.17 = (bf16[2,2,128,1024]{3,2,1,0:T(8,128)(2,1)}, bf16[2,2,128,1024]{3,2,1,0:T(8,128)(2,1)}, u32[]{:S(2)}, u32[]{:S(2)}) collective-permute-start(bf16[2,2,128,1024]{3,2,1,0:T(8,128)(2,1)} %after.12.refs_0_), channel_id=1, source_target_pairs={{0,16},{1,17},{2,18},{3,19},{4,20},{5,21},{6,22},{7,23},{8,24},{9,... | collective-permute-start | bytes 3145736 | tf_op jit(solution)/shard_map/ppermute | solution.py:38
  156.7 30.9 %collective-permute-start.18 = (bf16[2,2,128,1024]{3,2,1,0:T(8,128)(2,1)}, bf16[2,2,128,1024]{3,2,1,0:T(8,128)(2,1)}, u32[]{:S(2)}, u32[]{:S(2)}) collective-permute-start(bf16[2,2,128,1024]{3,2,1,0:T(8,128)(2,1)} %after.12.refs_0_), channel_id=1, source_target_pairs={{0,48},{1,49},{2,50},{3,51},{4,52},{5,53},{6,54},{7,55},{8,56},{9,... | collective-permute-start | bytes 3145736 | tf_op jit(solution)/shard_map/ppermute | solution.py:38
  158.4 20.3 %collective-permute-start.13 = (bf16[256,1024]{1,0:T(8,128)(2,1)}, bf16[256,1024]{1,0:T(8,128)(2,1)}, u32[]{:S(2)}, u32[]{:S(2)}) collective-permute-start(bf16[256,1024]{1,0:T(8,128)(2,1)} %collective-permute-done.11.refs_2_), channel_id=1, source_target_pairs={{0,64},{1,65},{2,66},{3,67},{4,68},{5,69},{6,70},{7,71},{8,72},{9,... | collective-permute-start | bytes 1572872 | tf_op jit(solution)/shard_map/ppermute | solution.py:38
  158.5 24.2 %collective-permute-start.14 = (bf16[256,1024]{1,0:T(8,128)(2,1)}, bf16[256,1024]{1,0:T(8,128)(2,1)}, u32[]{:S(2)}, u32[]{:S(2)}) collective-permute-start(bf16[256,1024]{1,0:T(8,128)(2,1)} %collective-permute-done.12.refs_3_), channel_id=1, source_target_pairs={{0,64},{1,65},{2,66},{3,67},{4,68},{5,69},{6,70},{7,71},{8,72},{9,... | collective-permute-start | bytes 1572872 | tf_op jit(solution)/shard_map/ppermute | solution.py:38
  163.6 23.9 %slice-start = ((s8[5242880]{0:T(1024)(128)(4,1)}), s8[4194304]{0:T(1024)(128)(4,1)S(1)}, s32[]{:S(2)}) async-start(s8[5242880]{0:T(1024)(128)(4,1)} %bitcast.54), calls=%async_computation.7 | async-start | bytes 8388608
  170.9 16.6 %slice-start.1 = ((s8[5242880]{0:T(1024)(128)(4,1)}), s8[1048576]{0:T(1024)(128)(4,1)S(1)}, s32[]{:S(2)}) async-start(s8[5242880]{0:T(1024)(128)(4,1)} %bitcast.54), calls=%async_computation.8 | async-start | bytes 2097152
  200.8 9.6 %collective-permute-start.19 = (bf16[4,640,256]{2,1,0:T(8,128)(2,1)}, bf16[4,640,256]{2,1,0:T(8,128)(2,1)S(1)}, u32[]{:S(2)}, u32[]{:S(2)}) collective-permute-start(bf16[4,640,256]{2,1,0:T(8,128)(2,1)} %get-tuple-element.24.refs_5_), channel_id=1, source_target_pairs={{0,8},{1,9},{2,10},{3,11},{4,12},{5,13},{6,14},{7,15},{8,0},{9,1},... | collective-permute-start | bytes 3932168 | tf_op jit(solution)/shard_map/ppermute | solution.py:38
  201.3 9.0 %copy-start.20 = (bf16[4,640,256]{2,1,0:T(8,128)(2,1)S(1)}, bf16[4,640,256]{2,1,0:T(8,128)(2,1)}, u32[]{:S(2)}) copy-start(bf16[4,640,256]{2,1,0:T(8,128)(2,1)} %get-tuple-element.23) | copy-start | bytes 3932164
  208.4 3.5 %collective-permute-start.21 = (bf16[4,640,256]{2,1,0:T(8,128)(2,1)}, bf16[4,640,256]{2,1,0:T(8,128)(2,1)}, u32[]{:S(2)}, u32[]{:S(2)}) collective-permute-start(bf16[4,640,256]{2,1,0:T(8,128)(2,1)} %get-tuple-element.26.refs_5_), channel_id=1, source_target_pairs={{0,8},{1,9},{2,10},{3,11},{4,12},{5,13},{6,14},{7,15},{8,0},{9,1},... | collective-permute-start | bytes 3932168 | tf_op jit(solution)/shard_map/ppermute | solution.py:38
  210.0 32.9 %collective-permute-start.26 = (bf16[2,128,1024]{2,1,0:T(8,128)(2,1)S(1)}, bf16[2,128,1024]{2,1,0:T(8,128)(2,1)S(1)}, u32[]{:S(2)}, u32[]{:S(2)}) collective-permute-start(bf16[2,128,1024]{2,1,0:T(8,128)(2,1)S(1)} %slice_bitcast_fusion.1), channel_id=1, source_target_pairs={{0,16},{1,17},{2,18},{3,19},{4,20},{5,21},{6,22},{7,23},{8,24},{9,... | collective-permute-start | bytes 1572872 | tf_op jit(solution)/shard_map/ppermute | solution.py:38
  211.7 88.5 %reduce-scatter.5.cloned.1.call-start = ((), (), s32[]{:S(2)}) async-start(), calls=%async_computation.4 | async-start | bytes 1638400 | tf_op jit(solution)/shard_map/reduce_scatter | solution.py:357
  214.4 28.5 %copy-start.18 = (bf16[640,256]{1,0:T(8,128)(2,1)}, bf16[640,256]{1,0:T(8,128)(2,1)S(1)}, u32[]{:S(2)}) copy-start(bf16[640,256]{1,0:T(8,128)(2,1)S(1)} %get-tuple-element.36.refs_7_) | copy-start | bytes 983044
  214.4 15.4 %collective-permute-start.24 = (bf16[640,256]{1,0:T(8,128)(2,1)S(1)}, bf16[640,256]{1,0:T(8,128)(2,1)S(1)}, u32[]{:S(2)}, u32[]{:S(2)}) collective-permute-start(bf16[640,256]{1,0:T(8,128)(2,1)S(1)} %get-tuple-element.35), channel_id=1, source_target_pairs={{0,6},{1,7},{2,0},{3,1},{4,2},{5,3},{6,4},{7,5},{8,14},{9,15},{10,... | collective-permute-start | bytes 983048 | tf_op jit(solution)/shard_map/ppermute | solution.py:38
  216.5 17.8 %collective-permute-start.23 = (bf16[640,256]{1,0:T(8,128)(2,1)S(1)}, bf16[640,256]{1,0:T(8,128)(2,1)S(1)}, u32[]{:S(2)}, u32[]{:S(2)}) collective-permute-start(bf16[640,256]{1,0:T(8,128)(2,1)S(1)} %get-tuple-element.34), channel_id=1, source_target_pairs={{0,4},{1,5},{2,6},{3,7},{4,0},{5,1},{6,2},{7,3},{8,12},{9,13},{10,... | collective-permute-start | bytes 983048 | tf_op jit(solution)/shard_map/ppermute | solution.py:38
  216.9 24.1 %collective-permute-start.22 = (bf16[640,256]{1,0:T(8,128)(2,1)S(1)}, bf16[640,256]{1,0:T(8,128)(2,1)S(1)}, u32[]{:S(2)}, u32[]{:S(2)}) collective-permute-start(bf16[640,256]{1,0:T(8,128)(2,1)S(1)} %get-tuple-element.36.refs_7_), channel_id=1, source_target_pairs={{0,2},{1,3},{2,4},{3,5},{4,6},{5,7},{6,0},{7,1},{8,10},{9,11},{10,... | collective-permute-start | bytes 983048 | tf_op jit(solution)/shard_map/ppermute | solution.py:38
  218.6 24.4 %collective-permute-start.27 = (bf16[2,128,1024]{2,1,0:T(8,128)(2,1)S(1)}, bf16[2,128,1024]{2,1,0:T(8,128)(2,1)S(1)}, u32[]{:S(2)}, u32[]{:S(2)}) collective-permute-start(bf16[2,128,1024]{2,1,0:T(8,128)(2,1)S(1)} %slice_bitcast_fusion), channel_id=1, source_target_pairs={{0,48},{1,49},{2,50},{3,51},{4,52},{5,53},{6,54},{7,55},{8,56},{9,... | collective-permute-start | bytes 1572872 | tf_op jit(solution)/shard_map/ppermute | solution.py:38
  251.0 3.2 %collective-permute-start.28 = (bf16[4,640,256]{2,1,0:T(8,128)(2,1)}, bf16[4,640,256]{2,1,0:T(8,128)(2,1)S(1)}, u32[]{:S(2)}, u32[]{:S(2)}) collective-permute-start(bf16[4,640,256]{2,1,0:T(8,128)(2,1)} %get-tuple-element.28.refs_5_), channel_id=1, source_target_pairs={{0,8},{1,9},{2,10},{3,11},{4,12},{5,13},{6,14},{7,15},{8,0},{9,1},... | collective-permute-start | bytes 3932168 | tf_op jit(solution)/shard_map/ppermute | solution.py:38
  264.1 3.2 %collective-permute-start.30 = (bf16[4,640,256]{2,1,0:T(8,128)(2,1)}, bf16[4,640,256]{2,1,0:T(8,128)(2,1)S(1)}, u32[]{:S(2)}, u32[]{:S(2)}) collective-permute-start(bf16[4,640,256]{2,1,0:T(8,128)(2,1)} %get-tuple-element.30), channel_id=1, source_target_pairs={{0,8},{1,9},{2,10},{3,11},{4,12},{5,13},{6,14},{7,15},{8,0},{9,1},... | collective-permute-start | bytes 3932168 | tf_op jit(solution)/shard_map/ppermute | solution.py:38
  264.3 10.4 %collective-permute-start.25 = (bf16[640,128]{1,0:T(8,128)(2,1)S(1)}, bf16[640,128]{1,0:T(8,128)(2,1)S(1)}, u32[]{:S(2)}, u32[]{:S(2)}) collective-permute-start(bf16[640,128]{1,0:T(8,128)(2,1)S(1)} %constant_dynamic-slice_fusion.1), channel_id=1, source_target_pairs={{0,1},{1,0},{2,3},{3,2},{4,5},{5,4},{6,7},{7,6},{8,9},{9,8},{10,11... | collective-permute-start | bytes 491528 | tf_op jit(solution)/shard_map/ppermute | solution.py:38
  269.6 22.4 %collective-permute-start.33 = (bf16[640,256]{1,0:T(8,128)(2,1)}, bf16[640,256]{1,0:T(8,128)(2,1)S(1)}, u32[]{:S(2)}, u32[]{:S(2)}) collective-permute-start(bf16[640,256]{1,0:T(8,128)(2,1)} %get-tuple-element.32), channel_id=1, source_target_pairs={{0,6},{1,7},{2,0},{3,1},{4,2},{5,3},{6,4},{7,5},{8,14},{9,15},{10,... | collective-permute-start | bytes 983048 | tf_op jit(solution)/shard_map/ppermute | solution.py:38
  273.8 18.2 %collective-permute-start.32 = (bf16[640,256]{1,0:T(8,128)(2,1)}, bf16[640,256]{1,0:T(8,128)(2,1)S(1)}, u32[]{:S(2)}, u32[]{:S(2)}) collective-permute-start(bf16[640,256]{1,0:T(8,128)(2,1)} %get-tuple-element.33), channel_id=1, source_target_pairs={{0,4},{1,5},{2,6},{3,7},{4,0},{5,1},{6,2},{7,3},{8,12},{9,13},{10,... | collective-permute-start | bytes 983048 | tf_op jit(solution)/shard_map/ppermute | solution.py:38
  273.8 20.4 %collective-permute-start.31 = (bf16[640,256]{1,0:T(8,128)(2,1)S(1)}, bf16[640,256]{1,0:T(8,128)(2,1)}, u32[]{:S(2)}, u32[]{:S(2)}) collective-permute-start(bf16[640,256]{1,0:T(8,128)(2,1)S(1)} %get-tuple-element.31), channel_id=1, source_target_pairs={{0,2},{1,3},{2,4},{3,5},{4,6},{5,7},{6,0},{7,1},{8,10},{9,11},{10,... | collective-permute-start | bytes 983048 | tf_op jit(solution)/shard_map/ppermute | solution.py:38
  274.6 20.9 %copy-start.21 = (bf16[640,128]{1,0:T(8,128)(2,1)}, bf16[640,128]{1,0:T(8,128)(2,1)S(1)}, u32[]{:S(2)}) copy-start(bf16[640,128]{1,0:T(8,128)(2,1)S(1)} %collective-permute-done.25.refs_2_) | copy-start | bytes 491524
  275.7 23.6 %copy-start.23 = (bf16[1,640,256]{2,1,0:T(8,128)(2,1)S(1)}, bf16[1,640,256]{2,1,0:T(8,128)(2,1)}, u32[]{:S(2)}) copy-start(bf16[1,640,256]{2,1,0:T(8,128)(2,1)} %reduce-scatter.3.cloned.1.call-done) | copy-start | bytes 983044
  275.7 20.5 %collective-permute-start.20 = (bf16[640,128]{1,0:T(8,128)(2,1)S(1)}, bf16[640,128]{1,0:T(8,128)(2,1)S(1)}, u32[]{:S(2)}, u32[]{:S(2)}) collective-permute-start(bf16[640,128]{1,0:T(8,128)(2,1)S(1)} %dynamic-slice_bitcast_fusion.1), channel_id=1, source_target_pairs={{0,1},{1,0},{2,3},{3,2},{4,5},{5,4},{6,7},{7,6},{8,9},{9,8},{10,11... | collective-permute-start | bytes 491528 | tf_op jit(solution)/shard_map/ppermute | solution.py:38
  296.9 7.6 %collective-permute-start.34 = (bf16[640,128]{1,0:T(8,128)(2,1)}, bf16[640,128]{1,0:T(8,128)(2,1)S(1)}, u32[]{:S(2)}, u32[]{:S(2)}) collective-permute-start(bf16[640,128]{1,0:T(8,128)(2,1)} %after.13), channel_id=1, source_target_pairs={{0,1},{1,0},{2,3},{3,2},{4,5},{5,4},{6,7},{7,6},{8,9},{9,8},{10,11... | collective-permute-start | bytes 491528 | tf_op jit(solution)/shard_map/ppermute | solution.py:38
  301.2 7.3 %collective-permute-start.29 = (bf16[640,128]{1,0:T(8,128)(2,1)S(1)}, bf16[640,128]{1,0:T(8,128)(2,1)S(1)}, u32[]{:S(2)}, u32[]{:S(2)}) collective-permute-start(bf16[640,128]{1,0:T(8,128)(2,1)S(1)} %dynamic-slice_bitcast_fusion), channel_id=1, source_target_pairs={{0,1},{1,0},{2,3},{3,2},{4,5},{5,4},{6,7},{7,6},{8,9},{9,8},{10,11... | collective-permute-start | bytes 491528 | tf_op jit(solution)/shard_map/ppermute | solution.py:38
  (19 other events, 34.3 us)
Sparse Core Ops, SparseCore 0:
  9.7 37.6 all-gather.4
  73.0 31.8 all-gather.6
  211.9 33.6 reduce-scatter.2
  257.1 34.2 reduce-scatter.4

commit v9 on v7

--- a/solution.py
+++ b/solution.py
@@ -297,12 +297,12 @@
     ylo_a = send(down_a, ylo=1)
     up_updated, columns = up_step(up_master, up_gradient, up_first, up_second, down_a)
     ylo_a = after(ylo_a, columns)
-    down_updated, down_b = down_step(1, down_args, (down_half,), (ylo_a,))
+    down_updated, down_b = down_step(1, down_args, (down_half,), (columns,))
 
     st_a = jnp.stack([down_a, ylo_a])
     low_a, high_a = both_ways(st_a, st_a)
     u0 = lax.all_to_all(columns, ("core", "x", "yhi"), 0, 0, tiled=True).reshape(512, 1024)
-    u0 = after(u0, down_b, low_a, high_a)
+    u0 = after(u0, down_b)
     opp_a = both_ways(low_a[0], high_a[1])
     ws_a = (st_a, low_a, high_a, *opp_a)
 

time: 315 us -> 314 us (level)
  starting transfers between devices: 51.7 us -> 61.1 us
  waiting for transfers between devices: 125 us -> 119 us
  local copies, waits for them, and re-layouts: 27.7 us -> 21.8 us
    ppermute x35, starting transfers between devices: 44.5 us -> 53.9 us  [send(): return lax.ppermute(v, AXES, shifted(**steps))]
    unnamed x83 -> x71, local copies, waits for them, and re-layouts: 17.3 us -> 11.4 us
    ppermute x35, waiting for transfers between devices: 114 us -> 109 us  [send(): return lax.ppermute(v, AXES, shifted(**steps))]
  transfers between devices with their start and end apart: 40 -> 40, of which waited for: 16 -> 19; matrix products, arithmetic and copies ran while one was open for 9% -> 9% of each run, Pallas kernels for 18% -> 19%
where the time goes in v9:
time: 314 us; the launch traced here: 313 us
  waiting for transfers between devices  119 us (38%)
  Pallas kernels  77.1 us (25%)
  starting transfers between devices  61.1 us (19%)
  local copies, waits for them, and re-layouts  21.8 us (7%)
  other arithmetic  19.3 us (6%)
  between operations  14.2 us (5%)
    ppermute x35, waiting for transfers between devices, send(): return lax.ppermute(v, AXES, shifted(**steps))  109 us
    ppermute x35, starting transfers between devices, send(): return lax.ppermute(v, AXES, shifted(**steps))  53.9 us
    pallas_call x4, Pallas kernels, partial_of(): pl.pallas_call(partial_kernel, out_shape=(shape, shape), grid_spec=pltpu....  28.1 us
    pallas_call x2, Pallas kernels, hidden_first(): pl.pallas_call(first_kernel, out_shape=jax.ShapeDtypeStruct((640, 1024),...  13.6 us
    pallas_call x2, Pallas kernels, down_step(): pl.pallas_call(down_kernel, out_shape=(jax.ShapeDtypeStruct((128, D), jnp...  12.7 us
    unnamed x71, local copies, waits for them, and re-layouts  11.4 us
    all_to_all x1, waiting for transfers between devices, body(): lax.all_to_all(columns, ('core', 'x', 'yhi'), 0, 0, tiled=True)  9.92 us
    convert_element_type x8, other arithmetic, body(): (a.astype(jnp.float32) + b.astype(jnp.float32)).astype(jnp.bfloat16)  9.74 us
  transfers between devices with their start and end apart: 40, of which 19 were waited for; matrix products, arithmetic and copies ran while one was open for 9% of the time, Pallas kernels for 19%

profile of v9, /device:TPU:0, one launch (start us, length us, event | category | flops | bytes accessed | tf_op | source)
XLA Modules:
  0.0 312.7 jit_solution(8282248092440639149)
XLA Ops:
  7.9 6.3 %adam_down.2 = (f32[128,4096]{1,0:T(8,128)}, bf16[2,128,1024]{2,1,0:T(8,128)(2,1)}) custom-call(f32[128,4096]{1,0:T(8,128)} %w_ref.5, bf16[128,4096]{1,0:T(8,128)(2,1)} %g_ref.5, f32[128,4096]{1,0:T(8,128)} %m_ref.5, f32[128,4096]{1,0:T(8,128)} %v_ref.5), custom_call_target="tpu_custom_call" | custom-call | flops 7864 | bytes 5242 | tf_op jit(solution)/shard_map/adam_down/pallas_call | solution.py:110
  15.9 7.8 %adam_up.1 = (f32[32,16384]{1,0:T(8,128)}, bf16[16,32,1024]{2,1,0:T(8,128)(2,1)}) custom-call(f32[32,16384]{1,0:T(8,128)} %w_ref.4, bf16[32,16384]{1,0:T(8,128)(2,1)} %g_ref.4, f32[32,16384]{1,0:T(8,128)} %m_ref.4, f32[32,16384]{1,0:T(8,128)} %v_ref.4, bf16[2,128,1024]{2,1,0:T(8,128)(2,1)} %get-tuple-element.17.dep_ref), custom_call_target="tpu_custom_call" | custom-call | flops 15728 | bytes 10485 | tf_op jit(solution)/shard_map/adam_up/pallas_call | solution.py:84
  23.7 4.4 %collective-permute-done.4.refs_0_ = bf16[2,128,1024]{2,1,0:T(8,128)(2,1)S(1)} collective-permute-done((bf16[2,128,1024]{2,1,0:T(8,128)(2,1)}, bf16[2,128,1024]{2,1,0:T(8,128)(2,1)S(1)}, u32[]{:S(2)}, u32[]{:S(2)}) %collective-permute-start.4) | collective-permute-done | bytes 524320 | tf_op jit(solution)/shard_map/ppermute | solution.py:38
  28.8 2.1 pad_maximum_fusion.refs_0_
  31.0 2.1 collective-permute-start.5
  33.1 7.0 %all-to-all-start = ((bf16[16,32,1024]{2,1,0:T(8,128)(2,1)}), bf16[16,32,1024]{2,1,0:T(8,128)(2,1)S(1)}, u32[]{:S(2)}, u32[]{:S(2)}) async-start(bf16[16,32,1024]{2,1,0:T(8,128)(2,1)} %get-tuple-element.20.refs_1_), calls=%async_computation | async-start | bytes 2097152 | tf_op jit(solution)/shard_map/all_to_all | solution.py:304
  40.2 2.2 collective-permute-start.7
  42.4 3.4 %collective-permute-start = (bf16[2,320,512]{2,1,0:T(8,128)(2,1)}, bf16[2,320,512]{2,1,0:T(8,128)(2,1)}, u32[]{:S(2)}, u32[]{:S(2)}) collective-permute-start(bf16[2,320,512]{2,1,0:T(8,128)(2,1)} %param.11), channel_id=1, source_target_pairs={{0,1},{1,0},{2,3},{3,2},{4,5},{5,4},{6,7},{7,6},{8,9},{9,8},{10,11... | collective-permute-start | bytes 1966088 | tf_op jit(solution)/shard_map/ppermute | solution.py:38
  45.8 6.3 %adam_down.3 = (f32[128,4096]{1,0:T(8,128)}, bf16[2,128,1024]{2,1,0:T(8,128)(2,1)}) custom-call(f32[128,4096]{1,0:T(8,128)} %w_ref.5, bf16[128,4096]{1,0:T(8,128)(2,1)} %g_ref.5, f32[128,4096]{1,0:T(8,128)} %m_ref.5, f32[128,4096]{1,0:T(8,128)} %v_ref.5, f32[128,4096]{1,0:T(8,128)} %get-tuple-element.19.refs_0_, ...), custom_call_target="tpu_custom_call", output_to_operand_aliasing={{0}: (4, {})} | custom-call | flops 7864 | bytes 5242 | tf_op jit(solution)/shard_map/adam_down/pallas_call | solution.py:110
  52.1 9.9 %all-to-all-done = bf16[16,32,1024]{2,1,0:T(8,128)(2,1)S(1)} async-done(((bf16[16,32,1024]{2,1,0:T(8,128)(2,1)}), bf16[16,32,1024]{2,1,0:T(8,128)(2,1)S(1)}, u32[]{:S(2)}, u32[]{:S(2)}) %all-to-all-start) | async-done | bytes 1048608 | tf_op jit(solution)/shard_map/all_to_all | solution.py:304
  65.1 1.7 collective-permute-start.2
  70.6 2.1 collective-permute-start.8
  72.7 19.3 %collective-permute-done.3.refs_3_.refs_1_.refs_7_ = bf16[512,1024]{1,0:T(8,128)(2,1)S(1)} collective-permute-done((bf16[512,1024]{1,0:T(8,128)(2,1)}, bf16[512,1024]{1,0:T(8,128)(2,1)S(1)}, u32[]{:S(2)}, u32[]{:S(2)}) %collective-permute-start.3) | collective-permute-done | bytes 1048608 | tf_op jit(solution)/shard_map/ppermute | solution.py:38
  92.1 8.7 %collective-permute-done.6.refs_4_.refs_2_.refs_3_ = bf16[2,128,1024]{2,1,0:T(8,128)(2,1)} collective-permute-done((bf16[2,128,1024]{2,1,0:T(8,128)(2,1)S(1)}, bf16[2,128,1024]{2,1,0:T(8,128)(2,1)}, u32[]{:S(2)}, u32[]{:S(2)}) %collective-permute-start.6) | collective-permute-done | bytes 524320 | tf_op jit(solution)/shard_map/ppermute | solution.py:38
  106.5 1.7 collective-permute-start.12
  110.4 5.8 %collective-permute-done.13.refs_4_ = bf16[2,128,1024]{2,1,0:T(8,128)(2,1)} collective-permute-done((bf16[2,128,1024]{2,1,0:T(8,128)(2,1)}, bf16[2,128,1024]{2,1,0:T(8,128)(2,1)}, u32[]{:S(2)}, u32[]{:S(2)}) %collective-permute-start.13) | collective-permute-done | bytes 524320 | tf_op jit(solution)/shard_map/ppermute | solution.py:38
  116.2 20.8 %collective-permute-done.12.refs_3_ = bf16[256,1024]{1,0:T(8,128)(2,1)S(1)} collective-permute-done((bf16[256,1024]{1,0:T(8,128)(2,1)}, bf16[256,1024]{1,0:T(8,128)(2,1)S(1)}, u32[]{:S(2)}, u32[]{:S(2)}) %collective-permute-start.12) | collective-permute-done | bytes 524320 | tf_op jit(solution)/shard_map/ppermute | solution.py:38
  138.5 6.3 %norm.1.refs_0_.refs_1_.refs_2_.refs_3_.refs_4_.refs_5_ = bf16[8,640,512]{2,1,0:T(8,128)(2,1)} custom-call(bf16[4,640,512]{2,1,0:T(8,128)(2,1)} %bitcast.58, bf16[4,640,512]{2,1,0:T(8,128)(2,1)} %bitcast.59, f32[8,512]{1,0:T(8,128)} %pad_maximum_fusion.3.g_ref, bf16[512,1024]{1,0:T(8,128)(2,1)} %copy-done.7, ...), custom_call_target="tpu_custom_call" | custom-call | flops 20971 | bytes 10485 | tf_op jit(solution)/shard_map/norm/pallas_call | solution.py:145
  144.8 2.1 pad_maximum_fusion.1.refs_0_
  148.1 2.1 collective-permute-start.18
  152.9 2.5 copy-done
  157.8 6.4 %hidden_first.2.refs_6_.acc_ref = f32[640,1024]{1,0:T(8,128)S(1)} custom-call(s32[16]{0:T(128)S(1)} %fusion.17.s_ref, bf16[8,640,512]{2,1,0:T(8,128)(2,1)S(1)} %copy-done, bf16[8,640,512]{2,1,0:T(8,128)(2,1)S(1)} %copy-done, bf16[8,640,512]{2,1,0:T(8,128)(2,1)S(1)} %copy-done, bf16[8,640,512]{2,1,0:T(8,128)(2,1)S(1)} %copy-done, ...), custom_call_target="tpu_custom_call" | custom-call | flops 4026531 | bytes 14680 | tf_op jit(solution)/shard_map/hidden_first/pallas_call | solution.py:193
  164.3 7.2 %hidden_first.3.acc_ref = f32[640,1024]{1,0:T(8,128)S(1)} custom-call(s32[16]{0:T(128)S(1)} %fusion.17.s_ref, bf16[8,640,512]{2,1,0:T(8,128)(2,1)} %collective-permute-done.16.refs_0_.refs_1_.refs_2_.refs_3_.refs_4_.refs_5_, bf16[8,640,512]{2,1,0:T(8,128)(2,1)} %collective-permute-done.16.refs_0_.refs_1_.refs_2_.refs_3_.refs_4_.refs_5_, ...), custom_call_target="tpu_custom_call" | custom-call | flops 4026531 | bytes 14680 | tf_op jit(solution)/shard_map/hidden_first/pallas_call | solution.py:193
  171.5 4.2 %collective-permute-done.14.refs_4_ = bf16[256,1024]{1,0:T(8,128)(2,1)} collective-permute-done((bf16[256,1024]{1,0:T(8,128)(2,1)}, bf16[256,1024]{1,0:T(8,128)(2,1)}, u32[]{:S(2)}, u32[]{:S(2)}) %collective-permute-start.14) | collective-permute-done | bytes 524320 | tf_op jit(solution)/shard_map/ppermute | solution.py:38
  175.7 4.5 %hidden_last.2.refs_6_.sib_ref = bf16[640,1024]{1,0:T(8,128)(2,1)S(1)} custom-call(s32[16]{0:T(128)S(1)} %fusion.17.s_ref, f32[640,1024]{1,0:T(8,128)S(1)} %hidden_first.3.acc_ref, bf16[8,640,512]{2,1,0:T(8,128)(2,1)} %collective-permute-done.16.refs_0_.refs_1_.refs_2_.refs_3_.refs_4_.refs_5_, ...), custom_call_target="tpu_custom_call" | custom-call | flops 1342177 | bytes 8388 | tf_op jit(solution)/shard_map/hidden_last/pallas_call | solution.py:211
  180.2 4.2 %hidden_last.3.own_ref = bf16[640,1024]{1,0:T(8,128)(2,1)S(1)} custom-call(s32[16]{0:T(128)S(1)} %fusion.17.s_ref, f32[640,1024]{1,0:T(8,128)S(1)} %hidden_first.2.refs_6_.acc_ref, bf16[8,640,512]{2,1,0:T(8,128)(2,1)S(1)} %bitcast.55, bf16[8,640,512]{2,1,0:T(8,128)(2,1)S(1)} %bitcast.55, bf16[256,1024]{1,0:T(8,128)(2,1)S(1)} %copy-done.19, ...), custom_call_target="tpu_custom_call" | custom-call | flops 1342177 | bytes 8388 | tf_op jit(solution)/shard_map/hidden_last/pallas_call | solution.py:211
  186.0 6.9 %partial.4 = (bf16[4,640,256]{2,1,0:T(8,128)(2,1)}, bf16[4,640,256]{2,1,0:T(8,128)(2,1)}) custom-call(s32[4]{0:T(128)} %iota.7.s_ref, bf16[640,1024]{1,0:T(8,128)(2,1)} %copy-done.2, bf16[640,1024]{1,0:T(8,128)(2,1)} %copy-done.1, bf16[2,2,128,1024]{3,2,1,0:T(8,128)(2,1)} %pad_maximum_fusion.refs_0_, ...), custom_call_target="tpu_custom_call" | custom-call | flops 2684354 | bytes 8388 | tf_op jit(solution)/shard_map/partial/pallas_call | solution.py:251
  193.6 7.1 %partial.5 = (bf16[4,640,256]{2,1,0:T(8,128)(2,1)}, bf16[4,640,256]{2,1,0:T(8,128)(2,1)}) custom-call(s32[4]{0:T(128)} %and_select_fusion.s_ref, bf16[640,1024]{1,0:T(8,128)(2,1)} %copy-done.2, bf16[640,1024]{1,0:T(8,128)(2,1)} %copy-done.1, bf16[2,2,128,1024]{3,2,1,0:T(8,128)(2,1)} %pad_maximum_fusion.refs_0_, ...), custom_call_target="tpu_custom_call" | custom-call | flops 2684354 | bytes 8388 | tf_op jit(solution)/shard_map/partial/pallas_call | solution.py:251
  206.4 2.1 collective-permute-start.22
  208.6 2.9 collective-permute-start.23
  214.0 3.2 %collective-permute-start.27 = (bf16[2,128,1024]{2,1,0:T(8,128)(2,1)S(1)}, bf16[2,128,1024]{2,1,0:T(8,128)(2,1)S(1)}, u32[]{:S(2)}, u32[]{:S(2)}) collective-permute-start(bf16[2,128,1024]{2,1,0:T(8,128)(2,1)S(1)} %slice_bitcast_fusion), channel_id=1, source_target_pairs={{0,48},{1,49},{2,50},{3,51},{4,52},{5,53},{6,54},{7,55},{8,56},{9,... | collective-permute-start | bytes 1572872 | tf_op jit(solution)/shard_map/ppermute | solution.py:38
  217.2 2.2 collective-permute-done.22
  219.3 15.7 %collective-permute-done.23 = bf16[640,256]{1,0:T(8,128)(2,1)S(1)} collective-permute-done((bf16[640,256]{1,0:T(8,128)(2,1)S(1)}, bf16[640,256]{1,0:T(8,128)(2,1)S(1)}, u32[]{:S(2)}, u32[]{:S(2)}) %collective-permute-start.23) | collective-permute-done | bytes 327712 | tf_op jit(solution)/shard_map/ppermute | solution.py:38
  235.0 1.9 fusion.5.refs_8_
  237.9 7.0 %partial.6 = (bf16[4,640,256]{2,1,0:T(8,128)(2,1)}, bf16[4,640,256]{2,1,0:T(8,128)(2,1)}) custom-call(s32[4]{0:T(128)} %iota.9.s_ref, bf16[640,1024]{1,0:T(8,128)(2,1)} %copy-done.2, bf16[640,1024]{1,0:T(8,128)(2,1)} %copy-done.1, bf16[2,2,128,1024]{3,2,1,0:T(8,128)(2,1)} %after.12.refs_0_, ...), custom_call_target="tpu_custom_call" | custom-call | flops 2684354 | bytes 8388 | tf_op jit(solution)/shard_map/partial/pallas_call | solution.py:251
  244.9 3.2 %collective-permute-done.28 = bf16[4,640,256]{2,1,0:T(8,128)(2,1)S(1)} collective-permute-done((bf16[4,640,256]{2,1,0:T(8,128)(2,1)}, bf16[4,640,256]{2,1,0:T(8,128)(2,1)S(1)}, u32[]{:S(2)}, u32[]{:S(2)}) %collective-permute-start.28) | collective-permute-done | bytes 1310752 | tf_op jit(solution)/shard_map/ppermute | solution.py:38
  248.1 2.7 add_convert_fusion
  250.9 7.1 %partial.7 = (bf16[4,640,256]{2,1,0:T(8,128)(2,1)}, bf16[4,640,256]{2,1,0:T(8,128)(2,1)}) custom-call(s32[4]{0:T(128)} %and_select_fusion.s_ref, bf16[640,1024]{1,0:T(8,128)(2,1)} %copy-done.2, bf16[640,1024]{1,0:T(8,128)(2,1)} %copy-done.1, bf16[2,2,128,1024]{3,2,1,0:T(8,128)(2,1)} %after.12.refs_0_, ...), custom_call_target="tpu_custom_call" | custom-call | flops 2684354 | bytes 8388 | tf_op jit(solution)/shard_map/partial/pallas_call | solution.py:251
  258.2 3.0 collective-permute-start.25
  261.3 2.2 fusion.11
  263.5 3.8 %collective-permute-start.32 = (bf16[640,256]{1,0:T(8,128)(2,1)}, bf16[640,256]{1,0:T(8,128)(2,1)S(1)}, u32[]{:S(2)}, u32[]{:S(2)}) collective-permute-start(bf16[640,256]{1,0:T(8,128)(2,1)} %get-tuple-element.33), channel_id=1, source_target_pairs={{0,4},{1,5},{2,6},{3,7},{4,0},{5,1},{6,2},{7,3},{8,12},{9,13},{10,... | collective-permute-start | bytes 983048 | tf_op jit(solution)/shard_map/ppermute | solution.py:38
  267.3 2.6 collective-permute-start.33
  271.0 2.7 collective-permute-start.20
  273.7 8.1 %collective-permute-done.31 = bf16[640,256]{1,0:T(8,128)(2,1)S(1)} collective-permute-done((bf16[640,256]{1,0:T(8,128)(2,1)}, bf16[640,256]{1,0:T(8,128)(2,1)S(1)}, u32[]{:S(2)}, u32[]{:S(2)}) %collective-permute-start.31) | collective-permute-done | bytes 327712 | tf_op jit(solution)/shard_map/ppermute | solution.py:38
  281.8 7.6 %collective-permute-done.32 = bf16[640,256]{1,0:T(8,128)(2,1)S(1)} collective-permute-done((bf16[640,256]{1,0:T(8,128)(2,1)}, bf16[640,256]{1,0:T(8,128)(2,1)S(1)}, u32[]{:S(2)}, u32[]{:S(2)}) %collective-permute-start.32) | collective-permute-done | bytes 327712 | tf_op jit(solution)/shard_map/ppermute | solution.py:38
  292.0 3.0 collective-permute-start.34
  297.6 2.4 collective-permute-done.34
  300.0 4.3 %collective-permute-done.29 = bf16[640,128]{1,0:T(8,128)(2,1)S(1)} collective-permute-done((bf16[640,128]{1,0:T(8,128)(2,1)S(1)}, bf16[640,128]{1,0:T(8,128)(2,1)S(1)}, u32[]{:S(2)}, u32[]{:S(2)}) %collective-permute-start.29) | collective-permute-done | bytes 163872 | tf_op jit(solution)/shard_map/ppermute | solution.py:38
  (157 shorter events, 45.6 us)
Async XLA Ops:
  7.2 130.0 %all-gather.5.cloned.1.call-start = ((), (), s32[]{:S(2)}) async-start(), calls=%async_computation.5 | async-start | bytes 3276800 | tf_op jit(solution)/shard_map/all_gather | solution.py:293
  14.2 13.8 %collective-permute-start.4 = (bf16[2,128,1024]{2,1,0:T(8,128)(2,1)}, bf16[2,128,1024]{2,1,0:T(8,128)(2,1)S(1)}, u32[]{:S(2)}, u32[]{:S(2)}) collective-permute-start(bf16[2,128,1024]{2,1,0:T(8,128)(2,1)} %get-tuple-element.17.dep_ref), channel_id=1, source_target_pairs={{0,64},{1,65},{2,66},{3,67},{4,68},{5,69},{6,70},{7,71},{8,72},{9,... | collective-permute-start | bytes 1572872 | tf_op jit(solution)/shard_map/ppermute | solution.py:38
  31.0 34.2 %collective-permute-start.5 = (bf16[2,2,128,1024]{3,2,1,0:T(8,128)(2,1)}, bf16[2,2,128,1024]{3,2,1,0:T(8,128)(2,1)}, u32[]{:S(2)}, u32[]{:S(2)}) collective-permute-start(bf16[2,2,128,1024]{3,2,1,0:T(8,128)(2,1)} %pad_maximum_fusion.refs_0_), channel_id=1, source_target_pairs={{0,16},{1,17},{2,18},{3,19},{4,20},{5,21},{6,22},{7,23},{8,24},{9,... | collective-permute-start | bytes 3145736 | tf_op jit(solution)/shard_map/ppermute | solution.py:38
  33.1 28.9 %all-to-all-start = ((bf16[16,32,1024]{2,1,0:T(8,128)(2,1)}), bf16[16,32,1024]{2,1,0:T(8,128)(2,1)S(1)}, u32[]{:S(2)}, u32[]{:S(2)}) async-start(bf16[16,32,1024]{2,1,0:T(8,128)(2,1)} %get-tuple-element.20.refs_1_), calls=%async_computation | async-start | bytes 2097152 | tf_op jit(solution)/shard_map/all_to_all | solution.py:304
  40.1 97.1 %all-gather.7.cloned.1.call-start = ((), (), s32[]{:S(2)}) async-start(), calls=%async_computation.6 | async-start | bytes 3276800 | tf_op jit(solution)/shard_map/all_gather | solution.py:311
  40.2 27.7 %collective-permute-start.7 = (bf16[2,2,128,1024]{3,2,1,0:T(8,128)(2,1)}, bf16[2,2,128,1024]{3,2,1,0:T(8,128)(2,1)}, u32[]{:S(2)}, u32[]{:S(2)}) collective-permute-start(bf16[2,2,128,1024]{3,2,1,0:T(8,128)(2,1)} %pad_maximum_fusion.refs_0_), channel_id=1, source_target_pairs={{0,48},{1,49},{2,50},{3,51},{4,52},{5,53},{6,54},{7,55},{8,56},{9,... | collective-permute-start | bytes 3145736 | tf_op jit(solution)/shard_map/ppermute | solution.py:38
  42.4 28.3 %collective-permute-start = (bf16[2,320,512]{2,1,0:T(8,128)(2,1)}, bf16[2,320,512]{2,1,0:T(8,128)(2,1)}, u32[]{:S(2)}, u32[]{:S(2)}) collective-permute-start(bf16[2,320,512]{2,1,0:T(8,128)(2,1)} %param.11), channel_id=1, source_target_pairs={{0,1},{1,0},{2,3},{3,2},{4,5},{5,4},{6,7},{7,6},{8,9},{9,8},{10,11... | collective-permute-start | bytes 1966088 | tf_op jit(solution)/shard_map/ppermute | solution.py:38
  63.0 29.1 %collective-permute-start.3 = (bf16[512,1024]{1,0:T(8,128)(2,1)}, bf16[512,1024]{1,0:T(8,128)(2,1)S(1)}, u32[]{:S(2)}, u32[]{:S(2)}) collective-permute-start(bf16[512,1024]{1,0:T(8,128)(2,1)} %after.7.refs_6_), channel_id=1, source_target_pairs={{0,64},{1,65},{2,66},{3,67},{4,68},{5,69},{6,70},{7,71},{8,72},{9,... | collective-permute-start | bytes 3145736 | tf_op jit(solution)/shard_map/ppermute | solution.py:38
  63.6 28.5 %collective-permute-start.1 = (bf16[512,1024]{1,0:T(8,128)(2,1)}, bf16[512,1024]{1,0:T(8,128)(2,1)S(1)}, u32[]{:S(2)}, u32[]{:S(2)}) collective-permute-start(bf16[512,1024]{1,0:T(8,128)(2,1)} %after.7.refs_6_), channel_id=1, source_target_pairs={{0,16},{1,17},{2,18},{3,19},{4,20},{5,21},{6,22},{7,23},{8,24},{9,... | collective-permute-start | bytes 3145736 | tf_op jit(solution)/shard_map/ppermute | solution.py:38
  65.1 26.9 %collective-permute-start.2 = (bf16[512,1024]{1,0:T(8,128)(2,1)}, bf16[512,1024]{1,0:T(8,128)(2,1)S(1)}, u32[]{:S(2)}, u32[]{:S(2)}) collective-permute-start(bf16[512,1024]{1,0:T(8,128)(2,1)} %after.7.refs_6_), channel_id=1, source_target_pairs={{0,48},{1,49},{2,50},{3,51},{4,52},{5,53},{6,54},{7,55},{8,56},{9,... | collective-permute-start | bytes 3145736 | tf_op jit(solution)/shard_map/ppermute | solution.py:38
  67.9 32.9 %collective-permute-start.6 = (bf16[2,128,1024]{2,1,0:T(8,128)(2,1)S(1)}, bf16[2,128,1024]{2,1,0:T(8,128)(2,1)}, u32[]{:S(2)}, u32[]{:S(2)}) collective-permute-start(bf16[2,128,1024]{2,1,0:T(8,128)(2,1)S(1)} %slice_bitcast_fusion.3), channel_id=1, source_target_pairs={{0,16},{1,17},{2,18},{3,19},{4,20},{5,21},{6,22},{7,23},{8,24},{9,... | collective-permute-start | bytes 1572872 | tf_op jit(solution)/shard_map/ppermute | solution.py:38
  70.6 30.2 %collective-permute-start.8 = (bf16[2,128,1024]{2,1,0:T(8,128)(2,1)S(1)}, bf16[2,128,1024]{2,1,0:T(8,128)(2,1)}, u32[]{:S(2)}, u32[]{:S(2)}) collective-permute-start(bf16[2,128,1024]{2,1,0:T(8,128)(2,1)S(1)} %slice_bitcast_fusion.2), channel_id=1, source_target_pairs={{0,48},{1,49},{2,50},{3,51},{4,52},{5,53},{6,54},{7,55},{8,56},{9,... | collective-permute-start | bytes 1572872 | tf_op jit(solution)/shard_map/ppermute | solution.py:38
  92.0 8.8 %copy-start.3 = (bf16[512,1024]{1,0:T(8,128)(2,1)}, bf16[512,1024]{1,0:T(8,128)(2,1)S(1)}, u32[]{:S(2)}) copy-start(bf16[512,1024]{1,0:T(8,128)(2,1)S(1)} %collective-permute-done.3.refs_3_.refs_1_.refs_7_) | copy-start | bytes 3145732
  100.9 169.1 %reduce-scatter.3.cloned.1.call-start = ((), (), s32[]{:S(2)}) async-start(), calls=%async_computation.3 | async-start | bytes 1638400 | tf_op jit(solution)/shard_map/reduce_scatter | solution.py:357
  101.0 36.2 %collective-permute-start.9 = (bf16[512,1024]{1,0:T(8,128)(2,1)}, bf16[512,1024]{1,0:T(8,128)(2,1)S(1)}, u32[]{:S(2)}, u32[]{:S(2)}) collective-permute-start(bf16[512,1024]{1,0:T(8,128)(2,1)} %copy-done.3), channel_id=1, source_target_pairs={{0,16},{1,17},{2,18},{3,19},{4,20},{5,21},{6,22},{7,23},{8,24},{9,... | collective-permute-start | bytes 3145736 | tf_op jit(solution)/shard_map/ppermute | solution.py:38
  102.6 34.5 %collective-permute-start.10 = (bf16[512,1024]{1,0:T(8,128)(2,1)}, bf16[512,1024]{1,0:T(8,128)(2,1)}, u32[]{:S(2)}, u32[]{:S(2)}) collective-permute-start(bf16[512,1024]{1,0:T(8,128)(2,1)} %copy-done.3), channel_id=1, source_target_pairs={{0,48},{1,49},{2,50},{3,51},{4,52},{5,53},{6,54},{7,55},{8,56},{9,... | collective-permute-start | bytes 3145736 | tf_op jit(solution)/shard_map/ppermute | solution.py:38
  104.3 11.9 %collective-permute-start.13 = (bf16[2,128,1024]{2,1,0:T(8,128)(2,1)}, bf16[2,128,1024]{2,1,0:T(8,128)(2,1)}, u32[]{:S(2)}, u32[]{:S(2)}) collective-permute-start(bf16[2,128,1024]{2,1,0:T(8,128)(2,1)} %after.11), channel_id=1, source_target_pairs={{0,64},{1,65},{2,66},{3,67},{4,68},{5,69},{6,70},{7,71},{8,72},{9,... | collective-permute-start | bytes 1572872 | tf_op jit(solution)/shard_map/ppermute | solution.py:38
  106.5 30.5 %collective-permute-start.12 = (bf16[256,1024]{1,0:T(8,128)(2,1)}, bf16[256,1024]{1,0:T(8,128)(2,1)S(1)}, u32[]{:S(2)}, u32[]{:S(2)}) collective-permute-start(bf16[256,1024]{1,0:T(8,128)(2,1)} %slice.91), channel_id=1, source_target_pairs={{0,48},{1,49},{2,50},{3,51},{4,52},{5,53},{6,54},{7,55},{8,56},{9,... | collective-permute-start | bytes 1572872 | tf_op jit(solution)/shard_map/ppermute | solution.py:38
  109.0 28.1 %collective-permute-start.11 = (bf16[256,1024]{1,0:T(8,128)(2,1)}, bf16[256,1024]{1,0:T(8,128)(2,1)S(1)}, u32[]{:S(2)}, u32[]{:S(2)}) collective-permute-start(bf16[256,1024]{1,0:T(8,128)(2,1)} %after.10), channel_id=1, source_target_pairs={{0,16},{1,17},{2,18},{3,19},{4,20},{5,21},{6,22},{7,23},{8,24},{9,... | collective-permute-start | bytes 1572872 | tf_op jit(solution)/shard_map/ppermute | solution.py:38
  144.7 19.6 %collective-permute-start.16 = (bf16[8,640,512]{2,1,0:T(8,128)(2,1)}, bf16[8,640,512]{2,1,0:T(8,128)(2,1)}, u32[]{:S(2)}, u32[]{:S(2)}) collective-permute-start(bf16[8,640,512]{2,1,0:T(8,128)(2,1)} %norm.1.refs_0_.refs_1_.refs_2_.refs_3_.refs_4_.refs_5_), channel_id=1, source_target_pairs={{0,8},{1,9},{2,10},{3,11},{4,12},{5,13},{6,14},{7,15},{8,0},{9,1},... | collective-permute-start | bytes 15728648 | tf_op jit(solution)/shard_map/ppermute | solution.py:38
  146.9 33.3 %collective-permute-start.17 = (bf16[2,2,128,1024]{3,2,1,0:T(8,128)(2,1)}, bf16[2,2,128,1024]{3,2,1,0:T(8,128)(2,1)}, u32[]{:S(2)}, u32[]{:S(2)}) collective-permute-start(bf16[2,2,128,1024]{3,2,1,0:T(8,128)(2,1)} %after.12.refs_0_), channel_id=1, source_target_pairs={{0,16},{1,17},{2,18},{3,19},{4,20},{5,21},{6,22},{7,23},{8,24},{9,... | collective-permute-start | bytes 3145736 | tf_op jit(solution)/shard_map/ppermute | solution.py:38
  148.1 32.1 %collective-permute-start.18 = (bf16[2,2,128,1024]{3,2,1,0:T(8,128)(2,1)}, bf16[2,2,128,1024]{3,2,1,0:T(8,128)(2,1)}, u32[]{:S(2)}, u32[]{:S(2)}) collective-permute-start(bf16[2,2,128,1024]{3,2,1,0:T(8,128)(2,1)} %after.12.refs_0_), channel_id=1, source_target_pairs={{0,48},{1,49},{2,50},{3,51},{4,52},{5,53},{6,54},{7,55},{8,56},{9,... | collective-permute-start | bytes 3145736 | tf_op jit(solution)/shard_map/ppermute | solution.py:38
  150.2 21.3 %collective-permute-start.15 = (bf16[256,1024]{1,0:T(8,128)(2,1)}, bf16[256,1024]{1,0:T(8,128)(2,1)}, u32[]{:S(2)}, u32[]{:S(2)}) collective-permute-start(bf16[256,1024]{1,0:T(8,128)(2,1)} %copy-done.16), channel_id=1, source_target_pairs={{0,64},{1,65},{2,66},{3,67},{4,68},{5,69},{6,70},{7,71},{8,72},{9,... | collective-permute-start | bytes 1572872 | tf_op jit(solution)/shard_map/ppermute | solution.py:38
  151.6 24.1 %collective-permute-start.14 = (bf16[256,1024]{1,0:T(8,128)(2,1)}, bf16[256,1024]{1,0:T(8,128)(2,1)}, u32[]{:S(2)}, u32[]{:S(2)}) collective-permute-start(bf16[256,1024]{1,0:T(8,128)(2,1)} %copy-done.18), channel_id=1, source_target_pairs={{0,64},{1,65},{2,66},{3,67},{4,68},{5,69},{6,70},{7,71},{8,72},{9,... | collective-permute-start | bytes 1572872 | tf_op jit(solution)/shard_map/ppermute | solution.py:38
  157.8 22.4 %slice-start = ((s8[5242880]{0:T(1024)(128)(4,1)}), s8[4194304]{0:T(1024)(128)(4,1)S(1)}, s32[]{:S(2)}) async-start(s8[5242880]{0:T(1024)(128)(4,1)} %bitcast.54), calls=%async_computation.7 | async-start | bytes 8388608
  164.3 11.4 %copy-start.17 = (bf16[256,1024]{1,0:T(8,128)(2,1)S(1)}, bf16[256,1024]{1,0:T(8,128)(2,1)}, u32[]{:S(2)}) copy-start(bf16[256,1024]{1,0:T(8,128)(2,1)} %copy-done.16) | copy-start | bytes 1572868
  164.3 11.4 %copy-start.19 = (bf16[256,1024]{1,0:T(8,128)(2,1)S(1)}, bf16[256,1024]{1,0:T(8,128)(2,1)}, u32[]{:S(2)}) copy-start(bf16[256,1024]{1,0:T(8,128)(2,1)} %copy-done.18) | copy-start | bytes 1572868
  164.3 15.9 %slice-start.1 = ((s8[5242880]{0:T(1024)(128)(4,1)}), s8[1048576]{0:T(1024)(128)(4,1)S(1)}, s32[]{:S(2)}) async-start(s8[5242880]{0:T(1024)(128)(4,1)} %bitcast.54), calls=%async_computation.8 | async-start | bytes 2097152
  193.0 9.3 %collective-permute-start.19 = (bf16[4,640,256]{2,1,0:T(8,128)(2,1)}, bf16[4,640,256]{2,1,0:T(8,128)(2,1)S(1)}, u32[]{:S(2)}, u32[]{:S(2)}) collective-permute-start(bf16[4,640,256]{2,1,0:T(8,128)(2,1)} %get-tuple-element.24.refs_5_), channel_id=1, source_target_pairs={{0,8},{1,9},{2,10},{3,11},{4,12},{5,13},{6,14},{7,15},{8,0},{9,1},... | collective-permute-start | bytes 3932168 | tf_op jit(solution)/shard_map/ppermute | solution.py:38
  200.7 3.5 %collective-permute-start.21 = (bf16[4,640,256]{2,1,0:T(8,128)(2,1)}, bf16[4,640,256]{2,1,0:T(8,128)(2,1)}, u32[]{:S(2)}, u32[]{:S(2)}) collective-permute-start(bf16[4,640,256]{2,1,0:T(8,128)(2,1)} %get-tuple-element.26.refs_5_), channel_id=1, source_target_pairs={{0,8},{1,9},{2,10},{3,11},{4,12},{5,13},{6,14},{7,15},{8,0},{9,1},... | collective-permute-start | bytes 3932168 | tf_op jit(solution)/shard_map/ppermute | solution.py:38
  202.2 34.7 %collective-permute-start.26 = (bf16[2,128,1024]{2,1,0:T(8,128)(2,1)S(1)}, bf16[2,128,1024]{2,1,0:T(8,128)(2,1)S(1)}, u32[]{:S(2)}, u32[]{:S(2)}) collective-permute-start(bf16[2,128,1024]{2,1,0:T(8,128)(2,1)S(1)} %slice_bitcast_fusion.1), channel_id=1, source_target_pairs={{0,16},{1,17},{2,18},{3,19},{4,20},{5,21},{6,22},{7,23},{8,24},{9,... | collective-permute-start | bytes 1572872 | tf_op jit(solution)/shard_map/ppermute | solution.py:38
  203.7 92.3 %reduce-scatter.5.cloned.1.call-start = ((), (), s32[]{:S(2)}) async-start(), calls=%async_computation.4 | async-start | bytes 1638400 | tf_op jit(solution)/shard_map/reduce_scatter | solution.py:357
  206.4 30.5 %copy-start.26 = (bf16[640,256]{1,0:T(8,128)(2,1)}, bf16[640,256]{1,0:T(8,128)(2,1)S(1)}, u32[]{:S(2)}) copy-start(bf16[640,256]{1,0:T(8,128)(2,1)S(1)} %get-tuple-element.36.refs_7_) | copy-start | bytes 983044
  206.4 12.9 %collective-permute-start.22 = (bf16[640,256]{1,0:T(8,128)(2,1)S(1)}, bf16[640,256]{1,0:T(8,128)(2,1)S(1)}, u32[]{:S(2)}, u32[]{:S(2)}) collective-permute-start(bf16[640,256]{1,0:T(8,128)(2,1)S(1)} %get-tuple-element.36.refs_7_), channel_id=1, source_target_pairs={{0,2},{1,3},{2,4},{3,5},{4,6},{5,7},{6,0},{7,1},{8,10},{9,11},{10,... | collective-permute-start | bytes 983048 | tf_op jit(solution)/shard_map/ppermute | solution.py:38
  208.6 26.5 %collective-permute-start.23 = (bf16[640,256]{1,0:T(8,128)(2,1)S(1)}, bf16[640,256]{1,0:T(8,128)(2,1)S(1)}, u32[]{:S(2)}, u32[]{:S(2)}) collective-permute-start(bf16[640,256]{1,0:T(8,128)(2,1)S(1)} %get-tuple-element.34), channel_id=1, source_target_pairs={{0,4},{1,5},{2,6},{3,7},{4,0},{5,1},{6,2},{7,3},{8,12},{9,13},{10,... | collective-permute-start | bytes 983048 | tf_op jit(solution)/shard_map/ppermute | solution.py:38
  211.4 23.6 %collective-permute-start.24 = (bf16[640,256]{1,0:T(8,128)(2,1)S(1)}, bf16[640,256]{1,0:T(8,128)(2,1)S(1)}, u32[]{:S(2)}, u32[]{:S(2)}) collective-permute-start(bf16[640,256]{1,0:T(8,128)(2,1)S(1)} %get-tuple-element.35), channel_id=1, source_target_pairs={{0,6},{1,7},{2,0},{3,1},{4,2},{5,3},{6,4},{7,5},{8,14},{9,15},{10,... | collective-permute-start | bytes 983048 | tf_op jit(solution)/shard_map/ppermute | solution.py:38
  214.0 23.0 %collective-permute-start.27 = (bf16[2,128,1024]{2,1,0:T(8,128)(2,1)S(1)}, bf16[2,128,1024]{2,1,0:T(8,128)(2,1)S(1)}, u32[]{:S(2)}, u32[]{:S(2)}) collective-permute-start(bf16[2,128,1024]{2,1,0:T(8,128)(2,1)S(1)} %slice_bitcast_fusion), channel_id=1, source_target_pairs={{0,48},{1,49},{2,50},{3,51},{4,52},{5,53},{6,54},{7,55},{8,56},{9,... | collective-permute-start | bytes 1572872 | tf_op jit(solution)/shard_map/ppermute | solution.py:38
  244.9 3.2 %collective-permute-start.28 = (bf16[4,640,256]{2,1,0:T(8,128)(2,1)}, bf16[4,640,256]{2,1,0:T(8,128)(2,1)S(1)}, u32[]{:S(2)}, u32[]{:S(2)}) collective-permute-start(bf16[4,640,256]{2,1,0:T(8,128)(2,1)} %get-tuple-element.28.refs_5_), channel_id=1, source_target_pairs={{0,8},{1,9},{2,10},{3,11},{4,12},{5,13},{6,14},{7,15},{8,0},{9,1},... | collective-permute-start | bytes 3932168 | tf_op jit(solution)/shard_map/ppermute | solution.py:38
  258.0 3.2 %collective-permute-start.30 = (bf16[4,640,256]{2,1,0:T(8,128)(2,1)}, bf16[4,640,256]{2,1,0:T(8,128)(2,1)S(1)}, u32[]{:S(2)}, u32[]{:S(2)}) collective-permute-start(bf16[4,640,256]{2,1,0:T(8,128)(2,1)} %get-tuple-element.30), channel_id=1, source_target_pairs={{0,8},{1,9},{2,10},{3,11},{4,12},{5,13},{6,14},{7,15},{8,0},{9,1},... | collective-permute-start | bytes 3932168 | tf_op jit(solution)/shard_map/ppermute | solution.py:38
  258.2 11.8 %collective-permute-start.25 = (bf16[640,128]{1,0:T(8,128)(2,1)S(1)}, bf16[640,128]{1,0:T(8,128)(2,1)S(1)}, u32[]{:S(2)}, u32[]{:S(2)}) collective-permute-start(bf16[640,128]{1,0:T(8,128)(2,1)S(1)} %constant_dynamic-slice_fusion.1), channel_id=1, source_target_pairs={{0,1},{1,0},{2,3},{3,2},{4,5},{5,4},{6,7},{7,6},{8,9},{9,8},{10,11... | collective-permute-start | bytes 491528 | tf_op jit(solution)/shard_map/ppermute | solution.py:38
  263.5 18.3 %collective-permute-start.31 = (bf16[640,256]{1,0:T(8,128)(2,1)}, bf16[640,256]{1,0:T(8,128)(2,1)S(1)}, u32[]{:S(2)}, u32[]{:S(2)}) collective-permute-start(bf16[640,256]{1,0:T(8,128)(2,1)} %get-tuple-element.31), channel_id=1, source_target_pairs={{0,2},{1,3},{2,4},{3,5},{4,6},{5,7},{6,0},{7,1},{8,10},{9,11},{10,... | collective-permute-start | bytes 983048 | tf_op jit(solution)/shard_map/ppermute | solution.py:38
  263.5 25.9 %collective-permute-start.32 = (bf16[640,256]{1,0:T(8,128)(2,1)}, bf16[640,256]{1,0:T(8,128)(2,1)S(1)}, u32[]{:S(2)}, u32[]{:S(2)}) collective-permute-start(bf16[640,256]{1,0:T(8,128)(2,1)} %get-tuple-element.33), channel_id=1, source_target_pairs={{0,4},{1,5},{2,6},{3,7},{4,0},{5,1},{6,2},{7,3},{8,12},{9,13},{10,... | collective-permute-start | bytes 983048 | tf_op jit(solution)/shard_map/ppermute | solution.py:38
  267.3 22.1 %collective-permute-start.33 = (bf16[640,256]{1,0:T(8,128)(2,1)S(1)}, bf16[640,256]{1,0:T(8,128)(2,1)}, u32[]{:S(2)}, u32[]{:S(2)}) collective-permute-start(bf16[640,256]{1,0:T(8,128)(2,1)S(1)} %get-tuple-element.32), channel_id=1, source_target_pairs={{0,6},{1,7},{2,0},{3,1},{4,2},{5,3},{6,4},{7,5},{8,14},{9,15},{10,... | collective-permute-start | bytes 983048 | tf_op jit(solution)/shard_map/ppermute | solution.py:38
  270.0 20.7 %copy-start.29 = (bf16[640,128]{1,0:T(8,128)(2,1)}, bf16[640,128]{1,0:T(8,128)(2,1)S(1)}, u32[]{:S(2)}) copy-start(bf16[640,128]{1,0:T(8,128)(2,1)S(1)} %collective-permute-done.25.refs_2_) | copy-start | bytes 491524
  271.0 24.1 %copy-start.31 = (bf16[1,640,256]{2,1,0:T(8,128)(2,1)S(1)}, bf16[1,640,256]{2,1,0:T(8,128)(2,1)}, u32[]{:S(2)}) copy-start(bf16[1,640,256]{2,1,0:T(8,128)(2,1)} %reduce-scatter.3.cloned.1.call-done) | copy-start | bytes 983044
  271.0 20.4 %collective-permute-start.20 = (bf16[640,128]{1,0:T(8,128)(2,1)S(1)}, bf16[640,128]{1,0:T(8,128)(2,1)S(1)}, u32[]{:S(2)}, u32[]{:S(2)}) collective-permute-start(bf16[640,128]{1,0:T(8,128)(2,1)S(1)} %dynamic-slice_bitcast_fusion.1), channel_id=1, source_target_pairs={{0,1},{1,0},{2,3},{3,2},{4,5},{5,4},{6,7},{7,6},{8,9},{9,8},{10,11... | collective-permute-start | bytes 491528 | tf_op jit(solution)/shard_map/ppermute | solution.py:38
  292.0 7.9 %collective-permute-start.34 = (bf16[640,128]{1,0:T(8,128)(2,1)}, bf16[640,128]{1,0:T(8,128)(2,1)S(1)}, u32[]{:S(2)}, u32[]{:S(2)}) collective-permute-start(bf16[640,128]{1,0:T(8,128)(2,1)} %after.13), channel_id=1, source_target_pairs={{0,1},{1,0},{2,3},{3,2},{4,5},{5,4},{6,7},{7,6},{8,9},{9,8},{10,11... | collective-permute-start | bytes 491528 | tf_op jit(solution)/shard_map/ppermute | solution.py:38
  297.0 7.3 %collective-permute-start.29 = (bf16[640,128]{1,0:T(8,128)(2,1)S(1)}, bf16[640,128]{1,0:T(8,128)(2,1)S(1)}, u32[]{:S(2)}, u32[]{:S(2)}) collective-permute-start(bf16[640,128]{1,0:T(8,128)(2,1)S(1)} %dynamic-slice_bitcast_fusion), channel_id=1, source_target_pairs={{0,1},{1,0},{2,3},{3,2},{4,5},{5,4},{6,7},{7,6},{8,9},{9,8},{10,11... | collective-permute-start | bytes 491528 | tf_op jit(solution)/shard_map/ppermute | solution.py:38
  (27 other events, 101.5 us)
Sparse Core Ops, SparseCore 0:
  9.7 42.9 all-gather.4
  101.0 35.8 all-gather.6
  203.8 34.1 reduce-scatter.2
  251.0 35.3 reduce-scatter.4
